TPU v7x, 256 devices: a whole 4x4x8 slice. The times are simulated.
256 devices in a mesh: space: 32 (over z_lo, x, y), chan: 8 (over z_hi, core).
Axes of the slice: x: 4, y: 4, z: 8 (z_hi: 4, z_lo: 2; z = z_hi * 2 + z_lo), core: 2. Of those that a mesh axis runs over, the one named last changes fastest.
Arguments:
- volume: bfloat16 [128, 32, 64, 128], P('chan', 'space'), may hold values from -6 to 6
- weight_one: bfloat16 [27, 128, 128], replicated, may hold values from -0.109375 to 0.109375
- bias_one: float32 [128], replicated, may hold values from -3 to 3
- weight_two: bfloat16 [27, 128, 128], replicated, may hold values from -0.109375 to 0.109375
- bias_two: float32 [128], replicated, may hold values from -3 to 3
Outputs:
- features: bfloat16 [128, 32, 64, 128], P('chan', 'space')
All inputs are finite; a program needn't handle non-finite values.
Results may differ from a plain program's by a relative error of at most 0.0045.
Values may be sent and summed in bfloat16 or wider, within the bound.
No kernel may reach another device: no remote copies, remote signals or barrier semaphores. Data moves between devices by JAX's collectives and lax.ppermute only.
A program may use at most 64 MiB of HBM per device.

v0:
```python
import jax
import jax.numpy as jnp
from jax import lax
from jax.sharding import PartitionSpec as P


def extended(array, sides, width):
    for axis, dim in sides:
        count, length = (lax.axis_size(axis), array.shape[dim])
        up = [(i, (i + 1) % count) for i in range(count - 1)]
        down = [(j, i) for i, j in up]
        last = lax.slice_in_dim(array, length - width, length, axis=dim)
        initial = lax.slice_in_dim(array, 0, width, axis=dim)
        before = lax.ppermute(last, axis, up)
        after = lax.ppermute(initial, axis, down)
        array = jnp.concatenate([before, array, after], axis=dim)
    return array


def convolve(rimmed, kernel, planes):
    rows_out = rimmed.shape[2]
    depth = rimmed.shape[3]
    summed = None
    for shift_x in range(3):
        slab_in = rimmed[:, shift_x : shift_x + planes]
        tap_weights = kernel[9 * shift_x : 9 * shift_x + 9]
        products = jnp.einsum(
            "tio,ixyz->toxyz", tap_weights, slab_in, preferred_element_type=jnp.float32
        )
        padded = jnp.pad(products, ((0, 0), (0, 0), (0, 0), (1, 1), (1, 1)))
        for shift_y in range(3):
            for shift_z in range(3):
                term = padded[
                    3 * shift_y + shift_z,
                    :,
                    :,
                    shift_y : shift_y + rows_out,
                    shift_z : shift_z + depth,
                ]
                summed = term if summed is None else summed + term
    return summed


def per_device(volume, weight_one, bias_one, weight_two, bias_two):
    slices = volume.shape[0]
    planes = volume.shape[1]
    layers = ((weight_one, bias_one), (weight_two, bias_two))
    first_filter = lax.axis_index("chan") * slices
    current = volume
    for kernel, offsets in layers:
        gathered = lax.all_gather(current, "chan", axis=0, tiled=True)
        rimmed = extended(gathered, (("space", 1),), 1)
        own_kernel = lax.dynamic_slice_in_dim(kernel, first_filter, slices, 2)
        own_offsets = lax.dynamic_slice_in_dim(offsets, first_filter, slices, 0)
        summed = convolve(rimmed, own_kernel, planes)
        current = jax.nn.relu(summed + own_offsets[:, None, None, None]).astype(jnp.bfloat16)
    return current


def solution(mesh):
    placed = (P("chan", "space", None, None), P(), P(), P(), P())
    return jax.shard_map(
        per_device,
        mesh=mesh,
        in_specs=placed,
        out_specs=P("chan", "space", None, None),
        check_vma=False,
    )
```

profile of v0, /device:TPU:31, one launch (start us, length us, event | category | flops | bytes accessed | tf_op | source)
XLA Modules:
  0.0 218.4 jit_solution(15522419170952133631)
XLA Ops:
  6.5 0.0 copy-start
  6.5 0.0 all-gather.3.cloned.1.call-start
  6.5 1.9 copy.8
  8.4 0.0 all-gather.3.cloned.1.call-update
  8.5 0.0 all-gather.5.cloned.1.call-start
  8.5 44.5 %all-gather.3.cloned.1.call-done = bf16[128,1,64,128]{3,0,2,1:T(8,128)(2,1)} async-done(((bf16[16,1,64,128]{3,0,2,1:T(8,128)(2,1)}), bf16[128,1,64,128]{3,0,2,1:T(8,128)(2,1)}) %all-gather.3.cloned.1.call-update) | async-done | bytes 2097168 | tf_op jit(solution)/shard_map/all_gather | solution.py:51
  53.0 1.9 collective-permute-start
  54.9 3.4 %collective-permute-start.1 = (bf16[128,1,64,128]{3,0,2,1:T(8,128)(2,1)}, bf16[128,1,64,128]{3,0,2,1:T(8,128)(2,1)}, u32[]{:S(2)}, u32[]{:S(2)}) collective-permute-start(bf16[128,1,64,128]{3,0,2,1:T(8,128)(2,1)} %all-gather.3.cloned.1.call-done), channel_id=1, source_target_pairs={{8,0},{16,8},{24,16},{32,24},{40,32},{48,40},{56,48},{64,56},{72,6... | collective-permute-start | bytes 6291464 | tf_op jit(solution)/shard_map/ppermute | solution.py:15
  58.3 0.7 dynamic_slice.14
  59.0 0.0 copy-done
  59.0 2.5 %fusion.8 = f32[9,16,64,128]{3,1,2,0:T(8,128)S(1)} fusion(bf16[128,1,64,128]{3,0,2,1:T(8,128)(2,1)} %all-gather.3.cloned.1.call-done, bf16[27,128,128]{2,1,0:T(8,128)(2,1)S(1)} %copy-done, s32[]{:T(128)S(6)} %add.691, s32[]{:T(128)S(6)} %select_n.2), kind=kOutput, calls=%fused_computation.56 | convolution fusion | flops 301989888 | bytes 7110664 | tf_op jit(solution)/shard_map/tio,ixyz->toxyz/dot_general | solution.py:27
  61.5 40.6 %collective-permute-done = bf16[128,1,64,128]{3,0,2,1:T(8,128)(2,1)S(1)} collective-permute-done((bf16[128,1,64,128]{3,0,2,1:T(8,128)(2,1)}, bf16[128,1,64,128]{3,0,2,1:T(8,128)(2,1)S(1)}, u32[]{:S(2)}, u32[]{:S(2)}) %collective-permute-start) | collective-permute-done | bytes 2097184 | tf_op jit(solution)/shard_map/ppermute | solution.py:14
  102.2 0.9 fusion.10
  103.1 5.2 %collective-permute-done.1 = bf16[128,1,64,128]{3,0,2,1:T(8,128)(2,1)} collective-permute-done((bf16[128,1,64,128]{3,0,2,1:T(8,128)(2,1)}, bf16[128,1,64,128]{3,0,2,1:T(8,128)(2,1)}, u32[]{:S(2)}, u32[]{:S(2)}) %collective-permute-start.1) | collective-permute-done | bytes 2097184 | tf_op jit(solution)/shard_map/ppermute | solution.py:15
  108.3 2.5 %fusion.6 = f32[9,16,64,128]{3,1,2,0:T(8,128)S(1)} fusion(bf16[128,1,64,128]{3,0,2,1:T(8,128)(2,1)} %collective-permute-done.1, bf16[27,128,128]{2,1,0:T(8,128)(2,1)S(1)} %copy-done, s32[]{:T(128)S(6)} %add.692, s32[]{:T(128)S(6)} %select_n.2), kind=kOutput, calls=%fused_computation.54 | convolution fusion | flops 301989888 | bytes 7110664 | tf_op jit(solution)/shard_map/tio,ixyz->toxyz/dot_general | solution.py:27
  110.8 0.0 copy-start.2
  110.8 0.0 copy-start.1
  110.9 3.2 %maximum_convert_fusion.1 = bf16[16,1,64,128]{3,0,2,1:T(8,128)(2,1)} fusion(f32[9,16,1,64,128]{4,1,3,2,0:T(8,128)S(1)} %bitcast.483, f32[9,16,64,128]{3,1,2,0:T(8,128)S(1)} %fusion.6, f32[9,16,1,64,128]{4,1,3,2,0:T(8,128)S(1)} %bitcast.481, f32[9,16,64,128]{3,1,2,0:T(8,128)S(1)} %fusion.8, f32[9,16,1,64,128]{4,1,3,2,0:T(8,128)S(1)} %bitcast.479, ...), kind=kLoop, calls=%fused_computation.159 | loop fusion | flops 3801088 | bytes 15990848 | tf_op jit(solution)/shard_map/convert_element_type | solution.py:56
  114.0 0.0 all-gather.5.cloned.1.call-update
  114.1 38.1 %all-gather.5.cloned.1.call-done = bf16[128,1,64,128]{3,0,2,1:T(8,128)(2,1)} async-done(((bf16[16,1,64,128]{3,0,2,1:T(8,128)(2,1)}), bf16[128,1,64,128]{3,0,2,1:T(8,128)(2,1)}) %all-gather.5.cloned.1.call-update) | async-done | bytes 2097168 | tf_op jit(solution)/shard_map/all_gather | solution.py:51
  152.2 1.9 collective-permute-start.2
  154.1 3.4 %collective-permute-start.3 = (bf16[128,1,64,128]{3,0,2,1:T(8,128)(2,1)}, bf16[128,1,64,128]{3,0,2,1:T(8,128)(2,1)S(1)}, u32[]{:S(2)}, u32[]{:S(2)}) collective-permute-start(bf16[128,1,64,128]{3,0,2,1:T(8,128)(2,1)} %all-gather.5.cloned.1.call-done), channel_id=1, source_target_pairs={{8,0},{16,8},{24,16},{32,24},{40,32},{48,40},{56,48},{64,56},{72,6... | collective-permute-start | bytes 6291464 | tf_op jit(solution)/shard_map/ppermute | solution.py:15
  157.5 0.0 copy-done.2
  157.5 0.1 dynamic_slice.15
  157.6 0.0 copy-done.1
  157.6 2.5 %fusion.2 = f32[9,16,64,128]{3,1,2,0:T(8,128)S(1)} fusion(bf16[128,1,64,128]{3,0,2,1:T(8,128)(2,1)} %all-gather.5.cloned.1.call-done, bf16[27,128,128]{2,1,0:T(8,128)(2,1)S(1)} %copy-done.1, s32[]{:T(128)S(6)} %add.691, s32[]{:T(128)S(6)} %select_n.2), kind=kOutput, calls=%fused_computation.50 | convolution fusion | flops 301989888 | bytes 7110664 | tf_op jit(solution)/shard_map/tio,ixyz->toxyz/dot_general | solution.py:27
  160.1 41.2 %collective-permute-done.2 = bf16[128,1,64,128]{3,0,2,1:T(8,128)(2,1)S(1)} collective-permute-done((bf16[128,1,64,128]{3,0,2,1:T(8,128)(2,1)}, bf16[128,1,64,128]{3,0,2,1:T(8,128)(2,1)S(1)}, u32[]{:S(2)}, u32[]{:S(2)}) %collective-permute-start.2) | collective-permute-done | bytes 2097184 | tf_op jit(solution)/shard_map/ppermute | solution.py:14
  201.2 0.9 fusion.4
  202.2 5.2 %collective-permute-done.3 = bf16[128,1,64,128]{3,0,2,1:T(8,128)(2,1)S(1)} collective-permute-done((bf16[128,1,64,128]{3,0,2,1:T(8,128)(2,1)}, bf16[128,1,64,128]{3,0,2,1:T(8,128)(2,1)S(1)}, u32[]{:S(2)}, u32[]{:S(2)}) %collective-permute-start.3) | collective-permute-done | bytes 2097184 | tf_op jit(solution)/shard_map/ppermute | solution.py:15
  207.4 0.9 fusion
  208.3 2.5 %maximum_convert_fusion = bf16[16,1,64,128]{3,0,2,1:T(8,128)(2,1)S(1)} fusion(f32[9,16,1,64,128]{4,1,3,2,0:T(8,128)S(1)} %bitcast.482, f32[9,16,64,128]{3,1,2,0:T(8,128)S(1)} %fusion, f32[9,16,1,64,128]{4,1,3,2,0:T(8,128)S(1)} %bitcast.480, f32[9,16,64,128]{3,1,2,0:T(8,128)S(1)} %fusion.2, f32[9,16,1,64,128]{4,1,3,2,0:T(8,128)S(1)} %bitcast.478, ...), kind=kLoop, calls=%fused_computation.158 | loop fusion | flops 3801088 | bytes 15990848 | tf_op jit(solution)/shard_map/convert_element_type | solution.py:56
  210.8 0.8 copy.9
Async XLA Ops:
  6.5 52.5 %copy-start = (bf16[27,128,128]{2,1,0:T(8,128)(2,1)S(1)}, bf16[27,128,128]{2,1,0:T(8,128)(2,1)}, u32[]{:S(2)}) copy-start(bf16[27,128,128]{2,1,0:T(8,128)(2,1)} %param.6) | copy-start | bytes 2654212
  6.5 46.5 %all-gather.3.cloned.1.call-start = ((), (), s32[]{:S(2)}) async-start(), calls=%async_computation | async-start | bytes 2359296 | tf_op jit(solution)/shard_map/all_gather | solution.py:51
  8.5 143.7 %all-gather.5.cloned.1.call-start = ((), (), s32[]{:S(2)}) async-start(), calls=%async_computation.1 | async-start | bytes 2359296 | tf_op jit(solution)/shard_map/all_gather | solution.py:51
  53.0 49.2 %collective-permute-start = (bf16[128,1,64,128]{3,0,2,1:T(8,128)(2,1)}, bf16[128,1,64,128]{3,0,2,1:T(8,128)(2,1)S(1)}, u32[]{:S(2)}, u32[]{:S(2)}) collective-permute-start(bf16[128,1,64,128]{3,0,2,1:T(8,128)(2,1)} %all-gather.3.cloned.1.call-done), channel_id=1, source_target_pairs={{0,8},{8,16},{16,24},{24,32},{32,40},{40,48},{48,56},{56,64},{64,7... | collective-permute-start | bytes 6291464 | tf_op jit(solution)/shard_map/ppermute | solution.py:14
  54.9 53.4 %collective-permute-start.1 = (bf16[128,1,64,128]{3,0,2,1:T(8,128)(2,1)}, bf16[128,1,64,128]{3,0,2,1:T(8,128)(2,1)}, u32[]{:S(2)}, u32[]{:S(2)}) collective-permute-start(bf16[128,1,64,128]{3,0,2,1:T(8,128)(2,1)} %all-gather.3.cloned.1.call-done), channel_id=1, source_target_pairs={{8,0},{16,8},{24,16},{32,24},{40,32},{48,40},{56,48},{64,56},{72,6... | collective-permute-start | bytes 6291464 | tf_op jit(solution)/shard_map/ppermute | solution.py:15
  110.8 46.6 %copy-start.2 = (f32[128]{0:T(128)S(1)}, f32[128]{0:T(128)}, u32[]{:S(2)}) copy-start(f32[128]{0:T(128)} %param.9) | copy-start | bytes 1540
  110.8 46.7 %copy-start.1 = (bf16[27,128,128]{2,1,0:T(8,128)(2,1)S(1)}, bf16[27,128,128]{2,1,0:T(8,128)(2,1)}, u32[]{:S(2)}) copy-start(bf16[27,128,128]{2,1,0:T(8,128)(2,1)} %param.8) | copy-start | bytes 2654212
  152.2 49.1 %collective-permute-start.2 = (bf16[128,1,64,128]{3,0,2,1:T(8,128)(2,1)}, bf16[128,1,64,128]{3,0,2,1:T(8,128)(2,1)S(1)}, u32[]{:S(2)}, u32[]{:S(2)}) collective-permute-start(bf16[128,1,64,128]{3,0,2,1:T(8,128)(2,1)} %all-gather.5.cloned.1.call-done), channel_id=1, source_target_pairs={{0,8},{8,16},{16,24},{24,32},{32,40},{40,48},{48,56},{56,64},{64,7... | collective-permute-start | bytes 6291464 | tf_op jit(solution)/shard_map/ppermute | solution.py:14
  154.1 53.3 %collective-permute-start.3 = (bf16[128,1,64,128]{3,0,2,1:T(8,128)(2,1)}, bf16[128,1,64,128]{3,0,2,1:T(8,128)(2,1)S(1)}, u32[]{:S(2)}, u32[]{:S(2)}) collective-permute-start(bf16[128,1,64,128]{3,0,2,1:T(8,128)(2,1)} %all-gather.5.cloned.1.call-done), channel_id=1, source_target_pairs={{8,0},{16,8},{24,16},{32,24},{40,32},{48,40},{56,48},{64,56},{72,6... | collective-permute-start | bytes 6291464 | tf_op jit(solution)/shard_map/ppermute | solution.py:15
Sparse Core Ops, SparseCore 0:
  9.2 43.7 all-gather.2
  114.2 37.9 all-gather.4
where the time goes:
time: 219 us; the launch traced here: 218 us
  waiting for transfers between devices  175 us (80%)
  between operations  13.5 us (6%)
  starting transfers between devices  10.6 us (5%)
  matrix products  10.4 us (5%)
  other arithmetic  5.65 us (3%)
  local copies, waits for them, and re-layouts  3.51 us (2%)
    all_gather x2, waiting for transfers between devices, per_device(): gathered = lax.all_gather(current, 'chan', axis=0, tiled=True)  82.6 us
    ppermute x2, waiting for transfers between devices, extended(): before = lax.ppermute(last, axis, up)  81.8 us
    ppermute x2, waiting for transfers between devices, extended(): after = lax.ppermute(initial, axis, down)  10.4 us
    dot_general x6, matrix products, convolve(): jnp.einsum('tio,ixyz->toxyz', tap_weights, slab_in, preferred_element_typ...  10.4 us
    ppermute x2, starting transfers between devices, extended(): after = lax.ppermute(initial, axis, down)  6.72 us
    convert_element_type x2, other arithmetic, per_device(): jax.nn.relu(summed + own_offsets[:, None, None, None]).astype(jnp.bfloat16)  5.65 us
  transfers between devices with their start and end apart: 6, of which 6 were waited for; matrix products, arithmetic and copies ran while one was open for 4% of the time, Pallas kernels for 0%

commit v1 on v0

v1 whole, which is shorter than its diff:
```python
import jax
import jax.numpy as jnp
from jax import lax
from jax.experimental import pallas as pl
from jax.experimental.pallas import tpu as pltpu
from jax.sharding import PartitionSpec as P

BF16 = jnp.bfloat16
F32 = jnp.float32


def along_lanes(total, lanes):
    chans = total.shape[0] // 3
    lane = lax.broadcasted_iota(jnp.int32, (chans, lanes), 1)
    low = pltpu.roll(total[:chans], 1, 1)
    high = pltpu.roll(total[2 * chans :], lanes - 1, 1)
    return (
        total[chans : 2 * chans]
        + jnp.where(lane == 0, 0.0, low)
        + jnp.where(lane == lanes - 1, 0.0, high)
    )


def conv_rows(get, weight, bias, store, rows, lanes):
    for start in range(0, rows, 2):
        parts = []
        for a in range(3):
            for e in range(3):
                pair = [get(a, start + e + n) for n in range(2)]
                parts.append(jnp.concatenate(pair, axis=1))
        stacked = jnp.concatenate(parts, axis=0)
        total = jnp.dot(weight, stacked, preferred_element_type=F32)
        for n in range(2):
            u = along_lanes(total[:, n * lanes : (n + 1) * lanes], lanes)
            store(start + n, jnp.maximum(u + bias, 0.0))


def first_kernel(block_ref, before_ref, own_ref, after_ref, weight_ref, bias_ref, out_ref):
    refs = (before_ref, own_ref, after_ref)
    groups = own_ref.shape[0]
    rows, _, lanes = out_ref.shape
    block = block_ref[0]

    def get(a, row):
        return jnp.concatenate([refs[a][g, row] for g in range(groups)], axis=0)

    def store(row, value):
        if row == 0:
            value = jnp.where(block == 0, 0.0, value)
        if row == rows - 1:
            value = jnp.where(block == block_ref[1] - 1, 0.0, value)
        out_ref[row] = value.astype(BF16)

    conv_rows(get, weight_ref[...], bias_ref[...], store, rows, lanes)


def second_kernel(before_ref, own_ref, after_ref, weight_ref, bias_ref, out_ref):
    refs = (before_ref, own_ref, after_ref)
    cores, groups, rows, width, lanes = out_ref.shape

    def get(a, row):
        return refs[a][row]

    def store(row, value):
        value = value.astype(BF16)
        for g in range(groups):
            for c in range(cores):
                at = (g * cores + c) * width
                out_ref[c, g, row] = value[at : at + width]

    conv_rows(get, weight_ref[...], bias_ref[...], store, rows, lanes)


def arranged(weight):
    _, inner, outer = weight.shape
    taps = weight.reshape(9, 3, inner, outer)
    return taps.transpose(1, 3, 0, 2).reshape(3 * outer, 9 * inner)


def solution(mesh):
    space = mesh.shape["space"]
    chan = mesh.shape["chan"]
    cores = 2
    groups = chan // cores
    up = [(i, i + 1) for i in range(space - 1)]
    down = [(i + 1, i) for i in range(space - 1)]
    swap = [(i, i ^ 1) for i in range(chan)]

    def ahead(k):
        return [(i, (i + cores * k) % chan) for i in range(chan)]

    vmem = pl.BlockSpec(memory_space=pltpu.VMEM)
    smem = pl.BlockSpec(memory_space=pltpu.SMEM)

    def per_device(volume, weight_one, bias_one, weight_two, bias_two):
        width, _, length, lanes = volume.shape
        full = width * chan
        rows = length // chan
        index = lax.axis_index("chan")
        group, core = index // cores, index % cores

        one = arranged(weight_one)
        two = arranged(weight_two)

        flat = volume[:, 0].transpose(1, 0, 2)
        flat = jnp.pad(flat, ((2, 2), (0, 0), (0, 0)))
        blocks = jnp.stack([flat[rows * i : rows * i + rows + 4] for i in range(chan)])
        blocks = blocks.reshape(groups, cores, rows + 4, width, lanes)
        mine = lax.dynamic_index_in_dim(blocks, core, 1, keepdims=False)
        theirs = lax.dynamic_index_in_dim(blocks, 1 - core, 1, keepdims=False)
        swapped = lax.ppermute(theirs, "chan", swap)
        first = jnp.where(core == 0, mine, swapped)
        second = jnp.where(core == 0, swapped, mine)
        both = jnp.concatenate([first, second], axis=2)
        whole = both
        for k in range(1, groups):
            sent = lax.dynamic_index_in_dim(both, (group + k) % groups, 0, keepdims=True)
            got = lax.ppermute(sent, "chan", ahead(k))
            whole = lax.dynamic_update_slice_in_dim(whole, got, (group + groups - k) % groups, 0)

        before = lax.ppermute(whole, "space", up)
        after = lax.ppermute(whole, "space", down)
        where = jnp.stack([index.astype(jnp.int32), jnp.int32(chan)])
        hidden = pl.pallas_call(
            first_kernel,
            out_shape=jax.ShapeDtypeStruct((rows + 2, full, lanes), BF16),
            in_specs=[smem] + [vmem] * 5,
            out_specs=vmem,
            name="first_layer",
        )(where, before, whole, after, one, bias_one[:, None])

        before = lax.ppermute(hidden, "space", up)
        after = lax.ppermute(hidden, "space", down)
        out = pl.pallas_call(
            second_kernel,
            out_shape=jax.ShapeDtypeStruct((cores, groups, rows, width, lanes), BF16),
            in_specs=[vmem] * 5,
            out_specs=vmem,
            name="second_layer",
        )(before, hidden, after, two, bias_two[:, None])

        back = out
        for k in range(1, groups):
            sent = lax.dynamic_index_in_dim(out, (group + k) % groups, 1, keepdims=True)
            got = lax.ppermute(sent, "chan", ahead(k))
            back = lax.dynamic_update_slice_in_dim(back, got, (group + groups - k) % groups, 1)
        mine = lax.dynamic_index_in_dim(back, core, 0, keepdims=False)
        theirs = lax.dynamic_index_in_dim(back, 1 - core, 0, keepdims=False)
        swapped = lax.ppermute(theirs, "chan", swap)
        first = jnp.where(core == 0, mine, swapped)
        second = jnp.where(core == 0, swapped, mine)
        features = jnp.stack([first, second], axis=1).reshape(length, width, lanes)
        return features.transpose(1, 0, 2)[:, None]

    placed = (P("chan", "space", None, None), P(), P(), P(), P())
    return jax.shard_map(
        per_device,
        mesh=mesh,
        in_specs=placed,
        out_specs=P("chan", "space", None, None),
        check_vma=False,
    )
```

time: 219 us -> 94.8 us (0.43)
  waiting for transfers between devices: 175 us -> 36.2 us
  starting transfers between devices: 10.6 us -> 29 us
  local copies, waits for them, and re-layouts: 3.51 us -> 20 us
  between operations: 13.5 us -> 0.24 us
  matrix products: 10.4 us -> 0 us
  Pallas kernels: 0 us -> 7.2 us
  other arithmetic: 5.65 us -> 1.65 us
    all_gather x2 -> x0, waiting for transfers between devices: 82.6 us -> none  [per_device(): gathered = lax.all_gather(current, 'chan', axis=0, tiled=True)]
    ppermute x4 -> x12, waiting for transfers between devices: 92.2 us -> 36.2 us  [the longest x6 17.5 us: per_device(): got = lax.ppermute(sent, 'chan', ahead(k))]
    ppermute x4 -> x12, starting transfers between devices: 10.5 us -> 29 us  [the longest x6 13 us: per_device(): got = lax.ppermute(sent, 'chan', ahead(k))]
    dot_general x6 -> x0, matrix products: 10.4 us -> none  [convolve(): jnp.einsum('tio,ixyz->toxyz', tap_weights, slab_in, preferred_element_typ...]
    pallas_call x0 -> x2, Pallas kernels: none -> 7.2 us  [the longest x1 3.78 us: per_device(): pl.pallas_call(first_kernel, out_shape=jax.ShapeDtypeStruct((rows + 2, fu...]
    unnamed x7 -> x30, local copies, waits for them, and re-layouts: 1.92 us -> 8.38 us
    convert_element_type x2 -> x0, other arithmetic: 5.65 us -> none  [per_device(): jax.nn.relu(summed + own_offsets[:, None, None, None]).astype(jnp.bfloat16)]
    reshape x0 -> x4, local copies, waits for them, and re-layouts: none -> 4.64 us  [the longest x2 3.11 us: arranged(): return taps.transpose(1, 3, 0, 2).reshape(3 * outer, 9 * inner)]
  transfers between devices with their start and end apart: 6 -> 12, of which waited for: 6 -> 10; matrix products, arithmetic and copies ran while one was open for 4% -> 8% of each run, Pallas kernels for 0% -> 0%
where the time goes in v1:
time: 94.8 us; the launch traced here: 94.2 us
  waiting for transfers between devices  36.2 us (38%)
  starting transfers between devices  29 us (31%)
  local copies, waits for them, and re-layouts  20 us (21%)
  Pallas kernels  7.2 us (8%)
  other arithmetic  1.65 us (2%)
    ppermute x6, waiting for transfers between devices, per_device(): got = lax.ppermute(sent, 'chan', ahead(k))  17.5 us
    ppermute x6, starting transfers between devices, per_device(): got = lax.ppermute(sent, 'chan', ahead(k))  13 us
    unnamed x30, local copies, waits for them, and re-layouts  8.38 us
    ppermute x1, waiting for transfers between devices, per_device(): after = lax.ppermute(whole, 'space', down)  6.14 us
    ppermute x1, waiting for transfers between devices, per_device(): after = lax.ppermute(hidden, 'space', down)  6.14 us
    ppermute x2, starting transfers between devices, per_device(): swapped = lax.ppermute(theirs, 'chan', swap)  5.41 us
    pallas_call x1, Pallas kernels, per_device(): pl.pallas_call(first_kernel, out_shape=jax.ShapeDtypeStruct((rows + 2, fu...  3.78 us
    pallas_call x1, Pallas kernels, per_device(): pl.pallas_call(second_kernel, out_shape=jax.ShapeDtypeStruct((cores, grou...  3.43 us
  transfers between devices with their start and end apart: 12, of which 10 were waited for; matrix products, arithmetic and copies ran while one was open for 8% of the time, Pallas kernels for 0%

profile of v1, /device:TPU:31, one launch (start us, length us, event | category | flops | bytes accessed | tf_op | source)
XLA Modules:
  0.0 94.2 jit_solution(9754892738199995659)
XLA Ops:
  0.0 0.9 fusion.6
  0.9 0.9 fusion.14
  1.9 0.9 fusion.13
  2.8 0.9 fusion.12
  3.7 0.9 fusion.11
  4.7 0.9 fusion.10
  5.6 0.9 fusion.9
  6.5 0.0 copy-done
  6.6 0.1 copy.45
  6.7 0.8 collective-permute-start
  7.5 1.1 %collective-permute-done = bf16[4,12,16,128]{3,2,1,0:T(8,128)(2,1)S(1)} collective-permute-done((bf16[4,12,16,128]{3,2,1,0:T(8,128)(2,1)S(1)}, bf16[4,12,16,128]{3,2,1,0:T(8,128)(2,1)S(1)}, u32[]{:S(2)}, u32[]{:S(2)}) %collective-permute-start) | collective-permute-done | bytes 196640 | tf_op jit(solution)/shard_map/ppermute | solution.py:111
  8.6 0.0 copy-start.2
  8.6 3.1 %collective-permute-start.1 = (bf16[1,12,32,128]{3,2,1,0:T(8,128)(2,1)S(1)}, bf16[1,12,32,128]{3,2,1,0:T(8,128)(2,1)S(1)}, u32[]{:S(2)}, u32[]{:S(2)}) collective-permute-start(bf16[1,12,32,128]{3,2,1,0:T(8,128)(2,1)S(1)} %get-tuple-element.12), channel_id=1, source_target_pairs={{0,2},{1,3},{2,4},{3,5},{4,6},{5,7},{6,0},{7,1},{8,10},{9,11},{10,... | collective-permute-start | bytes 294920 | tf_op jit(solution)/shard_map/ppermute | solution.py:118
  11.7 5.1 %collective-permute-start.2 = (bf16[1,12,32,128]{3,2,1,0:T(8,128)(2,1)S(1)}, bf16[1,12,32,128]{3,2,1,0:T(8,128)(2,1)S(1)}, u32[]{:S(2)}, u32[]{:S(2)}) collective-permute-start(bf16[1,12,32,128]{3,2,1,0:T(8,128)(2,1)S(1)} %get-tuple-element.13), channel_id=1, source_target_pairs={{0,4},{1,5},{2,6},{3,7},{4,0},{5,1},{6,2},{7,3},{8,12},{9,13},{10,... | collective-permute-start | bytes 294920 | tf_op jit(solution)/shard_map/ppermute | solution.py:118
  16.8 2.4 %collective-permute-start.3 = (bf16[1,12,32,128]{3,2,1,0:T(8,128)(2,1)S(1)}, bf16[1,12,32,128]{3,2,1,0:T(8,128)(2,1)S(1)}, u32[]{:S(2)}, u32[]{:S(2)}) collective-permute-start(bf16[1,12,32,128]{3,2,1,0:T(8,128)(2,1)S(1)} %get-tuple-element.11), channel_id=1, source_target_pairs={{0,6},{1,7},{2,0},{3,1},{4,2},{5,3},{6,4},{7,5},{8,14},{9,15},{10,... | collective-permute-start | bytes 294920 | tf_op jit(solution)/shard_map/ppermute | solution.py:118
  19.2 0.0 collective-permute-done.1
  19.3 4.3 %collective-permute-done.2 = bf16[1,12,32,128]{3,2,1,0:T(8,128)(2,1)S(1)} collective-permute-done((bf16[1,12,32,128]{3,2,1,0:T(8,128)(2,1)S(1)}, bf16[1,12,32,128]{3,2,1,0:T(8,128)(2,1)S(1)}, u32[]{:S(2)}, u32[]{:S(2)}) %collective-permute-start.2) | collective-permute-done | bytes 98336 | tf_op jit(solution)/shard_map/ppermute | solution.py:118
  23.6 3.3 %collective-permute-done.3 = bf16[1,12,32,128]{3,2,1,0:T(8,128)(2,1)S(1)} collective-permute-done((bf16[1,12,32,128]{3,2,1,0:T(8,128)(2,1)S(1)}, bf16[1,12,32,128]{3,2,1,0:T(8,128)(2,1)S(1)}, u32[]{:S(2)}, u32[]{:S(2)}) %collective-permute-start.3) | collective-permute-done | bytes 98336 | tf_op jit(solution)/shard_map/ppermute | solution.py:118
  27.0 0.0 copy-start.1
  27.0 1.9 %collective-permute-start.4 = (bf16[4,12,32,128]{3,2,1,0:T(8,128)(2,1)S(1)}, bf16[4,12,32,128]{3,2,1,0:T(8,128)(2,1)S(1)}, u32[]{:S(2)}, u32[]{:S(2)}) collective-permute-start(bf16[4,12,32,128]{3,2,1,0:T(8,128)(2,1)S(1)} %constant_dynamic-update-slice_fusion.3.own_ref), channel_id=1, source_target_pairs={{0,8},{8,16},{16,24},{24,32},{32,40},{40,48},{48,56},{56,64},{64,7... | collective-permute-start | bytes 1179656 | tf_op jit(solution)/shard_map/ppermute | solution.py:121
  28.9 3.4 %collective-permute-start.5 = (bf16[4,12,32,128]{3,2,1,0:T(8,128)(2,1)S(1)}, bf16[4,12,32,128]{3,2,1,0:T(8,128)(2,1)S(1)}, u32[]{:S(2)}, u32[]{:S(2)}) collective-permute-start(bf16[4,12,32,128]{3,2,1,0:T(8,128)(2,1)S(1)} %constant_dynamic-update-slice_fusion.3.own_ref), channel_id=1, source_target_pairs={{8,0},{16,8},{24,16},{32,24},{40,32},{48,40},{56,48},{64,56},{72,6... | collective-permute-start | bytes 1179656 | tf_op jit(solution)/shard_map/ppermute | solution.py:122
  32.3 0.0 copy-done.2
  32.3 0.8 copy.23
  33.1 0.1 copy.44
  33.2 0.0 copy-done.1
  33.2 0.0 copy-start.8
  33.2 1.6 %copy.24.weight_ref = bf16[384,1152]{1,0:T(8,128)(2,1)} copy(bf16[384,1152]{0,1:T(8,128)(2,1)S(1)} %bitcast.86) | data formatting | bytes 1769472 | tf_op jit(solution)/shard_map/reshape | solution.py:77
  34.8 0.0 copy-done.8
  34.8 0.7 copy.25.bias_ref
  35.5 0.6 pad_add_fusion.block_ref
  36.1 3.0 %collective-permute-done.4.before_ref = bf16[4,12,32,128]{3,2,1,0:T(8,128)(2,1)S(1)} collective-permute-done((bf16[4,12,32,128]{3,2,1,0:T(8,128)(2,1)S(1)}, bf16[4,12,32,128]{3,2,1,0:T(8,128)(2,1)S(1)}, u32[]{:S(2)}, u32[]{:S(2)}) %collective-permute-start.4) | collective-permute-done | bytes 393248 | tf_op jit(solution)/shard_map/ppermute | solution.py:121
  39.1 6.1 %collective-permute-done.5.after_ref = bf16[4,12,32,128]{3,2,1,0:T(8,128)(2,1)S(1)} collective-permute-done((bf16[4,12,32,128]{3,2,1,0:T(8,128)(2,1)S(1)}, bf16[4,12,32,128]{3,2,1,0:T(8,128)(2,1)S(1)}, u32[]{:S(2)}, u32[]{:S(2)}) %collective-permute-start.5) | collective-permute-done | bytes 393248 | tf_op jit(solution)/shard_map/ppermute | solution.py:122
  45.2 0.0 copy-done.4
  45.2 0.8 copy-done.5
  46.0 3.8 %first_layer.1.own_ref = bf16[10,128,128]{2,1,0:T(8,128)(2,1)} custom-call(s32[2]{0:T(128)} %pad_add_fusion.block_ref, bf16[4,12,32,128]{3,2,1,0:T(8,128)(2,1)} %copy-done.4, bf16[4,12,32,128]{3,2,1,0:T(8,128)(2,1)} %copy-done.1, bf16[4,12,32,128]{3,2,1,0:T(8,128)(2,1)} %copy-done.5, bf16[384,1152]{1,0:T(8,128)(2,1)} %copy.24.weight_ref, f32[128,1]{1,0:T(8,128)} %copy.25.bias_ref), custom_call_target="tpu_custom_call" | custom-call | tf_op jit(solution)/shard_map/first_layer/pallas_call | solution.py:124
  49.7 1.9 %collective-permute-start.6 = (bf16[10,128,128]{2,1,0:T(8,128)(2,1)}, bf16[10,128,128]{2,1,0:T(8,128)(2,1)S(1)}, u32[]{:S(2)}, u32[]{:S(2)}) collective-permute-start(bf16[10,128,128]{2,1,0:T(8,128)(2,1)} %first_layer.1.own_ref), channel_id=1, source_target_pairs={{0,8},{8,16},{16,24},{24,32},{32,40},{40,48},{48,56},{56,64},{64,7... | collective-permute-start | bytes 983048 | tf_op jit(solution)/shard_map/ppermute | solution.py:132
  51.7 3.4 %collective-permute-start.7 = (bf16[10,128,128]{2,1,0:T(8,128)(2,1)}, bf16[10,128,128]{2,1,0:T(8,128)(2,1)S(1)}, u32[]{:S(2)}, u32[]{:S(2)}) collective-permute-start(bf16[10,128,128]{2,1,0:T(8,128)(2,1)} %first_layer.1.own_ref), channel_id=1, source_target_pairs={{8,0},{16,8},{24,16},{32,24},{40,32},{48,40},{56,48},{64,56},{72,6... | collective-permute-start | bytes 983048 | tf_op jit(solution)/shard_map/ppermute | solution.py:133
  55.0 0.0 copy-done.3
  55.0 0.8 copy.26
  55.8 0.1 copy.43
  56.0 0.0 copy-start.9
  56.0 1.6 %copy.27.weight_ref = bf16[384,1152]{1,0:T(8,128)(2,1)} copy(bf16[384,1152]{0,1:T(8,128)(2,1)S(1)} %bitcast.87) | data formatting | bytes 1769472 | tf_op jit(solution)/shard_map/reshape | solution.py:77
  57.5 0.0 copy-done.9
  57.5 0.7 copy.28.bias_ref
  58.3 1.4 %collective-permute-done.6.before_ref = bf16[10,128,128]{2,1,0:T(8,128)(2,1)S(1)} collective-permute-done((bf16[10,128,128]{2,1,0:T(8,128)(2,1)}, bf16[10,128,128]{2,1,0:T(8,128)(2,1)S(1)}, u32[]{:S(2)}, u32[]{:S(2)}) %collective-permute-start.6) | collective-permute-done | bytes 327712 | tf_op jit(solution)/shard_map/ppermute | solution.py:132
  59.7 6.1 %collective-permute-done.7.after_ref = bf16[10,128,128]{2,1,0:T(8,128)(2,1)S(1)} collective-permute-done((bf16[10,128,128]{2,1,0:T(8,128)(2,1)}, bf16[10,128,128]{2,1,0:T(8,128)(2,1)S(1)}, u32[]{:S(2)}, u32[]{:S(2)}) %collective-permute-start.7) | collective-permute-done | bytes 327712 | tf_op jit(solution)/shard_map/ppermute | solution.py:133
  65.8 0.0 copy-done.6
  65.8 0.7 copy-done.7
  66.6 3.4 %second_layer.1 = bf16[2,4,8,16,128]{4,3,2,1,0:T(8,128)(2,1)} custom-call(bf16[10,128,128]{2,1,0:T(8,128)(2,1)} %copy-done.6, bf16[10,128,128]{2,1,0:T(8,128)(2,1)} %first_layer.1.own_ref, bf16[10,128,128]{2,1,0:T(8,128)(2,1)} %copy-done.7, bf16[384,1152]{1,0:T(8,128)(2,1)} %copy.27.weight_ref, f32[128,1]{1,0:T(8,128)} %copy.28.bias_ref), custom_call_target="tpu_custom_call" | custom-call | tf_op jit(solution)/shard_map/second_layer/pallas_call | solution.py:134
  70.0 0.8 constant_dynamic-slice_fusion.2
  70.8 0.0 collective-permute-start.8
  70.8 5.2 %collective-permute-done.8 = bf16[2,1,8,16,128]{4,3,2,1,0:T(8,128)(2,1)S(1)} collective-permute-done((bf16[2,1,8,16,128]{4,3,2,1,0:T(8,128)(2,1)S(1)}, bf16[2,1,8,16,128]{4,3,2,1,0:T(8,128)(2,1)S(1)}, u32[]{:S(2)}, u32[]{:S(2)}) %collective-permute-start.8) | collective-permute-done | bytes 65568 | tf_op jit(solution)/shard_map/ppermute | solution.py:145
  76.1 1.5 %constant_dynamic-slice_fusion = (bf16[2,1,8,16,128]{4,3,2,1,0:T(8,128)(2,1)S(1)}, bf16[2,1,8,16,128]{4,3,2,1,0:T(8,128)(2,1)S(1)}, bf16[2,4,8,16,128]{4,3,2,1,0:T(8,128)(2,1)}) fusion(bf16[2,4,8,16,128]{4,3,2,1,0:T(8,128)(2,1)} %second_layer.1, s32[]{:T(128)S(6)} %select_n.106, s32[]{:T(128)S(6)} %select_n.108, ...), kind=kLoop, calls=%fused_computation.41 | loop fusion | bytes 393224 | tf_op jit(solution)/shard_map/jit(dynamic_index_in_dim)/dynamic_slice | solution.py:144
  77.6 2.4 %collective-permute-start.9 = (bf16[2,1,8,16,128]{4,3,2,1,0:T(8,128)(2,1)S(1)}, bf16[2,1,8,16,128]{4,3,2,1,0:T(8,128)(2,1)S(1)}, u32[]{:S(2)}, u32[]{:S(2)}) collective-permute-start(bf16[2,1,8,16,128]{4,3,2,1,0:T(8,128)(2,1)S(1)} %get-tuple-element.15), channel_id=1, source_target_pairs={{0,4},{1,5},{2,6},{3,7},{4,0},{5,1},{6,2},{7,3},{8,12},{9,13},{10,... | collective-permute-start | bytes 196616 | tf_op jit(solution)/shard_map/ppermute | solution.py:145
  80.0 0.0 collective-permute-start.10
  80.0 4.6 %collective-permute-done.9 = bf16[2,1,8,16,128]{4,3,2,1,0:T(8,128)(2,1)S(1)} collective-permute-done((bf16[2,1,8,16,128]{4,3,2,1,0:T(8,128)(2,1)S(1)}, bf16[2,1,8,16,128]{4,3,2,1,0:T(8,128)(2,1)S(1)}, u32[]{:S(2)}, u32[]{:S(2)}) %collective-permute-start.9) | collective-permute-done | bytes 65568 | tf_op jit(solution)/shard_map/ppermute | solution.py:145
  84.6 0.6 constant_dynamic-update-slice_fusion.1
  85.3 0.0 collective-permute-done.10
  85.3 0.6 constant_dynamic-update-slice_fusion
  85.9 0.9 dynamic-slice_bitcast_fusion
  86.8 4.7 %collective-permute-start.11 = (bf16[4,8,16,128]{3,2,1,0:T(8,128)(2,1)S(1)}, bf16[4,8,16,128]{3,2,1,0:T(8,128)(2,1)S(1)}, u32[]{:S(2)}, u32[]{:S(2)}) collective-permute-start(bf16[4,8,16,128]{3,2,1,0:T(8,128)(2,1)S(1)} %dynamic-slice_bitcast_fusion), channel_id=1, source_target_pairs={{0,1},{1,0},{2,3},{3,2},{4,5},{5,4},{6,7},{7,6},{8,9},{9,8},{10,11... | collective-permute-start | bytes 393224 | tf_op jit(solution)/shard_map/ppermute | solution.py:149
  91.5 1.0 %collective-permute-done.11 = bf16[4,8,16,128]{3,2,1,0:T(8,128)(2,1)S(1)} collective-permute-done((bf16[4,8,16,128]{3,2,1,0:T(8,128)(2,1)S(1)}, bf16[4,8,16,128]{3,2,1,0:T(8,128)(2,1)S(1)}, u32[]{:S(2)}, u32[]{:S(2)}) %collective-permute-start.11) | collective-permute-done | bytes 131104 | tf_op jit(solution)/shard_map/ppermute | solution.py:149
  92.5 0.9 fusion
  93.5 0.8 copy.30
  (16 shorter events, 0.3 us)
Async XLA Ops:
  0.0 6.5 %copy-start = (bf16[16,1,64,128]{3,2,1,0:T(8,128)(2,1)S(1)}, bf16[16,1,64,128]{3,2,1,0:T(8,128)(2,1)}, u32[]{:S(2)}) copy-start(bf16[16,1,64,128]{3,2,1,0:T(8,128)(2,1)} %param.5) | copy-start | bytes 786436
  6.7 1.8 %collective-permute-start = (bf16[4,12,16,128]{3,2,1,0:T(8,128)(2,1)S(1)}, bf16[4,12,16,128]{3,2,1,0:T(8,128)(2,1)S(1)}, u32[]{:S(2)}, u32[]{:S(2)}) collective-permute-start(bf16[4,12,16,128]{3,2,1,0:T(8,128)(2,1)S(1)} %bitcast.100), channel_id=1, source_target_pairs={{0,1},{1,0},{2,3},{3,2},{4,5},{5,4},{6,7},{7,6},{8,9},{9,8},{10,11... | collective-permute-start | bytes 589832 | tf_op jit(solution)/shard_map/ppermute | solution.py:111
  8.6 23.7 %copy-start.2 = (bf16[27,128,128]{2,1,0:T(8,128)(2,1)S(1)}, bf16[27,128,128]{2,1,0:T(8,128)(2,1)}, u32[]{:S(2)}) copy-start(bf16[27,128,128]{2,1,0:T(8,128)(2,1)} %param.6) | copy-start | bytes 2654212
  8.6 10.6 %collective-permute-start.1 = (bf16[1,12,32,128]{3,2,1,0:T(8,128)(2,1)S(1)}, bf16[1,12,32,128]{3,2,1,0:T(8,128)(2,1)S(1)}, u32[]{:S(2)}, u32[]{:S(2)}) collective-permute-start(bf16[1,12,32,128]{3,2,1,0:T(8,128)(2,1)S(1)} %get-tuple-element.12), channel_id=1, source_target_pairs={{0,2},{1,3},{2,4},{3,5},{4,6},{5,7},{6,0},{7,1},{8,10},{9,11},{10,... | collective-permute-start | bytes 294920 | tf_op jit(solution)/shard_map/ppermute | solution.py:118
  11.7 11.9 %collective-permute-start.2 = (bf16[1,12,32,128]{3,2,1,0:T(8,128)(2,1)S(1)}, bf16[1,12,32,128]{3,2,1,0:T(8,128)(2,1)S(1)}, u32[]{:S(2)}, u32[]{:S(2)}) collective-permute-start(bf16[1,12,32,128]{3,2,1,0:T(8,128)(2,1)S(1)} %get-tuple-element.13), channel_id=1, source_target_pairs={{0,4},{1,5},{2,6},{3,7},{4,0},{5,1},{6,2},{7,3},{8,12},{9,13},{10,... | collective-permute-start | bytes 294920 | tf_op jit(solution)/shard_map/ppermute | solution.py:118
  16.8 10.1 %collective-permute-start.3 = (bf16[1,12,32,128]{3,2,1,0:T(8,128)(2,1)S(1)}, bf16[1,12,32,128]{3,2,1,0:T(8,128)(2,1)S(1)}, u32[]{:S(2)}, u32[]{:S(2)}) collective-permute-start(bf16[1,12,32,128]{3,2,1,0:T(8,128)(2,1)S(1)} %get-tuple-element.11), channel_id=1, source_target_pairs={{0,6},{1,7},{2,0},{3,1},{4,2},{5,3},{6,4},{7,5},{8,14},{9,15},{10,... | collective-permute-start | bytes 294920 | tf_op jit(solution)/shard_map/ppermute | solution.py:118
  27.0 6.2 %copy-start.1 = (bf16[4,12,32,128]{3,2,1,0:T(8,128)(2,1)}, bf16[4,12,32,128]{3,2,1,0:T(8,128)(2,1)S(1)}, u32[]{:S(2)}) copy-start(bf16[4,12,32,128]{3,2,1,0:T(8,128)(2,1)S(1)} %constant_dynamic-update-slice_fusion.3.own_ref) | copy-start | bytes 1179652
  27.0 12.1 %collective-permute-start.4 = (bf16[4,12,32,128]{3,2,1,0:T(8,128)(2,1)S(1)}, bf16[4,12,32,128]{3,2,1,0:T(8,128)(2,1)S(1)}, u32[]{:S(2)}, u32[]{:S(2)}) collective-permute-start(bf16[4,12,32,128]{3,2,1,0:T(8,128)(2,1)S(1)} %constant_dynamic-update-slice_fusion.3.own_ref), channel_id=1, source_target_pairs={{0,8},{8,16},{16,24},{24,32},{32,40},{40,48},{48,56},{56,64},{64,7... | collective-permute-start | bytes 1179656 | tf_op jit(solution)/shard_map/ppermute | solution.py:121
  28.9 16.3 %collective-permute-start.5 = (bf16[4,12,32,128]{3,2,1,0:T(8,128)(2,1)S(1)}, bf16[4,12,32,128]{3,2,1,0:T(8,128)(2,1)S(1)}, u32[]{:S(2)}, u32[]{:S(2)}) collective-permute-start(bf16[4,12,32,128]{3,2,1,0:T(8,128)(2,1)S(1)} %constant_dynamic-update-slice_fusion.3.own_ref), channel_id=1, source_target_pairs={{8,0},{16,8},{24,16},{32,24},{40,32},{48,40},{56,48},{64,56},{72,6... | collective-permute-start | bytes 1179656 | tf_op jit(solution)/shard_map/ppermute | solution.py:122
  33.2 1.6 %copy-start.8 = (f32[128]{0:T(128)S(1)}, f32[128]{0:T(128)}, u32[]{:S(2)}) copy-start(f32[128]{0:T(128)} %param.7) | copy-start | bytes 1540
  36.1 18.9 %copy-start.3 = (bf16[27,128,128]{2,1,0:T(8,128)(2,1)S(1)}, bf16[27,128,128]{2,1,0:T(8,128)(2,1)}, u32[]{:S(2)}) copy-start(bf16[27,128,128]{2,1,0:T(8,128)(2,1)} %param.8) | copy-start | bytes 2654212
  39.1 6.1 %copy-start.4 = (bf16[4,12,32,128]{3,2,1,0:T(8,128)(2,1)}, bf16[4,12,32,128]{3,2,1,0:T(8,128)(2,1)S(1)}, u32[]{:S(2)}) copy-start(bf16[4,12,32,128]{3,2,1,0:T(8,128)(2,1)S(1)} %collective-permute-done.4.before_ref) | copy-start | bytes 1179652
  45.2 0.8 copy-start.5
  49.7 10.0 %collective-permute-start.6 = (bf16[10,128,128]{2,1,0:T(8,128)(2,1)}, bf16[10,128,128]{2,1,0:T(8,128)(2,1)S(1)}, u32[]{:S(2)}, u32[]{:S(2)}) collective-permute-start(bf16[10,128,128]{2,1,0:T(8,128)(2,1)} %first_layer.1.own_ref), channel_id=1, source_target_pairs={{0,8},{8,16},{16,24},{24,32},{32,40},{40,48},{48,56},{56,64},{64,7... | collective-permute-start | bytes 983048 | tf_op jit(solution)/shard_map/ppermute | solution.py:132
  51.7 14.2 %collective-permute-start.7 = (bf16[10,128,128]{2,1,0:T(8,128)(2,1)}, bf16[10,128,128]{2,1,0:T(8,128)(2,1)S(1)}, u32[]{:S(2)}, u32[]{:S(2)}) collective-permute-start(bf16[10,128,128]{2,1,0:T(8,128)(2,1)} %first_layer.1.own_ref), channel_id=1, source_target_pairs={{8,0},{16,8},{24,16},{32,24},{40,32},{48,40},{56,48},{64,56},{72,6... | collective-permute-start | bytes 983048 | tf_op jit(solution)/shard_map/ppermute | solution.py:133
  56.0 1.6 %copy-start.9 = (f32[128]{0:T(128)S(1)}, f32[128]{0:T(128)}, u32[]{:S(2)}) copy-start(f32[128]{0:T(128)} %param.9) | copy-start | bytes 1540
  59.7 6.1 %copy-start.6 = (bf16[10,128,128]{2,1,0:T(8,128)(2,1)}, bf16[10,128,128]{2,1,0:T(8,128)(2,1)S(1)}, u32[]{:S(2)}) copy-start(bf16[10,128,128]{2,1,0:T(8,128)(2,1)S(1)} %collective-permute-done.6.before_ref) | copy-start | bytes 983044
  65.8 0.7 copy-start.7
  70.8 5.2 %collective-permute-start.8 = (bf16[2,1,8,16,128]{4,3,2,1,0:T(8,128)(2,1)S(1)}, bf16[2,1,8,16,128]{4,3,2,1,0:T(8,128)(2,1)S(1)}, u32[]{:S(2)}, u32[]{:S(2)}) collective-permute-start(bf16[2,1,8,16,128]{4,3,2,1,0:T(8,128)(2,1)S(1)} %constant_dynamic-slice_fusion.2), channel_id=1, source_target_pairs={{0,2},{1,3},{2,4},{3,5},{4,6},{5,7},{6,0},{7,1},{8,10},{9,11},{10,... | collective-permute-start | bytes 196616 | tf_op jit(solution)/shard_map/ppermute | solution.py:145
  77.6 7.0 %collective-permute-start.9 = (bf16[2,1,8,16,128]{4,3,2,1,0:T(8,128)(2,1)S(1)}, bf16[2,1,8,16,128]{4,3,2,1,0:T(8,128)(2,1)S(1)}, u32[]{:S(2)}, u32[]{:S(2)}) collective-permute-start(bf16[2,1,8,16,128]{4,3,2,1,0:T(8,128)(2,1)S(1)} %get-tuple-element.15), channel_id=1, source_target_pairs={{0,4},{1,5},{2,6},{3,7},{4,0},{5,1},{6,2},{7,3},{8,12},{9,13},{10,... | collective-permute-start | bytes 196616 | tf_op jit(solution)/shard_map/ppermute | solution.py:145
  80.0 5.2 %collective-permute-start.10 = (bf16[2,1,8,16,128]{4,3,2,1,0:T(8,128)(2,1)S(1)}, bf16[2,1,8,16,128]{4,3,2,1,0:T(8,128)(2,1)S(1)}, u32[]{:S(2)}, u32[]{:S(2)}) collective-permute-start(bf16[2,1,8,16,128]{4,3,2,1,0:T(8,128)(2,1)S(1)} %get-tuple-element.14), channel_id=1, source_target_pairs={{0,6},{1,7},{2,0},{3,1},{4,2},{5,3},{6,4},{7,5},{8,14},{9,15},{10,... | collective-permute-start | bytes 196616 | tf_op jit(solution)/shard_map/ppermute | solution.py:145
  86.8 5.6 %collective-permute-start.11 = (bf16[4,8,16,128]{3,2,1,0:T(8,128)(2,1)S(1)}, bf16[4,8,16,128]{3,2,1,0:T(8,128)(2,1)S(1)}, u32[]{:S(2)}, u32[]{:S(2)}) collective-permute-start(bf16[4,8,16,128]{3,2,1,0:T(8,128)(2,1)S(1)} %dynamic-slice_bitcast_fusion), channel_id=1, source_target_pairs={{0,1},{1,0},{2,3},{3,2},{4,5},{5,4},{6,7},{7,6},{8,9},{9,8},{10,11... | collective-permute-start | bytes 393224 | tf_op jit(solution)/shard_map/ppermute | solution.py:149

commit v2 on v1

v2 whole, which is shorter than its diff:
```python
import jax
import jax.numpy as jnp
from jax import lax
from jax.experimental import pallas as pl
from jax.experimental.pallas import tpu as pltpu
from jax.sharding import PartitionSpec as P

BF16 = jnp.bfloat16
F32 = jnp.float32
CORES = 2
RIM = 2
PARAMS = pltpu.CompilerParams(vmem_limit_bytes=24 * 1024 * 1024)
VMEM = pl.BlockSpec(memory_space=pltpu.VMEM)
SMEM = pl.BlockSpec(memory_space=pltpu.SMEM)


def along_lanes(total, lanes):
    chans = total.shape[0] // 3
    lane = lax.broadcasted_iota(jnp.int32, (chans, lanes), 1)
    low = pltpu.roll(total[:chans], 1, 1)
    high = pltpu.roll(total[2 * chans :], lanes - 1, 1)
    return (
        total[chans : 2 * chans]
        + jnp.where(lane == 0, 0.0, low)
        + jnp.where(lane == lanes - 1, 0.0, high)
    )


def conv_rows(get, planes, weight, store, rows, lanes):
    for start in range(0, rows, 2):
        parts = []
        for a in range(planes):
            for e in range(3):
                pair = [get(a, start + e + n) for n in range(2)]
                parts.append(jnp.concatenate(pair, axis=1))
        stacked = jnp.concatenate(parts, axis=0)
        total = jnp.dot(weight, stacked, preferred_element_type=F32)
        for n in range(2):
            store(start + n, along_lanes(total[:, n * lanes : (n + 1) * lanes], lanes))


def pack_kernel(place_ref, volume_ref, mine_ref, theirs_ref, rows_ref):
    width, _, length, lanes = volume_ref.shape
    groups = mine_ref.shape[0]
    rows = length // (groups * CORES)
    edge = jnp.zeros((RIM, width, lanes), BF16)
    rows_ref[:RIM] = edge
    rows_ref[RIM + length :] = edge
    turned = jnp.swapaxes(volume_ref[:, 0].astype(F32), 0, 1)
    rows_ref[RIM : RIM + length] = turned.astype(BF16)
    group, core = place_ref[0], place_ref[1]
    for k in range(groups):
        target = lax.rem(group + k, groups) * CORES
        mine_ref[k] = rows_ref[pl.ds((target + core) * rows, rows + 2 * RIM)]
        theirs_ref[k] = rows_ref[pl.ds((target + 1 - core) * rows, rows + 2 * RIM)]


def own_kernel(own_ref, weight_ref, out_ref):
    rows, _, lanes = out_ref.shape

    def get(_, row):
        if len(own_ref.shape) == 3:
            return own_ref[row]
        return jnp.concatenate([own_ref[g, row] for g in range(own_ref.shape[0])], axis=0)

    def store(row, value):
        out_ref[row] = value

    conv_rows(get, 1, weight_ref[...], store, rows, lanes)


def reader(place_ref, before_ref, after_ref):
    outside = (place_ref[2] == 0, place_ref[2] == place_ref[3] - 1)
    refs = (before_ref, after_ref)

    def get(a, row):
        ref = refs[a]
        if len(ref.shape) == 3:
            value = ref[row]
        else:
            value = jnp.concatenate([ref[g, row] for g in range(ref.shape[0])], axis=0)
        return jnp.where(outside[a], jnp.zeros_like(value), value)

    return get


def first_kernel(place_ref, before_ref, after_ref, own_ref, weight_ref, bias_ref, out_ref):
    rows, _, lanes = out_ref.shape
    group, core = place_ref[0], place_ref[1]
    block = group * CORES + core
    bias = bias_ref[...]

    def store(row, value):
        value = jnp.maximum(value + own_ref[row] + bias, 0.0)
        if row == 0:
            value = jnp.where(block == 0, 0.0, value)
        if row == rows - 1:
            value = jnp.where(block == place_ref[4] - 1, 0.0, value)
        out_ref[row] = value.astype(BF16)

    get = reader(place_ref, before_ref, after_ref)
    conv_rows(get, 2, weight_ref[...], store, rows, lanes)


def second_kernel(place_ref, before_ref, after_ref, own_ref, weight_ref, bias_ref, *refs):
    outs, all_ref = refs[:-1], refs[-1]
    groups, cores, rows, width, lanes = all_ref.shape
    bias = bias_ref[...]

    def store(row, value):
        value = jnp.maximum(value + own_ref[row] + bias, 0.0).astype(BF16)
        for g in range(groups):
            for c in range(cores):
                at = (g * cores + c) * width
                all_ref[g, c, row] = value[at : at + width]

    get = reader(place_ref, before_ref, after_ref)
    conv_rows(get, 2, weight_ref[...], store, rows, lanes)
    for k in range(groups):
        outs[k][...] = all_ref[lax.rem(place_ref[0] + k, groups)]


def unpack_kernel(place_ref, swapped_ref, *refs):
    blocks, out_ref, rows_ref = refs[:-2], refs[-2], refs[-1]
    groups = len(blocks)
    _, rows, width, lanes = blocks[0].shape
    group, core = place_ref[0], place_ref[1]
    for k in range(groups):
        source = lax.rem(group + groups - k, groups) * CORES
        rows_ref[source + core] = blocks[k][core]
        rows_ref[source + 1 - core] = swapped_ref[k]
    length = groups * CORES * rows
    turned = rows_ref[...].reshape(length, width, lanes).astype(F32)
    out_ref[:, 0] = jnp.swapaxes(turned, 0, 1).astype(BF16)


def arranged(weight):
    _, inner, outer = weight.shape
    taps = weight.reshape(3, 3, 3, inner, outer)
    own = taps[1].transpose(1, 3, 0, 2).reshape(3 * outer, 3 * inner)
    beside = taps[::2].transpose(2, 4, 0, 1, 3).reshape(3 * outer, 6 * inner)
    return own, beside


def cost(rows, planes, full, lanes):
    flops = 2 * rows * lanes * full * full * 9 * planes
    return pl.CostEstimate(flops=flops, bytes_accessed=4_000_000, transcendentals=0)


def solution(mesh):
    space = mesh.shape["space"]
    chan = mesh.shape["chan"]
    groups = chan // CORES
    up = [(i, (i + 1) % space) for i in range(space)]
    down = [(i, (i + space - 1) % space) for i in range(space)]
    swap = [(i, i ^ 1) for i in range(chan)]

    def ahead(k):
        return [(i, (i + CORES * k) % chan) for i in range(chan)]

    def call(kernel, shapes, inputs, scratch=(), **kwargs):
        single = not isinstance(shapes, list)
        return pl.pallas_call(
            kernel,
            out_shape=shapes,
            in_specs=[SMEM if x.ndim == 1 else VMEM for x in inputs],
            out_specs=VMEM if single else [VMEM] * len(shapes),
            scratch_shapes=scratch,
            compiler_params=PARAMS,
            **kwargs,
        )(*inputs)

    def per_device(volume, weight_one, bias_one, weight_two, bias_two):
        width, _, length, lanes = volume.shape
        full = width * chan
        rows = length // chan
        index = lax.axis_index("chan")
        plane = lax.axis_index("space")
        group, core = index // CORES, index % CORES
        place = jnp.stack([group, core, plane, jnp.int32(space), jnp.int32(chan)]).astype(jnp.int32)

        own_one, beside_one = arranged(weight_one)
        own_two, beside_two = arranged(weight_two)

        piece = jax.ShapeDtypeStruct((groups, rows + 2 * RIM, width, lanes), BF16)
        mine, theirs = call(
            pack_kernel,
            [piece, piece],
            [place, volume],
            [pltpu.VMEM((length + 2 * RIM, width, lanes), BF16)],
            name="pack_rows",
        )
        swapped = lax.ppermute(theirs, "chan", swap)
        first = jnp.where(core == 0, mine, swapped)
        second = jnp.where(core == 0, swapped, mine)
        both = jnp.concatenate([first, second], axis=2)
        whole = jnp.zeros_like(both)
        whole = lax.dynamic_update_slice_in_dim(whole, both[:1], group, 0)
        for k in range(1, groups):
            got = lax.ppermute(both[k : k + 1], "chan", ahead(k))
            whole = lax.dynamic_update_slice_in_dim(whole, got, (group + groups - k) % groups, 0)

        before = lax.ppermute(whole, "space", up)
        after = lax.ppermute(whole, "space", down)
        own = call(
            own_kernel,
            jax.ShapeDtypeStruct((rows + RIM, full, lanes), F32),
            [whole, own_one],
            cost_estimate=cost(rows + RIM, 1, full, lanes),
            name="first_own",
        )
        hidden = call(
            first_kernel,
            jax.ShapeDtypeStruct((rows + RIM, full, lanes), BF16),
            [place, before, after, own, beside_one, bias_one[:, None]],
            cost_estimate=cost(rows + RIM, 2, full, lanes),
            name="first_layer",
        )

        before = lax.ppermute(hidden, "space", up)
        after = lax.ppermute(hidden, "space", down)
        own = call(
            own_kernel,
            jax.ShapeDtypeStruct((rows, full, lanes), F32),
            [hidden, own_two],
            cost_estimate=cost(rows, 1, full, lanes),
            name="second_own",
        )
        blocks = call(
            second_kernel,
            [jax.ShapeDtypeStruct((CORES, rows, width, lanes), BF16)] * groups,
            [place, before, after, own, beside_two, bias_two[:, None]],
            [pltpu.VMEM((groups, CORES, rows, width, lanes), BF16)],
            cost_estimate=cost(rows, 2, full, lanes),
            name="second_layer",
        )

        blocks = [blocks[0]] + [lax.ppermute(blocks[k], "chan", ahead(k)) for k in range(1, groups)]
        theirs = jnp.stack([lax.dynamic_index_in_dim(b, 1 - core, 0, keepdims=False) for b in blocks])
        swapped = lax.ppermute(theirs, "chan", swap)
        return call(
            unpack_kernel,
            jax.ShapeDtypeStruct(volume.shape, BF16),
            [place, swapped, *blocks],
            [pltpu.VMEM((chan, rows, width, lanes), BF16)],
            name="unpack_rows",
        )

    placed = (P("chan", "space", None, None), P(), P(), P(), P())
    return jax.shard_map(
        per_device,
        mesh=mesh,
        in_specs=placed,
        out_specs=P("chan", "space", None, None),
        check_vma=False,
    )
```

time: 94.8 us -> 69.8 us (0.74)
  local copies, waits for them, and re-layouts: 20 us -> 6.79 us
  starting transfers between devices: 29 us -> 23 us
  waiting for transfers between devices: 36.2 us -> 32.1 us
  other arithmetic: 1.65 us -> 0.09 us
    unnamed x30 -> x14, local copies, waits for them, and re-layouts: 8.38 us -> 3.71 us
    ppermute x6, waiting for transfers between devices: 17.5 us -> 13.3 us  [the longest x3 7.76 us: per_device(): got = lax.ppermute(both[k:k + 1], 'chan', ahead(k))]
    ppermute x6, starting transfers between devices: 13 us -> 16.6 us  [the longest x3 10.6 us: per_device(): got = lax.ppermute(both[k:k + 1], 'chan', ahead(k))]
    reshape x4 -> x2, local copies, waits for them, and re-layouts: 4.64 us -> 1.09 us  [arranged(): beside = taps[::2].transpose(2, 4, 0, 1, 3).reshape(3 * outer, 6 * inner)]
    ppermute x1, waiting for transfers between devices: 2.95 us -> 5.57 us  [per_device(): before = lax.ppermute(whole, 'space', up)]
    dynamic_slice x3 -> x4, local copies, waits for them, and re-layouts: 2.43 us -> 0.01 us  [per_device(): lax.dynamic_index_in_dim(b, 1 - core, 0, keepdims=False)]
    ppermute x1, starting transfers between devices: 3.36 us -> 1.22 us  [per_device(): after = lax.ppermute(hidden, 'space', down)]
    ppermute x2, starting transfers between devices: 5.41 us -> 3.34 us  [per_device(): swapped = lax.ppermute(theirs, 'chan', swap)]
  transfers between devices with their start and end apart: 12 -> 12, of which waited for: 10 -> 11; matrix products, arithmetic and copies ran while one was open for 8% -> 5% of each run, Pallas kernels for 0% -> 2%
where the time goes in v2:
time: 69.8 us; the launch traced here: 68.8 us
  waiting for transfers between devices  32.1 us (46%)
  starting transfers between devices  23 us (33%)
  local copies, waits for them, and re-layouts  6.79 us (10%)
  Pallas kernels  6.57 us (9%)
    ppermute x3, starting transfers between devices, per_device(): got = lax.ppermute(both[k:k + 1], 'chan', ahead(k))  10.6 us
    ppermute x3, waiting for transfers between devices, per_device(): got = lax.ppermute(both[k:k + 1], 'chan', ahead(k))  7.76 us
    pallas_call x6, Pallas kernels, call(): pl.pallas_call(kernel, out_shape=shapes, in_specs=[SMEM if x.ndim == 1 el...  6.57 us
    ppermute x3, starting transfers between devices, per_device(): lax.ppermute(blocks[k], 'chan', ahead(k))  6.04 us
    ppermute x3, waiting for transfers between devices, per_device(): lax.ppermute(blocks[k], 'chan', ahead(k))  5.58 us
    ppermute x1, waiting for transfers between devices, per_device(): before = lax.ppermute(whole, 'space', up)  5.57 us
    ppermute x1, waiting for transfers between devices, per_device(): after = lax.ppermute(hidden, 'space', down)  4.5 us
    ppermute x1, waiting for transfers between devices, per_device(): after = lax.ppermute(whole, 'space', down)  4.31 us
  transfers between devices with their start and end apart: 12, of which 11 were waited for; matrix products, arithmetic and copies ran while one was open for 5% of the time, Pallas kernels for 2%

profile of v2, /device:TPU:31, one launch (start us, length us, event | category | flops | bytes accessed | tf_op | source)
XLA Modules:
  0.0 68.8 jit_solution(2702684568855085535)
XLA Ops:
  0.0 0.1 stack.22.place_ref
  0.1 0.0 copy-start
  0.1 0.9 %copy-done = bf16[16,1,64,128]{3,2,1,0:T(8,128)(2,1)S(1)} copy-done((bf16[16,1,64,128]{3,2,1,0:T(8,128)(2,1)S(1)}, bf16[16,1,64,128]{3,2,1,0:T(8,128)(2,1)}, u32[]{:S(2)}) %copy-start) | copy-done | bytes 262168
  1.0 0.7 %pack_rows.1 = (bf16[4,12,16,128]{3,2,1,0:T(8,128)(2,1)S(1)}, bf16[4,12,16,128]{3,2,1,0:T(8,128)(2,1)S(1)}) custom-call(s32[5]{0:T(128)S(1)} %stack.22.place_ref, bf16[16,1,64,128]{3,2,1,0:T(8,128)(2,1)S(1)} %copy-done), custom_call_target="tpu_custom_call" | custom-call | tf_op jit(solution)/shard_map/pack_rows/pallas_call | solution.py:163
  1.8 0.8 %collective-permute-start = (bf16[4,12,16,128]{3,2,1,0:T(8,128)(2,1)S(1)}, bf16[4,12,16,128]{3,2,1,0:T(8,128)(2,1)S(1)}, u32[]{:S(2)}, u32[]{:S(2)}) collective-permute-start(bf16[4,12,16,128]{3,2,1,0:T(8,128)(2,1)S(1)} %get-tuple-element.12), channel_id=1, source_target_pairs={{0,1},{1,0},{2,3},{3,2},{4,5},{5,4},{6,7},{7,6},{8,9},{9,8},{10,11... | collective-permute-start | bytes 589832 | tf_op jit(solution)/shard_map/ppermute | solution.py:193
  2.5 1.1 %collective-permute-done = bf16[4,12,16,128]{3,2,1,0:T(8,128)(2,1)S(1)} collective-permute-done((bf16[4,12,16,128]{3,2,1,0:T(8,128)(2,1)S(1)}, bf16[4,12,16,128]{3,2,1,0:T(8,128)(2,1)S(1)}, u32[]{:S(2)}, u32[]{:S(2)}) %collective-permute-start) | collective-permute-done | bytes 196640 | tf_op jit(solution)/shard_map/ppermute | solution.py:193
  3.6 0.1 broadcast_in_dim.9
  3.7 3.1 %collective-permute-start.1 = (bf16[1,12,32,128]{3,2,1,0:T(8,128)(2,1)S(1)}, bf16[1,12,32,128]{3,2,1,0:T(8,128)(2,1)S(1)}, u32[]{:S(2)}, u32[]{:S(2)}) collective-permute-start(bf16[1,12,32,128]{3,2,1,0:T(8,128)(2,1)S(1)} %get-tuple-element.19), channel_id=1, source_target_pairs={{0,2},{1,3},{2,4},{3,5},{4,6},{5,7},{6,0},{7,1},{8,10},{9,11},{10,... | collective-permute-start | bytes 294920 | tf_op jit(solution)/shard_map/ppermute | solution.py:200
  6.8 5.1 %collective-permute-start.2 = (bf16[1,12,32,128]{3,2,1,0:T(8,128)(2,1)S(1)}, bf16[1,12,32,128]{3,2,1,0:T(8,128)(2,1)S(1)}, u32[]{:S(2)}, u32[]{:S(2)}) collective-permute-start(bf16[1,12,32,128]{3,2,1,0:T(8,128)(2,1)S(1)} %get-tuple-element.20), channel_id=1, source_target_pairs={{0,4},{1,5},{2,6},{3,7},{4,0},{5,1},{6,2},{7,3},{8,12},{9,13},{10,... | collective-permute-start | bytes 294920 | tf_op jit(solution)/shard_map/ppermute | solution.py:200
  11.9 2.4 %collective-permute-start.3 = (bf16[1,12,32,128]{3,2,1,0:T(8,128)(2,1)S(1)}, bf16[1,12,32,128]{3,2,1,0:T(8,128)(2,1)S(1)}, u32[]{:S(2)}, u32[]{:S(2)}) collective-permute-start(bf16[1,12,32,128]{3,2,1,0:T(8,128)(2,1)S(1)} %get-tuple-element.17), channel_id=1, source_target_pairs={{0,6},{1,7},{2,0},{3,1},{4,2},{5,3},{6,4},{7,5},{8,14},{9,15},{10,... | collective-permute-start | bytes 294920 | tf_op jit(solution)/shard_map/ppermute | solution.py:200
  14.3 0.0 collective-permute-done.1
  14.3 4.4 %collective-permute-done.2 = bf16[1,12,32,128]{3,2,1,0:T(8,128)(2,1)S(1)} collective-permute-done((bf16[1,12,32,128]{3,2,1,0:T(8,128)(2,1)S(1)}, bf16[1,12,32,128]{3,2,1,0:T(8,128)(2,1)S(1)}, u32[]{:S(2)}, u32[]{:S(2)}) %collective-permute-start.2) | collective-permute-done | bytes 98336 | tf_op jit(solution)/shard_map/ppermute | solution.py:200
  18.7 3.4 %collective-permute-done.3 = bf16[1,12,32,128]{3,2,1,0:T(8,128)(2,1)S(1)} collective-permute-done((bf16[1,12,32,128]{3,2,1,0:T(8,128)(2,1)S(1)}, bf16[1,12,32,128]{3,2,1,0:T(8,128)(2,1)S(1)}, u32[]{:S(2)}, u32[]{:S(2)}) %collective-permute-start.3) | collective-permute-done | bytes 98336 | tf_op jit(solution)/shard_map/ppermute | solution.py:200
  22.1 0.0 slice-start
  22.1 0.0 copy-start.1
  22.1 0.1 collective-permute-start.4
  22.2 1.5 %collective-permute-start.5 = (bf16[4,12,32,128]{3,2,1,0:T(8,128)(2,1)S(1)}, bf16[4,12,32,128]{3,2,1,0:T(8,128)(2,1)S(1)}, u32[]{:S(2)}, u32[]{:S(2)}) collective-permute-start(bf16[4,12,32,128]{3,2,1,0:T(8,128)(2,1)S(1)} %constant_dynamic-update-slice_fusion.own_ref), channel_id=1, source_target_pairs={{0,248},{8,0},{16,8},{24,16},{32,24},{40,32},{48,40},{56,48},{64,5... | collective-permute-start | bytes 1179656 | tf_op jit(solution)/shard_map/ppermute | solution.py:204
  23.7 0.0 slice-done
  23.7 0.3 copy.12
  24.0 0.0 copy-done.1
  24.1 0.7 copy.18
  24.8 0.5 reshape.24.weight_ref
  25.3 0.0 copy-start.3
  25.3 0.6 copy-done.3
  26.0 0.1 copy.14.bias_ref
  26.1 0.8 %first_own.1.own_ref = f32[10,128,128]{2,1,0:T(8,128)S(1)} custom-call(bf16[4,12,32,128]{3,2,1,0:T(8,128)(2,1)S(1)} %constant_dynamic-update-slice_fusion.own_ref, bf16[384,384]{1,0:T(8,128)(2,1)S(1)} %bitcast.24), custom_call_target="tpu_custom_call" | custom-call | flops 377487360 | bytes 4000000 | tf_op jit(solution)/shard_map/first_own/pallas_call | solution.py:163
  26.8 5.6 %collective-permute-done.4.before_ref = bf16[4,12,32,128]{3,2,1,0:T(8,128)(2,1)S(1)} collective-permute-done((bf16[4,12,32,128]{3,2,1,0:T(8,128)(2,1)S(1)}, bf16[4,12,32,128]{3,2,1,0:T(8,128)(2,1)S(1)}, u32[]{:S(2)}, u32[]{:S(2)}) %collective-permute-start.4) | collective-permute-done | bytes 393248 | tf_op jit(solution)/shard_map/ppermute | solution.py:203
  32.4 4.3 %collective-permute-done.5.after_ref = bf16[4,12,32,128]{3,2,1,0:T(8,128)(2,1)S(1)} collective-permute-done((bf16[4,12,32,128]{3,2,1,0:T(8,128)(2,1)S(1)}, bf16[4,12,32,128]{3,2,1,0:T(8,128)(2,1)S(1)}, u32[]{:S(2)}, u32[]{:S(2)}) %collective-permute-start.5) | collective-permute-done | bytes 393248 | tf_op jit(solution)/shard_map/ppermute | solution.py:204
  36.7 1.6 %first_layer.1.own_ref = bf16[10,128,128]{2,1,0:T(8,128)(2,1)S(1)} custom-call(s32[5]{0:T(128)S(1)} %stack.22.place_ref, bf16[4,12,32,128]{3,2,1,0:T(8,128)(2,1)S(1)} %collective-permute-done.4.before_ref, bf16[4,12,32,128]{3,2,1,0:T(8,128)(2,1)S(1)} %collective-permute-done.5.after_ref, f32[10,128,128]{2,1,0:T(8,128)S(1)} %first_own.1.own_ref, ...), custom_call_target="tpu_custom_call" | custom-call | flops 754974720 | bytes 4000000 | tf_op jit(solution)/shard_map/first_layer/pallas_call | solution.py:163
  38.3 0.3 collective-permute-start.6
  38.6 1.2 %collective-permute-start.7 = (bf16[10,128,128]{2,1,0:T(8,128)(2,1)S(1)}, bf16[10,128,128]{2,1,0:T(8,128)(2,1)S(1)}, u32[]{:S(2)}, u32[]{:S(2)}) collective-permute-start(bf16[10,128,128]{2,1,0:T(8,128)(2,1)S(1)} %first_layer.1.own_ref), channel_id=1, source_target_pairs={{0,248},{8,0},{16,8},{24,16},{32,24},{40,32},{48,40},{56,48},{64,5... | collective-permute-start | bytes 983048 | tf_op jit(solution)/shard_map/ppermute | solution.py:221
  39.9 0.0 slice-start.1
  39.9 0.0 copy-start.2
  39.9 1.0 %slice-done.1 = bf16[9,128,128]{2,1,0:T(8,128)(2,1)S(1)} async-done(((bf16[27,128,128]{2,1,0:T(8,128)(2,1)}), bf16[9,128,128]{2,1,0:T(8,128)(2,1)S(1)}, s32[]{:S(2)}) %slice-start.1) | async-done | bytes 294936 | tf_op jit(solution)/shard_map/slice | solution.py:140
  40.8 0.3 copy.15
  41.1 0.0 copy-done.2
  41.2 0.7 copy.19
  41.9 0.5 reshape.27.weight_ref
  42.4 0.0 copy-start.4
  42.4 0.6 copy-done.4
  43.1 0.1 copy.17.bias_ref
  43.2 0.7 second_own.1.own_ref
  43.9 2.4 %collective-permute-done.6.before_ref = bf16[10,128,128]{2,1,0:T(8,128)(2,1)S(1)} collective-permute-done((bf16[10,128,128]{2,1,0:T(8,128)(2,1)S(1)}, bf16[10,128,128]{2,1,0:T(8,128)(2,1)S(1)}, u32[]{:S(2)}, u32[]{:S(2)}) %collective-permute-start.6) | collective-permute-done | bytes 327712 | tf_op jit(solution)/shard_map/ppermute | solution.py:220
  46.3 4.5 %collective-permute-done.7.after_ref = bf16[10,128,128]{2,1,0:T(8,128)(2,1)S(1)} collective-permute-done((bf16[10,128,128]{2,1,0:T(8,128)(2,1)S(1)}, bf16[10,128,128]{2,1,0:T(8,128)(2,1)S(1)}, u32[]{:S(2)}, u32[]{:S(2)}) %collective-permute-start.7) | collective-permute-done | bytes 327712 | tf_op jit(solution)/shard_map/ppermute | solution.py:221
  50.8 1.5 %second_layer.1 = (bf16[2,8,16,128]{3,2,1,0:T(8,128)(2,1)S(1)}, bf16[2,8,16,128]{3,2,1,0:T(8,128)(2,1)S(1)}, bf16[2,8,16,128]{3,2,1,0:T(8,128)(2,1)S(1)}, bf16[2,8,16,128]{3,2,1,0:T(8,128)(2,1)S(1)}) custom-call(s32[5]{0:T(128)S(1)} %stack.22.place_ref, bf16[10,128,128]{2,1,0:T(8,128)(2,1)S(1)} %collective-permute-done.6.before_ref, ...), custom_call_target="tpu_custom_call" | custom-call | flops 603979776 | bytes 4000000 | tf_op jit(solution)/shard_map/second_layer/pallas_call | solution.py:163
  52.2 2.5 %collective-permute-start.9 = (bf16[2,8,16,128]{3,2,1,0:T(8,128)(2,1)S(1)}, bf16[2,8,16,128]{3,2,1,0:T(8,128)(2,1)S(1)}, u32[]{:S(2)}, u32[]{:S(2)}) collective-permute-start(bf16[2,8,16,128]{3,2,1,0:T(8,128)(2,1)S(1)} %get-tuple-element.15), channel_id=1, source_target_pairs={{0,4},{1,5},{2,6},{3,7},{4,0},{5,1},{6,2},{7,3},{8,12},{9,13},{10,... | collective-permute-start | bytes 196616 | tf_op jit(solution)/shard_map/ppermute | solution.py:238
  54.7 3.0 %collective-permute-start.8 = (bf16[2,8,16,128]{3,2,1,0:T(8,128)(2,1)S(1)}, bf16[2,8,16,128]{3,2,1,0:T(8,128)(2,1)S(1)}, u32[]{:S(2)}, u32[]{:S(2)}) collective-permute-start(bf16[2,8,16,128]{3,2,1,0:T(8,128)(2,1)S(1)} %get-tuple-element.14), channel_id=1, source_target_pairs={{0,2},{1,3},{2,4},{3,5},{4,6},{5,7},{6,0},{7,1},{8,10},{9,11},{10,... | collective-permute-start | bytes 196616 | tf_op jit(solution)/shard_map/ppermute | solution.py:238
  57.7 0.6 collective-permute-start.10
  58.3 1.2 %collective-permute-done.9.refs_2_ = bf16[2,8,16,128]{3,2,1,0:T(8,128)(2,1)S(1)} collective-permute-done((bf16[2,8,16,128]{3,2,1,0:T(8,128)(2,1)S(1)}, bf16[2,8,16,128]{3,2,1,0:T(8,128)(2,1)S(1)}, u32[]{:S(2)}, u32[]{:S(2)}) %collective-permute-start.9) | collective-permute-done | bytes 65568 | tf_op jit(solution)/shard_map/ppermute | solution.py:238
  59.5 1.4 %collective-permute-done.8.refs_1_ = bf16[2,8,16,128]{3,2,1,0:T(8,128)(2,1)S(1)} collective-permute-done((bf16[2,8,16,128]{3,2,1,0:T(8,128)(2,1)S(1)}, bf16[2,8,16,128]{3,2,1,0:T(8,128)(2,1)S(1)}, u32[]{:S(2)}, u32[]{:S(2)}) %collective-permute-start.8) | collective-permute-done | bytes 65568 | tf_op jit(solution)/shard_map/ppermute | solution.py:238
  60.8 3.0 %collective-permute-done.10.refs_3_ = bf16[2,8,16,128]{3,2,1,0:T(8,128)(2,1)S(1)} collective-permute-done((bf16[2,8,16,128]{3,2,1,0:T(8,128)(2,1)S(1)}, bf16[2,8,16,128]{3,2,1,0:T(8,128)(2,1)S(1)}, u32[]{:S(2)}, u32[]{:S(2)}) %collective-permute-start.10) | collective-permute-done | bytes 65568 | tf_op jit(solution)/shard_map/ppermute | solution.py:238
  63.9 2.6 %collective-permute-start.11 = (bf16[4,8,16,128]{3,2,1,0:T(8,128)(2,1)S(1)}, bf16[4,8,16,128]{3,2,1,0:T(8,128)(2,1)S(1)}, u32[]{:S(2)}, u32[]{:S(2)}) collective-permute-start(bf16[4,8,16,128]{3,2,1,0:T(8,128)(2,1)S(1)} %pad_maximum_fusion), channel_id=1, source_target_pairs={{0,1},{1,0},{2,3},{3,2},{4,5},{5,4},{6,7},{7,6},{8,9},{9,8},{10,11... | collective-permute-start | bytes 393224 | tf_op jit(solution)/shard_map/ppermute | solution.py:240
  66.5 1.0 %collective-permute-done.11.swapped_ref = bf16[4,8,16,128]{3,2,1,0:T(8,128)(2,1)S(1)} collective-permute-done((bf16[4,8,16,128]{3,2,1,0:T(8,128)(2,1)S(1)}, bf16[4,8,16,128]{3,2,1,0:T(8,128)(2,1)S(1)}, u32[]{:S(2)}, u32[]{:S(2)}) %collective-permute-start.11) | collective-permute-done | bytes 131104 | tf_op jit(solution)/shard_map/ppermute | solution.py:240
  67.4 1.4 %unpack_rows.1 = bf16[16,1,64,128]{3,2,1,0:T(8,128)(2,1)} custom-call(s32[5]{0:T(128)S(1)} %stack.22.place_ref, bf16[4,8,16,128]{3,2,1,0:T(8,128)(2,1)S(1)} %collective-permute-done.11.swapped_ref, bf16[2,8,16,128]{3,2,1,0:T(8,128)(2,1)S(1)} %get-tuple-element.13.refs_0_, bf16[2,8,16,128]{3,2,1,0:T(8,128)(2,1)S(1)} %collective-permute-done.8.refs_1_, ...), custom_call_target="tpu_custom_call" | custom-call | tf_op jit(solution)/shard_map/unpack_rows/pallas_call | solution.py:163
  (14 shorter events, 0.3 us)
Async XLA Ops:
  0.1 1.0 %copy-start = (bf16[16,1,64,128]{3,2,1,0:T(8,128)(2,1)S(1)}, bf16[16,1,64,128]{3,2,1,0:T(8,128)(2,1)}, u32[]{:S(2)}) copy-start(bf16[16,1,64,128]{3,2,1,0:T(8,128)(2,1)} %volume_ref.1) | copy-start | bytes 786436
  1.8 1.8 %collective-permute-start = (bf16[4,12,16,128]{3,2,1,0:T(8,128)(2,1)S(1)}, bf16[4,12,16,128]{3,2,1,0:T(8,128)(2,1)S(1)}, u32[]{:S(2)}, u32[]{:S(2)}) collective-permute-start(bf16[4,12,16,128]{3,2,1,0:T(8,128)(2,1)S(1)} %get-tuple-element.12), channel_id=1, source_target_pairs={{0,1},{1,0},{2,3},{3,2},{4,5},{5,4},{6,7},{7,6},{8,9},{9,8},{10,11... | collective-permute-start | bytes 589832 | tf_op jit(solution)/shard_map/ppermute | solution.py:193
  3.7 10.6 %collective-permute-start.1 = (bf16[1,12,32,128]{3,2,1,0:T(8,128)(2,1)S(1)}, bf16[1,12,32,128]{3,2,1,0:T(8,128)(2,1)S(1)}, u32[]{:S(2)}, u32[]{:S(2)}) collective-permute-start(bf16[1,12,32,128]{3,2,1,0:T(8,128)(2,1)S(1)} %get-tuple-element.19), channel_id=1, source_target_pairs={{0,2},{1,3},{2,4},{3,5},{4,6},{5,7},{6,0},{7,1},{8,10},{9,11},{10,... | collective-permute-start | bytes 294920 | tf_op jit(solution)/shard_map/ppermute | solution.py:200
  6.8 11.9 %collective-permute-start.2 = (bf16[1,12,32,128]{3,2,1,0:T(8,128)(2,1)S(1)}, bf16[1,12,32,128]{3,2,1,0:T(8,128)(2,1)S(1)}, u32[]{:S(2)}, u32[]{:S(2)}) collective-permute-start(bf16[1,12,32,128]{3,2,1,0:T(8,128)(2,1)S(1)} %get-tuple-element.20), channel_id=1, source_target_pairs={{0,4},{1,5},{2,6},{3,7},{4,0},{5,1},{6,2},{7,3},{8,12},{9,13},{10,... | collective-permute-start | bytes 294920 | tf_op jit(solution)/shard_map/ppermute | solution.py:200
  11.9 10.2 %collective-permute-start.3 = (bf16[1,12,32,128]{3,2,1,0:T(8,128)(2,1)S(1)}, bf16[1,12,32,128]{3,2,1,0:T(8,128)(2,1)S(1)}, u32[]{:S(2)}, u32[]{:S(2)}) collective-permute-start(bf16[1,12,32,128]{3,2,1,0:T(8,128)(2,1)S(1)} %get-tuple-element.17), channel_id=1, source_target_pairs={{0,6},{1,7},{2,0},{3,1},{4,2},{5,3},{6,4},{7,5},{8,14},{9,15},{10,... | collective-permute-start | bytes 294920 | tf_op jit(solution)/shard_map/ppermute | solution.py:200
  22.1 1.6 %slice-start = ((bf16[27,128,128]{2,1,0:T(8,128)(2,1)}), bf16[9,128,128]{2,1,0:T(8,128)(2,1)S(1)}, s32[]{:S(2)}) async-start(bf16[27,128,128]{2,1,0:T(8,128)(2,1)} %param.6), calls=%async_computation | async-start | bytes 589824 | tf_op jit(solution)/shard_map/slice | solution.py:140
  22.1 1.9 %copy-start.1 = (bf16[27,128,128]{2,1,0:T(8,128)(2,1)S(1)}, bf16[27,128,128]{2,1,0:T(8,128)(2,1)}, u32[]{:S(2)}) copy-start(bf16[27,128,128]{2,1,0:T(8,128)(2,1)} %param.6) | copy-start | bytes 2654212
  22.1 10.3 %collective-permute-start.4 = (bf16[4,12,32,128]{3,2,1,0:T(8,128)(2,1)S(1)}, bf16[4,12,32,128]{3,2,1,0:T(8,128)(2,1)S(1)}, u32[]{:S(2)}, u32[]{:S(2)}) collective-permute-start(bf16[4,12,32,128]{3,2,1,0:T(8,128)(2,1)S(1)} %constant_dynamic-update-slice_fusion.own_ref), channel_id=1, source_target_pairs={{0,8},{8,16},{16,24},{24,32},{32,40},{40,48},{48,56},{56,64},{64,7... | collective-permute-start | bytes 1179656 | tf_op jit(solution)/shard_map/ppermute | solution.py:203
  22.2 14.5 %collective-permute-start.5 = (bf16[4,12,32,128]{3,2,1,0:T(8,128)(2,1)S(1)}, bf16[4,12,32,128]{3,2,1,0:T(8,128)(2,1)S(1)}, u32[]{:S(2)}, u32[]{:S(2)}) collective-permute-start(bf16[4,12,32,128]{3,2,1,0:T(8,128)(2,1)S(1)} %constant_dynamic-update-slice_fusion.own_ref), channel_id=1, source_target_pairs={{0,248},{8,0},{16,8},{24,16},{32,24},{40,32},{48,40},{56,48},{64,5... | collective-permute-start | bytes 1179656 | tf_op jit(solution)/shard_map/ppermute | solution.py:204
  25.3 0.7 copy-start.3
  38.3 7.9 %collective-permute-start.6 = (bf16[10,128,128]{2,1,0:T(8,128)(2,1)S(1)}, bf16[10,128,128]{2,1,0:T(8,128)(2,1)S(1)}, u32[]{:S(2)}, u32[]{:S(2)}) collective-permute-start(bf16[10,128,128]{2,1,0:T(8,128)(2,1)S(1)} %first_layer.1.own_ref), channel_id=1, source_target_pairs={{0,8},{8,16},{16,24},{24,32},{32,40},{40,48},{48,56},{56,64},{64,7... | collective-permute-start | bytes 983048 | tf_op jit(solution)/shard_map/ppermute | solution.py:220
  38.6 12.1 %collective-permute-start.7 = (bf16[10,128,128]{2,1,0:T(8,128)(2,1)S(1)}, bf16[10,128,128]{2,1,0:T(8,128)(2,1)S(1)}, u32[]{:S(2)}, u32[]{:S(2)}) collective-permute-start(bf16[10,128,128]{2,1,0:T(8,128)(2,1)S(1)} %first_layer.1.own_ref), channel_id=1, source_target_pairs={{0,248},{8,0},{16,8},{24,16},{32,24},{40,32},{48,40},{56,48},{64,5... | collective-permute-start | bytes 983048 | tf_op jit(solution)/shard_map/ppermute | solution.py:221
  39.9 1.0 %slice-start.1 = ((bf16[27,128,128]{2,1,0:T(8,128)(2,1)}), bf16[9,128,128]{2,1,0:T(8,128)(2,1)S(1)}, s32[]{:S(2)}) async-start(bf16[27,128,128]{2,1,0:T(8,128)(2,1)} %param.8), calls=%async_computation.1 | async-start | bytes 589824 | tf_op jit(solution)/shard_map/slice | solution.py:140
  39.9 1.3 %copy-start.2 = (bf16[27,128,128]{2,1,0:T(8,128)(2,1)S(1)}, bf16[27,128,128]{2,1,0:T(8,128)(2,1)}, u32[]{:S(2)}) copy-start(bf16[27,128,128]{2,1,0:T(8,128)(2,1)} %param.8) | copy-start | bytes 2654212
  42.4 0.7 copy-start.4
  52.2 7.3 %collective-permute-start.9 = (bf16[2,8,16,128]{3,2,1,0:T(8,128)(2,1)S(1)}, bf16[2,8,16,128]{3,2,1,0:T(8,128)(2,1)S(1)}, u32[]{:S(2)}, u32[]{:S(2)}) collective-permute-start(bf16[2,8,16,128]{3,2,1,0:T(8,128)(2,1)S(1)} %get-tuple-element.15), channel_id=1, source_target_pairs={{0,4},{1,5},{2,6},{3,7},{4,0},{5,1},{6,2},{7,3},{8,12},{9,13},{10,... | collective-permute-start | bytes 196616 | tf_op jit(solution)/shard_map/ppermute | solution.py:238
  54.7 6.2 %collective-permute-start.8 = (bf16[2,8,16,128]{3,2,1,0:T(8,128)(2,1)S(1)}, bf16[2,8,16,128]{3,2,1,0:T(8,128)(2,1)S(1)}, u32[]{:S(2)}, u32[]{:S(2)}) collective-permute-start(bf16[2,8,16,128]{3,2,1,0:T(8,128)(2,1)S(1)} %get-tuple-element.14), channel_id=1, source_target_pairs={{0,2},{1,3},{2,4},{3,5},{4,6},{5,7},{6,0},{7,1},{8,10},{9,11},{10,... | collective-permute-start | bytes 196616 | tf_op jit(solution)/shard_map/ppermute | solution.py:238
  57.7 6.2 %collective-permute-start.10 = (bf16[2,8,16,128]{3,2,1,0:T(8,128)(2,1)S(1)}, bf16[2,8,16,128]{3,2,1,0:T(8,128)(2,1)S(1)}, u32[]{:S(2)}, u32[]{:S(2)}) collective-permute-start(bf16[2,8,16,128]{3,2,1,0:T(8,128)(2,1)S(1)} %get-tuple-element.16), channel_id=1, source_target_pairs={{0,6},{1,7},{2,0},{3,1},{4,2},{5,3},{6,4},{7,5},{8,14},{9,15},{10,... | collective-permute-start | bytes 196616 | tf_op jit(solution)/shard_map/ppermute | solution.py:238
  63.9 3.6 %collective-permute-start.11 = (bf16[4,8,16,128]{3,2,1,0:T(8,128)(2,1)S(1)}, bf16[4,8,16,128]{3,2,1,0:T(8,128)(2,1)S(1)}, u32[]{:S(2)}, u32[]{:S(2)}) collective-permute-start(bf16[4,8,16,128]{3,2,1,0:T(8,128)(2,1)S(1)} %pad_maximum_fusion), channel_id=1, source_target_pairs={{0,1},{1,0},{2,3},{3,2},{4,5},{5,4},{6,7},{7,6},{8,9},{9,8},{10,11... | collective-permute-start | bytes 393224 | tf_op jit(solution)/shard_map/ppermute | solution.py:240

commit v3 on v2

--- a/solution.py
+++ b/solution.py
@@ -39,29 +39,48 @@
             store(start + n, along_lanes(total[:, n * lanes : (n + 1) * lanes], lanes))
 
 
-def pack_kernel(place_ref, volume_ref, mine_ref, theirs_ref, rows_ref):
+def pack_kernel(place_ref, volume_ref, *refs):
+    outs, rows_ref = refs[:-1], refs[-1]
     width, _, length, lanes = volume_ref.shape
-    groups = mine_ref.shape[0]
-    rows = length // (groups * CORES)
+    groups = len(outs)
+    rows = length // groups
     edge = jnp.zeros((RIM, width, lanes), BF16)
     rows_ref[:RIM] = edge
     rows_ref[RIM + length :] = edge
     turned = jnp.swapaxes(volume_ref[:, 0].astype(F32), 0, 1)
     rows_ref[RIM : RIM + length] = turned.astype(BF16)
-    group, core = place_ref[0], place_ref[1]
     for k in range(groups):
-        target = lax.rem(group + k, groups) * CORES
-        mine_ref[k] = rows_ref[pl.ds((target + core) * rows, rows + 2 * RIM)]
-        theirs_ref[k] = rows_ref[pl.ds((target + 1 - core) * rows, rows + 2 * RIM)]
-
-
-def own_kernel(own_ref, weight_ref, out_ref):
+        target = lax.rem(place_ref[0] + k, groups)
+        outs[k][0] = rows_ref[pl.ds(target * rows, rows + 2 * RIM)]
+
+
+def gather_rows(place_ref, kept_ref, other_ref, joined_ref, outside=None):
+    core = place_ref[1]
+    groups, rows, width, lanes = other_ref.shape
+    offset = core * (kept_ref.shape[1] - rows)
+    for row in range(rows):
+        parts = []
+        for g in range(groups):
+            kept = kept_ref[g, offset + row]
+            other = other_ref[g, row]
+            parts += [jnp.where(core == 0, kept, other), jnp.where(core == 0, other, kept)]
+        joined = jnp.concatenate(parts, axis=0)
+        if outside is not None:
+            joined = jnp.where(outside, jnp.zeros_like(joined), joined)
+        joined_ref[row] = joined
+
+
+def first_own_kernel(place_ref, kept_ref, other_ref, weight_ref, later_ref, bias_ref, out_ref, core_ref, joined_ref):
+    core_ref[0] = place_ref[1]
+    gather_rows(place_ref, kept_ref, other_ref, joined_ref)
+    second_own_kernel(joined_ref, weight_ref, out_ref)
+
+
+def second_own_kernel(own_ref, weight_ref, out_ref):
     rows, _, lanes = out_ref.shape
 
     def get(_, row):
-        if len(own_ref.shape) == 3:
-            return own_ref[row]
-        return jnp.concatenate([own_ref[g, row] for g in range(own_ref.shape[0])], axis=0)
+        return own_ref[row]
 
     def store(row, value):
         out_ref[row] = value
@@ -69,26 +88,22 @@
     conv_rows(get, 1, weight_ref[...], store, rows, lanes)
 
 
-def reader(place_ref, before_ref, after_ref):
-    outside = (place_ref[2] == 0, place_ref[2] == place_ref[3] - 1)
-    refs = (before_ref, after_ref)
+def outside_of(place_ref):
+    return place_ref[2] == 0, place_ref[2] == place_ref[3] - 1
+
+
+def first_kernel(
+    place_ref, before_ref, before_other_ref, after_ref, after_other_ref, own_ref, weight_ref, bias_ref, out_ref, joined_ref
+):
+    rows, _, lanes = out_ref.shape
+    block = place_ref[0] * CORES + place_ref[1]
+    bias = bias_ref[...]
+    outside = outside_of(place_ref)
+    gather_rows(place_ref, before_ref, before_other_ref, joined_ref.at[0], outside[0])
+    gather_rows(place_ref, after_ref, after_other_ref, joined_ref.at[1], outside[1])
 
     def get(a, row):
-        ref = refs[a]
-        if len(ref.shape) == 3:
-            value = ref[row]
-        else:
-            value = jnp.concatenate([ref[g, row] for g in range(ref.shape[0])], axis=0)
-        return jnp.where(outside[a], jnp.zeros_like(value), value)
-
-    return get
-
-
-def first_kernel(place_ref, before_ref, after_ref, own_ref, weight_ref, bias_ref, out_ref):
-    rows, _, lanes = out_ref.shape
-    group, core = place_ref[0], place_ref[1]
-    block = group * CORES + core
-    bias = bias_ref[...]
+        return joined_ref[a, row]
 
     def store(row, value):
         value = jnp.maximum(value + own_ref[row] + bias, 0.0)
@@ -98,7 +113,6 @@
             value = jnp.where(block == place_ref[4] - 1, 0.0, value)
         out_ref[row] = value.astype(BF16)
 
-    get = reader(place_ref, before_ref, after_ref)
     conv_rows(get, 2, weight_ref[...], store, rows, lanes)
 
 
@@ -114,7 +128,13 @@
                 at = (g * cores + c) * width
                 all_ref[g, c, row] = value[at : at + width]
 
-    get = reader(place_ref, before_ref, after_ref)
+    beside = (before_ref, after_ref)
+    outside = outside_of(place_ref)
+
+    def get(a, row):
+        value = beside[a][row]
+        return jnp.where(outside[a], jnp.zeros_like(value), value)
+
     conv_rows(get, 2, weight_ref[...], store, rows, lanes)
     for k in range(groups):
         outs[k][...] = all_ref[lax.rem(place_ref[0] + k, groups)]
@@ -164,7 +184,7 @@
             kernel,
             out_shape=shapes,
             in_specs=[SMEM if x.ndim == 1 else VMEM for x in inputs],
-            out_specs=VMEM if single else [VMEM] * len(shapes),
+            out_specs=VMEM if single else [SMEM if len(x.shape) == 1 else VMEM for x in shapes],
             scratch_shapes=scratch,
             compiler_params=PARAMS,
             **kwargs,
@@ -182,37 +202,40 @@
         own_one, beside_one = arranged(weight_one)
         own_two, beside_two = arranged(weight_two)
 
-        piece = jax.ShapeDtypeStruct((groups, rows + 2 * RIM, width, lanes), BF16)
-        mine, theirs = call(
+        tall = CORES * rows + 2 * RIM
+        pieces = call(
             pack_kernel,
-            [piece, piece],
+            [jax.ShapeDtypeStruct((1, tall, width, lanes), BF16)] * groups,
             [place, volume],
             [pltpu.VMEM((length + 2 * RIM, width, lanes), BF16)],
             name="pack_rows",
         )
-        swapped = lax.ppermute(theirs, "chan", swap)
-        first = jnp.where(core == 0, mine, swapped)
-        second = jnp.where(core == 0, swapped, mine)
-        both = jnp.concatenate([first, second], axis=2)
-        whole = jnp.zeros_like(both)
-        whole = lax.dynamic_update_slice_in_dim(whole, both[:1], group, 0)
+        kept = jnp.zeros((groups, tall, width, lanes), BF16)
+        kept = lax.dynamic_update_slice_in_dim(kept, pieces[0], group, 0)
         for k in range(1, groups):
-            got = lax.ppermute(both[k : k + 1], "chan", ahead(k))
-            whole = lax.dynamic_update_slice_in_dim(whole, got, (group + groups - k) % groups, 0)
-
-        before = lax.ppermute(whole, "space", up)
-        after = lax.ppermute(whole, "space", down)
-        own = call(
-            own_kernel,
-            jax.ShapeDtypeStruct((rows + RIM, full, lanes), F32),
-            [whole, own_one],
+            got = lax.ppermute(pieces[k], "chan", ahead(k))
+            kept = lax.dynamic_update_slice_in_dim(kept, got, (group + groups - k) % groups, 0)
+
+        def from_other_core(array, core):
+            sent = lax.dynamic_slice_in_dim(array, (1 - core) * rows, rows + 2 * RIM, 1)
+            return lax.ppermute(sent, "chan", swap)
+
+        before = lax.ppermute(kept, "space", up)
+        after = lax.ppermute(kept, "space", down)
+        joined = (rows + 2 * RIM, full, lanes)
+        own, done = call(
+            first_own_kernel,
+            [jax.ShapeDtypeStruct((rows + RIM, full, lanes), F32), jax.ShapeDtypeStruct((1,), jnp.int32)],
+            [place, kept, from_other_core(kept, core), own_one, beside_one, bias_one[:, None]],
+            [pltpu.VMEM(joined, BF16)],
             cost_estimate=cost(rows + RIM, 1, full, lanes),
             name="first_own",
         )
         hidden = call(
             first_kernel,
             jax.ShapeDtypeStruct((rows + RIM, full, lanes), BF16),
-            [place, before, after, own, beside_one, bias_one[:, None]],
+            [place, before, from_other_core(before, done[0]), after, from_other_core(after, done[0]), own, beside_one, bias_one[:, None]],
+            [pltpu.VMEM((2, *joined), BF16)],
             cost_estimate=cost(rows + RIM, 2, full, lanes),
             name="first_layer",
         )
@@ -220,7 +243,7 @@
         before = lax.ppermute(hidden, "space", up)
         after = lax.ppermute(hidden, "space", down)
         own = call(
-            own_kernel,
+            second_own_kernel,
             jax.ShapeDtypeStruct((rows, full, lanes), F32),
             [hidden, own_two],
             cost_estimate=cost(rows, 1, full, lanes),

time: 69.8 us -> 73.2 us (1.049)
  starting transfers between devices: 23 us -> 33.9 us
  waiting for transfers between devices: 32.1 us -> 22 us
  Pallas kernels: 6.57 us -> 7.62 us
  local copies, waits for them, and re-layouts: 6.79 us -> 7.8 us
    ppermute x5 -> x8, waiting for transfers between devices: 17.6 us -> 8.45 us  [the longest x3 6.39 us: per_device(): got = lax.ppermute(pieces[k], 'chan', ahead(k))]
    ppermute x5 -> x8, starting transfers between devices: 12.1 us -> 18.8 us  [the longest x3 10.6 us: per_device(): got = lax.ppermute(pieces[k], 'chan', ahead(k))]
    ppermute x1, starting transfers between devices: 0.32 us -> 6.17 us  [per_device(): before = lax.ppermute(hidden, 'space', up)]
    ppermute x3, waiting for transfers between devices: 5.58 us -> 3.74 us  [per_device(): lax.ppermute(blocks[k], 'chan', ahead(k))]
    ppermute x2 -> x1, starting transfers between devices: 3.34 us -> 1.5 us  [per_device(): swapped = lax.ppermute(theirs, 'chan', swap)]
    ppermute x1, waiting for transfers between devices: 4.5 us -> 6.1 us  [per_device(): after = lax.ppermute(hidden, 'space', down)]
    ppermute x3, starting transfers between devices: 6.04 us -> 7.44 us  [per_device(): lax.ppermute(blocks[k], 'chan', ahead(k))]
    ppermute x1, starting transfers between devices: 1.22 us -> 0.01 us  [per_device(): after = lax.ppermute(hidden, 'space', down)]
  transfers between devices with their start and end apart: 12 -> 14, of which waited for: 11 -> 9; matrix products, arithmetic and copies ran while one was open for 5% -> 6% of each run, Pallas kernels for 2% -> 3%
where the time goes in v3:
time: 73.2 us; the launch traced here: 72.2 us
  starting transfers between devices  33.9 us (46%)
  waiting for transfers between devices  22 us (30%)
  local copies, waits for them, and re-layouts  7.8 us (11%)
  Pallas kernels  7.62 us (10%)
  between operations  0.89 us (1%)
    ppermute x3, starting transfers between devices, per_device(): got = lax.ppermute(pieces[k], 'chan', ahead(k))  10.6 us
    pallas_call x6, Pallas kernels, call(): pl.pallas_call(kernel, out_shape=shapes, in_specs=[SMEM if x.ndim == 1 el...  7.62 us
    ppermute x3, starting transfers between devices, per_device(): lax.ppermute(blocks[k], 'chan', ahead(k))  7.44 us
    ppermute x3, waiting for transfers between devices, per_device(): got = lax.ppermute(pieces[k], 'chan', ahead(k))  6.39 us
    ppermute x1, starting transfers between devices, per_device(): before = lax.ppermute(hidden, 'space', up)  6.17 us
    ppermute x1, waiting for transfers between devices, per_device(): after = lax.ppermute(hidden, 'space', down)  6.1 us
    ppermute x1, starting transfers between devices, per_device(): before = lax.ppermute(kept, 'space', up)  5.24 us
    ppermute x3, waiting for transfers between devices, per_device(): lax.ppermute(blocks[k], 'chan', ahead(k))  3.74 us
  transfers between devices with their start and end apart: 14, of which 9 were waited for; matrix products, arithmetic and copies ran while one was open for 6% of the time, Pallas kernels for 3%

profile of v3, /device:TPU:31, one launch (start us, length us, event | category | flops | bytes accessed | tf_op | source)
XLA Modules:
  0.0 72.2 jit_solution(14370294506958000475)
XLA Ops:
  0.0 0.1 stack.22.place_ref
  0.1 0.0 copy-start
  0.1 0.9 %copy-done = bf16[16,1,64,128]{3,2,1,0:T(8,128)(2,1)S(1)} copy-done((bf16[16,1,64,128]{3,2,1,0:T(8,128)(2,1)S(1)}, bf16[16,1,64,128]{3,2,1,0:T(8,128)(2,1)}, u32[]{:S(2)}) %copy-start) | copy-done | bytes 262168
  1.0 0.7 pack_rows.1
  1.7 3.1 %collective-permute-start = (bf16[1,20,16,128]{3,2,1,0:T(8,128)(2,1)S(1)}, bf16[1,20,16,128]{3,2,1,0:T(8,128)(2,1)S(1)}, u32[]{:S(2)}, u32[]{:S(2)}) collective-permute-start(bf16[1,20,16,128]{3,2,1,0:T(8,128)(2,1)S(1)} %get-tuple-element.16), channel_id=1, source_target_pairs={{0,2},{1,3},{2,4},{3,5},{4,6},{5,7},{6,0},{7,1},{8,10},{9,11},{10,... | collective-permute-start | bytes 245768 | tf_op jit(solution)/shard_map/ppermute | solution.py:216
  4.8 5.1 %collective-permute-start.1 = (bf16[1,20,16,128]{3,2,1,0:T(8,128)(2,1)S(1)}, bf16[1,20,16,128]{3,2,1,0:T(8,128)(2,1)S(1)}, u32[]{:S(2)}, u32[]{:S(2)}) collective-permute-start(bf16[1,20,16,128]{3,2,1,0:T(8,128)(2,1)S(1)} %get-tuple-element.17), channel_id=1, source_target_pairs={{0,4},{1,5},{2,6},{3,7},{4,0},{5,1},{6,2},{7,3},{8,12},{9,13},{10,... | collective-permute-start | bytes 245768 | tf_op jit(solution)/shard_map/ppermute | solution.py:216
  9.9 2.4 %collective-permute-start.2 = (bf16[1,20,16,128]{3,2,1,0:T(8,128)(2,1)S(1)}, bf16[1,20,16,128]{3,2,1,0:T(8,128)(2,1)S(1)}, u32[]{:S(2)}, u32[]{:S(2)}) collective-permute-start(bf16[1,20,16,128]{3,2,1,0:T(8,128)(2,1)S(1)} %get-tuple-element.18), channel_id=1, source_target_pairs={{0,6},{1,7},{2,0},{3,1},{4,2},{5,3},{6,4},{7,5},{8,14},{9,15},{10,... | collective-permute-start | bytes 245768 | tf_op jit(solution)/shard_map/ppermute | solution.py:216
  12.4 0.0 copy-start.2
  12.4 0.0 collective-permute-done
  12.4 2.6 %collective-permute-done.1 = bf16[1,20,16,128]{3,2,1,0:T(8,128)(2,1)S(1)} collective-permute-done((bf16[1,20,16,128]{3,2,1,0:T(8,128)(2,1)S(1)}, bf16[1,20,16,128]{3,2,1,0:T(8,128)(2,1)S(1)}, u32[]{:S(2)}, u32[]{:S(2)}) %collective-permute-start.1) | collective-permute-done | bytes 81952 | tf_op jit(solution)/shard_map/ppermute | solution.py:216
  15.1 3.7 %collective-permute-done.2 = bf16[1,20,16,128]{3,2,1,0:T(8,128)(2,1)S(1)} collective-permute-done((bf16[1,20,16,128]{3,2,1,0:T(8,128)(2,1)S(1)}, bf16[1,20,16,128]{3,2,1,0:T(8,128)(2,1)S(1)}, u32[]{:S(2)}, u32[]{:S(2)}) %collective-permute-start.2) | collective-permute-done | bytes 81952 | tf_op jit(solution)/shard_map/ppermute | solution.py:216
  18.8 0.5 collective-permute-start.6
  19.4 0.9 %collective-permute-start.4 = (bf16[4,12,16,128]{3,2,1,0:T(8,128)(2,1)S(1)}, bf16[4,12,16,128]{3,2,1,0:T(8,128)(2,1)S(1)}, u32[]{:S(2)}, u32[]{:S(2)}) collective-permute-start(bf16[4,12,16,128]{3,2,1,0:T(8,128)(2,1)S(1)} %constant_dynamic-slice_fusion.6), channel_id=1, source_target_pairs={{0,1},{1,0},{2,3},{3,2},{4,5},{5,4},{6,7},{7,6},{8,9},{9,8},{10,11... | collective-permute-start | bytes 589832 | tf_op jit(solution)/shard_map/ppermute | solution.py:221
  20.3 5.2 %collective-permute-start.3 = (bf16[4,20,16,128]{3,2,1,0:T(8,128)(2,1)S(1)}, bf16[4,20,16,128]{3,2,1,0:T(8,128)(2,1)S(1)}, u32[]{:S(2)}, u32[]{:S(2)}) collective-permute-start(bf16[4,20,16,128]{3,2,1,0:T(8,128)(2,1)S(1)} %constant_dynamic-update-slice_fusion.kept_ref), channel_id=1, source_target_pairs={{0,8},{8,16},{16,24},{24,32},{32,40},{40,48},{48,56},{56,64},{64,7... | collective-permute-start | bytes 983048 | tf_op jit(solution)/shard_map/ppermute | solution.py:223
  25.5 1.0 %slice.14 = bf16[9,128,128]{2,1,0:T(8,128)(2,1)S(1)} slice(bf16[27,128,128]{2,1,0:T(8,128)(2,1)} %param.6), slice={[9:18], [0:128], [0:128]} | slice | bytes 589824 | tf_op jit(solution)/shard_map/slice | solution.py:160
  26.5 0.0 copy-done.2
  26.5 0.7 copy.20
  27.2 0.5 reshape.28.later_ref.weight_ref
  27.8 0.0 copy-start.3
  27.8 0.6 copy-done.3
  28.4 0.1 copy.15.bias_ref
  28.6 0.2 copy.13
  28.9 0.0 collective-permute-done.4.other_ref
  28.9 1.7 %first_own.1 = (f32[10,128,128]{2,1,0:T(8,128)S(1)}, s32[1]{0:T(128)}) custom-call(s32[5]{0:T(128)S(1)} %stack.22.place_ref, bf16[4,20,16,128]{3,2,1,0:T(8,128)(2,1)S(1)} %constant_dynamic-update-slice_fusion.kept_ref, bf16[4,12,16,128]{3,2,1,0:T(8,128)(2,1)S(1)} %collective-permute-done.4.other_ref, bf16[384,384]{1,0:T(8,128)(2,1)S(1)} %bitcast.25, ...), custom_call_target="tpu_custom_call" | custom-call | flops 377487360 | bytes 4000000 | tf_op jit(solution)/shard_map/first_own/pallas_call | solution.py:183
  31.3 0.7 collective-permute-done.6.after_ref
  31.9 1.4 %collective-permute-start.7 = (bf16[4,12,16,128]{3,2,1,0:T(8,128)(2,1)S(1)}, bf16[4,12,16,128]{3,2,1,0:T(8,128)(2,1)S(1)}, u32[]{:S(2)}, u32[]{:S(2)}) collective-permute-start(bf16[4,12,16,128]{3,2,1,0:T(8,128)(2,1)S(1)} %constant_dynamic-slice_fusion.4), channel_id=1, source_target_pairs={{0,1},{1,0},{2,3},{3,2},{4,5},{5,4},{6,7},{7,6},{8,9},{9,8},{10,11... | collective-permute-start | bytes 589832 | tf_op jit(solution)/shard_map/ppermute | solution.py:221
  33.4 0.0 collective-permute-done.3.before_ref
  33.4 0.1 collective-permute-start.5
  33.5 0.9 %collective-permute-done.7.after_other_ref = bf16[4,12,16,128]{3,2,1,0:T(8,128)(2,1)S(1)} collective-permute-done((bf16[4,12,16,128]{3,2,1,0:T(8,128)(2,1)S(1)}, bf16[4,12,16,128]{3,2,1,0:T(8,128)(2,1)S(1)}, u32[]{:S(2)}, u32[]{:S(2)}) %collective-permute-start.7) | collective-permute-done | bytes 196640 | tf_op jit(solution)/shard_map/ppermute | solution.py:221
  34.4 0.5 collective-permute-done.5.before_other_ref
  34.9 1.7 %first_layer.1.own_ref = bf16[10,128,128]{2,1,0:T(8,128)(2,1)S(1)} custom-call(s32[5]{0:T(128)S(1)} %stack.22.place_ref, bf16[4,20,16,128]{3,2,1,0:T(8,128)(2,1)S(1)} %collective-permute-done.3.before_ref, bf16[4,12,16,128]{3,2,1,0:T(8,128)(2,1)S(1)} %collective-permute-done.5.before_other_ref, ...), custom_call_target="tpu_custom_call" | custom-call | flops 754974720 | bytes 4000000 | tf_op jit(solution)/shard_map/first_layer/pallas_call | solution.py:183
  36.6 6.2 %collective-permute-start.8 = (bf16[10,128,128]{2,1,0:T(8,128)(2,1)S(1)}, bf16[10,128,128]{2,1,0:T(8,128)(2,1)S(1)}, u32[]{:S(2)}, u32[]{:S(2)}) collective-permute-start(bf16[10,128,128]{2,1,0:T(8,128)(2,1)S(1)} %first_layer.1.own_ref), channel_id=1, source_target_pairs={{0,8},{8,16},{16,24},{24,32},{32,40},{40,48},{48,56},{56,64},{64,7... | collective-permute-start | bytes 983048 | tf_op jit(solution)/shard_map/ppermute | solution.py:243
  42.8 0.0 collective-permute-start.9
  42.8 0.0 slice-start
  42.8 0.0 copy-start.1
  42.8 1.0 %slice-done = bf16[9,128,128]{2,1,0:T(8,128)(2,1)S(1)} async-done(((bf16[27,128,128]{2,1,0:T(8,128)(2,1)}), bf16[9,128,128]{2,1,0:T(8,128)(2,1)S(1)}, s32[]{:S(2)}) %slice-start) | async-done | bytes 294936 | tf_op jit(solution)/shard_map/slice | solution.py:160
  43.7 0.3 copy.17
  44.1 0.0 copy-done.1
  44.1 0.7 copy.21
  44.8 0.5 reshape.31.weight_ref
  45.4 0.0 copy-start.4
  45.4 0.6 copy-done.4
  46.0 0.1 copy.19.bias_ref
  46.1 0.7 second_own.1.own_ref
  46.8 2.7 %collective-permute-done.8.before_ref = bf16[10,128,128]{2,1,0:T(8,128)(2,1)S(1)} collective-permute-done((bf16[10,128,128]{2,1,0:T(8,128)(2,1)S(1)}, bf16[10,128,128]{2,1,0:T(8,128)(2,1)S(1)}, u32[]{:S(2)}, u32[]{:S(2)}) %collective-permute-start.8) | collective-permute-done | bytes 327712 | tf_op jit(solution)/shard_map/ppermute | solution.py:243
  49.5 6.1 %collective-permute-done.9.after_ref = bf16[10,128,128]{2,1,0:T(8,128)(2,1)S(1)} collective-permute-done((bf16[10,128,128]{2,1,0:T(8,128)(2,1)S(1)}, bf16[10,128,128]{2,1,0:T(8,128)(2,1)S(1)}, u32[]{:S(2)}, u32[]{:S(2)}) %collective-permute-start.9) | collective-permute-done | bytes 327712 | tf_op jit(solution)/shard_map/ppermute | solution.py:244
  55.6 1.5 %second_layer.1 = (bf16[2,8,16,128]{3,2,1,0:T(8,128)(2,1)S(1)}, bf16[2,8,16,128]{3,2,1,0:T(8,128)(2,1)S(1)}, bf16[2,8,16,128]{3,2,1,0:T(8,128)(2,1)S(1)}, bf16[2,8,16,128]{3,2,1,0:T(8,128)(2,1)S(1)}) custom-call(s32[5]{0:T(128)S(1)} %stack.22.place_ref, bf16[10,128,128]{2,1,0:T(8,128)(2,1)S(1)} %collective-permute-done.8.before_ref, ...), custom_call_target="tpu_custom_call" | custom-call | flops 603979776 | bytes 4000000 | tf_op jit(solution)/shard_map/second_layer/pallas_call | solution.py:183
  57.1 3.9 %collective-permute-start.11 = (bf16[2,8,16,128]{3,2,1,0:T(8,128)(2,1)S(1)}, bf16[2,8,16,128]{3,2,1,0:T(8,128)(2,1)S(1)}, u32[]{:S(2)}, u32[]{:S(2)}) collective-permute-start(bf16[2,8,16,128]{3,2,1,0:T(8,128)(2,1)S(1)} %get-tuple-element.23), channel_id=1, source_target_pairs={{0,4},{1,5},{2,6},{3,7},{4,0},{5,1},{6,2},{7,3},{8,12},{9,13},{10,... | collective-permute-start | bytes 196616 | tf_op jit(solution)/shard_map/ppermute | solution.py:261
  60.9 1.4 %collective-permute-start.10 = (bf16[2,8,16,128]{3,2,1,0:T(8,128)(2,1)S(1)}, bf16[2,8,16,128]{3,2,1,0:T(8,128)(2,1)S(1)}, u32[]{:S(2)}, u32[]{:S(2)}) collective-permute-start(bf16[2,8,16,128]{3,2,1,0:T(8,128)(2,1)S(1)} %get-tuple-element.22), channel_id=1, source_target_pairs={{0,2},{1,3},{2,4},{3,5},{4,6},{5,7},{6,0},{7,1},{8,10},{9,11},{10,... | collective-permute-start | bytes 196616 | tf_op jit(solution)/shard_map/ppermute | solution.py:261
  62.4 2.1 %collective-permute-start.12 = (bf16[2,8,16,128]{3,2,1,0:T(8,128)(2,1)S(1)}, bf16[2,8,16,128]{3,2,1,0:T(8,128)(2,1)S(1)}, u32[]{:S(2)}, u32[]{:S(2)}) collective-permute-start(bf16[2,8,16,128]{3,2,1,0:T(8,128)(2,1)S(1)} %get-tuple-element.24), channel_id=1, source_target_pairs={{0,6},{1,7},{2,0},{3,1},{4,2},{5,3},{6,4},{7,5},{8,14},{9,15},{10,... | collective-permute-start | bytes 196616 | tf_op jit(solution)/shard_map/ppermute | solution.py:261
  64.5 0.0 collective-permute-done.11.refs_2_
  64.5 3.7 %collective-permute-done.10.refs_1_ = bf16[2,8,16,128]{3,2,1,0:T(8,128)(2,1)S(1)} collective-permute-done((bf16[2,8,16,128]{3,2,1,0:T(8,128)(2,1)S(1)}, bf16[2,8,16,128]{3,2,1,0:T(8,128)(2,1)S(1)}, u32[]{:S(2)}, u32[]{:S(2)}) %collective-permute-start.10) | collective-permute-done | bytes 65568 | tf_op jit(solution)/shard_map/ppermute | solution.py:261
  68.3 0.0 collective-permute-done.12.refs_3_
  68.3 1.5 %collective-permute-start.13 = (bf16[4,8,16,128]{3,2,1,0:T(8,128)(2,1)S(1)}, bf16[4,8,16,128]{3,2,1,0:T(8,128)(2,1)S(1)}, u32[]{:S(2)}, u32[]{:S(2)}) collective-permute-start(bf16[4,8,16,128]{3,2,1,0:T(8,128)(2,1)S(1)} %pad_maximum_fusion), channel_id=1, source_target_pairs={{0,1},{1,0},{2,3},{3,2},{4,5},{5,4},{6,7},{7,6},{8,9},{9,8},{10,11... | collective-permute-start | bytes 393224 | tf_op jit(solution)/shard_map/ppermute | solution.py:263
  69.8 1.0 %collective-permute-done.13.swapped_ref = bf16[4,8,16,128]{3,2,1,0:T(8,128)(2,1)S(1)} collective-permute-done((bf16[4,8,16,128]{3,2,1,0:T(8,128)(2,1)S(1)}, bf16[4,8,16,128]{3,2,1,0:T(8,128)(2,1)S(1)}, u32[]{:S(2)}, u32[]{:S(2)}) %collective-permute-start.13) | collective-permute-done | bytes 131104 | tf_op jit(solution)/shard_map/ppermute | solution.py:263
  70.8 1.4 %unpack_rows.1 = bf16[16,1,64,128]{3,2,1,0:T(8,128)(2,1)} custom-call(s32[5]{0:T(128)S(1)} %stack.22.place_ref, bf16[4,8,16,128]{3,2,1,0:T(8,128)(2,1)S(1)} %collective-permute-done.13.swapped_ref, bf16[2,8,16,128]{3,2,1,0:T(8,128)(2,1)S(1)} %get-tuple-element.21.refs_0_, bf16[2,8,16,128]{3,2,1,0:T(8,128)(2,1)S(1)} %collective-permute-done.10.refs_1_, ...), custom_call_target="tpu_custom_call" | custom-call | tf_op jit(solution)/shard_map/unpack_rows/pallas_call | solution.py:183
  (17 shorter events, 0.4 us)
Async XLA Ops:
  0.1 1.0 %copy-start = (bf16[16,1,64,128]{3,2,1,0:T(8,128)(2,1)S(1)}, bf16[16,1,64,128]{3,2,1,0:T(8,128)(2,1)}, u32[]{:S(2)}) copy-start(bf16[16,1,64,128]{3,2,1,0:T(8,128)(2,1)} %volume_ref.1) | copy-start | bytes 786436
  1.7 10.7 %collective-permute-start = (bf16[1,20,16,128]{3,2,1,0:T(8,128)(2,1)S(1)}, bf16[1,20,16,128]{3,2,1,0:T(8,128)(2,1)S(1)}, u32[]{:S(2)}, u32[]{:S(2)}) collective-permute-start(bf16[1,20,16,128]{3,2,1,0:T(8,128)(2,1)S(1)} %get-tuple-element.16), channel_id=1, source_target_pairs={{0,2},{1,3},{2,4},{3,5},{4,6},{5,7},{6,0},{7,1},{8,10},{9,11},{10,... | collective-permute-start | bytes 245768 | tf_op jit(solution)/shard_map/ppermute | solution.py:216
  4.8 10.3 %collective-permute-start.1 = (bf16[1,20,16,128]{3,2,1,0:T(8,128)(2,1)S(1)}, bf16[1,20,16,128]{3,2,1,0:T(8,128)(2,1)S(1)}, u32[]{:S(2)}, u32[]{:S(2)}) collective-permute-start(bf16[1,20,16,128]{3,2,1,0:T(8,128)(2,1)S(1)} %get-tuple-element.17), channel_id=1, source_target_pairs={{0,4},{1,5},{2,6},{3,7},{4,0},{5,1},{6,2},{7,3},{8,12},{9,13},{10,... | collective-permute-start | bytes 245768 | tf_op jit(solution)/shard_map/ppermute | solution.py:216
  9.9 8.9 %collective-permute-start.2 = (bf16[1,20,16,128]{3,2,1,0:T(8,128)(2,1)S(1)}, bf16[1,20,16,128]{3,2,1,0:T(8,128)(2,1)S(1)}, u32[]{:S(2)}, u32[]{:S(2)}) collective-permute-start(bf16[1,20,16,128]{3,2,1,0:T(8,128)(2,1)S(1)} %get-tuple-element.18), channel_id=1, source_target_pairs={{0,6},{1,7},{2,0},{3,1},{4,2},{5,3},{6,4},{7,5},{8,14},{9,15},{10,... | collective-permute-start | bytes 245768 | tf_op jit(solution)/shard_map/ppermute | solution.py:216
  12.4 14.1 %copy-start.2 = (bf16[27,128,128]{2,1,0:T(8,128)(2,1)S(1)}, bf16[27,128,128]{2,1,0:T(8,128)(2,1)}, u32[]{:S(2)}) copy-start(bf16[27,128,128]{2,1,0:T(8,128)(2,1)} %param.6) | copy-start | bytes 2654212
  18.8 13.1 %collective-permute-start.6 = (bf16[4,20,16,128]{3,2,1,0:T(8,128)(2,1)S(1)}, bf16[4,20,16,128]{3,2,1,0:T(8,128)(2,1)S(1)}, u32[]{:S(2)}, u32[]{:S(2)}) collective-permute-start(bf16[4,20,16,128]{3,2,1,0:T(8,128)(2,1)S(1)} %constant_dynamic-update-slice_fusion.kept_ref), channel_id=1, source_target_pairs={{0,248},{8,0},{16,8},{24,16},{32,24},{40,32},{48,40},{56,48},{64,5... | collective-permute-start | bytes 983048 | tf_op jit(solution)/shard_map/ppermute | solution.py:224
  19.4 9.5 %collective-permute-start.4 = (bf16[4,12,16,128]{3,2,1,0:T(8,128)(2,1)S(1)}, bf16[4,12,16,128]{3,2,1,0:T(8,128)(2,1)S(1)}, u32[]{:S(2)}, u32[]{:S(2)}) collective-permute-start(bf16[4,12,16,128]{3,2,1,0:T(8,128)(2,1)S(1)} %constant_dynamic-slice_fusion.6), channel_id=1, source_target_pairs={{0,1},{1,0},{2,3},{3,2},{4,5},{5,4},{6,7},{7,6},{8,9},{9,8},{10,11... | collective-permute-start | bytes 589832 | tf_op jit(solution)/shard_map/ppermute | solution.py:221
  20.3 13.1 %collective-permute-start.3 = (bf16[4,20,16,128]{3,2,1,0:T(8,128)(2,1)S(1)}, bf16[4,20,16,128]{3,2,1,0:T(8,128)(2,1)S(1)}, u32[]{:S(2)}, u32[]{:S(2)}) collective-permute-start(bf16[4,20,16,128]{3,2,1,0:T(8,128)(2,1)S(1)} %constant_dynamic-update-slice_fusion.kept_ref), channel_id=1, source_target_pairs={{0,8},{8,16},{16,24},{24,32},{32,40},{40,48},{48,56},{56,64},{64,7... | collective-permute-start | bytes 983048 | tf_op jit(solution)/shard_map/ppermute | solution.py:223
  27.8 0.7 copy-start.3
  31.9 2.5 %collective-permute-start.7 = (bf16[4,12,16,128]{3,2,1,0:T(8,128)(2,1)S(1)}, bf16[4,12,16,128]{3,2,1,0:T(8,128)(2,1)S(1)}, u32[]{:S(2)}, u32[]{:S(2)}) collective-permute-start(bf16[4,12,16,128]{3,2,1,0:T(8,128)(2,1)S(1)} %constant_dynamic-slice_fusion.4), channel_id=1, source_target_pairs={{0,1},{1,0},{2,3},{3,2},{4,5},{5,4},{6,7},{7,6},{8,9},{9,8},{10,11... | collective-permute-start | bytes 589832 | tf_op jit(solution)/shard_map/ppermute | solution.py:221
  33.4 1.5 %collective-permute-start.5 = (bf16[4,12,16,128]{3,2,1,0:T(8,128)(2,1)S(1)}, bf16[4,12,16,128]{3,2,1,0:T(8,128)(2,1)S(1)}, u32[]{:S(2)}, u32[]{:S(2)}) collective-permute-start(bf16[4,12,16,128]{3,2,1,0:T(8,128)(2,1)S(1)} %constant_dynamic-slice_fusion.5), channel_id=1, source_target_pairs={{0,1},{1,0},{2,3},{3,2},{4,5},{5,4},{6,7},{7,6},{8,9},{9,8},{10,11... | collective-permute-start | bytes 589832 | tf_op jit(solution)/shard_map/ppermute | solution.py:221
  36.6 12.9 %collective-permute-start.8 = (bf16[10,128,128]{2,1,0:T(8,128)(2,1)S(1)}, bf16[10,128,128]{2,1,0:T(8,128)(2,1)S(1)}, u32[]{:S(2)}, u32[]{:S(2)}) collective-permute-start(bf16[10,128,128]{2,1,0:T(8,128)(2,1)S(1)} %first_layer.1.own_ref), channel_id=1, source_target_pairs={{0,8},{8,16},{16,24},{24,32},{32,40},{40,48},{48,56},{56,64},{64,7... | collective-permute-start | bytes 983048 | tf_op jit(solution)/shard_map/ppermute | solution.py:243
  42.8 12.8 %collective-permute-start.9 = (bf16[10,128,128]{2,1,0:T(8,128)(2,1)S(1)}, bf16[10,128,128]{2,1,0:T(8,128)(2,1)S(1)}, u32[]{:S(2)}, u32[]{:S(2)}) collective-permute-start(bf16[10,128,128]{2,1,0:T(8,128)(2,1)S(1)} %first_layer.1.own_ref), channel_id=1, source_target_pairs={{0,248},{8,0},{16,8},{24,16},{32,24},{40,32},{48,40},{56,48},{64,5... | collective-permute-start | bytes 983048 | tf_op jit(solution)/shard_map/ppermute | solution.py:244
  42.8 1.0 %slice-start = ((bf16[27,128,128]{2,1,0:T(8,128)(2,1)}), bf16[9,128,128]{2,1,0:T(8,128)(2,1)S(1)}, s32[]{:S(2)}) async-start(bf16[27,128,128]{2,1,0:T(8,128)(2,1)} %param.8), calls=%async_computation | async-start | bytes 589824 | tf_op jit(solution)/shard_map/slice | solution.py:160
  42.8 1.3 %copy-start.1 = (bf16[27,128,128]{2,1,0:T(8,128)(2,1)S(1)}, bf16[27,128,128]{2,1,0:T(8,128)(2,1)}, u32[]{:S(2)}) copy-start(bf16[27,128,128]{2,1,0:T(8,128)(2,1)} %param.8) | copy-start | bytes 2654212
  45.4 0.7 copy-start.4
  57.1 7.4 %collective-permute-start.11 = (bf16[2,8,16,128]{3,2,1,0:T(8,128)(2,1)S(1)}, bf16[2,8,16,128]{3,2,1,0:T(8,128)(2,1)S(1)}, u32[]{:S(2)}, u32[]{:S(2)}) collective-permute-start(bf16[2,8,16,128]{3,2,1,0:T(8,128)(2,1)S(1)} %get-tuple-element.23), channel_id=1, source_target_pairs={{0,4},{1,5},{2,6},{3,7},{4,0},{5,1},{6,2},{7,3},{8,12},{9,13},{10,... | collective-permute-start | bytes 196616 | tf_op jit(solution)/shard_map/ppermute | solution.py:261
  60.9 7.3 %collective-permute-start.10 = (bf16[2,8,16,128]{3,2,1,0:T(8,128)(2,1)S(1)}, bf16[2,8,16,128]{3,2,1,0:T(8,128)(2,1)S(1)}, u32[]{:S(2)}, u32[]{:S(2)}) collective-permute-start(bf16[2,8,16,128]{3,2,1,0:T(8,128)(2,1)S(1)} %get-tuple-element.22), channel_id=1, source_target_pairs={{0,2},{1,3},{2,4},{3,5},{4,6},{5,7},{6,0},{7,1},{8,10},{9,11},{10,... | collective-permute-start | bytes 196616 | tf_op jit(solution)/shard_map/ppermute | solution.py:261
  62.4 5.9 %collective-permute-start.12 = (bf16[2,8,16,128]{3,2,1,0:T(8,128)(2,1)S(1)}, bf16[2,8,16,128]{3,2,1,0:T(8,128)(2,1)S(1)}, u32[]{:S(2)}, u32[]{:S(2)}) collective-permute-start(bf16[2,8,16,128]{3,2,1,0:T(8,128)(2,1)S(1)} %get-tuple-element.24), channel_id=1, source_target_pairs={{0,6},{1,7},{2,0},{3,1},{4,2},{5,3},{6,4},{7,5},{8,14},{9,15},{10,... | collective-permute-start | bytes 196616 | tf_op jit(solution)/shard_map/ppermute | solution.py:261
  68.3 2.5 %collective-permute-start.13 = (bf16[4,8,16,128]{3,2,1,0:T(8,128)(2,1)S(1)}, bf16[4,8,16,128]{3,2,1,0:T(8,128)(2,1)S(1)}, u32[]{:S(2)}, u32[]{:S(2)}) collective-permute-start(bf16[4,8,16,128]{3,2,1,0:T(8,128)(2,1)S(1)} %pad_maximum_fusion), channel_id=1, source_target_pairs={{0,1},{1,0},{2,3},{3,2},{4,5},{5,4},{6,7},{7,6},{8,9},{9,8},{10,11... | collective-permute-start | bytes 393224 | tf_op jit(solution)/shard_map/ppermute | solution.py:263

commit v4 on v2

--- a/solution.py
+++ b/solution.py
@@ -39,20 +39,19 @@
             store(start + n, along_lanes(total[:, n * lanes : (n + 1) * lanes], lanes))
 
 
-def pack_kernel(place_ref, volume_ref, mine_ref, theirs_ref, rows_ref):
+def pack_kernel(place_ref, volume_ref, *refs):
+    outs, rows_ref = refs[:-1], refs[-1]
     width, _, length, lanes = volume_ref.shape
-    groups = mine_ref.shape[0]
-    rows = length // (groups * CORES)
+    groups = len(outs)
+    rows = length // groups
     edge = jnp.zeros((RIM, width, lanes), BF16)
     rows_ref[:RIM] = edge
     rows_ref[RIM + length :] = edge
     turned = jnp.swapaxes(volume_ref[:, 0].astype(F32), 0, 1)
     rows_ref[RIM : RIM + length] = turned.astype(BF16)
-    group, core = place_ref[0], place_ref[1]
     for k in range(groups):
-        target = lax.rem(group + k, groups) * CORES
-        mine_ref[k] = rows_ref[pl.ds((target + core) * rows, rows + 2 * RIM)]
-        theirs_ref[k] = rows_ref[pl.ds((target + 1 - core) * rows, rows + 2 * RIM)]
+        target = lax.rem(place_ref[0] + k, groups)
+        outs[k][0] = rows_ref[pl.ds(target * rows, rows + 2 * RIM)]
 
 
 def own_kernel(own_ref, weight_ref, out_ref):
@@ -151,12 +150,18 @@
     space = mesh.shape["space"]
     chan = mesh.shape["chan"]
     groups = chan // CORES
-    up = [(i, (i + 1) % space) for i in range(space)]
-    down = [(i, (i + space - 1) % space) for i in range(space)]
     swap = [(i, i ^ 1) for i in range(chan)]
 
+    half = space // 2
+    moved = {half - 1: space - 1, space - 1: half - 1}
+    spot = [moved.get(i, i) for i in range(space)]
+    up = [(spot[i], spot[(i + 1) % space]) for i in range(space)]
+    down = [(j, i) for i, j in up]
+
     def ahead(k):
-        return [(i, (i + CORES * k) % chan) for i in range(chan)]
+        return [
+            (i * chan + j, spot[i] * chan + (j + CORES * k) % chan) for i in range(space) for j in range(chan)
+        ]
 
     def call(kernel, shapes, inputs, scratch=(), **kwargs):
         single = not isinstance(shapes, list)
@@ -175,30 +180,33 @@
         full = width * chan
         rows = length // chan
         index = lax.axis_index("chan")
-        plane = lax.axis_index("space")
+        spot_index = lax.axis_index("space")
+        plane = jnp.where(spot_index == half - 1, space - 1, jnp.where(spot_index == space - 1, half - 1, spot_index))
         group, core = index // CORES, index % CORES
         place = jnp.stack([group, core, plane, jnp.int32(space), jnp.int32(chan)]).astype(jnp.int32)
 
         own_one, beside_one = arranged(weight_one)
         own_two, beside_two = arranged(weight_two)
 
-        piece = jax.ShapeDtypeStruct((groups, rows + 2 * RIM, width, lanes), BF16)
-        mine, theirs = call(
+        tall = CORES * rows + 2 * RIM
+        pieces = call(
             pack_kernel,
-            [piece, piece],
+            [jax.ShapeDtypeStruct((1, tall, width, lanes), BF16)] * groups,
             [place, volume],
             [pltpu.VMEM((length + 2 * RIM, width, lanes), BF16)],
             name="pack_rows",
         )
+        kept = jnp.zeros((groups, tall, width, lanes), BF16)
+        for k in range(groups):
+            got = lax.ppermute(pieces[k], ("space", "chan"), ahead(k))
+            kept = lax.dynamic_update_slice_in_dim(kept, got, (group + groups - k) % groups, 0)
+
+        mine = lax.dynamic_slice_in_dim(kept, core * rows, rows + 2 * RIM, 1)
+        theirs = lax.dynamic_slice_in_dim(kept, (1 - core) * rows, rows + 2 * RIM, 1)
         swapped = lax.ppermute(theirs, "chan", swap)
         first = jnp.where(core == 0, mine, swapped)
         second = jnp.where(core == 0, swapped, mine)
-        both = jnp.concatenate([first, second], axis=2)
-        whole = jnp.zeros_like(both)
-        whole = lax.dynamic_update_slice_in_dim(whole, both[:1], group, 0)
-        for k in range(1, groups):
-            got = lax.ppermute(both[k : k + 1], "chan", ahead(k))
-            whole = lax.dynamic_update_slice_in_dim(whole, got, (group + groups - k) % groups, 0)
+        whole = jnp.concatenate([first, second], axis=2)
 
         before = lax.ppermute(whole, "space", up)
         after = lax.ppermute(whole, "space", down)
@@ -235,7 +243,7 @@
             name="second_layer",
         )
 
-        blocks = [blocks[0]] + [lax.ppermute(blocks[k], "chan", ahead(k)) for k in range(1, groups)]
+        blocks = [lax.ppermute(blocks[k], ("space", "chan"), ahead(k)) for k in range(groups)]
         theirs = jnp.stack([lax.dynamic_index_in_dim(b, 1 - core, 0, keepdims=False) for b in blocks])
         swapped = lax.ppermute(theirs, "chan", swap)
         return call(

time: 69.8 us -> 69.4 us (level); the launches traced: 68.8 us -> 69.3 us
  starting transfers between devices: 23 us -> 33 us
  waiting for transfers between devices: 32.1 us -> 23.5 us
  local copies, waits for them, and re-layouts: 6.79 us -> 5.87 us
    ppermute x6 -> x8, waiting for transfers between devices: 13.3 us -> 7.23 us  [the longest x4 4.28 us: per_device(): lax.ppermute(blocks[k], ('space', 'chan'), ahead(k))]
    ppermute x6 -> x8, starting transfers between devices: 16.6 us -> 21.8 us  [the longest x4 12.8 us: per_device(): got = lax.ppermute(pieces[k], ('space', 'chan'), ahead(k))]
    ppermute x2, starting transfers between devices: 3.34 us -> 6.34 us  [per_device(): swapped = lax.ppermute(theirs, 'chan', swap)]
    ppermute x1, waiting for transfers between devices: 4.5 us -> 2.54 us  [per_device(): after = lax.ppermute(hidden, 'space', down)]
    ppermute x1, waiting for transfers between devices: 4.31 us -> 2.51 us  [per_device(): after = lax.ppermute(whole, 'space', down)]
    ppermute x1, waiting for transfers between devices: 2.36 us -> 3.47 us  [per_device(): before = lax.ppermute(hidden, 'space', up)]
    ppermute x1, starting transfers between devices: 1.22 us -> 2.2 us  [per_device(): after = lax.ppermute(hidden, 'space', down)]
    slice x4, local copies, waits for them, and re-layouts: 0.97 us -> 0.02 us  [arranged(): own = taps[1].transpose(1, 3, 0, 2).reshape(3 * outer, 3 * inner)]
  transfers between devices with their start and end apart: 12 -> 14, of which waited for: 11 -> 11; matrix products, arithmetic and copies ran while one was open for 5% -> 5% of each run, Pallas kernels for 2% -> 2%
where the time goes in v4:
time: 69.4 us; the launch traced here: 69.3 us
  starting transfers between devices  33 us (48%)
  waiting for transfers between devices  23.5 us (34%)
  Pallas kernels  6.56 us (9%)
  local copies, waits for them, and re-layouts  5.87 us (8%)
    ppermute x4, starting transfers between devices, per_device(): got = lax.ppermute(pieces[k], ('space', 'chan'), ahead(k))  12.8 us
    ppermute x4, starting transfers between devices, per_device(): lax.ppermute(blocks[k], ('space', 'chan'), ahead(k))  9.01 us
    pallas_call x6, Pallas kernels, call(): pl.pallas_call(kernel, out_shape=shapes, in_specs=[SMEM if x.ndim == 1 el...  6.56 us
    ppermute x2, starting transfers between devices, per_device(): swapped = lax.ppermute(theirs, 'chan', swap)  6.34 us
    ppermute x1, waiting for transfers between devices, per_device(): before = lax.ppermute(whole, 'space', up)  5.7 us
    ppermute x4, waiting for transfers between devices, per_device(): lax.ppermute(blocks[k], ('space', 'chan'), ahead(k))  4.28 us
    unnamed x14, local copies, waits for them, and re-layouts  3.71 us
    ppermute x1, waiting for transfers between devices, per_device(): before = lax.ppermute(hidden, 'space', up)  3.47 us
  transfers between devices with their start and end apart: 14, of which 11 were waited for; matrix products, arithmetic and copies ran while one was open for 5% of the time, Pallas kernels for 2%

profile of v4, /device:TPU:31, one launch (start us, length us, event | category | flops | bytes accessed | tf_op | source)
XLA Modules:
  0.0 69.3 jit_solution(9739109104149964707)
XLA Ops:
  0.0 0.1 stack.22.place_ref
  0.1 0.0 copy-start
  0.1 0.9 %copy-done = bf16[16,1,64,128]{3,2,1,0:T(8,128)(2,1)S(1)} copy-done((bf16[16,1,64,128]{3,2,1,0:T(8,128)(2,1)S(1)}, bf16[16,1,64,128]{3,2,1,0:T(8,128)(2,1)}, u32[]{:S(2)}) %copy-start) | copy-done | bytes 262168
  1.0 0.7 %pack_rows.1 = (bf16[1,20,16,128]{3,2,1,0:T(8,128)(2,1)S(1)}, bf16[1,20,16,128]{3,2,1,0:T(8,128)(2,1)S(1)}, bf16[1,20,16,128]{3,2,1,0:T(8,128)(2,1)S(1)}, bf16[1,20,16,128]{3,2,1,0:T(8,128)(2,1)S(1)}) custom-call(s32[5]{0:T(128)S(1)} %stack.22.place_ref, bf16[16,1,64,128]{3,2,1,0:T(8,128)(2,1)S(1)} %copy-done), custom_call_target="tpu_custom_call" | custom-call | tf_op jit(solution)/shard_map/pack_rows/pallas_call | solution.py:168
  1.7 3.5 %collective-permute-start = (bf16[1,20,16,128]{3,2,1,0:T(8,128)(2,1)S(1)}, bf16[1,20,16,128]{3,2,1,0:T(8,128)(2,1)S(1)}, u32[]{:S(2)}, u32[]{:S(2)}) collective-permute-start(bf16[1,20,16,128]{3,2,1,0:T(8,128)(2,1)S(1)} %get-tuple-element.13), channel_id=1, source_target_pairs={{0,0},{1,1},{2,2},{3,3},{4,4},{5,5},{6,6},{7,7},{8,8},{9,9},{10,10... | collective-permute-start | bytes 245768 | tf_op jit(solution)/shard_map/ppermute | solution.py:201
  5.3 2.8 %collective-permute-start.1 = (bf16[1,20,16,128]{3,2,1,0:T(8,128)(2,1)S(1)}, bf16[1,20,16,128]{3,2,1,0:T(8,128)(2,1)S(1)}, u32[]{:S(2)}, u32[]{:S(2)}) collective-permute-start(bf16[1,20,16,128]{3,2,1,0:T(8,128)(2,1)S(1)} %get-tuple-element.14), channel_id=1, source_target_pairs={{0,2},{1,3},{2,4},{3,5},{4,6},{5,7},{6,0},{7,1},{8,10},{9,11},{10,... | collective-permute-start | bytes 245768 | tf_op jit(solution)/shard_map/ppermute | solution.py:201
  8.1 3.6 %collective-permute-start.2 = (bf16[1,20,16,128]{3,2,1,0:T(8,128)(2,1)S(1)}, bf16[1,20,16,128]{3,2,1,0:T(8,128)(2,1)S(1)}, u32[]{:S(2)}, u32[]{:S(2)}) collective-permute-start(bf16[1,20,16,128]{3,2,1,0:T(8,128)(2,1)S(1)} %get-tuple-element.15), channel_id=1, source_target_pairs={{0,4},{1,5},{2,6},{3,7},{4,0},{5,1},{6,2},{7,3},{8,12},{9,13},{10,... | collective-permute-start | bytes 245768 | tf_op jit(solution)/shard_map/ppermute | solution.py:201
  11.7 2.8 %collective-permute-start.3 = (bf16[1,20,16,128]{3,2,1,0:T(8,128)(2,1)S(1)}, bf16[1,20,16,128]{3,2,1,0:T(8,128)(2,1)S(1)}, u32[]{:S(2)}, u32[]{:S(2)}) collective-permute-start(bf16[1,20,16,128]{3,2,1,0:T(8,128)(2,1)S(1)} %get-tuple-element.16), channel_id=1, source_target_pairs={{0,6},{1,7},{2,0},{3,1},{4,2},{5,3},{6,4},{7,5},{8,14},{9,15},{10,... | collective-permute-start | bytes 245768 | tf_op jit(solution)/shard_map/ppermute | solution.py:201
  14.5 0.0 collective-permute-done
  14.6 0.0 collective-permute-done.1
  14.6 2.1 %collective-permute-done.2 = bf16[1,20,16,128]{3,2,1,0:T(8,128)(2,1)S(1)} collective-permute-done((bf16[1,20,16,128]{3,2,1,0:T(8,128)(2,1)S(1)}, bf16[1,20,16,128]{3,2,1,0:T(8,128)(2,1)S(1)}, u32[]{:S(2)}, u32[]{:S(2)}) %collective-permute-start.2) | collective-permute-done | bytes 81952 | tf_op jit(solution)/shard_map/ppermute | solution.py:201
  16.7 0.8 %collective-permute-done.3 = bf16[1,20,16,128]{3,2,1,0:T(8,128)(2,1)S(1)} collective-permute-done((bf16[1,20,16,128]{3,2,1,0:T(8,128)(2,1)S(1)}, bf16[1,20,16,128]{3,2,1,0:T(8,128)(2,1)S(1)}, u32[]{:S(2)}, u32[]{:S(2)}) %collective-permute-start.3) | collective-permute-done | bytes 81952 | tf_op jit(solution)/shard_map/ppermute | solution.py:201
  17.6 2.6 %collective-permute-start.4 = (bf16[4,12,16,128]{3,2,1,0:T(8,128)(2,1)S(1)}, bf16[4,12,16,128]{3,2,1,0:T(8,128)(2,1)S(1)}, u32[]{:S(2)}, u32[]{:S(2)}) collective-permute-start(bf16[4,12,16,128]{3,2,1,0:T(8,128)(2,1)S(1)} %constant_dynamic-slice_fusion.4), channel_id=1, source_target_pairs={{0,1},{1,0},{2,3},{3,2},{4,5},{5,4},{6,7},{7,6},{8,9},{9,8},{10,11... | collective-permute-start | bytes 589832 | tf_op jit(solution)/shard_map/ppermute | solution.py:206
  20.2 1.1 %collective-permute-done.4 = bf16[4,12,16,128]{3,2,1,0:T(8,128)(2,1)S(1)} collective-permute-done((bf16[4,12,16,128]{3,2,1,0:T(8,128)(2,1)S(1)}, bf16[4,12,16,128]{3,2,1,0:T(8,128)(2,1)S(1)}, u32[]{:S(2)}, u32[]{:S(2)}) %collective-permute-start.4) | collective-permute-done | bytes 196640 | tf_op jit(solution)/shard_map/ppermute | solution.py:206
  21.3 0.0 slice-start
  21.4 0.0 copy-start.1
  21.4 0.1 collective-permute-start.5
  21.5 2.4 %collective-permute-start.6 = (bf16[4,12,32,128]{3,2,1,0:T(8,128)(2,1)S(1)}, bf16[4,12,32,128]{3,2,1,0:T(8,128)(2,1)S(1)}, u32[]{:S(2)}, u32[]{:S(2)}) collective-permute-start(bf16[4,12,32,128]{3,2,1,0:T(8,128)(2,1)S(1)} %pad_maximum_fusion.own_ref), channel_id=1, source_target_pairs={{8,0},{16,8},{24,16},{32,24},{40,32},{48,40},{56,48},{64,56},{72,6... | collective-permute-start | bytes 1179656 | tf_op jit(solution)/shard_map/ppermute | solution.py:212
  23.8 0.0 slice-done
  23.8 0.3 copy.12
  24.1 0.0 copy-done.1
  24.2 0.7 copy.18
  24.9 0.5 reshape.24.weight_ref
  25.4 0.0 copy-start.3
  25.4 0.6 copy-done.3
  26.1 0.1 copy.14.bias_ref
  26.2 0.8 %first_own.1.own_ref = f32[10,128,128]{2,1,0:T(8,128)S(1)} custom-call(bf16[4,12,32,128]{3,2,1,0:T(8,128)(2,1)S(1)} %pad_maximum_fusion.own_ref, bf16[384,384]{1,0:T(8,128)(2,1)S(1)} %bitcast.24), custom_call_target="tpu_custom_call" | custom-call | flops 377487360 | bytes 4000000 | tf_op jit(solution)/shard_map/first_own/pallas_call | solution.py:168
  27.0 5.7 %collective-permute-done.5.before_ref = bf16[4,12,32,128]{3,2,1,0:T(8,128)(2,1)S(1)} collective-permute-done((bf16[4,12,32,128]{3,2,1,0:T(8,128)(2,1)S(1)}, bf16[4,12,32,128]{3,2,1,0:T(8,128)(2,1)S(1)}, u32[]{:S(2)}, u32[]{:S(2)}) %collective-permute-start.5) | collective-permute-done | bytes 393248 | tf_op jit(solution)/shard_map/ppermute | solution.py:211
  32.7 2.5 %collective-permute-done.6.after_ref = bf16[4,12,32,128]{3,2,1,0:T(8,128)(2,1)S(1)} collective-permute-done((bf16[4,12,32,128]{3,2,1,0:T(8,128)(2,1)S(1)}, bf16[4,12,32,128]{3,2,1,0:T(8,128)(2,1)S(1)}, u32[]{:S(2)}, u32[]{:S(2)}) %collective-permute-start.6) | collective-permute-done | bytes 393248 | tf_op jit(solution)/shard_map/ppermute | solution.py:212
  35.2 1.6 %first_layer.1.own_ref = bf16[10,128,128]{2,1,0:T(8,128)(2,1)S(1)} custom-call(s32[5]{0:T(128)S(1)} %stack.22.place_ref, bf16[4,12,32,128]{3,2,1,0:T(8,128)(2,1)S(1)} %collective-permute-done.5.before_ref, bf16[4,12,32,128]{3,2,1,0:T(8,128)(2,1)S(1)} %collective-permute-done.6.after_ref, f32[10,128,128]{2,1,0:T(8,128)S(1)} %first_own.1.own_ref, ...), custom_call_target="tpu_custom_call" | custom-call | flops 754974720 | bytes 4000000 | tf_op jit(solution)/shard_map/first_layer/pallas_call | solution.py:168
  36.8 0.0 slice-start.1
  36.8 0.0 copy-start.2
  36.8 0.2 collective-permute-start.7
  37.0 2.2 %collective-permute-start.8 = (bf16[10,128,128]{2,1,0:T(8,128)(2,1)S(1)}, bf16[10,128,128]{2,1,0:T(8,128)(2,1)S(1)}, u32[]{:S(2)}, u32[]{:S(2)}) collective-permute-start(bf16[10,128,128]{2,1,0:T(8,128)(2,1)S(1)} %first_layer.1.own_ref), channel_id=1, source_target_pairs={{8,0},{16,8},{24,16},{32,24},{40,32},{48,40},{56,48},{64,56},{72,6... | collective-permute-start | bytes 983048 | tf_op jit(solution)/shard_map/ppermute | solution.py:229
  39.2 0.0 slice-done.1
  39.2 0.3 copy.15
  39.6 0.0 copy-done.2
  39.6 0.7 copy.19
  40.3 0.5 reshape.27.weight_ref
  40.9 0.0 copy-start.4
  40.9 0.6 copy-done.4
  41.5 0.1 copy.17.bias_ref
  41.6 0.7 second_own.1.own_ref
  42.3 3.5 %collective-permute-done.7.before_ref = bf16[10,128,128]{2,1,0:T(8,128)(2,1)S(1)} collective-permute-done((bf16[10,128,128]{2,1,0:T(8,128)(2,1)S(1)}, bf16[10,128,128]{2,1,0:T(8,128)(2,1)S(1)}, u32[]{:S(2)}, u32[]{:S(2)}) %collective-permute-start.7) | collective-permute-done | bytes 327712 | tf_op jit(solution)/shard_map/ppermute | solution.py:228
  45.8 2.5 %collective-permute-done.8.after_ref = bf16[10,128,128]{2,1,0:T(8,128)(2,1)S(1)} collective-permute-done((bf16[10,128,128]{2,1,0:T(8,128)(2,1)S(1)}, bf16[10,128,128]{2,1,0:T(8,128)(2,1)S(1)}, u32[]{:S(2)}, u32[]{:S(2)}) %collective-permute-start.8) | collective-permute-done | bytes 327712 | tf_op jit(solution)/shard_map/ppermute | solution.py:229
  48.3 1.5 %second_layer.1 = (bf16[2,8,16,128]{3,2,1,0:T(8,128)(2,1)S(1)}, bf16[2,8,16,128]{3,2,1,0:T(8,128)(2,1)S(1)}, bf16[2,8,16,128]{3,2,1,0:T(8,128)(2,1)S(1)}, bf16[2,8,16,128]{3,2,1,0:T(8,128)(2,1)S(1)}) custom-call(s32[5]{0:T(128)S(1)} %stack.22.place_ref, bf16[10,128,128]{2,1,0:T(8,128)(2,1)S(1)} %collective-permute-done.7.before_ref, ...), custom_call_target="tpu_custom_call" | custom-call | flops 603979776 | bytes 4000000 | tf_op jit(solution)/shard_map/second_layer/pallas_call | solution.py:168
  49.8 4.1 %collective-permute-start.11 = (bf16[2,8,16,128]{3,2,1,0:T(8,128)(2,1)S(1)}, bf16[2,8,16,128]{3,2,1,0:T(8,128)(2,1)S(1)}, u32[]{:S(2)}, u32[]{:S(2)}) collective-permute-start(bf16[2,8,16,128]{3,2,1,0:T(8,128)(2,1)S(1)} %get-tuple-element.19), channel_id=1, source_target_pairs={{0,4},{1,5},{2,6},{3,7},{4,0},{5,1},{6,2},{7,3},{8,12},{9,13},{10,... | collective-permute-start | bytes 196616 | tf_op jit(solution)/shard_map/ppermute | solution.py:246
  53.9 2.1 %collective-permute-start.10 = (bf16[2,8,16,128]{3,2,1,0:T(8,128)(2,1)S(1)}, bf16[2,8,16,128]{3,2,1,0:T(8,128)(2,1)S(1)}, u32[]{:S(2)}, u32[]{:S(2)}) collective-permute-start(bf16[2,8,16,128]{3,2,1,0:T(8,128)(2,1)S(1)} %get-tuple-element.18), channel_id=1, source_target_pairs={{0,2},{1,3},{2,4},{3,5},{4,6},{5,7},{6,0},{7,1},{8,10},{9,11},{10,... | collective-permute-start | bytes 196616 | tf_op jit(solution)/shard_map/ppermute | solution.py:246
  56.0 1.9 %collective-permute-start.9 = (bf16[2,8,16,128]{3,2,1,0:T(8,128)(2,1)S(1)}, bf16[2,8,16,128]{3,2,1,0:T(8,128)(2,1)S(1)}, u32[]{:S(2)}, u32[]{:S(2)}) collective-permute-start(bf16[2,8,16,128]{3,2,1,0:T(8,128)(2,1)S(1)} %get-tuple-element.17), channel_id=1, source_target_pairs={{0,0},{1,1},{2,2},{3,3},{4,4},{5,5},{6,6},{7,7},{8,8},{9,9},{10,10... | collective-permute-start | bytes 196616 | tf_op jit(solution)/shard_map/ppermute | solution.py:246
  57.9 0.9 %collective-permute-start.12 = (bf16[2,8,16,128]{3,2,1,0:T(8,128)(2,1)S(1)}, bf16[2,8,16,128]{3,2,1,0:T(8,128)(2,1)S(1)}, u32[]{:S(2)}, u32[]{:S(2)}) collective-permute-start(bf16[2,8,16,128]{3,2,1,0:T(8,128)(2,1)S(1)} %get-tuple-element.20), channel_id=1, source_target_pairs={{0,6},{1,7},{2,0},{3,1},{4,2},{5,3},{6,4},{7,5},{8,14},{9,15},{10,... | collective-permute-start | bytes 196616 | tf_op jit(solution)/shard_map/ppermute | solution.py:246
  58.8 0.0 collective-permute-done.11.refs_2_
  58.8 1.7 %collective-permute-done.10.refs_1_ = bf16[2,8,16,128]{3,2,1,0:T(8,128)(2,1)S(1)} collective-permute-done((bf16[2,8,16,128]{3,2,1,0:T(8,128)(2,1)S(1)}, bf16[2,8,16,128]{3,2,1,0:T(8,128)(2,1)S(1)}, u32[]{:S(2)}, u32[]{:S(2)}) %collective-permute-start.10) | collective-permute-done | bytes 65568 | tf_op jit(solution)/shard_map/ppermute | solution.py:246
  60.5 0.8 %collective-permute-done.9.refs_0_ = bf16[2,8,16,128]{3,2,1,0:T(8,128)(2,1)S(1)} collective-permute-done((bf16[2,8,16,128]{3,2,1,0:T(8,128)(2,1)S(1)}, bf16[2,8,16,128]{3,2,1,0:T(8,128)(2,1)S(1)}, u32[]{:S(2)}, u32[]{:S(2)}) %collective-permute-start.9) | collective-permute-done | bytes 65568 | tf_op jit(solution)/shard_map/ppermute | solution.py:246
  61.3 1.8 %collective-permute-done.12.refs_3_ = bf16[2,8,16,128]{3,2,1,0:T(8,128)(2,1)S(1)} collective-permute-done((bf16[2,8,16,128]{3,2,1,0:T(8,128)(2,1)S(1)}, bf16[2,8,16,128]{3,2,1,0:T(8,128)(2,1)S(1)}, u32[]{:S(2)}, u32[]{:S(2)}) %collective-permute-start.12) | collective-permute-done | bytes 65568 | tf_op jit(solution)/shard_map/ppermute | solution.py:246
  63.1 3.8 %collective-permute-start.13 = (bf16[4,8,16,128]{3,2,1,0:T(8,128)(2,1)S(1)}, bf16[4,8,16,128]{3,2,1,0:T(8,128)(2,1)S(1)}, u32[]{:S(2)}, u32[]{:S(2)}) collective-permute-start(bf16[4,8,16,128]{3,2,1,0:T(8,128)(2,1)S(1)} %pad_maximum_fusion.1), channel_id=1, source_target_pairs={{0,1},{1,0},{2,3},{3,2},{4,5},{5,4},{6,7},{7,6},{8,9},{9,8},{10,11... | collective-permute-start | bytes 393224 | tf_op jit(solution)/shard_map/ppermute | solution.py:248
  66.9 1.0 %collective-permute-done.13.swapped_ref = bf16[4,8,16,128]{3,2,1,0:T(8,128)(2,1)S(1)} collective-permute-done((bf16[4,8,16,128]{3,2,1,0:T(8,128)(2,1)S(1)}, bf16[4,8,16,128]{3,2,1,0:T(8,128)(2,1)S(1)}, u32[]{:S(2)}, u32[]{:S(2)}) %collective-permute-start.13) | collective-permute-done | bytes 131104 | tf_op jit(solution)/shard_map/ppermute | solution.py:248
  67.9 1.4 %unpack_rows.1 = bf16[16,1,64,128]{3,2,1,0:T(8,128)(2,1)} custom-call(s32[5]{0:T(128)S(1)} %stack.22.place_ref, bf16[4,8,16,128]{3,2,1,0:T(8,128)(2,1)S(1)} %collective-permute-done.13.swapped_ref, bf16[2,8,16,128]{3,2,1,0:T(8,128)(2,1)S(1)} %collective-permute-done.9.refs_0_, bf16[2,8,16,128]{3,2,1,0:T(8,128)(2,1)S(1)} %collective-permute-done.10.refs_1_, ...), custom_call_target="tpu_custom_call" | custom-call | tf_op jit(solution)/shard_map/unpack_rows/pallas_call | solution.py:168
  (17 shorter events, 0.4 us)
Async XLA Ops:
  0.1 1.0 %copy-start = (bf16[16,1,64,128]{3,2,1,0:T(8,128)(2,1)S(1)}, bf16[16,1,64,128]{3,2,1,0:T(8,128)(2,1)}, u32[]{:S(2)}) copy-start(bf16[16,1,64,128]{3,2,1,0:T(8,128)(2,1)} %volume_ref.1) | copy-start | bytes 786436
  1.7 12.8 %collective-permute-start = (bf16[1,20,16,128]{3,2,1,0:T(8,128)(2,1)S(1)}, bf16[1,20,16,128]{3,2,1,0:T(8,128)(2,1)S(1)}, u32[]{:S(2)}, u32[]{:S(2)}) collective-permute-start(bf16[1,20,16,128]{3,2,1,0:T(8,128)(2,1)S(1)} %get-tuple-element.13), channel_id=1, source_target_pairs={{0,0},{1,1},{2,2},{3,3},{4,4},{5,5},{6,6},{7,7},{8,8},{9,9},{10,10... | collective-permute-start | bytes 245768 | tf_op jit(solution)/shard_map/ppermute | solution.py:201
  5.3 9.3 %collective-permute-start.1 = (bf16[1,20,16,128]{3,2,1,0:T(8,128)(2,1)S(1)}, bf16[1,20,16,128]{3,2,1,0:T(8,128)(2,1)S(1)}, u32[]{:S(2)}, u32[]{:S(2)}) collective-permute-start(bf16[1,20,16,128]{3,2,1,0:T(8,128)(2,1)S(1)} %get-tuple-element.14), channel_id=1, source_target_pairs={{0,2},{1,3},{2,4},{3,5},{4,6},{5,7},{6,0},{7,1},{8,10},{9,11},{10,... | collective-permute-start | bytes 245768 | tf_op jit(solution)/shard_map/ppermute | solution.py:201
  8.1 8.6 %collective-permute-start.2 = (bf16[1,20,16,128]{3,2,1,0:T(8,128)(2,1)S(1)}, bf16[1,20,16,128]{3,2,1,0:T(8,128)(2,1)S(1)}, u32[]{:S(2)}, u32[]{:S(2)}) collective-permute-start(bf16[1,20,16,128]{3,2,1,0:T(8,128)(2,1)S(1)} %get-tuple-element.15), channel_id=1, source_target_pairs={{0,4},{1,5},{2,6},{3,7},{4,0},{5,1},{6,2},{7,3},{8,12},{9,13},{10,... | collective-permute-start | bytes 245768 | tf_op jit(solution)/shard_map/ppermute | solution.py:201
  11.7 5.9 %collective-permute-start.3 = (bf16[1,20,16,128]{3,2,1,0:T(8,128)(2,1)S(1)}, bf16[1,20,16,128]{3,2,1,0:T(8,128)(2,1)S(1)}, u32[]{:S(2)}, u32[]{:S(2)}) collective-permute-start(bf16[1,20,16,128]{3,2,1,0:T(8,128)(2,1)S(1)} %get-tuple-element.16), channel_id=1, source_target_pairs={{0,6},{1,7},{2,0},{3,1},{4,2},{5,3},{6,4},{7,5},{8,14},{9,15},{10,... | collective-permute-start | bytes 245768 | tf_op jit(solution)/shard_map/ppermute | solution.py:201
  17.6 3.6 %collective-permute-start.4 = (bf16[4,12,16,128]{3,2,1,0:T(8,128)(2,1)S(1)}, bf16[4,12,16,128]{3,2,1,0:T(8,128)(2,1)S(1)}, u32[]{:S(2)}, u32[]{:S(2)}) collective-permute-start(bf16[4,12,16,128]{3,2,1,0:T(8,128)(2,1)S(1)} %constant_dynamic-slice_fusion.4), channel_id=1, source_target_pairs={{0,1},{1,0},{2,3},{3,2},{4,5},{5,4},{6,7},{7,6},{8,9},{9,8},{10,11... | collective-permute-start | bytes 589832 | tf_op jit(solution)/shard_map/ppermute | solution.py:206
  21.3 2.5 %slice-start = ((bf16[27,128,128]{2,1,0:T(8,128)(2,1)}), bf16[9,128,128]{2,1,0:T(8,128)(2,1)S(1)}, s32[]{:S(2)}) async-start(bf16[27,128,128]{2,1,0:T(8,128)(2,1)} %param.6), calls=%async_computation | async-start | bytes 589824 | tf_op jit(solution)/shard_map/slice | solution.py:139
  21.4 2.8 %copy-start.1 = (bf16[27,128,128]{2,1,0:T(8,128)(2,1)S(1)}, bf16[27,128,128]{2,1,0:T(8,128)(2,1)}, u32[]{:S(2)}) copy-start(bf16[27,128,128]{2,1,0:T(8,128)(2,1)} %param.6) | copy-start | bytes 2654212
  21.4 11.3 %collective-permute-start.5 = (bf16[4,12,32,128]{3,2,1,0:T(8,128)(2,1)S(1)}, bf16[4,12,32,128]{3,2,1,0:T(8,128)(2,1)S(1)}, u32[]{:S(2)}, u32[]{:S(2)}) collective-permute-start(bf16[4,12,32,128]{3,2,1,0:T(8,128)(2,1)S(1)} %pad_maximum_fusion.own_ref), channel_id=1, source_target_pairs={{0,8},{8,16},{16,24},{24,32},{32,40},{40,48},{48,56},{56,64},{64,7... | collective-permute-start | bytes 1179656 | tf_op jit(solution)/shard_map/ppermute | solution.py:211
  21.5 13.7 %collective-permute-start.6 = (bf16[4,12,32,128]{3,2,1,0:T(8,128)(2,1)S(1)}, bf16[4,12,32,128]{3,2,1,0:T(8,128)(2,1)S(1)}, u32[]{:S(2)}, u32[]{:S(2)}) collective-permute-start(bf16[4,12,32,128]{3,2,1,0:T(8,128)(2,1)S(1)} %pad_maximum_fusion.own_ref), channel_id=1, source_target_pairs={{8,0},{16,8},{24,16},{32,24},{40,32},{48,40},{56,48},{64,56},{72,6... | collective-permute-start | bytes 1179656 | tf_op jit(solution)/shard_map/ppermute | solution.py:212
  25.4 0.7 copy-start.3
  36.8 2.5 %slice-start.1 = ((bf16[27,128,128]{2,1,0:T(8,128)(2,1)}), bf16[9,128,128]{2,1,0:T(8,128)(2,1)S(1)}, s32[]{:S(2)}) async-start(bf16[27,128,128]{2,1,0:T(8,128)(2,1)} %param.8), calls=%async_computation.1 | async-start | bytes 589824 | tf_op jit(solution)/shard_map/slice | solution.py:139
  36.8 2.8 %copy-start.2 = (bf16[27,128,128]{2,1,0:T(8,128)(2,1)S(1)}, bf16[27,128,128]{2,1,0:T(8,128)(2,1)}, u32[]{:S(2)}) copy-start(bf16[27,128,128]{2,1,0:T(8,128)(2,1)} %param.8) | copy-start | bytes 2654212
  36.8 9.0 %collective-permute-start.7 = (bf16[10,128,128]{2,1,0:T(8,128)(2,1)S(1)}, bf16[10,128,128]{2,1,0:T(8,128)(2,1)S(1)}, u32[]{:S(2)}, u32[]{:S(2)}) collective-permute-start(bf16[10,128,128]{2,1,0:T(8,128)(2,1)S(1)} %first_layer.1.own_ref), channel_id=1, source_target_pairs={{0,8},{8,16},{16,24},{24,32},{32,40},{40,48},{48,56},{56,64},{64,7... | collective-permute-start | bytes 983048 | tf_op jit(solution)/shard_map/ppermute | solution.py:228
  37.0 11.3 %collective-permute-start.8 = (bf16[10,128,128]{2,1,0:T(8,128)(2,1)S(1)}, bf16[10,128,128]{2,1,0:T(8,128)(2,1)S(1)}, u32[]{:S(2)}, u32[]{:S(2)}) collective-permute-start(bf16[10,128,128]{2,1,0:T(8,128)(2,1)S(1)} %first_layer.1.own_ref), channel_id=1, source_target_pairs={{8,0},{16,8},{24,16},{32,24},{40,32},{48,40},{56,48},{64,56},{72,6... | collective-permute-start | bytes 983048 | tf_op jit(solution)/shard_map/ppermute | solution.py:229
  40.9 0.7 copy-start.4
  49.8 9.0 %collective-permute-start.11 = (bf16[2,8,16,128]{3,2,1,0:T(8,128)(2,1)S(1)}, bf16[2,8,16,128]{3,2,1,0:T(8,128)(2,1)S(1)}, u32[]{:S(2)}, u32[]{:S(2)}) collective-permute-start(bf16[2,8,16,128]{3,2,1,0:T(8,128)(2,1)S(1)} %get-tuple-element.19), channel_id=1, source_target_pairs={{0,4},{1,5},{2,6},{3,7},{4,0},{5,1},{6,2},{7,3},{8,12},{9,13},{10,... | collective-permute-start | bytes 196616 | tf_op jit(solution)/shard_map/ppermute | solution.py:246
  53.9 6.6 %collective-permute-start.10 = (bf16[2,8,16,128]{3,2,1,0:T(8,128)(2,1)S(1)}, bf16[2,8,16,128]{3,2,1,0:T(8,128)(2,1)S(1)}, u32[]{:S(2)}, u32[]{:S(2)}) collective-permute-start(bf16[2,8,16,128]{3,2,1,0:T(8,128)(2,1)S(1)} %get-tuple-element.18), channel_id=1, source_target_pairs={{0,2},{1,3},{2,4},{3,5},{4,6},{5,7},{6,0},{7,1},{8,10},{9,11},{10,... | collective-permute-start | bytes 196616 | tf_op jit(solution)/shard_map/ppermute | solution.py:246
  56.0 5.3 %collective-permute-start.9 = (bf16[2,8,16,128]{3,2,1,0:T(8,128)(2,1)S(1)}, bf16[2,8,16,128]{3,2,1,0:T(8,128)(2,1)S(1)}, u32[]{:S(2)}, u32[]{:S(2)}) collective-permute-start(bf16[2,8,16,128]{3,2,1,0:T(8,128)(2,1)S(1)} %get-tuple-element.17), channel_id=1, source_target_pairs={{0,0},{1,1},{2,2},{3,3},{4,4},{5,5},{6,6},{7,7},{8,8},{9,9},{10,10... | collective-permute-start | bytes 196616 | tf_op jit(solution)/shard_map/ppermute | solution.py:246
  57.9 5.2 %collective-permute-start.12 = (bf16[2,8,16,128]{3,2,1,0:T(8,128)(2,1)S(1)}, bf16[2,8,16,128]{3,2,1,0:T(8,128)(2,1)S(1)}, u32[]{:S(2)}, u32[]{:S(2)}) collective-permute-start(bf16[2,8,16,128]{3,2,1,0:T(8,128)(2,1)S(1)} %get-tuple-element.20), channel_id=1, source_target_pairs={{0,6},{1,7},{2,0},{3,1},{4,2},{5,3},{6,4},{7,5},{8,14},{9,15},{10,... | collective-permute-start | bytes 196616 | tf_op jit(solution)/shard_map/ppermute | solution.py:246
  63.1 4.8 %collective-permute-start.13 = (bf16[4,8,16,128]{3,2,1,0:T(8,128)(2,1)S(1)}, bf16[4,8,16,128]{3,2,1,0:T(8,128)(2,1)S(1)}, u32[]{:S(2)}, u32[]{:S(2)}) collective-permute-start(bf16[4,8,16,128]{3,2,1,0:T(8,128)(2,1)S(1)} %pad_maximum_fusion.1), channel_id=1, source_target_pairs={{0,1},{1,0},{2,3},{3,2},{4,5},{5,4},{6,7},{7,6},{8,9},{9,8},{10,11... | collective-permute-start | bytes 393224 | tf_op jit(solution)/shard_map/ppermute | solution.py:248

commit v5 on v4

--- a/solution.py
+++ b/solution.py
@@ -54,67 +54,69 @@
         outs[k][0] = rows_ref[pl.ds(target * rows, rows + 2 * RIM)]
 
 
-def own_kernel(own_ref, weight_ref, out_ref):
-    rows, _, lanes = out_ref.shape
-
+def rows_of(place_ref, ref, masked):
     def get(_, row):
-        if len(own_ref.shape) == 3:
-            return own_ref[row]
-        return jnp.concatenate([own_ref[g, row] for g in range(own_ref.shape[0])], axis=0)
-
-    def store(row, value):
-        out_ref[row] = value
-
-    conv_rows(get, 1, weight_ref[...], store, rows, lanes)
-
-
-def reader(place_ref, before_ref, after_ref):
-    outside = (place_ref[2] == 0, place_ref[2] == place_ref[3] - 1)
-    refs = (before_ref, after_ref)
-
-    def get(a, row):
-        ref = refs[a]
         if len(ref.shape) == 3:
             value = ref[row]
         else:
             value = jnp.concatenate([ref[g, row] for g in range(ref.shape[0])], axis=0)
-        return jnp.where(outside[a], jnp.zeros_like(value), value)
+        if masked:
+            value = jnp.where(place_ref[3] == 1, jnp.zeros_like(value), value)
+        return value
 
     return get
 
 
-def first_kernel(place_ref, before_ref, after_ref, own_ref, weight_ref, bias_ref, out_ref):
+def own_kernel(place_ref, plane_ref, weight_ref, out_ref):
     rows, _, lanes = out_ref.shape
-    group, core = place_ref[0], place_ref[1]
-    block = group * CORES + core
+
+    def store(row, value):
+        out_ref[row] = value
+
+    conv_rows(rows_of(place_ref, plane_ref, False), 1, weight_ref[...], store, rows, lanes)
+
+
+def near_kernel(place_ref, plane_ref, weight_ref, before_ref, out_ref):
+    rows, _, lanes = out_ref.shape
+
+    def store(row, value):
+        out_ref[row] = before_ref[row] + value
+
+    weight = weight_ref[1 - place_ref[2]]
+    conv_rows(rows_of(place_ref, plane_ref, False), 1, weight, store, rows, lanes)
+
+
+def first_kernel(place_ref, plane_ref, weight_ref, before_ref, bias_ref, out_ref):
+    rows, _, lanes = out_ref.shape
+    block = place_ref[0] * CORES + place_ref[1]
     bias = bias_ref[...]
 
     def store(row, value):
-        value = jnp.maximum(value + own_ref[row] + bias, 0.0)
+        value = jnp.maximum(value + before_ref[row] + bias, 0.0)
         if row == 0:
             value = jnp.where(block == 0, 0.0, value)
         if row == rows - 1:
             value = jnp.where(block == place_ref[4] - 1, 0.0, value)
         out_ref[row] = value.astype(BF16)
 
-    get = reader(place_ref, before_ref, after_ref)
-    conv_rows(get, 2, weight_ref[...], store, rows, lanes)
-
-
-def second_kernel(place_ref, before_ref, after_ref, own_ref, weight_ref, bias_ref, *refs):
+    weight = weight_ref[place_ref[2]]
+    conv_rows(rows_of(place_ref, plane_ref, True), 1, weight, store, rows, lanes)
+
+
+def second_kernel(place_ref, plane_ref, weight_ref, before_ref, bias_ref, *refs):
     outs, all_ref = refs[:-1], refs[-1]
     groups, cores, rows, width, lanes = all_ref.shape
     bias = bias_ref[...]
 
     def store(row, value):
-        value = jnp.maximum(value + own_ref[row] + bias, 0.0).astype(BF16)
+        value = jnp.maximum(value + before_ref[row] + bias, 0.0).astype(BF16)
         for g in range(groups):
             for c in range(cores):
                 at = (g * cores + c) * width
                 all_ref[g, c, row] = value[at : at + width]
 
-    get = reader(place_ref, before_ref, after_ref)
-    conv_rows(get, 2, weight_ref[...], store, rows, lanes)
+    weight = weight_ref[place_ref[2]]
+    conv_rows(rows_of(place_ref, plane_ref, True), 1, weight, store, rows, lanes)
     for k in range(groups):
         outs[k][...] = all_ref[lax.rem(place_ref[0] + k, groups)]
 
@@ -137,7 +139,7 @@
     _, inner, outer = weight.shape
     taps = weight.reshape(3, 3, 3, inner, outer)
     own = taps[1].transpose(1, 3, 0, 2).reshape(3 * outer, 3 * inner)
-    beside = taps[::2].transpose(2, 4, 0, 1, 3).reshape(3 * outer, 6 * inner)
+    beside = taps[::2].transpose(0, 2, 4, 1, 3).reshape(2, 3 * outer, 3 * inner)
     return own, beside
 
 
@@ -152,16 +154,17 @@
     groups = chan // CORES
     swap = [(i, i ^ 1) for i in range(chan)]
 
-    half = space // 2
-    moved = {half - 1: space - 1, space - 1: half - 1}
-    spot = [moved.get(i, i) for i in range(space)]
-    up = [(spot[i], spot[(i + 1) % space]) for i in range(space)]
-    down = [(j, i) for i, j in up]
+    near = [(i, i ^ 1) for i in range(space)]
+
+    def far_partner(i, j):
+        if i in (0, space - 1):
+            return i * chan + (j ^ 1)
+        return (((i - 1) ^ 1) + 1) * chan + j
+
+    far = [(i * chan + j, far_partner(i, j)) for i in range(space) for j in range(chan)]
 
     def ahead(k):
-        return [
-            (i * chan + j, spot[i] * chan + (j + CORES * k) % chan) for i in range(space) for j in range(chan)
-        ]
+        return [(i, (i + CORES * k) % chan) for i in range(chan)]
 
     def call(kernel, shapes, inputs, scratch=(), **kwargs):
         single = not isinstance(shapes, list)
@@ -180,10 +183,10 @@
         full = width * chan
         rows = length // chan
         index = lax.axis_index("chan")
-        spot_index = lax.axis_index("space")
-        plane = jnp.where(spot_index == half - 1, space - 1, jnp.where(spot_index == space - 1, half - 1, spot_index))
+        plane = lax.axis_index("space")
+        edge = (plane == 0) | (plane == space - 1)
         group, core = index // CORES, index % CORES
-        place = jnp.stack([group, core, plane, jnp.int32(space), jnp.int32(chan)]).astype(jnp.int32)
+        place = jnp.stack([group, core, plane % 2, edge.astype(jnp.int32), jnp.int32(chan)]).astype(jnp.int32)
 
         own_one, beside_one = arranged(weight_one)
         own_two, beside_two = arranged(weight_two)
@@ -197,8 +200,9 @@
             name="pack_rows",
         )
         kept = jnp.zeros((groups, tall, width, lanes), BF16)
-        for k in range(groups):
-            got = lax.ppermute(pieces[k], ("space", "chan"), ahead(k))
+        kept = lax.dynamic_update_slice_in_dim(kept, pieces[0], group, 0)
+        for k in range(1, groups):
+            got = lax.ppermute(pieces[k], "chan", ahead(k))
             kept = lax.dynamic_update_slice_in_dim(kept, got, (group + groups - k) % groups, 0)
 
         mine = lax.dynamic_slice_in_dim(kept, core * rows, rows + 2 * RIM, 1)
@@ -208,42 +212,51 @@
         second = jnp.where(core == 0, swapped, mine)
         whole = jnp.concatenate([first, second], axis=2)
 
-        before = lax.ppermute(whole, "space", up)
-        after = lax.ppermute(whole, "space", down)
-        own = call(
-            own_kernel,
-            jax.ShapeDtypeStruct((rows + RIM, full, lanes), F32),
-            [whole, own_one],
-            cost_estimate=cost(rows + RIM, 1, full, lanes),
-            name="first_own",
-        )
-        hidden = call(
+        def layer(array, name, own_weight, beside_weight, bias, height, kernel, shapes, scratch=()):
+            far_plane = lax.ppermute(array, ("space", "chan"), far)
+            near_plane = lax.ppermute(array, "space", near)
+            partial = jax.ShapeDtypeStruct((height, full, lanes), F32)
+            work = cost(height, 1, full, lanes)
+            total = call(own_kernel, partial, [place, array, own_weight], cost_estimate=work, name=name + "_own")
+            total = call(
+                near_kernel,
+                partial,
+                [place, near_plane, beside_weight, total],
+                cost_estimate=work,
+                name=name + "_near",
+            )
+            return call(
+                kernel,
+                shapes,
+                [place, far_plane, beside_weight, total, bias[:, None]],
+                scratch,
+                cost_estimate=work,
+                name=name + "_far",
+            )
+
+        hidden = layer(
+            whole,
+            "first",
+            own_one,
+            beside_one,
+            bias_one,
+            rows + RIM,
             first_kernel,
             jax.ShapeDtypeStruct((rows + RIM, full, lanes), BF16),
-            [place, before, after, own, beside_one, bias_one[:, None]],
-            cost_estimate=cost(rows + RIM, 2, full, lanes),
-            name="first_layer",
-        )
-
-        before = lax.ppermute(hidden, "space", up)
-        after = lax.ppermute(hidden, "space", down)
-        own = call(
-            own_kernel,
-            jax.ShapeDtypeStruct((rows, full, lanes), F32),
-            [hidden, own_two],
-            cost_estimate=cost(rows, 1, full, lanes),
-            name="second_own",
-        )
-        blocks = call(
+        )
+        blocks = layer(
+            hidden,
+            "second",
+            own_two,
+            beside_two,
+            bias_two,
+            rows,
             second_kernel,
             [jax.ShapeDtypeStruct((CORES, rows, width, lanes), BF16)] * groups,
-            [place, before, after, own, beside_two, bias_two[:, None]],
             [pltpu.VMEM((groups, CORES, rows, width, lanes), BF16)],
-            cost_estimate=cost(rows, 2, full, lanes),
-            name="second_layer",
-        )
-
-        blocks = [lax.ppermute(blocks[k], ("space", "chan"), ahead(k)) for k in range(groups)]
+        )
+
+        blocks = [blocks[0]] + [lax.ppermute(blocks[k], "chan", ahead(k)) for k in range(1, groups)]
         theirs = jnp.stack([lax.dynamic_index_in_dim(b, 1 - core, 0, keepdims=False) for b in blocks])
         swapped = lax.ppermute(theirs, "chan", swap)
         return call(

time: 69.4 us -> 68.9 us (level)
  starting transfers between devices: 33 us -> 23.8 us
  waiting for transfers between devices: 23.5 us -> 29.3 us
  Pallas kernels: 6.56 us -> 9.7 us
    ppermute x12 -> x10, starting transfers between devices: 26.6 us -> 17.8 us  [the longest x3 10.6 us: per_device(): got = lax.ppermute(pieces[k], 'chan', ahead(k))]
    ppermute x12 -> x10, waiting for transfers between devices: 21.5 us -> 27.3 us  [the longest x2 10 us: layer(): near_plane = lax.ppermute(array, 'space', near)]
    pallas_call x6 -> x8, Pallas kernels: 6.56 us -> 9.7 us  [call(): pl.pallas_call(kernel, out_shape=shapes, in_specs=[SMEM if x.ndim == 1 el...]
  transfers between devices with their start and end apart: 14 -> 12, of which waited for: 11 -> 10; matrix products, arithmetic and copies ran while one was open for 5% -> 5% of each run, Pallas kernels for 2% -> 7%
where the time goes in v5:
time: 68.9 us; the launch traced here: 68.8 us
  waiting for transfers between devices  29.3 us (43%)
  starting transfers between devices  23.8 us (35%)
  Pallas kernels  9.7 us (14%)
  local copies, waits for them, and re-layouts  5.65 us (8%)
    ppermute x3, starting transfers between devices, per_device(): got = lax.ppermute(pieces[k], 'chan', ahead(k))  10.6 us
    ppermute x2, waiting for transfers between devices, layer(): near_plane = lax.ppermute(array, 'space', near)  10 us
    pallas_call x8, Pallas kernels, call(): pl.pallas_call(kernel, out_shape=shapes, in_specs=[SMEM if x.ndim == 1 el...  9.7 us
    ppermute x2, waiting for transfers between devices, layer(): far_plane = lax.ppermute(array, ('space', 'chan'), far)  6.83 us
    ppermute x3, waiting for transfers between devices, per_device(): got = lax.ppermute(pieces[k], 'chan', ahead(k))  6.4 us
    ppermute x3, starting transfers between devices, per_device(): lax.ppermute(blocks[k], 'chan', ahead(k))  6.22 us
    ppermute x2, starting transfers between devices, per_device(): swapped = lax.ppermute(theirs, 'chan', swap)  5.94 us
    ppermute x3, waiting for transfers between devices, per_device(): lax.ppermute(blocks[k], 'chan', ahead(k))  4.01 us
  transfers between devices with their start and end apart: 12, of which 10 were waited for; matrix products, arithmetic and copies ran while one was open for 5% of the time, Pallas kernels for 7%

profile of v5, /device:TPU:31, one launch (start us, length us, event | category | flops | bytes accessed | tf_op | source)
XLA Modules:
  0.0 68.8 jit_solution(7870458628249405109)
XLA Ops:
  0.0 0.1 stack.30.place_ref
  0.1 0.0 copy-start
  0.1 0.9 %copy-done = bf16[16,1,64,128]{3,2,1,0:T(8,128)(2,1)S(1)} copy-done((bf16[16,1,64,128]{3,2,1,0:T(8,128)(2,1)S(1)}, bf16[16,1,64,128]{3,2,1,0:T(8,128)(2,1)}, u32[]{:S(2)}) %copy-start) | copy-done | bytes 262168
  1.0 0.7 %pack_rows.1 = (bf16[1,20,16,128]{3,2,1,0:T(8,128)(2,1)S(1)}, bf16[1,20,16,128]{3,2,1,0:T(8,128)(2,1)S(1)}, bf16[1,20,16,128]{3,2,1,0:T(8,128)(2,1)S(1)}, bf16[1,20,16,128]{3,2,1,0:T(8,128)(2,1)S(1)}) custom-call(s32[5]{0:T(128)S(1)} %stack.30.place_ref, bf16[16,1,64,128]{3,2,1,0:T(8,128)(2,1)S(1)} %copy-done), custom_call_target="tpu_custom_call" | custom-call | tf_op jit(solution)/shard_map/pack_rows/pallas_call | solution.py:171
  1.7 3.1 %collective-permute-start = (bf16[1,20,16,128]{3,2,1,0:T(8,128)(2,1)S(1)}, bf16[1,20,16,128]{3,2,1,0:T(8,128)(2,1)S(1)}, u32[]{:S(2)}, u32[]{:S(2)}) collective-permute-start(bf16[1,20,16,128]{3,2,1,0:T(8,128)(2,1)S(1)} %get-tuple-element.14), channel_id=1, source_target_pairs={{0,2},{1,3},{2,4},{3,5},{4,6},{5,7},{6,0},{7,1},{8,10},{9,11},{10,... | collective-permute-start | bytes 245768 | tf_op jit(solution)/shard_map/ppermute | solution.py:205
  4.8 5.1 %collective-permute-start.1 = (bf16[1,20,16,128]{3,2,1,0:T(8,128)(2,1)S(1)}, bf16[1,20,16,128]{3,2,1,0:T(8,128)(2,1)S(1)}, u32[]{:S(2)}, u32[]{:S(2)}) collective-permute-start(bf16[1,20,16,128]{3,2,1,0:T(8,128)(2,1)S(1)} %get-tuple-element.15), channel_id=1, source_target_pairs={{0,4},{1,5},{2,6},{3,7},{4,0},{5,1},{6,2},{7,3},{8,12},{9,13},{10,... | collective-permute-start | bytes 245768 | tf_op jit(solution)/shard_map/ppermute | solution.py:205
  9.9 2.4 %collective-permute-start.2 = (bf16[1,20,16,128]{3,2,1,0:T(8,128)(2,1)S(1)}, bf16[1,20,16,128]{3,2,1,0:T(8,128)(2,1)S(1)}, u32[]{:S(2)}, u32[]{:S(2)}) collective-permute-start(bf16[1,20,16,128]{3,2,1,0:T(8,128)(2,1)S(1)} %get-tuple-element.16), channel_id=1, source_target_pairs={{0,6},{1,7},{2,0},{3,1},{4,2},{5,3},{6,4},{7,5},{8,14},{9,15},{10,... | collective-permute-start | bytes 245768 | tf_op jit(solution)/shard_map/ppermute | solution.py:205
  12.4 0.0 collective-permute-done
  12.4 2.7 %collective-permute-done.1 = bf16[1,20,16,128]{3,2,1,0:T(8,128)(2,1)S(1)} collective-permute-done((bf16[1,20,16,128]{3,2,1,0:T(8,128)(2,1)S(1)}, bf16[1,20,16,128]{3,2,1,0:T(8,128)(2,1)S(1)}, u32[]{:S(2)}, u32[]{:S(2)}) %collective-permute-start.1) | collective-permute-done | bytes 81952 | tf_op jit(solution)/shard_map/ppermute | solution.py:205
  15.1 3.7 %collective-permute-done.2 = bf16[1,20,16,128]{3,2,1,0:T(8,128)(2,1)S(1)} collective-permute-done((bf16[1,20,16,128]{3,2,1,0:T(8,128)(2,1)S(1)}, bf16[1,20,16,128]{3,2,1,0:T(8,128)(2,1)S(1)}, u32[]{:S(2)}, u32[]{:S(2)}) %collective-permute-start.2) | collective-permute-done | bytes 81952 | tf_op jit(solution)/shard_map/ppermute | solution.py:205
  18.9 0.0 copy-start.1
  18.9 0.6 collective-permute-start.3
  19.5 1.1 %collective-permute-done.3 = bf16[4,12,16,128]{3,2,1,0:T(8,128)(2,1)S(1)} collective-permute-done((bf16[4,12,16,128]{3,2,1,0:T(8,128)(2,1)S(1)}, bf16[4,12,16,128]{3,2,1,0:T(8,128)(2,1)S(1)}, u32[]{:S(2)}, u32[]{:S(2)}) %collective-permute-start.3) | collective-permute-done | bytes 196640 | tf_op jit(solution)/shard_map/ppermute | solution.py:210
  20.6 0.6 collective-permute-start.5
  21.2 0.0 collective-permute-start.4
  21.2 0.0 copy-done.1
  21.2 0.6 copy.18
  21.8 0.5 reshape.23.weight_ref
  22.4 0.2 copy.13
  22.7 0.0 copy-start.3
  22.7 0.6 copy-done.3
  23.3 0.1 copy.14.bias_ref
  23.4 1.3 %first_own.1.before_ref = f32[10,128,128]{2,1,0:T(8,128)S(1)} custom-call(s32[5]{0:T(128)S(1)} %stack.30.place_ref, bf16[4,12,32,128]{3,2,1,0:T(8,128)(2,1)S(1)} %pad_maximum_fusion.plane_ref, bf16[384,384]{1,0:T(8,128)(2,1)S(1)} %bitcast.25), custom_call_target="tpu_custom_call" | custom-call | flops 377487360 | bytes 4000000 | tf_op jit(solution)/shard_map/first_own/pallas_call | solution.py:171
  24.8 6.3 %collective-permute-done.5.plane_ref = bf16[4,12,32,128]{3,2,1,0:T(8,128)(2,1)S(1)} collective-permute-done((bf16[4,12,32,128]{3,2,1,0:T(8,128)(2,1)S(1)}, bf16[4,12,32,128]{3,2,1,0:T(8,128)(2,1)S(1)}, u32[]{:S(2)}, u32[]{:S(2)}) %collective-permute-start.5) | collective-permute-done | bytes 393248 | tf_op jit(solution)/shard_map/ppermute | solution.py:217
  31.0 1.3 %first_near.1.before_ref = f32[10,128,128]{2,1,0:T(8,128)S(1)} custom-call(s32[5]{0:T(128)S(1)} %stack.30.place_ref, bf16[4,12,32,128]{3,2,1,0:T(8,128)(2,1)S(1)} %collective-permute-done.5.plane_ref, bf16[2,384,384]{2,1,0:T(8,128)(2,1)S(1)} %reshape.23.weight_ref, f32[10,128,128]{2,1,0:T(8,128)S(1)} %first_own.1.before_ref), custom_call_target="tpu_custom_call" | custom-call | flops 377487360 | bytes 4000000 | tf_op jit(solution)/shard_map/first_near/pallas_call | solution.py:171
  32.3 0.0 copy-start.2
  32.4 3.0 %collective-permute-done.4.plane_ref = bf16[4,12,32,128]{3,2,1,0:T(8,128)(2,1)S(1)} collective-permute-done((bf16[4,12,32,128]{3,2,1,0:T(8,128)(2,1)S(1)}, bf16[4,12,32,128]{3,2,1,0:T(8,128)(2,1)S(1)}, u32[]{:S(2)}, u32[]{:S(2)}) %collective-permute-start.4) | collective-permute-done | bytes 393248 | tf_op jit(solution)/shard_map/ppermute | solution.py:216
  35.4 1.3 %first_far.1.plane_ref = bf16[10,128,128]{2,1,0:T(8,128)(2,1)S(1)} custom-call(s32[5]{0:T(128)S(1)} %stack.30.place_ref, bf16[4,12,32,128]{3,2,1,0:T(8,128)(2,1)S(1)} %collective-permute-done.4.plane_ref, bf16[2,384,384]{2,1,0:T(8,128)(2,1)S(1)} %reshape.23.weight_ref, f32[10,128,128]{2,1,0:T(8,128)S(1)} %first_near.1.before_ref, f32[128,1]{1,0:T(8,128)S(1)} %copy.14.bias_ref), custom_call_target="tpu_custom_call" | custom-call | flops 377487360 | bytes 4000000 | tf_op jit(solution)/shard_map/first_far/pallas_call | solution.py:171
  36.7 0.1 collective-permute-start.7
  36.8 0.4 collective-permute-start.6
  37.2 0.0 copy-done.2
  37.3 0.6 copy.19
  37.9 0.5 reshape.26.weight_ref
  38.4 0.2 copy.16
  38.7 0.0 copy-start.4
  38.7 0.6 copy-done.4
  39.4 0.1 copy.17.bias_ref
  39.5 1.2 %second_own.1.before_ref = f32[8,128,128]{2,1,0:T(8,128)S(1)} custom-call(s32[5]{0:T(128)S(1)} %stack.30.place_ref, bf16[10,128,128]{2,1,0:T(8,128)(2,1)S(1)} %first_far.1.plane_ref, bf16[384,384]{1,0:T(8,128)(2,1)S(1)} %bitcast.24), custom_call_target="tpu_custom_call" | custom-call | flops 301989888 | bytes 4000000 | tf_op jit(solution)/shard_map/second_own/pallas_call | solution.py:171
  40.7 3.8 %collective-permute-done.7.plane_ref = bf16[10,128,128]{2,1,0:T(8,128)(2,1)S(1)} collective-permute-done((bf16[10,128,128]{2,1,0:T(8,128)(2,1)S(1)}, bf16[10,128,128]{2,1,0:T(8,128)(2,1)S(1)}, u32[]{:S(2)}, u32[]{:S(2)}) %collective-permute-start.7) | collective-permute-done | bytes 327712 | tf_op jit(solution)/shard_map/ppermute | solution.py:217
  44.5 1.2 %second_near.1.before_ref = f32[8,128,128]{2,1,0:T(8,128)S(1)} custom-call(s32[5]{0:T(128)S(1)} %stack.30.place_ref, bf16[10,128,128]{2,1,0:T(8,128)(2,1)S(1)} %collective-permute-done.7.plane_ref, bf16[2,384,384]{2,1,0:T(8,128)(2,1)S(1)} %reshape.26.weight_ref, f32[8,128,128]{2,1,0:T(8,128)S(1)} %second_own.1.before_ref), custom_call_target="tpu_custom_call" | custom-call | flops 301989888 | bytes 4000000 | tf_op jit(solution)/shard_map/second_near/pallas_call | solution.py:171
  45.7 3.8 %collective-permute-done.6.plane_ref = bf16[10,128,128]{2,1,0:T(8,128)(2,1)S(1)} collective-permute-done((bf16[10,128,128]{2,1,0:T(8,128)(2,1)S(1)}, bf16[10,128,128]{2,1,0:T(8,128)(2,1)S(1)}, u32[]{:S(2)}, u32[]{:S(2)}) %collective-permute-start.6) | collective-permute-done | bytes 327712 | tf_op jit(solution)/shard_map/ppermute | solution.py:216
  49.5 1.2 %second_far.1 = (bf16[2,8,16,128]{3,2,1,0:T(8,128)(2,1)S(1)}, bf16[2,8,16,128]{3,2,1,0:T(8,128)(2,1)S(1)}, bf16[2,8,16,128]{3,2,1,0:T(8,128)(2,1)S(1)}, bf16[2,8,16,128]{3,2,1,0:T(8,128)(2,1)S(1)}) custom-call(s32[5]{0:T(128)S(1)} %stack.30.place_ref, bf16[10,128,128]{2,1,0:T(8,128)(2,1)S(1)} %collective-permute-done.6.plane_ref, ...), custom_call_target="tpu_custom_call" | custom-call | flops 301989888 | bytes 4000000 | tf_op jit(solution)/shard_map/second_far/pallas_call | solution.py:171
  50.8 2.5 %collective-permute-start.10 = (bf16[2,8,16,128]{3,2,1,0:T(8,128)(2,1)S(1)}, bf16[2,8,16,128]{3,2,1,0:T(8,128)(2,1)S(1)}, u32[]{:S(2)}, u32[]{:S(2)}) collective-permute-start(bf16[2,8,16,128]{3,2,1,0:T(8,128)(2,1)S(1)} %get-tuple-element.20), channel_id=1, source_target_pairs={{0,6},{1,7},{2,0},{3,1},{4,2},{5,3},{6,4},{7,5},{8,14},{9,15},{10,... | collective-permute-start | bytes 196616 | tf_op jit(solution)/shard_map/ppermute | solution.py:259
  53.3 1.9 %collective-permute-start.9 = (bf16[2,8,16,128]{3,2,1,0:T(8,128)(2,1)S(1)}, bf16[2,8,16,128]{3,2,1,0:T(8,128)(2,1)S(1)}, u32[]{:S(2)}, u32[]{:S(2)}) collective-permute-start(bf16[2,8,16,128]{3,2,1,0:T(8,128)(2,1)S(1)} %get-tuple-element.19), channel_id=1, source_target_pairs={{0,4},{1,5},{2,6},{3,7},{4,0},{5,1},{6,2},{7,3},{8,12},{9,13},{10,... | collective-permute-start | bytes 196616 | tf_op jit(solution)/shard_map/ppermute | solution.py:259
  55.1 1.8 %collective-permute-start.8 = (bf16[2,8,16,128]{3,2,1,0:T(8,128)(2,1)S(1)}, bf16[2,8,16,128]{3,2,1,0:T(8,128)(2,1)S(1)}, u32[]{:S(2)}, u32[]{:S(2)}) collective-permute-start(bf16[2,8,16,128]{3,2,1,0:T(8,128)(2,1)S(1)} %get-tuple-element.18), channel_id=1, source_target_pairs={{0,2},{1,3},{2,4},{3,5},{4,6},{5,7},{6,0},{7,1},{8,10},{9,11},{10,... | collective-permute-start | bytes 196616 | tf_op jit(solution)/shard_map/ppermute | solution.py:259
  57.0 0.0 collective-permute-done.10.refs_3_
  57.0 3.4 %collective-permute-done.9.refs_2_ = bf16[2,8,16,128]{3,2,1,0:T(8,128)(2,1)S(1)} collective-permute-done((bf16[2,8,16,128]{3,2,1,0:T(8,128)(2,1)S(1)}, bf16[2,8,16,128]{3,2,1,0:T(8,128)(2,1)S(1)}, u32[]{:S(2)}, u32[]{:S(2)}) %collective-permute-start.9) | collective-permute-done | bytes 65568 | tf_op jit(solution)/shard_map/ppermute | solution.py:259
  60.4 0.6 collective-permute-done.8.refs_1_
  61.0 5.4 %collective-permute-start.11 = (bf16[4,8,16,128]{3,2,1,0:T(8,128)(2,1)S(1)}, bf16[4,8,16,128]{3,2,1,0:T(8,128)(2,1)S(1)}, u32[]{:S(2)}, u32[]{:S(2)}) collective-permute-start(bf16[4,8,16,128]{3,2,1,0:T(8,128)(2,1)S(1)} %pad_maximum_fusion.1), channel_id=1, source_target_pairs={{0,1},{1,0},{2,3},{3,2},{4,5},{5,4},{6,7},{7,6},{8,9},{9,8},{10,11... | collective-permute-start | bytes 393224 | tf_op jit(solution)/shard_map/ppermute | solution.py:261
  66.4 1.0 %collective-permute-done.11.swapped_ref = bf16[4,8,16,128]{3,2,1,0:T(8,128)(2,1)S(1)} collective-permute-done((bf16[4,8,16,128]{3,2,1,0:T(8,128)(2,1)S(1)}, bf16[4,8,16,128]{3,2,1,0:T(8,128)(2,1)S(1)}, u32[]{:S(2)}, u32[]{:S(2)}) %collective-permute-start.11) | collective-permute-done | bytes 131104 | tf_op jit(solution)/shard_map/ppermute | solution.py:261
  67.4 1.4 %unpack_rows.1 = bf16[16,1,64,128]{3,2,1,0:T(8,128)(2,1)} custom-call(s32[5]{0:T(128)S(1)} %stack.30.place_ref, bf16[4,8,16,128]{3,2,1,0:T(8,128)(2,1)S(1)} %collective-permute-done.11.swapped_ref, bf16[2,8,16,128]{3,2,1,0:T(8,128)(2,1)S(1)} %get-tuple-element.17.refs_0_, bf16[2,8,16,128]{3,2,1,0:T(8,128)(2,1)S(1)} %collective-permute-done.8.refs_1_, ...), custom_call_target="tpu_custom_call" | custom-call | tf_op jit(solution)/shard_map/unpack_rows/pallas_call | solution.py:171
  (19 shorter events, 0.4 us)
Async XLA Ops:
  0.1 1.0 %copy-start = (bf16[16,1,64,128]{3,2,1,0:T(8,128)(2,1)S(1)}, bf16[16,1,64,128]{3,2,1,0:T(8,128)(2,1)}, u32[]{:S(2)}) copy-start(bf16[16,1,64,128]{3,2,1,0:T(8,128)(2,1)} %volume_ref.1) | copy-start | bytes 786436
  1.7 10.6 %collective-permute-start = (bf16[1,20,16,128]{3,2,1,0:T(8,128)(2,1)S(1)}, bf16[1,20,16,128]{3,2,1,0:T(8,128)(2,1)S(1)}, u32[]{:S(2)}, u32[]{:S(2)}) collective-permute-start(bf16[1,20,16,128]{3,2,1,0:T(8,128)(2,1)S(1)} %get-tuple-element.14), channel_id=1, source_target_pairs={{0,2},{1,3},{2,4},{3,5},{4,6},{5,7},{6,0},{7,1},{8,10},{9,11},{10,... | collective-permute-start | bytes 245768 | tf_op jit(solution)/shard_map/ppermute | solution.py:205
  4.8 10.3 %collective-permute-start.1 = (bf16[1,20,16,128]{3,2,1,0:T(8,128)(2,1)S(1)}, bf16[1,20,16,128]{3,2,1,0:T(8,128)(2,1)S(1)}, u32[]{:S(2)}, u32[]{:S(2)}) collective-permute-start(bf16[1,20,16,128]{3,2,1,0:T(8,128)(2,1)S(1)} %get-tuple-element.15), channel_id=1, source_target_pairs={{0,4},{1,5},{2,6},{3,7},{4,0},{5,1},{6,2},{7,3},{8,12},{9,13},{10,... | collective-permute-start | bytes 245768 | tf_op jit(solution)/shard_map/ppermute | solution.py:205
  9.9 8.9 %collective-permute-start.2 = (bf16[1,20,16,128]{3,2,1,0:T(8,128)(2,1)S(1)}, bf16[1,20,16,128]{3,2,1,0:T(8,128)(2,1)S(1)}, u32[]{:S(2)}, u32[]{:S(2)}) collective-permute-start(bf16[1,20,16,128]{3,2,1,0:T(8,128)(2,1)S(1)} %get-tuple-element.16), channel_id=1, source_target_pairs={{0,6},{1,7},{2,0},{3,1},{4,2},{5,3},{6,4},{7,5},{8,14},{9,15},{10,... | collective-permute-start | bytes 245768 | tf_op jit(solution)/shard_map/ppermute | solution.py:205
  18.9 2.3 %copy-start.1 = (bf16[27,128,128]{2,1,0:T(8,128)(2,1)S(1)}, bf16[27,128,128]{2,1,0:T(8,128)(2,1)}, u32[]{:S(2)}) copy-start(bf16[27,128,128]{2,1,0:T(8,128)(2,1)} %param.6) | copy-start | bytes 2654212
  18.9 1.7 %collective-permute-start.3 = (bf16[4,12,16,128]{3,2,1,0:T(8,128)(2,1)S(1)}, bf16[4,12,16,128]{3,2,1,0:T(8,128)(2,1)S(1)}, u32[]{:S(2)}, u32[]{:S(2)}) collective-permute-start(bf16[4,12,16,128]{3,2,1,0:T(8,128)(2,1)S(1)} %constant_dynamic-slice_fusion.4), channel_id=1, source_target_pairs={{0,1},{1,0},{2,3},{3,2},{4,5},{5,4},{6,7},{7,6},{8,9},{9,8},{10,11... | collective-permute-start | bytes 589832 | tf_op jit(solution)/shard_map/ppermute | solution.py:210
  20.6 10.4 %collective-permute-start.5 = (bf16[4,12,32,128]{3,2,1,0:T(8,128)(2,1)S(1)}, bf16[4,12,32,128]{3,2,1,0:T(8,128)(2,1)S(1)}, u32[]{:S(2)}, u32[]{:S(2)}) collective-permute-start(bf16[4,12,32,128]{3,2,1,0:T(8,128)(2,1)S(1)} %pad_maximum_fusion.plane_ref), channel_id=1, source_target_pairs={{0,8},{8,0},{16,24},{24,16},{32,40},{40,32},{48,56},{56,48},{64,72... | collective-permute-start | bytes 1179656 | tf_op jit(solution)/shard_map/ppermute | solution.py:217
  21.2 14.2 %collective-permute-start.4 = (bf16[4,12,32,128]{3,2,1,0:T(8,128)(2,1)S(1)}, bf16[4,12,32,128]{3,2,1,0:T(8,128)(2,1)S(1)}, u32[]{:S(2)}, u32[]{:S(2)}) collective-permute-start(bf16[4,12,32,128]{3,2,1,0:T(8,128)(2,1)S(1)} %pad_maximum_fusion.plane_ref), channel_id=1, source_target_pairs={{0,1},{1,0},{2,3},{3,2},{4,5},{5,4},{6,7},{7,6},{8,16},{9,17},{10,... | collective-permute-start | bytes 1179656 | tf_op jit(solution)/shard_map/ppermute | solution.py:216
  22.7 0.7 copy-start.3
  32.3 4.9 %copy-start.2 = (bf16[27,128,128]{2,1,0:T(8,128)(2,1)S(1)}, bf16[27,128,128]{2,1,0:T(8,128)(2,1)}, u32[]{:S(2)}) copy-start(bf16[27,128,128]{2,1,0:T(8,128)(2,1)} %param.8) | copy-start | bytes 2654212
  36.7 7.8 %collective-permute-start.7 = (bf16[10,128,128]{2,1,0:T(8,128)(2,1)S(1)}, bf16[10,128,128]{2,1,0:T(8,128)(2,1)S(1)}, u32[]{:S(2)}, u32[]{:S(2)}) collective-permute-start(bf16[10,128,128]{2,1,0:T(8,128)(2,1)S(1)} %first_far.1.plane_ref), channel_id=1, source_target_pairs={{0,8},{8,0},{16,24},{24,16},{32,40},{40,32},{48,56},{56,48},{64,72... | collective-permute-start | bytes 983048 | tf_op jit(solution)/shard_map/ppermute | solution.py:217
  36.8 12.7 %collective-permute-start.6 = (bf16[10,128,128]{2,1,0:T(8,128)(2,1)S(1)}, bf16[10,128,128]{2,1,0:T(8,128)(2,1)S(1)}, u32[]{:S(2)}, u32[]{:S(2)}) collective-permute-start(bf16[10,128,128]{2,1,0:T(8,128)(2,1)S(1)} %first_far.1.plane_ref), channel_id=1, source_target_pairs={{0,1},{1,0},{2,3},{3,2},{4,5},{5,4},{6,7},{7,6},{8,16},{9,17},{10,... | collective-permute-start | bytes 983048 | tf_op jit(solution)/shard_map/ppermute | solution.py:216
  38.7 0.7 copy-start.4
  50.8 6.2 %collective-permute-start.10 = (bf16[2,8,16,128]{3,2,1,0:T(8,128)(2,1)S(1)}, bf16[2,8,16,128]{3,2,1,0:T(8,128)(2,1)S(1)}, u32[]{:S(2)}, u32[]{:S(2)}) collective-permute-start(bf16[2,8,16,128]{3,2,1,0:T(8,128)(2,1)S(1)} %get-tuple-element.20), channel_id=1, source_target_pairs={{0,6},{1,7},{2,0},{3,1},{4,2},{5,3},{6,4},{7,5},{8,14},{9,15},{10,... | collective-permute-start | bytes 196616 | tf_op jit(solution)/shard_map/ppermute | solution.py:259
  53.3 7.1 %collective-permute-start.9 = (bf16[2,8,16,128]{3,2,1,0:T(8,128)(2,1)S(1)}, bf16[2,8,16,128]{3,2,1,0:T(8,128)(2,1)S(1)}, u32[]{:S(2)}, u32[]{:S(2)}) collective-permute-start(bf16[2,8,16,128]{3,2,1,0:T(8,128)(2,1)S(1)} %get-tuple-element.19), channel_id=1, source_target_pairs={{0,4},{1,5},{2,6},{3,7},{4,0},{5,1},{6,2},{7,3},{8,12},{9,13},{10,... | collective-permute-start | bytes 196616 | tf_op jit(solution)/shard_map/ppermute | solution.py:259
  55.1 5.9 %collective-permute-start.8 = (bf16[2,8,16,128]{3,2,1,0:T(8,128)(2,1)S(1)}, bf16[2,8,16,128]{3,2,1,0:T(8,128)(2,1)S(1)}, u32[]{:S(2)}, u32[]{:S(2)}) collective-permute-start(bf16[2,8,16,128]{3,2,1,0:T(8,128)(2,1)S(1)} %get-tuple-element.18), channel_id=1, source_target_pairs={{0,2},{1,3},{2,4},{3,5},{4,6},{5,7},{6,0},{7,1},{8,10},{9,11},{10,... | collective-permute-start | bytes 196616 | tf_op jit(solution)/shard_map/ppermute | solution.py:259
  61.0 6.3 %collective-permute-start.11 = (bf16[4,8,16,128]{3,2,1,0:T(8,128)(2,1)S(1)}, bf16[4,8,16,128]{3,2,1,0:T(8,128)(2,1)S(1)}, u32[]{:S(2)}, u32[]{:S(2)}) collective-permute-start(bf16[4,8,16,128]{3,2,1,0:T(8,128)(2,1)S(1)} %pad_maximum_fusion.1), channel_id=1, source_target_pairs={{0,1},{1,0},{2,3},{3,2},{4,5},{5,4},{6,7},{7,6},{8,9},{9,8},{10,11... | collective-permute-start | bytes 393224 | tf_op jit(solution)/shard_map/ppermute | solution.py:261

commit v6 on v5

--- a/solution.py
+++ b/solution.py
@@ -11,7 +11,14 @@
 RIM = 2
 PARAMS = pltpu.CompilerParams(vmem_limit_bytes=24 * 1024 * 1024)
 VMEM = pl.BlockSpec(memory_space=pltpu.VMEM)
-SMEM = pl.BlockSpec(memory_space=pltpu.SMEM)
+
+
+def my_group():
+    return lax.axis_index("chan") // CORES
+
+
+def my_core():
+    return lax.axis_index("chan") % CORES
 
 
 def along_lanes(total, lanes):
@@ -39,7 +46,7 @@
             store(start + n, along_lanes(total[:, n * lanes : (n + 1) * lanes], lanes))
 
 
-def pack_kernel(place_ref, volume_ref, *refs):
+def pack_kernel(volume_ref, *refs):
     outs, rows_ref = refs[:-1], refs[-1]
     width, _, length, lanes = volume_ref.shape
     groups = len(outs)
@@ -50,45 +57,47 @@
     turned = jnp.swapaxes(volume_ref[:, 0].astype(F32), 0, 1)
     rows_ref[RIM : RIM + length] = turned.astype(BF16)
     for k in range(groups):
-        target = lax.rem(place_ref[0] + k, groups)
+        target = lax.rem(my_group() + k, groups)
         outs[k][0] = rows_ref[pl.ds(target * rows, rows + 2 * RIM)]
 
 
-def rows_of(place_ref, ref, masked):
+def rows_of(ref, masked):
     def get(_, row):
         if len(ref.shape) == 3:
             value = ref[row]
         else:
             value = jnp.concatenate([ref[g, row] for g in range(ref.shape[0])], axis=0)
         if masked:
-            value = jnp.where(place_ref[3] == 1, jnp.zeros_like(value), value)
+            plane = lax.axis_index("space")
+            edge = (plane == 0) | (plane == lax.axis_size("space") - 1)
+            value = jnp.where(edge, jnp.zeros_like(value), value)
         return value
 
     return get
 
 
-def own_kernel(place_ref, plane_ref, weight_ref, out_ref):
+def own_kernel(plane_ref, weight_ref, out_ref):
     rows, _, lanes = out_ref.shape
 
     def store(row, value):
         out_ref[row] = value
 
-    conv_rows(rows_of(place_ref, plane_ref, False), 1, weight_ref[...], store, rows, lanes)
-
-
-def near_kernel(place_ref, plane_ref, weight_ref, before_ref, out_ref):
+    conv_rows(rows_of(plane_ref, False), 1, weight_ref[...], store, rows, lanes)
+
+
+def near_kernel(plane_ref, weight_ref, before_ref, out_ref):
     rows, _, lanes = out_ref.shape
 
     def store(row, value):
         out_ref[row] = before_ref[row] + value
 
-    weight = weight_ref[1 - place_ref[2]]
-    conv_rows(rows_of(place_ref, plane_ref, False), 1, weight, store, rows, lanes)
-
-
-def first_kernel(place_ref, plane_ref, weight_ref, before_ref, bias_ref, out_ref):
+    weight = weight_ref[1 - lax.axis_index("space") % 2]
+    conv_rows(rows_of(plane_ref, False), 1, weight, store, rows, lanes)
+
+
+def first_kernel(plane_ref, weight_ref, before_ref, bias_ref, out_ref):
     rows, _, lanes = out_ref.shape
-    block = place_ref[0] * CORES + place_ref[1]
+    block = lax.axis_index("chan")
     bias = bias_ref[...]
 
     def store(row, value):
@@ -96,14 +105,14 @@
         if row == 0:
             value = jnp.where(block == 0, 0.0, value)
         if row == rows - 1:
-            value = jnp.where(block == place_ref[4] - 1, 0.0, value)
+            value = jnp.where(block == lax.axis_size("chan") - 1, 0.0, value)
         out_ref[row] = value.astype(BF16)
 
-    weight = weight_ref[place_ref[2]]
-    conv_rows(rows_of(place_ref, plane_ref, True), 1, weight, store, rows, lanes)
-
-
-def second_kernel(place_ref, plane_ref, weight_ref, before_ref, bias_ref, *refs):
+    weight = weight_ref[lax.axis_index("space") % 2]
+    conv_rows(rows_of(plane_ref, True), 1, weight, store, rows, lanes)
+
+
+def second_kernel(plane_ref, weight_ref, before_ref, bias_ref, *refs):
     outs, all_ref = refs[:-1], refs[-1]
     groups, cores, rows, width, lanes = all_ref.shape
     bias = bias_ref[...]
@@ -115,17 +124,17 @@
                 at = (g * cores + c) * width
                 all_ref[g, c, row] = value[at : at + width]
 
-    weight = weight_ref[place_ref[2]]
-    conv_rows(rows_of(place_ref, plane_ref, True), 1, weight, store, rows, lanes)
+    weight = weight_ref[lax.axis_index("space") % 2]
+    conv_rows(rows_of(plane_ref, True), 1, weight, store, rows, lanes)
     for k in range(groups):
-        outs[k][...] = all_ref[lax.rem(place_ref[0] + k, groups)]
-
-
-def unpack_kernel(place_ref, swapped_ref, *refs):
+        outs[k][...] = all_ref[lax.rem(my_group() + k, groups)]
+
+
+def unpack_kernel(swapped_ref, *refs):
     blocks, out_ref, rows_ref = refs[:-2], refs[-2], refs[-1]
     groups = len(blocks)
     _, rows, width, lanes = blocks[0].shape
-    group, core = place_ref[0], place_ref[1]
+    group, core = my_group(), my_core()
     for k in range(groups):
         source = lax.rem(group + groups - k, groups) * CORES
         rows_ref[source + core] = blocks[k][core]
@@ -171,7 +180,7 @@
         return pl.pallas_call(
             kernel,
             out_shape=shapes,
-            in_specs=[SMEM if x.ndim == 1 else VMEM for x in inputs],
+            in_specs=[VMEM] * len(inputs),
             out_specs=VMEM if single else [VMEM] * len(shapes),
             scratch_shapes=scratch,
             compiler_params=PARAMS,
@@ -183,10 +192,7 @@
         full = width * chan
         rows = length // chan
         index = lax.axis_index("chan")
-        plane = lax.axis_index("space")
-        edge = (plane == 0) | (plane == space - 1)
         group, core = index // CORES, index % CORES
-        place = jnp.stack([group, core, plane % 2, edge.astype(jnp.int32), jnp.int32(chan)]).astype(jnp.int32)
 
         own_one, beside_one = arranged(weight_one)
         own_two, beside_two = arranged(weight_two)
@@ -195,7 +201,7 @@
         pieces = call(
             pack_kernel,
             [jax.ShapeDtypeStruct((1, tall, width, lanes), BF16)] * groups,
-            [place, volume],
+            [volume],
             [pltpu.VMEM((length + 2 * RIM, width, lanes), BF16)],
             name="pack_rows",
         )
@@ -217,18 +223,18 @@
             near_plane = lax.ppermute(array, "space", near)
             partial = jax.ShapeDtypeStruct((height, full, lanes), F32)
             work = cost(height, 1, full, lanes)
-            total = call(own_kernel, partial, [place, array, own_weight], cost_estimate=work, name=name + "_own")
+            total = call(own_kernel, partial, [array, own_weight], cost_estimate=work, name=name + "_own")
             total = call(
                 near_kernel,
                 partial,
-                [place, near_plane, beside_weight, total],
+                [near_plane, beside_weight, total],
                 cost_estimate=work,
                 name=name + "_near",
             )
             return call(
                 kernel,
                 shapes,
-                [place, far_plane, beside_weight, total, bias[:, None]],
+                [far_plane, beside_weight, total, bias[:, None]],
                 scratch,
                 cost_estimate=work,
                 name=name + "_far",
@@ -262,7 +268,7 @@
         return call(
             unpack_kernel,
             jax.ShapeDtypeStruct(volume.shape, BF16),
-            [place, swapped, *blocks],
+            [swapped, *blocks],
             [pltpu.VMEM((chan, rows, width, lanes), BF16)],
             name="unpack_rows",
         )

time: 68.9 us -> 66.6 us (0.967)
  Pallas kernels: 9.7 us -> 5.35 us
  waiting for transfers between devices: 29.3 us -> 32.5 us
  starting transfers between devices: 23.8 us -> 22.7 us
    pallas_call x8, Pallas kernels: 9.7 us -> 5.35 us  [call(): pl.pallas_call(kernel, out_shape=shapes, in_specs=[VMEM] * len(inputs), o...]
    ppermute x2, waiting for transfers between devices: 6.83 us -> 8.63 us  [layer(): far_plane = lax.ppermute(array, ('space', 'chan'), far)]
    ppermute x2, starting transfers between devices: 5.94 us -> 4.86 us  [per_device(): swapped = lax.ppermute(theirs, 'chan', swap)]
    ppermute x2, waiting for transfers between devices: 10 us -> 11.1 us  [layer(): near_plane = lax.ppermute(array, 'space', near)]
  transfers between devices with their start and end apart: 12 -> 12, of which waited for: 10 -> 10; matrix products, arithmetic and copies ran while one was open for 5% -> 5% of each run, Pallas kernels for 7% -> 4%
where the time goes in v6:
time: 66.6 us; the launch traced here: 66.5 us
  waiting for transfers between devices  32.5 us (49%)
  starting transfers between devices  22.7 us (34%)
  local copies, waits for them, and re-layouts  5.6 us (8%)
  Pallas kernels  5.35 us (8%)
    ppermute x2, waiting for transfers between devices, layer(): near_plane = lax.ppermute(array, 'space', near)  11.1 us
    ppermute x3, starting transfers between devices, per_device(): got = lax.ppermute(pieces[k], 'chan', ahead(k))  10.6 us
    ppermute x2, waiting for transfers between devices, layer(): far_plane = lax.ppermute(array, ('space', 'chan'), far)  8.63 us
    ppermute x3, waiting for transfers between devices, per_device(): got = lax.ppermute(pieces[k], 'chan', ahead(k))  6.4 us
    ppermute x3, starting transfers between devices, per_device(): lax.ppermute(blocks[k], 'chan', ahead(k))  6.22 us
    pallas_call x8, Pallas kernels, call(): pl.pallas_call(kernel, out_shape=shapes, in_specs=[VMEM] * len(inputs), o...  5.35 us
    ppermute x2, starting transfers between devices, per_device(): swapped = lax.ppermute(theirs, 'chan', swap)  4.86 us
    ppermute x3, waiting for transfers between devices, per_device(): lax.ppermute(blocks[k], 'chan', ahead(k))  4.38 us
  transfers between devices with their start and end apart: 12, of which 10 were waited for; matrix products, arithmetic and copies ran while one was open for 5% of the time, Pallas kernels for 4%

profile of v6, /device:TPU:31, one launch (start us, length us, event | category | flops | bytes accessed | tf_op | source)
XLA Modules:
  0.0 66.5 jit_solution(1741840544011724075)
XLA Ops:
  0.0 0.0 copy-start
  0.0 0.9 %copy-done = bf16[16,1,64,128]{3,2,1,0:T(8,128)(2,1)S(1)} copy-done((bf16[16,1,64,128]{3,2,1,0:T(8,128)(2,1)S(1)}, bf16[16,1,64,128]{3,2,1,0:T(8,128)(2,1)}, u32[]{:S(2)}) %copy-start) | copy-done | bytes 262168
  1.0 0.2 pack_rows.1
  1.1 3.1 %collective-permute-start = (bf16[1,20,16,128]{3,2,1,0:T(8,128)(2,1)S(1)}, bf16[1,20,16,128]{3,2,1,0:T(8,128)(2,1)S(1)}, u32[]{:S(2)}, u32[]{:S(2)}) collective-permute-start(bf16[1,20,16,128]{3,2,1,0:T(8,128)(2,1)S(1)} %get-tuple-element.14), channel_id=1, source_target_pairs={{0,2},{1,3},{2,4},{3,5},{4,6},{5,7},{6,0},{7,1},{8,10},{9,11},{10,... | collective-permute-start | bytes 245768 | tf_op jit(solution)/shard_map/ppermute | solution.py:211
  4.2 5.1 %collective-permute-start.1 = (bf16[1,20,16,128]{3,2,1,0:T(8,128)(2,1)S(1)}, bf16[1,20,16,128]{3,2,1,0:T(8,128)(2,1)S(1)}, u32[]{:S(2)}, u32[]{:S(2)}) collective-permute-start(bf16[1,20,16,128]{3,2,1,0:T(8,128)(2,1)S(1)} %get-tuple-element.15), channel_id=1, source_target_pairs={{0,4},{1,5},{2,6},{3,7},{4,0},{5,1},{6,2},{7,3},{8,12},{9,13},{10,... | collective-permute-start | bytes 245768 | tf_op jit(solution)/shard_map/ppermute | solution.py:211
  9.3 2.4 %collective-permute-start.2 = (bf16[1,20,16,128]{3,2,1,0:T(8,128)(2,1)S(1)}, bf16[1,20,16,128]{3,2,1,0:T(8,128)(2,1)S(1)}, u32[]{:S(2)}, u32[]{:S(2)}) collective-permute-start(bf16[1,20,16,128]{3,2,1,0:T(8,128)(2,1)S(1)} %get-tuple-element.16), channel_id=1, source_target_pairs={{0,6},{1,7},{2,0},{3,1},{4,2},{5,3},{6,4},{7,5},{8,14},{9,15},{10,... | collective-permute-start | bytes 245768 | tf_op jit(solution)/shard_map/ppermute | solution.py:211
  11.8 0.0 collective-permute-done
  11.8 2.7 %collective-permute-done.1 = bf16[1,20,16,128]{3,2,1,0:T(8,128)(2,1)S(1)} collective-permute-done((bf16[1,20,16,128]{3,2,1,0:T(8,128)(2,1)S(1)}, bf16[1,20,16,128]{3,2,1,0:T(8,128)(2,1)S(1)}, u32[]{:S(2)}, u32[]{:S(2)}) %collective-permute-start.1) | collective-permute-done | bytes 81952 | tf_op jit(solution)/shard_map/ppermute | solution.py:211
  14.5 3.7 %collective-permute-done.2 = bf16[1,20,16,128]{3,2,1,0:T(8,128)(2,1)S(1)} collective-permute-done((bf16[1,20,16,128]{3,2,1,0:T(8,128)(2,1)S(1)}, bf16[1,20,16,128]{3,2,1,0:T(8,128)(2,1)S(1)}, u32[]{:S(2)}, u32[]{:S(2)}) %collective-permute-start.2) | collective-permute-done | bytes 81952 | tf_op jit(solution)/shard_map/ppermute | solution.py:211
  18.2 0.0 copy-start.1
  18.3 0.6 collective-permute-start.3
  18.8 1.1 %collective-permute-done.3 = bf16[4,12,16,128]{3,2,1,0:T(8,128)(2,1)S(1)} collective-permute-done((bf16[4,12,16,128]{3,2,1,0:T(8,128)(2,1)S(1)}, bf16[4,12,16,128]{3,2,1,0:T(8,128)(2,1)S(1)}, u32[]{:S(2)}, u32[]{:S(2)}) %collective-permute-start.3) | collective-permute-done | bytes 196640 | tf_op jit(solution)/shard_map/ppermute | solution.py:216
  20.0 0.6 collective-permute-start.5
  20.5 0.0 collective-permute-start.4
  20.5 0.0 copy-done.1
  20.6 0.6 copy.18
  21.2 0.5 reshape.23.weight_ref
  21.8 0.2 copy.13
  22.1 0.0 copy-start.3
  22.1 0.6 copy-done.3
  22.7 0.1 copy.14.bias_ref
  22.8 0.8 %first_own.1.before_ref = f32[10,128,128]{2,1,0:T(8,128)S(1)} custom-call(bf16[4,12,32,128]{3,2,1,0:T(8,128)(2,1)S(1)} %pad_maximum_fusion.plane_ref, bf16[384,384]{1,0:T(8,128)(2,1)S(1)} %bitcast.21), custom_call_target="tpu_custom_call" | custom-call | flops 377487360 | bytes 4000000 | tf_op jit(solution)/shard_map/first_own/pallas_call | solution.py:180
  23.6 6.8 %collective-permute-done.5.plane_ref = bf16[4,12,32,128]{3,2,1,0:T(8,128)(2,1)S(1)} collective-permute-done((bf16[4,12,32,128]{3,2,1,0:T(8,128)(2,1)S(1)}, bf16[4,12,32,128]{3,2,1,0:T(8,128)(2,1)S(1)}, u32[]{:S(2)}, u32[]{:S(2)}) %collective-permute-start.5) | collective-permute-done | bytes 393248 | tf_op jit(solution)/shard_map/ppermute | solution.py:223
  30.4 0.8 %first_near.1.before_ref = f32[10,128,128]{2,1,0:T(8,128)S(1)} custom-call(bf16[4,12,32,128]{3,2,1,0:T(8,128)(2,1)S(1)} %collective-permute-done.5.plane_ref, bf16[2,384,384]{2,1,0:T(8,128)(2,1)S(1)} %reshape.23.weight_ref, f32[10,128,128]{2,1,0:T(8,128)S(1)} %first_own.1.before_ref), custom_call_target="tpu_custom_call" | custom-call | flops 377487360 | bytes 4000000 | tf_op jit(solution)/shard_map/first_near/pallas_call | solution.py:180
  31.2 0.0 copy-start.2
  31.2 3.6 %collective-permute-done.4.plane_ref = bf16[4,12,32,128]{3,2,1,0:T(8,128)(2,1)S(1)} collective-permute-done((bf16[4,12,32,128]{3,2,1,0:T(8,128)(2,1)S(1)}, bf16[4,12,32,128]{3,2,1,0:T(8,128)(2,1)S(1)}, u32[]{:S(2)}, u32[]{:S(2)}) %collective-permute-start.4) | collective-permute-done | bytes 393248 | tf_op jit(solution)/shard_map/ppermute | solution.py:222
  34.8 0.8 %first_far.1.plane_ref = bf16[10,128,128]{2,1,0:T(8,128)(2,1)S(1)} custom-call(bf16[4,12,32,128]{3,2,1,0:T(8,128)(2,1)S(1)} %collective-permute-done.4.plane_ref, bf16[2,384,384]{2,1,0:T(8,128)(2,1)S(1)} %reshape.23.weight_ref, f32[10,128,128]{2,1,0:T(8,128)S(1)} %first_near.1.before_ref, f32[128,1]{1,0:T(8,128)S(1)} %copy.14.bias_ref), custom_call_target="tpu_custom_call" | custom-call | flops 377487360 | bytes 4000000 | tf_op jit(solution)/shard_map/first_far/pallas_call | solution.py:180
  35.5 0.1 collective-permute-start.7
  35.6 0.4 collective-permute-start.6
  36.0 0.0 copy-done.2
  36.1 0.6 copy.19
  36.7 0.5 reshape.26.weight_ref
  37.3 0.2 copy.16
  37.6 0.0 copy-start.4
  37.6 0.6 copy-done.4
  38.2 0.1 copy.17.bias_ref
  38.3 0.7 %second_own.1.before_ref = f32[8,128,128]{2,1,0:T(8,128)S(1)} custom-call(bf16[10,128,128]{2,1,0:T(8,128)(2,1)S(1)} %first_far.1.plane_ref, bf16[384,384]{1,0:T(8,128)(2,1)S(1)} %bitcast.20), custom_call_target="tpu_custom_call" | custom-call | flops 301989888 | bytes 4000000 | tf_op jit(solution)/shard_map/second_own/pallas_call | solution.py:180
  39.0 4.3 %collective-permute-done.7.plane_ref = bf16[10,128,128]{2,1,0:T(8,128)(2,1)S(1)} collective-permute-done((bf16[10,128,128]{2,1,0:T(8,128)(2,1)S(1)}, bf16[10,128,128]{2,1,0:T(8,128)(2,1)S(1)}, u32[]{:S(2)}, u32[]{:S(2)}) %collective-permute-start.7) | collective-permute-done | bytes 327712 | tf_op jit(solution)/shard_map/ppermute | solution.py:223
  43.3 0.7 %second_near.1.before_ref = f32[8,128,128]{2,1,0:T(8,128)S(1)} custom-call(bf16[10,128,128]{2,1,0:T(8,128)(2,1)S(1)} %collective-permute-done.7.plane_ref, bf16[2,384,384]{2,1,0:T(8,128)(2,1)S(1)} %reshape.26.weight_ref, f32[8,128,128]{2,1,0:T(8,128)S(1)} %second_own.1.before_ref), custom_call_target="tpu_custom_call" | custom-call | flops 301989888 | bytes 4000000 | tf_op jit(solution)/shard_map/second_near/pallas_call | solution.py:180
  44.0 5.0 %collective-permute-done.6.plane_ref = bf16[10,128,128]{2,1,0:T(8,128)(2,1)S(1)} collective-permute-done((bf16[10,128,128]{2,1,0:T(8,128)(2,1)S(1)}, bf16[10,128,128]{2,1,0:T(8,128)(2,1)S(1)}, u32[]{:S(2)}, u32[]{:S(2)}) %collective-permute-start.6) | collective-permute-done | bytes 327712 | tf_op jit(solution)/shard_map/ppermute | solution.py:222
  49.0 0.7 %second_far.1 = (bf16[2,8,16,128]{3,2,1,0:T(8,128)(2,1)S(1)}, bf16[2,8,16,128]{3,2,1,0:T(8,128)(2,1)S(1)}, bf16[2,8,16,128]{3,2,1,0:T(8,128)(2,1)S(1)}, bf16[2,8,16,128]{3,2,1,0:T(8,128)(2,1)S(1)}) custom-call(bf16[10,128,128]{2,1,0:T(8,128)(2,1)S(1)} %collective-permute-done.6.plane_ref, bf16[2,384,384]{2,1,0:T(8,128)(2,1)S(1)} %reshape.26.weight_ref, ...), custom_call_target="tpu_custom_call" | custom-call | flops 301989888 | bytes 4000000 | tf_op jit(solution)/shard_map/second_far/pallas_call | solution.py:180
  49.7 2.5 %collective-permute-start.10 = (bf16[2,8,16,128]{3,2,1,0:T(8,128)(2,1)S(1)}, bf16[2,8,16,128]{3,2,1,0:T(8,128)(2,1)S(1)}, u32[]{:S(2)}, u32[]{:S(2)}) collective-permute-start(bf16[2,8,16,128]{3,2,1,0:T(8,128)(2,1)S(1)} %get-tuple-element.20), channel_id=1, source_target_pairs={{0,6},{1,7},{2,0},{3,1},{4,2},{5,3},{6,4},{7,5},{8,14},{9,15},{10,... | collective-permute-start | bytes 196616 | tf_op jit(solution)/shard_map/ppermute | solution.py:265
  52.3 1.8 %collective-permute-start.9 = (bf16[2,8,16,128]{3,2,1,0:T(8,128)(2,1)S(1)}, bf16[2,8,16,128]{3,2,1,0:T(8,128)(2,1)S(1)}, u32[]{:S(2)}, u32[]{:S(2)}) collective-permute-start(bf16[2,8,16,128]{3,2,1,0:T(8,128)(2,1)S(1)} %get-tuple-element.19), channel_id=1, source_target_pairs={{0,4},{1,5},{2,6},{3,7},{4,0},{5,1},{6,2},{7,3},{8,12},{9,13},{10,... | collective-permute-start | bytes 196616 | tf_op jit(solution)/shard_map/ppermute | solution.py:265
  54.1 1.9 %collective-permute-start.8 = (bf16[2,8,16,128]{3,2,1,0:T(8,128)(2,1)S(1)}, bf16[2,8,16,128]{3,2,1,0:T(8,128)(2,1)S(1)}, u32[]{:S(2)}, u32[]{:S(2)}) collective-permute-start(bf16[2,8,16,128]{3,2,1,0:T(8,128)(2,1)S(1)} %get-tuple-element.18), channel_id=1, source_target_pairs={{0,2},{1,3},{2,4},{3,5},{4,6},{5,7},{6,0},{7,1},{8,10},{9,11},{10,... | collective-permute-start | bytes 196616 | tf_op jit(solution)/shard_map/ppermute | solution.py:265
  56.0 0.0 collective-permute-done.10.refs_3_
  56.0 3.4 %collective-permute-done.9.refs_2_ = bf16[2,8,16,128]{3,2,1,0:T(8,128)(2,1)S(1)} collective-permute-done((bf16[2,8,16,128]{3,2,1,0:T(8,128)(2,1)S(1)}, bf16[2,8,16,128]{3,2,1,0:T(8,128)(2,1)S(1)}, u32[]{:S(2)}, u32[]{:S(2)}) %collective-permute-start.9) | collective-permute-done | bytes 65568 | tf_op jit(solution)/shard_map/ppermute | solution.py:265
  59.4 1.0 %collective-permute-done.8.refs_1_ = bf16[2,8,16,128]{3,2,1,0:T(8,128)(2,1)S(1)} collective-permute-done((bf16[2,8,16,128]{3,2,1,0:T(8,128)(2,1)S(1)}, bf16[2,8,16,128]{3,2,1,0:T(8,128)(2,1)S(1)}, u32[]{:S(2)}, u32[]{:S(2)}) %collective-permute-start.8) | collective-permute-done | bytes 65568 | tf_op jit(solution)/shard_map/ppermute | solution.py:265
  60.4 4.3 %collective-permute-start.11 = (bf16[4,8,16,128]{3,2,1,0:T(8,128)(2,1)S(1)}, bf16[4,8,16,128]{3,2,1,0:T(8,128)(2,1)S(1)}, u32[]{:S(2)}, u32[]{:S(2)}) collective-permute-start(bf16[4,8,16,128]{3,2,1,0:T(8,128)(2,1)S(1)} %pad_maximum_fusion.1), channel_id=1, source_target_pairs={{0,1},{1,0},{2,3},{3,2},{4,5},{5,4},{6,7},{7,6},{8,9},{9,8},{10,11... | collective-permute-start | bytes 393224 | tf_op jit(solution)/shard_map/ppermute | solution.py:267
  64.7 1.0 %collective-permute-done.11.swapped_ref = bf16[4,8,16,128]{3,2,1,0:T(8,128)(2,1)S(1)} collective-permute-done((bf16[4,8,16,128]{3,2,1,0:T(8,128)(2,1)S(1)}, bf16[4,8,16,128]{3,2,1,0:T(8,128)(2,1)S(1)}, u32[]{:S(2)}, u32[]{:S(2)}) %collective-permute-start.11) | collective-permute-done | bytes 131104 | tf_op jit(solution)/shard_map/ppermute | solution.py:267
  65.7 0.8 %unpack_rows.1 = bf16[16,1,64,128]{3,2,1,0:T(8,128)(2,1)} custom-call(bf16[4,8,16,128]{3,2,1,0:T(8,128)(2,1)S(1)} %collective-permute-done.11.swapped_ref, bf16[2,8,16,128]{3,2,1,0:T(8,128)(2,1)S(1)} %get-tuple-element.17.refs_0_, bf16[2,8,16,128]{3,2,1,0:T(8,128)(2,1)S(1)} %collective-permute-done.8.refs_1_, ...), custom_call_target="tpu_custom_call" | custom-call | tf_op jit(solution)/shard_map/unpack_rows/pallas_call | solution.py:180
  (19 shorter events, 0.4 us)
Async XLA Ops:
  0.0 0.9 %copy-start = (bf16[16,1,64,128]{3,2,1,0:T(8,128)(2,1)S(1)}, bf16[16,1,64,128]{3,2,1,0:T(8,128)(2,1)}, u32[]{:S(2)}) copy-start(bf16[16,1,64,128]{3,2,1,0:T(8,128)(2,1)} %volume_ref.1) | copy-start | bytes 786436
  1.1 10.6 %collective-permute-start = (bf16[1,20,16,128]{3,2,1,0:T(8,128)(2,1)S(1)}, bf16[1,20,16,128]{3,2,1,0:T(8,128)(2,1)S(1)}, u32[]{:S(2)}, u32[]{:S(2)}) collective-permute-start(bf16[1,20,16,128]{3,2,1,0:T(8,128)(2,1)S(1)} %get-tuple-element.14), channel_id=1, source_target_pairs={{0,2},{1,3},{2,4},{3,5},{4,6},{5,7},{6,0},{7,1},{8,10},{9,11},{10,... | collective-permute-start | bytes 245768 | tf_op jit(solution)/shard_map/ppermute | solution.py:211
  4.2 10.3 %collective-permute-start.1 = (bf16[1,20,16,128]{3,2,1,0:T(8,128)(2,1)S(1)}, bf16[1,20,16,128]{3,2,1,0:T(8,128)(2,1)S(1)}, u32[]{:S(2)}, u32[]{:S(2)}) collective-permute-start(bf16[1,20,16,128]{3,2,1,0:T(8,128)(2,1)S(1)} %get-tuple-element.15), channel_id=1, source_target_pairs={{0,4},{1,5},{2,6},{3,7},{4,0},{5,1},{6,2},{7,3},{8,12},{9,13},{10,... | collective-permute-start | bytes 245768 | tf_op jit(solution)/shard_map/ppermute | solution.py:211
  9.3 8.9 %collective-permute-start.2 = (bf16[1,20,16,128]{3,2,1,0:T(8,128)(2,1)S(1)}, bf16[1,20,16,128]{3,2,1,0:T(8,128)(2,1)S(1)}, u32[]{:S(2)}, u32[]{:S(2)}) collective-permute-start(bf16[1,20,16,128]{3,2,1,0:T(8,128)(2,1)S(1)} %get-tuple-element.16), channel_id=1, source_target_pairs={{0,6},{1,7},{2,0},{3,1},{4,2},{5,3},{6,4},{7,5},{8,14},{9,15},{10,... | collective-permute-start | bytes 245768 | tf_op jit(solution)/shard_map/ppermute | solution.py:211
  18.2 2.3 %copy-start.1 = (bf16[27,128,128]{2,1,0:T(8,128)(2,1)S(1)}, bf16[27,128,128]{2,1,0:T(8,128)(2,1)}, u32[]{:S(2)}) copy-start(bf16[27,128,128]{2,1,0:T(8,128)(2,1)} %param.6) | copy-start | bytes 2654212
  18.3 1.7 %collective-permute-start.3 = (bf16[4,12,16,128]{3,2,1,0:T(8,128)(2,1)S(1)}, bf16[4,12,16,128]{3,2,1,0:T(8,128)(2,1)S(1)}, u32[]{:S(2)}, u32[]{:S(2)}) collective-permute-start(bf16[4,12,16,128]{3,2,1,0:T(8,128)(2,1)S(1)} %constant_dynamic-slice_fusion.4), channel_id=1, source_target_pairs={{0,1},{1,0},{2,3},{3,2},{4,5},{5,4},{6,7},{7,6},{8,9},{9,8},{10,11... | collective-permute-start | bytes 589832 | tf_op jit(solution)/shard_map/ppermute | solution.py:216
  20.0 10.4 %collective-permute-start.5 = (bf16[4,12,32,128]{3,2,1,0:T(8,128)(2,1)S(1)}, bf16[4,12,32,128]{3,2,1,0:T(8,128)(2,1)S(1)}, u32[]{:S(2)}, u32[]{:S(2)}) collective-permute-start(bf16[4,12,32,128]{3,2,1,0:T(8,128)(2,1)S(1)} %pad_maximum_fusion.plane_ref), channel_id=1, source_target_pairs={{0,8},{8,0},{16,24},{24,16},{32,40},{40,32},{48,56},{56,48},{64,72... | collective-permute-start | bytes 1179656 | tf_op jit(solution)/shard_map/ppermute | solution.py:223
  20.5 14.2 %collective-permute-start.4 = (bf16[4,12,32,128]{3,2,1,0:T(8,128)(2,1)S(1)}, bf16[4,12,32,128]{3,2,1,0:T(8,128)(2,1)S(1)}, u32[]{:S(2)}, u32[]{:S(2)}) collective-permute-start(bf16[4,12,32,128]{3,2,1,0:T(8,128)(2,1)S(1)} %pad_maximum_fusion.plane_ref), channel_id=1, source_target_pairs={{0,1},{1,0},{2,3},{3,2},{4,5},{5,4},{6,7},{7,6},{8,16},{9,17},{10,... | collective-permute-start | bytes 1179656 | tf_op jit(solution)/shard_map/ppermute | solution.py:222
  22.1 0.7 copy-start.3
  31.2 4.9 %copy-start.2 = (bf16[27,128,128]{2,1,0:T(8,128)(2,1)S(1)}, bf16[27,128,128]{2,1,0:T(8,128)(2,1)}, u32[]{:S(2)}) copy-start(bf16[27,128,128]{2,1,0:T(8,128)(2,1)} %param.8) | copy-start | bytes 2654212
  35.5 7.8 %collective-permute-start.7 = (bf16[10,128,128]{2,1,0:T(8,128)(2,1)S(1)}, bf16[10,128,128]{2,1,0:T(8,128)(2,1)S(1)}, u32[]{:S(2)}, u32[]{:S(2)}) collective-permute-start(bf16[10,128,128]{2,1,0:T(8,128)(2,1)S(1)} %first_far.1.plane_ref), channel_id=1, source_target_pairs={{0,8},{8,0},{16,24},{24,16},{32,40},{40,32},{48,56},{56,48},{64,72... | collective-permute-start | bytes 983048 | tf_op jit(solution)/shard_map/ppermute | solution.py:223
  35.6 13.4 %collective-permute-start.6 = (bf16[10,128,128]{2,1,0:T(8,128)(2,1)S(1)}, bf16[10,128,128]{2,1,0:T(8,128)(2,1)S(1)}, u32[]{:S(2)}, u32[]{:S(2)}) collective-permute-start(bf16[10,128,128]{2,1,0:T(8,128)(2,1)S(1)} %first_far.1.plane_ref), channel_id=1, source_target_pairs={{0,1},{1,0},{2,3},{3,2},{4,5},{5,4},{6,7},{7,6},{8,16},{9,17},{10,... | collective-permute-start | bytes 983048 | tf_op jit(solution)/shard_map/ppermute | solution.py:222
  37.6 0.7 copy-start.4
  49.7 6.2 %collective-permute-start.10 = (bf16[2,8,16,128]{3,2,1,0:T(8,128)(2,1)S(1)}, bf16[2,8,16,128]{3,2,1,0:T(8,128)(2,1)S(1)}, u32[]{:S(2)}, u32[]{:S(2)}) collective-permute-start(bf16[2,8,16,128]{3,2,1,0:T(8,128)(2,1)S(1)} %get-tuple-element.20), channel_id=1, source_target_pairs={{0,6},{1,7},{2,0},{3,1},{4,2},{5,3},{6,4},{7,5},{8,14},{9,15},{10,... | collective-permute-start | bytes 196616 | tf_op jit(solution)/shard_map/ppermute | solution.py:265
  52.3 7.1 %collective-permute-start.9 = (bf16[2,8,16,128]{3,2,1,0:T(8,128)(2,1)S(1)}, bf16[2,8,16,128]{3,2,1,0:T(8,128)(2,1)S(1)}, u32[]{:S(2)}, u32[]{:S(2)}) collective-permute-start(bf16[2,8,16,128]{3,2,1,0:T(8,128)(2,1)S(1)} %get-tuple-element.19), channel_id=1, source_target_pairs={{0,4},{1,5},{2,6},{3,7},{4,0},{5,1},{6,2},{7,3},{8,12},{9,13},{10,... | collective-permute-start | bytes 196616 | tf_op jit(solution)/shard_map/ppermute | solution.py:265
  54.1 6.3 %collective-permute-start.8 = (bf16[2,8,16,128]{3,2,1,0:T(8,128)(2,1)S(1)}, bf16[2,8,16,128]{3,2,1,0:T(8,128)(2,1)S(1)}, u32[]{:S(2)}, u32[]{:S(2)}) collective-permute-start(bf16[2,8,16,128]{3,2,1,0:T(8,128)(2,1)S(1)} %get-tuple-element.18), channel_id=1, source_target_pairs={{0,2},{1,3},{2,4},{3,5},{4,6},{5,7},{6,0},{7,1},{8,10},{9,11},{10,... | collective-permute-start | bytes 196616 | tf_op jit(solution)/shard_map/ppermute | solution.py:265
  60.4 5.3 %collective-permute-start.11 = (bf16[4,8,16,128]{3,2,1,0:T(8,128)(2,1)S(1)}, bf16[4,8,16,128]{3,2,1,0:T(8,128)(2,1)S(1)}, u32[]{:S(2)}, u32[]{:S(2)}) collective-permute-start(bf16[4,8,16,128]{3,2,1,0:T(8,128)(2,1)S(1)} %pad_maximum_fusion.1), channel_id=1, source_target_pairs={{0,1},{1,0},{2,3},{3,2},{4,5},{5,4},{6,7},{7,6},{8,9},{9,8},{10,11... | collective-permute-start | bytes 393224 | tf_op jit(solution)/shard_map/ppermute | solution.py:267

commit v7 on v6

--- a/solution.py
+++ b/solution.py
@@ -61,12 +61,22 @@
         outs[k][0] = rows_ref[pl.ds(target * rows, rows + 2 * RIM)]
 
 
+def gather_rows(kept_ref, other_ref, joined_ref):
+    core = my_core()
+    groups, rows, width, lanes = other_ref.shape
+    offset = core * (kept_ref.shape[1] - rows)
+    for row in range(rows):
+        parts = []
+        for g in range(groups):
+            kept = kept_ref[g, offset + row]
+            other = other_ref[g, row]
+            parts += [jnp.where(core == 0, kept, other), jnp.where(core == 0, other, kept)]
+        joined_ref[row] = jnp.concatenate(parts, axis=0)
+
+
 def rows_of(ref, masked):
     def get(_, row):
-        if len(ref.shape) == 3:
-            value = ref[row]
-        else:
-            value = jnp.concatenate([ref[g, row] for g in range(ref.shape[0])], axis=0)
+        value = ref[row]
         if masked:
             plane = lax.axis_index("space")
             edge = (plane == 0) | (plane == lax.axis_size("space") - 1)
@@ -95,7 +105,19 @@
     conv_rows(rows_of(plane_ref, False), 1, weight, store, rows, lanes)
 
 
-def first_kernel(plane_ref, weight_ref, before_ref, bias_ref, out_ref):
+def first_own_kernel(kept_ref, other_ref, weight_ref, later_ref, bias_ref, out_ref, zero_ref, joined_ref):
+    gather_rows(kept_ref, other_ref, joined_ref)
+    own_kernel(joined_ref, weight_ref, out_ref)
+    zero_ref[...] = jnp.zeros_like(zero_ref)
+
+
+def first_near_kernel(kept_ref, other_ref, weight_ref, before_ref, out_ref, joined_ref):
+    gather_rows(kept_ref, other_ref, joined_ref)
+    near_kernel(joined_ref, weight_ref, before_ref, out_ref)
+
+
+def first_far_kernel(kept_ref, other_ref, weight_ref, before_ref, bias_ref, out_ref, joined_ref):
+    gather_rows(kept_ref, other_ref, joined_ref)
     rows, _, lanes = out_ref.shape
     block = lax.axis_index("chan")
     bias = bias_ref[...]
@@ -109,7 +131,7 @@
         out_ref[row] = value.astype(BF16)
 
     weight = weight_ref[lax.axis_index("space") % 2]
-    conv_rows(rows_of(plane_ref, True), 1, weight, store, rows, lanes)
+    conv_rows(rows_of(joined_ref, True), 1, weight, store, rows, lanes)
 
 
 def second_kernel(plane_ref, weight_ref, before_ref, bias_ref, *refs):
@@ -211,55 +233,55 @@
             got = lax.ppermute(pieces[k], "chan", ahead(k))
             kept = lax.dynamic_update_slice_in_dim(kept, got, (group + groups - k) % groups, 0)
 
-        mine = lax.dynamic_slice_in_dim(kept, core * rows, rows + 2 * RIM, 1)
-        theirs = lax.dynamic_slice_in_dim(kept, (1 - core) * rows, rows + 2 * RIM, 1)
-        swapped = lax.ppermute(theirs, "chan", swap)
-        first = jnp.where(core == 0, mine, swapped)
-        second = jnp.where(core == 0, swapped, mine)
-        whole = jnp.concatenate([first, second], axis=2)
-
-        def layer(array, name, own_weight, beside_weight, bias, height, kernel, shapes, scratch=()):
-            far_plane = lax.ppermute(array, ("space", "chan"), far)
-            near_plane = lax.ppermute(array, "space", near)
-            partial = jax.ShapeDtypeStruct((height, full, lanes), F32)
-            work = cost(height, 1, full, lanes)
-            total = call(own_kernel, partial, [array, own_weight], cost_estimate=work, name=name + "_own")
-            total = call(
-                near_kernel,
-                partial,
-                [near_plane, beside_weight, total],
-                cost_estimate=work,
-                name=name + "_near",
-            )
-            return call(
-                kernel,
-                shapes,
-                [far_plane, beside_weight, total, bias[:, None]],
-                scratch,
-                cost_estimate=work,
-                name=name + "_far",
-            )
-
-        hidden = layer(
-            whole,
-            "first",
-            own_one,
-            beside_one,
-            bias_one,
-            rows + RIM,
-            first_kernel,
+        def from_other_core(array, core):
+            sent = lax.dynamic_slice_in_dim(array, (1 - core) * rows, rows + 2 * RIM, 1)
+            return lax.ppermute(sent, "chan", swap)
+
+        def halo(array):
+            return lax.ppermute(array, ("space", "chan"), far), lax.ppermute(array, "space", near)
+
+        partial = jax.ShapeDtypeStruct((rows + RIM, full, lanes), F32)
+        joined = [pltpu.VMEM((rows + 2 * RIM, full, lanes), BF16)]
+        work = cost(rows + RIM, 1, full, lanes)
+        far_plane, near_plane = halo(kept)
+        total, zero = call(
+            first_own_kernel,
+            [partial, jax.ShapeDtypeStruct((8, 128), jnp.int32)],
+            [kept, from_other_core(kept, core), own_one, beside_one, bias_one[:, None]],
+            joined,
+            cost_estimate=work,
+            name="first_own",
+        )
+        later_core = core + zero[0, 0]
+        total = call(
+            first_near_kernel,
+            partial,
+            [near_plane, from_other_core(near_plane, later_core), beside_one, total],
+            joined,
+            cost_estimate=work,
+            name="first_near",
+        )
+        hidden = call(
+            first_far_kernel,
             jax.ShapeDtypeStruct((rows + RIM, full, lanes), BF16),
-        )
-        blocks = layer(
-            hidden,
-            "second",
-            own_two,
-            beside_two,
-            bias_two,
-            rows,
+            [far_plane, from_other_core(far_plane, later_core), beside_one, total, bias_one[:, None]],
+            joined,
+            cost_estimate=work,
+            name="first_far",
+        )
+
+        partial = jax.ShapeDtypeStruct((rows, full, lanes), F32)
+        work = cost(rows, 1, full, lanes)
+        far_plane, near_plane = halo(hidden)
+        total = call(own_kernel, partial, [hidden, own_two], cost_estimate=work, name="second_own")
+        total = call(near_kernel, partial, [near_plane, beside_two, total], cost_estimate=work, name="second_near")
+        blocks = call(
             second_kernel,
             [jax.ShapeDtypeStruct((CORES, rows, width, lanes), BF16)] * groups,
+            [far_plane, beside_two, total, bias_two[:, None]],
             [pltpu.VMEM((groups, CORES, rows, width, lanes), BF16)],
+            cost_estimate=work,
+            name="second_far",
         )
 
         blocks = [blocks[0]] + [lax.ppermute(blocks[k], "chan", ahead(k)) for k in range(1, groups)]

time: 66.6 us -> 65.5 us (0.983); the launches traced: 66.5 us -> 64.4 us
  waiting for transfers between devices: 32.5 us -> 23.5 us
  local copies, waits for them, and re-layouts: 5.6 us -> 8.78 us
  starting transfers between devices: 22.7 us -> 25.7 us
    ppermute x4 -> x7, waiting for transfers between devices: 19.7 us -> 14.8 us  [the longest x2 8.42 us: halo(): lax.ppermute(array, ('space', 'chan'), far)]
    ppermute x4 -> x7, starting transfers between devices: 1.05 us -> 4.16 us  [the longest x3 3.24 us: from_other_core(): return lax.ppermute(sent, 'chan', swap)]
    ppermute x3, waiting for transfers between devices: 4.38 us -> 1.32 us  [per_device(): lax.ppermute(blocks[k], 'chan', ahead(k))]
    ppermute x2 -> x1, starting transfers between devices: 4.86 us -> 2.84 us  [per_device(): swapped = lax.ppermute(theirs, 'chan', swap)]
    ppermute x3, starting transfers between devices: 6.22 us -> 8.14 us  [per_device(): lax.ppermute(blocks[k], 'chan', ahead(k))]
    slice x2 -> x3, local copies, waits for them, and re-layouts: 0.04 us -> 1.69 us  [arranged(): own = taps[1].transpose(1, 3, 0, 2).reshape(3 * outer, 3 * inner)]
    ppermute x2 -> x1, waiting for transfers between devices: 2.06 us -> 0.99 us  [per_device(): swapped = lax.ppermute(theirs, 'chan', swap)]
    squeeze x2, local copies, waits for them, and re-layouts: 0.5 us -> 1.45 us  [arranged(): own = taps[1].transpose(1, 3, 0, 2).reshape(3 * outer, 3 * inner)]
  transfers between devices with their start and end apart: 12 -> 14, of which waited for: 10 -> 10; matrix products, arithmetic and copies ran while one was open for 5% -> 9% of each run, Pallas kernels for 4% -> 5%
where the time goes in v7:
time: 65.5 us; the launch traced here: 64.4 us
  starting transfers between devices  25.7 us (39%)
  waiting for transfers between devices  23.5 us (36%)
  local copies, waits for them, and re-layouts  8.78 us (13%)
  Pallas kernels  5.48 us (8%)
  between operations  0.9 us (1%)
    ppermute x3, starting transfers between devices, per_device(): got = lax.ppermute(pieces[k], 'chan', ahead(k))  10.6 us
    ppermute x2, waiting for transfers between devices, halo(): lax.ppermute(array, ('space', 'chan'), far)  8.42 us
    ppermute x3, starting transfers between devices, per_device(): lax.ppermute(blocks[k], 'chan', ahead(k))  8.14 us
    ppermute x3, waiting for transfers between devices, per_device(): got = lax.ppermute(pieces[k], 'chan', ahead(k))  6.4 us
    ppermute x2, waiting for transfers between devices, halo(): lax.ppermute(array, 'space', near)  6.12 us
    pallas_call x8, Pallas kernels, call(): pl.pallas_call(kernel, out_shape=shapes, in_specs=[VMEM] * len(inputs), o...  5.48 us
    unnamed x14, local copies, waits for them, and re-layouts  3.57 us
    ppermute x3, starting transfers between devices, from_other_core(): return lax.ppermute(sent, 'chan', swap)  3.24 us
  transfers between devices with their start and end apart: 14, of which 10 were waited for; matrix products, arithmetic and copies ran while one was open for 9% of the time, Pallas kernels for 5%

profile of v7, /device:TPU:31, one launch (start us, length us, event | category | flops | bytes accessed | tf_op | source)
XLA Modules:
  0.0 64.4 jit_solution(5837007597279213470)
XLA Ops:
  0.0 0.0 copy-start
  0.0 0.9 %copy-done = bf16[16,1,64,128]{3,2,1,0:T(8,128)(2,1)S(1)} copy-done((bf16[16,1,64,128]{3,2,1,0:T(8,128)(2,1)S(1)}, bf16[16,1,64,128]{3,2,1,0:T(8,128)(2,1)}, u32[]{:S(2)}) %copy-start) | copy-done | bytes 262168
  1.0 0.0 copy-start.2
  1.0 0.2 pack_rows.1
  1.1 3.1 %collective-permute-start = (bf16[1,20,16,128]{3,2,1,0:T(8,128)(2,1)S(1)}, bf16[1,20,16,128]{3,2,1,0:T(8,128)(2,1)S(1)}, u32[]{:S(2)}, u32[]{:S(2)}) collective-permute-start(bf16[1,20,16,128]{3,2,1,0:T(8,128)(2,1)S(1)} %get-tuple-element.16), channel_id=1, source_target_pairs={{0,2},{1,3},{2,4},{3,5},{4,6},{5,7},{6,0},{7,1},{8,10},{9,11},{10,... | collective-permute-start | bytes 245768 | tf_op jit(solution)/shard_map/ppermute | solution.py:233
  4.2 5.1 %collective-permute-start.1 = (bf16[1,20,16,128]{3,2,1,0:T(8,128)(2,1)S(1)}, bf16[1,20,16,128]{3,2,1,0:T(8,128)(2,1)S(1)}, u32[]{:S(2)}, u32[]{:S(2)}) collective-permute-start(bf16[1,20,16,128]{3,2,1,0:T(8,128)(2,1)S(1)} %get-tuple-element.17), channel_id=1, source_target_pairs={{0,4},{1,5},{2,6},{3,7},{4,0},{5,1},{6,2},{7,3},{8,12},{9,13},{10,... | collective-permute-start | bytes 245768 | tf_op jit(solution)/shard_map/ppermute | solution.py:233
  9.3 2.4 %collective-permute-start.2 = (bf16[1,20,16,128]{3,2,1,0:T(8,128)(2,1)S(1)}, bf16[1,20,16,128]{3,2,1,0:T(8,128)(2,1)S(1)}, u32[]{:S(2)}, u32[]{:S(2)}) collective-permute-start(bf16[1,20,16,128]{3,2,1,0:T(8,128)(2,1)S(1)} %get-tuple-element.18), channel_id=1, source_target_pairs={{0,6},{1,7},{2,0},{3,1},{4,2},{5,3},{6,4},{7,5},{8,14},{9,15},{10,... | collective-permute-start | bytes 245768 | tf_op jit(solution)/shard_map/ppermute | solution.py:233
  11.8 0.0 collective-permute-done
  11.8 2.7 %collective-permute-done.1 = bf16[1,20,16,128]{3,2,1,0:T(8,128)(2,1)S(1)} collective-permute-done((bf16[1,20,16,128]{3,2,1,0:T(8,128)(2,1)S(1)}, bf16[1,20,16,128]{3,2,1,0:T(8,128)(2,1)S(1)}, u32[]{:S(2)}, u32[]{:S(2)}) %collective-permute-start.1) | collective-permute-done | bytes 81952 | tf_op jit(solution)/shard_map/ppermute | solution.py:233
  14.5 3.7 %collective-permute-done.2 = bf16[1,20,16,128]{3,2,1,0:T(8,128)(2,1)S(1)} collective-permute-done((bf16[1,20,16,128]{3,2,1,0:T(8,128)(2,1)S(1)}, bf16[1,20,16,128]{3,2,1,0:T(8,128)(2,1)S(1)}, u32[]{:S(2)}, u32[]{:S(2)}) %collective-permute-start.2) | collective-permute-done | bytes 81952 | tf_op jit(solution)/shard_map/ppermute | solution.py:233
  18.2 0.6 collective-permute-start.6
  18.8 0.9 %collective-permute-start.4 = (bf16[4,12,16,128]{3,2,1,0:T(8,128)(2,1)S(1)}, bf16[4,12,16,128]{3,2,1,0:T(8,128)(2,1)S(1)}, u32[]{:S(2)}, u32[]{:S(2)}) collective-permute-start(bf16[4,12,16,128]{3,2,1,0:T(8,128)(2,1)S(1)} %constant_dynamic-slice_fusion.6), channel_id=1, source_target_pairs={{0,1},{1,0},{2,3},{3,2},{4,5},{5,4},{6,7},{7,6},{8,9},{9,8},{10,11... | collective-permute-start | bytes 589832 | tf_op jit(solution)/shard_map/ppermute | solution.py:238
  19.6 0.0 collective-permute-start.3
  19.7 0.0 copy-done.2
  19.7 0.7 %slice.17 = bf16[9,128,128]{2,1,0:T(8,128)(2,1)} slice(bf16[27,128,128]{2,1,0:T(8,128)(2,1)S(1)} %copy-done.2), slice={[9:18], [0:128], [0:128]} | slice | bytes 589824 | tf_op jit(solution)/shard_map/slice | solution.py:172
  20.4 0.6 copy.20
  21.0 0.5 reshape.24.later_ref.weight_ref
  21.6 0.0 copy-start.3
  21.6 0.6 %copy-done.3 = f32[128]{0:T(128)S(1)} copy-done((f32[128]{0:T(128)S(1)}, f32[128]{0:T(128)}, u32[]{:S(2)}) %copy-start.3) | copy-done | bytes 536
  22.2 0.1 copy.15.bias_ref
  22.4 1.2 %copy.13 = bf16[3,3,128,128]{2,0,3,1:T(4,128)(2,1)S(1)} copy(bf16[3,3,128,128]{3,2,1,0:T(8,128)(2,1)} %bitcast.27) | data formatting | bytes 589824 | tf_op jit(solution)/shard_map/squeeze | solution.py:172
  23.6 0.0 collective-permute-done.4.other_ref
  23.6 0.8 %first_own.1 = (f32[10,128,128]{2,1,0:T(8,128)S(1)}, s32[8,128]{1,0:T(8,128)S(1)}) custom-call(bf16[4,20,16,128]{3,2,1,0:T(8,128)(2,1)S(1)} %constant_dynamic-update-slice_fusion.kept_ref, bf16[4,12,16,128]{3,2,1,0:T(8,128)(2,1)S(1)} %collective-permute-done.4.other_ref, bf16[384,384]{1,0:T(8,128)(2,1)S(1)} %bitcast.22, ...), custom_call_target="tpu_custom_call" | custom-call | flops 377487360 | bytes 4000000 | tf_op jit(solution)/shard_map/first_own/pallas_call | solution.py:202
  24.4 0.5 slice.19
  25.6 1.5 %collective-permute-done.6.kept_ref = bf16[4,20,16,128]{3,2,1,0:T(8,128)(2,1)S(1)} collective-permute-done((bf16[4,20,16,128]{3,2,1,0:T(8,128)(2,1)S(1)}, bf16[4,20,16,128]{3,2,1,0:T(8,128)(2,1)S(1)}, u32[]{:S(2)}, u32[]{:S(2)}) %collective-permute-start.6) | collective-permute-done | bytes 327712 | tf_op jit(solution)/shard_map/ppermute | solution.py:241
  27.1 1.4 %collective-permute-start.7 = (bf16[4,12,16,128]{3,2,1,0:T(8,128)(2,1)S(1)}, bf16[4,12,16,128]{3,2,1,0:T(8,128)(2,1)S(1)}, u32[]{:S(2)}, u32[]{:S(2)}) collective-permute-start(bf16[4,12,16,128]{3,2,1,0:T(8,128)(2,1)S(1)} %constant_dynamic-slice_fusion.4), channel_id=1, source_target_pairs={{0,1},{1,0},{2,3},{3,2},{4,5},{5,4},{6,7},{7,6},{8,9},{9,8},{10,11... | collective-permute-start | bytes 589832 | tf_op jit(solution)/shard_map/ppermute | solution.py:238
  28.5 4.6 %collective-permute-done.3.kept_ref = bf16[4,20,16,128]{3,2,1,0:T(8,128)(2,1)S(1)} collective-permute-done((bf16[4,20,16,128]{3,2,1,0:T(8,128)(2,1)S(1)}, bf16[4,20,16,128]{3,2,1,0:T(8,128)(2,1)S(1)}, u32[]{:S(2)}, u32[]{:S(2)}) %collective-permute-start.3) | collective-permute-done | bytes 327712 | tf_op jit(solution)/shard_map/ppermute | solution.py:241
  33.2 1.0 %collective-permute-start.5 = (bf16[4,12,16,128]{3,2,1,0:T(8,128)(2,1)S(1)}, bf16[4,12,16,128]{3,2,1,0:T(8,128)(2,1)S(1)}, u32[]{:S(2)}, u32[]{:S(2)}) collective-permute-start(bf16[4,12,16,128]{3,2,1,0:T(8,128)(2,1)S(1)} %constant_dynamic-slice_fusion.5), channel_id=1, source_target_pairs={{0,1},{1,0},{2,3},{3,2},{4,5},{5,4},{6,7},{7,6},{8,9},{9,8},{10,11... | collective-permute-start | bytes 589832 | tf_op jit(solution)/shard_map/ppermute | solution.py:238
  34.1 0.0 collective-permute-done.7.other_ref
  34.1 0.8 %first_near.1.before_ref = f32[10,128,128]{2,1,0:T(8,128)S(1)} custom-call(bf16[4,20,16,128]{3,2,1,0:T(8,128)(2,1)S(1)} %collective-permute-done.6.kept_ref, bf16[4,12,16,128]{3,2,1,0:T(8,128)(2,1)S(1)} %collective-permute-done.7.other_ref, bf16[2,384,384]{2,1,0:T(8,128)(2,1)S(1)} %reshape.24.later_ref.weight_ref, ...), custom_call_target="tpu_custom_call" | custom-call | flops 377487360 | bytes 4000000 | tf_op jit(solution)/shard_map/first_near/pallas_call | solution.py:202
  34.9 0.3 collective-permute-done.5.other_ref
  35.2 0.8 %first_far.1.plane_ref = bf16[10,128,128]{2,1,0:T(8,128)(2,1)S(1)} custom-call(bf16[4,20,16,128]{3,2,1,0:T(8,128)(2,1)S(1)} %collective-permute-done.3.kept_ref, bf16[4,12,16,128]{3,2,1,0:T(8,128)(2,1)S(1)} %collective-permute-done.5.other_ref, bf16[2,384,384]{2,1,0:T(8,128)(2,1)S(1)} %reshape.24.later_ref.weight_ref, ...), custom_call_target="tpu_custom_call" | custom-call | flops 377487360 | bytes 4000000 | tf_op jit(solution)/shard_map/first_far/pallas_call | solution.py:202
  36.0 0.1 collective-permute-start.9
  36.1 0.3 collective-permute-start.8
  36.4 0.0 slice-start
  36.4 0.0 copy-start.1
  36.4 0.9 %slice-done = bf16[9,128,128]{2,1,0:T(8,128)(2,1)S(1)} async-done(((bf16[27,128,128]{2,1,0:T(8,128)(2,1)}), bf16[9,128,128]{2,1,0:T(8,128)(2,1)S(1)}, s32[]{:S(2)}) %slice-start) | async-done | bytes 294936 | tf_op jit(solution)/shard_map/slice | solution.py:172
  37.4 0.2 copy.18
  37.7 0.1 copy-done.1
  37.8 0.6 copy.21
  38.4 0.5 reshape.26.weight_ref
  38.9 0.0 copy-start.4
  38.9 0.6 %copy-done.4 = f32[128]{0:T(128)S(1)} copy-done((f32[128]{0:T(128)S(1)}, f32[128]{0:T(128)}, u32[]{:S(2)}) %copy-start.4) | copy-done | bytes 536
  39.6 0.1 copy.19.bias_ref
  39.7 0.7 %second_own.1.before_ref = f32[8,128,128]{2,1,0:T(8,128)S(1)} custom-call(bf16[10,128,128]{2,1,0:T(8,128)(2,1)S(1)} %first_far.1.plane_ref, bf16[384,384]{1,0:T(8,128)(2,1)S(1)} %bitcast.21), custom_call_target="tpu_custom_call" | custom-call | flops 301989888 | bytes 4000000 | tf_op jit(solution)/shard_map/second_own/pallas_call | solution.py:202
  40.4 4.6 %collective-permute-done.9.plane_ref = bf16[10,128,128]{2,1,0:T(8,128)(2,1)S(1)} collective-permute-done((bf16[10,128,128]{2,1,0:T(8,128)(2,1)S(1)}, bf16[10,128,128]{2,1,0:T(8,128)(2,1)S(1)}, u32[]{:S(2)}, u32[]{:S(2)}) %collective-permute-start.9) | collective-permute-done | bytes 327712 | tf_op jit(solution)/shard_map/ppermute | solution.py:241
  45.0 0.7 %second_near.1.before_ref = f32[8,128,128]{2,1,0:T(8,128)S(1)} custom-call(bf16[10,128,128]{2,1,0:T(8,128)(2,1)S(1)} %collective-permute-done.9.plane_ref, bf16[2,384,384]{2,1,0:T(8,128)(2,1)S(1)} %reshape.26.weight_ref, f32[8,128,128]{2,1,0:T(8,128)S(1)} %second_own.1.before_ref), custom_call_target="tpu_custom_call" | custom-call | flops 301989888 | bytes 4000000 | tf_op jit(solution)/shard_map/second_near/pallas_call | solution.py:202
  45.7 3.8 %collective-permute-done.8.plane_ref = bf16[10,128,128]{2,1,0:T(8,128)(2,1)S(1)} collective-permute-done((bf16[10,128,128]{2,1,0:T(8,128)(2,1)S(1)}, bf16[10,128,128]{2,1,0:T(8,128)(2,1)S(1)}, u32[]{:S(2)}, u32[]{:S(2)}) %collective-permute-start.8) | collective-permute-done | bytes 327712 | tf_op jit(solution)/shard_map/ppermute | solution.py:241
  49.5 0.7 %second_far.1 = (bf16[2,8,16,128]{3,2,1,0:T(8,128)(2,1)S(1)}, bf16[2,8,16,128]{3,2,1,0:T(8,128)(2,1)S(1)}, bf16[2,8,16,128]{3,2,1,0:T(8,128)(2,1)S(1)}, bf16[2,8,16,128]{3,2,1,0:T(8,128)(2,1)S(1)}) custom-call(bf16[10,128,128]{2,1,0:T(8,128)(2,1)S(1)} %collective-permute-done.8.plane_ref, bf16[2,384,384]{2,1,0:T(8,128)(2,1)S(1)} %reshape.26.weight_ref, ...), custom_call_target="tpu_custom_call" | custom-call | flops 301989888 | bytes 4000000 | tf_op jit(solution)/shard_map/second_far/pallas_call | solution.py:202
  50.2 1.8 %collective-permute-start.10 = (bf16[2,8,16,128]{3,2,1,0:T(8,128)(2,1)S(1)}, bf16[2,8,16,128]{3,2,1,0:T(8,128)(2,1)S(1)}, u32[]{:S(2)}, u32[]{:S(2)}) collective-permute-start(bf16[2,8,16,128]{3,2,1,0:T(8,128)(2,1)S(1)} %get-tuple-element.22), channel_id=1, source_target_pairs={{0,2},{1,3},{2,4},{3,5},{4,6},{5,7},{6,0},{7,1},{8,10},{9,11},{10,... | collective-permute-start | bytes 196616 | tf_op jit(solution)/shard_map/ppermute | solution.py:287
  52.0 3.5 %collective-permute-start.11 = (bf16[2,8,16,128]{3,2,1,0:T(8,128)(2,1)S(1)}, bf16[2,8,16,128]{3,2,1,0:T(8,128)(2,1)S(1)}, u32[]{:S(2)}, u32[]{:S(2)}) collective-permute-start(bf16[2,8,16,128]{3,2,1,0:T(8,128)(2,1)S(1)} %get-tuple-element.23), channel_id=1, source_target_pairs={{0,4},{1,5},{2,6},{3,7},{4,0},{5,1},{6,2},{7,3},{8,12},{9,13},{10,... | collective-permute-start | bytes 196616 | tf_op jit(solution)/shard_map/ppermute | solution.py:287
  55.5 2.8 %collective-permute-start.12 = (bf16[2,8,16,128]{3,2,1,0:T(8,128)(2,1)S(1)}, bf16[2,8,16,128]{3,2,1,0:T(8,128)(2,1)S(1)}, u32[]{:S(2)}, u32[]{:S(2)}) collective-permute-start(bf16[2,8,16,128]{3,2,1,0:T(8,128)(2,1)S(1)} %get-tuple-element.24), channel_id=1, source_target_pairs={{0,6},{1,7},{2,0},{3,1},{4,2},{5,3},{6,4},{7,5},{8,14},{9,15},{10,... | collective-permute-start | bytes 196616 | tf_op jit(solution)/shard_map/ppermute | solution.py:287
  58.4 0.0 collective-permute-done.10.refs_1_
  58.4 1.3 %collective-permute-done.11.refs_2_ = bf16[2,8,16,128]{3,2,1,0:T(8,128)(2,1)S(1)} collective-permute-done((bf16[2,8,16,128]{3,2,1,0:T(8,128)(2,1)S(1)}, bf16[2,8,16,128]{3,2,1,0:T(8,128)(2,1)S(1)}, u32[]{:S(2)}, u32[]{:S(2)}) %collective-permute-start.11) | collective-permute-done | bytes 65568 | tf_op jit(solution)/shard_map/ppermute | solution.py:287
  59.6 0.1 collective-permute-done.12.refs_3_
  59.7 2.8 %collective-permute-start.13 = (bf16[4,8,16,128]{3,2,1,0:T(8,128)(2,1)S(1)}, bf16[4,8,16,128]{3,2,1,0:T(8,128)(2,1)S(1)}, u32[]{:S(2)}, u32[]{:S(2)}) collective-permute-start(bf16[4,8,16,128]{3,2,1,0:T(8,128)(2,1)S(1)} %pad_maximum_fusion), channel_id=1, source_target_pairs={{0,1},{1,0},{2,3},{3,2},{4,5},{5,4},{6,7},{7,6},{8,9},{9,8},{10,11... | collective-permute-start | bytes 393224 | tf_op jit(solution)/shard_map/ppermute | solution.py:289
  62.6 1.0 %collective-permute-done.13.swapped_ref = bf16[4,8,16,128]{3,2,1,0:T(8,128)(2,1)S(1)} collective-permute-done((bf16[4,8,16,128]{3,2,1,0:T(8,128)(2,1)S(1)}, bf16[4,8,16,128]{3,2,1,0:T(8,128)(2,1)S(1)}, u32[]{:S(2)}, u32[]{:S(2)}) %collective-permute-start.13) | collective-permute-done | bytes 131104 | tf_op jit(solution)/shard_map/ppermute | solution.py:289
  63.6 0.8 %unpack_rows.1 = bf16[16,1,64,128]{3,2,1,0:T(8,128)(2,1)} custom-call(bf16[4,8,16,128]{3,2,1,0:T(8,128)(2,1)S(1)} %collective-permute-done.13.swapped_ref, bf16[2,8,16,128]{3,2,1,0:T(8,128)(2,1)S(1)} %get-tuple-element.21.refs_0_, bf16[2,8,16,128]{3,2,1,0:T(8,128)(2,1)S(1)} %collective-permute-done.10.refs_1_, ...), custom_call_target="tpu_custom_call" | custom-call | tf_op jit(solution)/shard_map/unpack_rows/pallas_call | solution.py:202
  (17 shorter events, 0.4 us)
Async XLA Ops:
  0.0 0.9 %copy-start = (bf16[16,1,64,128]{3,2,1,0:T(8,128)(2,1)S(1)}, bf16[16,1,64,128]{3,2,1,0:T(8,128)(2,1)}, u32[]{:S(2)}) copy-start(bf16[16,1,64,128]{3,2,1,0:T(8,128)(2,1)} %volume_ref.1) | copy-start | bytes 786436
  1.0 18.7 %copy-start.2 = (bf16[27,128,128]{2,1,0:T(8,128)(2,1)S(1)}, bf16[27,128,128]{2,1,0:T(8,128)(2,1)}, u32[]{:S(2)}) copy-start(bf16[27,128,128]{2,1,0:T(8,128)(2,1)} %param.6) | copy-start | bytes 2654212
  1.1 10.6 %collective-permute-start = (bf16[1,20,16,128]{3,2,1,0:T(8,128)(2,1)S(1)}, bf16[1,20,16,128]{3,2,1,0:T(8,128)(2,1)S(1)}, u32[]{:S(2)}, u32[]{:S(2)}) collective-permute-start(bf16[1,20,16,128]{3,2,1,0:T(8,128)(2,1)S(1)} %get-tuple-element.16), channel_id=1, source_target_pairs={{0,2},{1,3},{2,4},{3,5},{4,6},{5,7},{6,0},{7,1},{8,10},{9,11},{10,... | collective-permute-start | bytes 245768 | tf_op jit(solution)/shard_map/ppermute | solution.py:233
  4.2 10.3 %collective-permute-start.1 = (bf16[1,20,16,128]{3,2,1,0:T(8,128)(2,1)S(1)}, bf16[1,20,16,128]{3,2,1,0:T(8,128)(2,1)S(1)}, u32[]{:S(2)}, u32[]{:S(2)}) collective-permute-start(bf16[1,20,16,128]{3,2,1,0:T(8,128)(2,1)S(1)} %get-tuple-element.17), channel_id=1, source_target_pairs={{0,4},{1,5},{2,6},{3,7},{4,0},{5,1},{6,2},{7,3},{8,12},{9,13},{10,... | collective-permute-start | bytes 245768 | tf_op jit(solution)/shard_map/ppermute | solution.py:233
  9.3 8.9 %collective-permute-start.2 = (bf16[1,20,16,128]{3,2,1,0:T(8,128)(2,1)S(1)}, bf16[1,20,16,128]{3,2,1,0:T(8,128)(2,1)S(1)}, u32[]{:S(2)}, u32[]{:S(2)}) collective-permute-start(bf16[1,20,16,128]{3,2,1,0:T(8,128)(2,1)S(1)} %get-tuple-element.18), channel_id=1, source_target_pairs={{0,6},{1,7},{2,0},{3,1},{4,2},{5,3},{6,4},{7,5},{8,14},{9,15},{10,... | collective-permute-start | bytes 245768 | tf_op jit(solution)/shard_map/ppermute | solution.py:233
  18.2 8.9 %collective-permute-start.6 = (bf16[4,20,16,128]{3,2,1,0:T(8,128)(2,1)S(1)}, bf16[4,20,16,128]{3,2,1,0:T(8,128)(2,1)S(1)}, u32[]{:S(2)}, u32[]{:S(2)}) collective-permute-start(bf16[4,20,16,128]{3,2,1,0:T(8,128)(2,1)S(1)} %constant_dynamic-update-slice_fusion.kept_ref), channel_id=1, source_target_pairs={{0,8},{8,0},{16,24},{24,16},{32,40},{40,32},{48,56},{56,48},{64,72... | collective-permute-start | bytes 983048 | tf_op jit(solution)/shard_map/ppermute | solution.py:241
  18.8 4.8 %collective-permute-start.4 = (bf16[4,12,16,128]{3,2,1,0:T(8,128)(2,1)S(1)}, bf16[4,12,16,128]{3,2,1,0:T(8,128)(2,1)S(1)}, u32[]{:S(2)}, u32[]{:S(2)}) collective-permute-start(bf16[4,12,16,128]{3,2,1,0:T(8,128)(2,1)S(1)} %constant_dynamic-slice_fusion.6), channel_id=1, source_target_pairs={{0,1},{1,0},{2,3},{3,2},{4,5},{5,4},{6,7},{7,6},{8,9},{9,8},{10,11... | collective-permute-start | bytes 589832 | tf_op jit(solution)/shard_map/ppermute | solution.py:238
  19.6 13.5 %collective-permute-start.3 = (bf16[4,20,16,128]{3,2,1,0:T(8,128)(2,1)S(1)}, bf16[4,20,16,128]{3,2,1,0:T(8,128)(2,1)S(1)}, u32[]{:S(2)}, u32[]{:S(2)}) collective-permute-start(bf16[4,20,16,128]{3,2,1,0:T(8,128)(2,1)S(1)} %constant_dynamic-update-slice_fusion.kept_ref), channel_id=1, source_target_pairs={{0,1},{1,0},{2,3},{3,2},{4,5},{5,4},{6,7},{7,6},{8,16},{9,17},{10,... | collective-permute-start | bytes 983048 | tf_op jit(solution)/shard_map/ppermute | solution.py:241
  21.6 0.7 %copy-start.3 = (f32[128]{0:T(128)S(1)}, f32[128]{0:T(128)}, u32[]{:S(2)}) copy-start(f32[128]{0:T(128)} %param.7) | copy-start | bytes 1540
  27.1 7.0 %collective-permute-start.7 = (bf16[4,12,16,128]{3,2,1,0:T(8,128)(2,1)S(1)}, bf16[4,12,16,128]{3,2,1,0:T(8,128)(2,1)S(1)}, u32[]{:S(2)}, u32[]{:S(2)}) collective-permute-start(bf16[4,12,16,128]{3,2,1,0:T(8,128)(2,1)S(1)} %constant_dynamic-slice_fusion.4), channel_id=1, source_target_pairs={{0,1},{1,0},{2,3},{3,2},{4,5},{5,4},{6,7},{7,6},{8,9},{9,8},{10,11... | collective-permute-start | bytes 589832 | tf_op jit(solution)/shard_map/ppermute | solution.py:238
  33.2 2.0 %collective-permute-start.5 = (bf16[4,12,16,128]{3,2,1,0:T(8,128)(2,1)S(1)}, bf16[4,12,16,128]{3,2,1,0:T(8,128)(2,1)S(1)}, u32[]{:S(2)}, u32[]{:S(2)}) collective-permute-start(bf16[4,12,16,128]{3,2,1,0:T(8,128)(2,1)S(1)} %constant_dynamic-slice_fusion.5), channel_id=1, source_target_pairs={{0,1},{1,0},{2,3},{3,2},{4,5},{5,4},{6,7},{7,6},{8,9},{9,8},{10,11... | collective-permute-start | bytes 589832 | tf_op jit(solution)/shard_map/ppermute | solution.py:238
  36.0 9.0 %collective-permute-start.9 = (bf16[10,128,128]{2,1,0:T(8,128)(2,1)S(1)}, bf16[10,128,128]{2,1,0:T(8,128)(2,1)S(1)}, u32[]{:S(2)}, u32[]{:S(2)}) collective-permute-start(bf16[10,128,128]{2,1,0:T(8,128)(2,1)S(1)} %first_far.1.plane_ref), channel_id=1, source_target_pairs={{0,8},{8,0},{16,24},{24,16},{32,40},{40,32},{48,56},{56,48},{64,72... | collective-permute-start | bytes 983048 | tf_op jit(solution)/shard_map/ppermute | solution.py:241
  36.1 13.4 %collective-permute-start.8 = (bf16[10,128,128]{2,1,0:T(8,128)(2,1)S(1)}, bf16[10,128,128]{2,1,0:T(8,128)(2,1)S(1)}, u32[]{:S(2)}, u32[]{:S(2)}) collective-permute-start(bf16[10,128,128]{2,1,0:T(8,128)(2,1)S(1)} %first_far.1.plane_ref), channel_id=1, source_target_pairs={{0,1},{1,0},{2,3},{3,2},{4,5},{5,4},{6,7},{7,6},{8,16},{9,17},{10,... | collective-permute-start | bytes 983048 | tf_op jit(solution)/shard_map/ppermute | solution.py:241
  36.4 1.0 %slice-start = ((bf16[27,128,128]{2,1,0:T(8,128)(2,1)}), bf16[9,128,128]{2,1,0:T(8,128)(2,1)S(1)}, s32[]{:S(2)}) async-start(bf16[27,128,128]{2,1,0:T(8,128)(2,1)} %param.8), calls=%async_computation | async-start | bytes 589824 | tf_op jit(solution)/shard_map/slice | solution.py:172
  36.4 1.3 %copy-start.1 = (bf16[27,128,128]{2,1,0:T(8,128)(2,1)S(1)}, bf16[27,128,128]{2,1,0:T(8,128)(2,1)}, u32[]{:S(2)}) copy-start(bf16[27,128,128]{2,1,0:T(8,128)(2,1)} %param.8) | copy-start | bytes 2654212
  38.9 0.7 %copy-start.4 = (f32[128]{0:T(128)S(1)}, f32[128]{0:T(128)}, u32[]{:S(2)}) copy-start(f32[128]{0:T(128)} %param.9) | copy-start | bytes 1540
  50.2 8.1 %collective-permute-start.10 = (bf16[2,8,16,128]{3,2,1,0:T(8,128)(2,1)S(1)}, bf16[2,8,16,128]{3,2,1,0:T(8,128)(2,1)S(1)}, u32[]{:S(2)}, u32[]{:S(2)}) collective-permute-start(bf16[2,8,16,128]{3,2,1,0:T(8,128)(2,1)S(1)} %get-tuple-element.22), channel_id=1, source_target_pairs={{0,2},{1,3},{2,4},{3,5},{4,6},{5,7},{6,0},{7,1},{8,10},{9,11},{10,... | collective-permute-start | bytes 196616 | tf_op jit(solution)/shard_map/ppermute | solution.py:287
  52.0 7.6 %collective-permute-start.11 = (bf16[2,8,16,128]{3,2,1,0:T(8,128)(2,1)S(1)}, bf16[2,8,16,128]{3,2,1,0:T(8,128)(2,1)S(1)}, u32[]{:S(2)}, u32[]{:S(2)}) collective-permute-start(bf16[2,8,16,128]{3,2,1,0:T(8,128)(2,1)S(1)} %get-tuple-element.23), channel_id=1, source_target_pairs={{0,4},{1,5},{2,6},{3,7},{4,0},{5,1},{6,2},{7,3},{8,12},{9,13},{10,... | collective-permute-start | bytes 196616 | tf_op jit(solution)/shard_map/ppermute | solution.py:287
  55.5 4.2 %collective-permute-start.12 = (bf16[2,8,16,128]{3,2,1,0:T(8,128)(2,1)S(1)}, bf16[2,8,16,128]{3,2,1,0:T(8,128)(2,1)S(1)}, u32[]{:S(2)}, u32[]{:S(2)}) collective-permute-start(bf16[2,8,16,128]{3,2,1,0:T(8,128)(2,1)S(1)} %get-tuple-element.24), channel_id=1, source_target_pairs={{0,6},{1,7},{2,0},{3,1},{4,2},{5,3},{6,4},{7,5},{8,14},{9,15},{10,... | collective-permute-start | bytes 196616 | tf_op jit(solution)/shard_map/ppermute | solution.py:287
  59.7 3.8 %collective-permute-start.13 = (bf16[4,8,16,128]{3,2,1,0:T(8,128)(2,1)S(1)}, bf16[4,8,16,128]{3,2,1,0:T(8,128)(2,1)S(1)}, u32[]{:S(2)}, u32[]{:S(2)}) collective-permute-start(bf16[4,8,16,128]{3,2,1,0:T(8,128)(2,1)S(1)} %pad_maximum_fusion), channel_id=1, source_target_pairs={{0,1},{1,0},{2,3},{3,2},{4,5},{5,4},{6,7},{7,6},{8,9},{9,8},{10,11... | collective-permute-start | bytes 393224 | tf_op jit(solution)/shard_map/ppermute | solution.py:289

commit v8 on v7

--- a/solution.py
+++ b/solution.py
@@ -1,3 +1,5 @@
+import functools
+
 import jax
 import jax.numpy as jnp
 from jax import lax
@@ -105,7 +107,11 @@
     conv_rows(rows_of(plane_ref, False), 1, weight, store, rows, lanes)
 
 
-def first_own_kernel(kept_ref, other_ref, weight_ref, later_ref, bias_ref, out_ref, zero_ref, joined_ref):
+def ready_kernel(*refs):
+    refs[-1][...] = jnp.zeros_like(refs[-1])
+
+
+def first_own_kernel(kept_ref, other_ref, weight_ref, out_ref, zero_ref, joined_ref):
     gather_rows(kept_ref, other_ref, joined_ref)
     own_kernel(joined_ref, weight_ref, out_ref)
     zero_ref[...] = jnp.zeros_like(zero_ref)
@@ -134,44 +140,71 @@
     conv_rows(rows_of(joined_ref, True), 1, weight, store, rows, lanes)
 
 
-def second_kernel(plane_ref, weight_ref, before_ref, bias_ref, *refs):
+def second_own_kernel(plane_ref, weight_ref, out_ref):
+    rows, cores, _, lanes = out_ref.shape
+    for c in range(cores):
+
+        def store(row, value, c=c):
+            out_ref[row, c] = value
+
+        conv_rows(rows_of(plane_ref, False), 1, weight_ref[c], store, rows, lanes)
+
+
+def second_near_kernel(plane_ref, weight_ref, before_ref, out_ref):
+    rows, cores, _, lanes = out_ref.shape
+    side = 1 - lax.axis_index("space") % 2
+    for c in range(cores):
+
+        def store(row, value, c=c):
+            out_ref[row, c] = before_ref[row, c] + value
+
+        conv_rows(rows_of(plane_ref, False), 1, weight_ref[side, c], store, rows, lanes)
+
+
+def second_far_kernel(other, plane_ref, weight_ref, before_ref, bias_ref, *refs):
     outs, all_ref = refs[:-1], refs[-1]
-    groups, cores, rows, width, lanes = all_ref.shape
-    bias = bias_ref[...]
+    groups, rows, width, lanes = all_ref.shape
+    c = 1 - my_core() if other else my_core()
+    bias = bias_ref[c]
 
     def store(row, value):
-        value = jnp.maximum(value + before_ref[row] + bias, 0.0).astype(BF16)
+        value = jnp.maximum(value + before_ref[row, c] + bias, 0.0).astype(BF16)
         for g in range(groups):
-            for c in range(cores):
-                at = (g * cores + c) * width
-                all_ref[g, c, row] = value[at : at + width]
-
-    weight = weight_ref[lax.axis_index("space") % 2]
+            all_ref[g, row] = value[g * width : (g + 1) * width]
+
+    weight = weight_ref[lax.axis_index("space") % 2, c]
     conv_rows(rows_of(plane_ref, True), 1, weight, store, rows, lanes)
     for k in range(groups):
-        outs[k][...] = all_ref[lax.rem(my_group() + k, groups)]
-
-
-def unpack_kernel(swapped_ref, *refs):
+        target = lax.rem(my_group() + k, groups)
+        if other:
+            outs[0][k] = all_ref[target]
+        else:
+            outs[k][...] = all_ref[target]
+
+
+def unpack_kernel(*refs):
     blocks, out_ref, rows_ref = refs[:-2], refs[-2], refs[-1]
     groups = len(blocks)
     _, rows, width, lanes = blocks[0].shape
     group, core = my_group(), my_core()
     for k in range(groups):
         source = lax.rem(group + groups - k, groups) * CORES
-        rows_ref[source + core] = blocks[k][core]
-        rows_ref[source + 1 - core] = swapped_ref[k]
+        rows_ref[source + core] = blocks[k][0]
+        rows_ref[source + 1 - core] = blocks[k][1]
     length = groups * CORES * rows
     turned = rows_ref[...].reshape(length, width, lanes).astype(F32)
     out_ref[:, 0] = jnp.swapaxes(turned, 0, 1).astype(BF16)
 
 
-def arranged(weight):
+def arranged(weight, width=None):
     _, inner, outer = weight.shape
-    taps = weight.reshape(3, 3, 3, inner, outer)
-    own = taps[1].transpose(1, 3, 0, 2).reshape(3 * outer, 3 * inner)
-    beside = taps[::2].transpose(0, 2, 4, 1, 3).reshape(2, 3 * outer, 3 * inner)
-    return own, beside
+    taps = weight.reshape(3, 3, 3, inner, outer).transpose(0, 2, 4, 1, 3)
+    if width is None:
+        taps = taps.reshape(3, 3 * outer, 3 * inner)
+    else:
+        taps = taps.reshape(3, 3, -1, CORES, width, 3 * inner).transpose(0, 3, 1, 2, 4, 5)
+        taps = taps.reshape(3, CORES, 3 * outer // CORES, 3 * inner)
+    return taps[1], taps[::2]
 
 
 def cost(rows, planes, full, lanes):
@@ -217,7 +250,8 @@
         group, core = index // CORES, index % CORES
 
         own_one, beside_one = arranged(weight_one)
-        own_two, beside_two = arranged(weight_two)
+        own_two, beside_two = arranged(weight_two, width)
+        offsets_two = bias_two.reshape(groups, CORES, width).transpose(1, 0, 2).reshape(CORES, groups * width, 1)
 
         tall = CORES * rows + 2 * RIM
         pieces = call(
@@ -244,10 +278,12 @@
         joined = [pltpu.VMEM((rows + 2 * RIM, full, lanes), BF16)]
         work = cost(rows + RIM, 1, full, lanes)
         far_plane, near_plane = halo(kept)
+        zeros = jax.ShapeDtypeStruct((8, 128), jnp.int32)
+        zero = call(ready_kernel, zeros, [own_one, beside_one, bias_one[:, None]], name="ready")
         total, zero = call(
             first_own_kernel,
-            [partial, jax.ShapeDtypeStruct((8, 128), jnp.int32)],
-            [kept, from_other_core(kept, core), own_one, beside_one, bias_one[:, None]],
+            [partial, zeros],
+            [kept, from_other_core(kept, core + zero[0, 0]), own_one],
             joined,
             cost_estimate=work,
             name="first_own",
@@ -270,27 +306,35 @@
             name="first_far",
         )
 
-        partial = jax.ShapeDtypeStruct((rows, full, lanes), F32)
+        partial = jax.ShapeDtypeStruct((rows, CORES, groups * width, lanes), F32)
         work = cost(rows, 1, full, lanes)
         far_plane, near_plane = halo(hidden)
-        total = call(own_kernel, partial, [hidden, own_two], cost_estimate=work, name="second_own")
-        total = call(near_kernel, partial, [near_plane, beside_two, total], cost_estimate=work, name="second_near")
-        blocks = call(
-            second_kernel,
-            [jax.ShapeDtypeStruct((CORES, rows, width, lanes), BF16)] * groups,
-            [far_plane, beside_two, total, bias_two[:, None]],
-            [pltpu.VMEM((groups, CORES, rows, width, lanes), BF16)],
-            cost_estimate=work,
-            name="second_far",
-        )
-
+        total = call(second_own_kernel, partial, [hidden, own_two], cost_estimate=work, name="second_own")
+        total = call(
+            second_near_kernel, partial, [near_plane, beside_two, total], cost_estimate=work, name="second_near"
+        )
+        block = (rows, width, lanes)
+        ends = [
+            call(
+                functools.partial(second_far_kernel, other),
+                [jax.ShapeDtypeStruct(shape, BF16) for shape in shapes],
+                [far_plane, beside_two, total, offsets_two],
+                [pltpu.VMEM((groups, *block), BF16)],
+                cost_estimate=cost(rows // 2, 1, full, lanes),
+                name=name,
+            )
+            for other, shapes, name in (
+                (True, [(groups, *block)], "second_far_other"),
+                (False, [block] * groups, "second_far_own"),
+            )
+        ]
+        swapped = lax.ppermute(ends[0][0], "chan", swap)
+        blocks = [jnp.stack([ends[1][k], swapped[k]]) for k in range(groups)]
         blocks = [blocks[0]] + [lax.ppermute(blocks[k], "chan", ahead(k)) for k in range(1, groups)]
-        theirs = jnp.stack([lax.dynamic_index_in_dim(b, 1 - core, 0, keepdims=False) for b in blocks])
-        swapped = lax.ppermute(theirs, "chan", swap)
         return call(
             unpack_kernel,
             jax.ShapeDtypeStruct(volume.shape, BF16),
-            [swapped, *blocks],
+            blocks,
             [pltpu.VMEM((chan, rows, width, lanes), BF16)],
             name="unpack_rows",
         )

time: 65.5 us -> 68 us (1.038)
  the two profiles are of different devices: /device:TPU:31 before, /device:TPU:30 now
where the time goes in v8:
time: 68 us; the launch traced here: 67.7 us
  waiting for transfers between devices  26.8 us (39%)
  starting transfers between devices  23.1 us (34%)
  local copies, waits for them, and re-layouts  10.4 us (15%)
  Pallas kernels  5.72 us (8%)
  between operations  1.72 us (3%)
    ppermute x3, starting transfers between devices, per_device(): got = lax.ppermute(pieces[k], 'chan', ahead(k))  11.4 us
    ppermute x2, waiting for transfers between devices, halo(): lax.ppermute(array, ('space', 'chan'), far)  10.6 us
    ppermute x2, waiting for transfers between devices, halo(): lax.ppermute(array, 'space', near)  8.52 us
    ppermute x3, starting transfers between devices, per_device(): lax.ppermute(blocks[k], 'chan', ahead(k))  7.18 us
    ppermute x3, waiting for transfers between devices, per_device(): lax.ppermute(blocks[k], 'chan', ahead(k))  6.22 us
    pallas_call x10, Pallas kernels, call(): pl.pallas_call(kernel, out_shape=shapes, in_specs=[VMEM] * len(inputs), o...  5.72 us
    reshape x2, local copies, waits for them, and re-layouts, arranged(): taps = weight.reshape(3, 3, 3, inner, outer).transpose(0, 2, 4, 1, 3)  4.86 us
    ppermute x2, starting transfers between devices, halo(): lax.ppermute(array, ('space', 'chan'), far)  3.02 us
  transfers between devices with their start and end apart: 14, of which 7 were waited for; matrix products, arithmetic and copies ran while one was open for 13% of the time, Pallas kernels for 5%

profile of v8, /device:TPU:30, one launch (start us, length us, event | category | flops | bytes accessed | tf_op | source)
XLA Modules:
  0.0 67.7 jit_solution(9567677811473813966)
XLA Ops:
  0.0 0.0 copy-start
  0.0 0.9 %copy-done = bf16[16,1,64,128]{3,2,1,0:T(8,128)(2,1)S(1)} copy-done((bf16[16,1,64,128]{3,2,1,0:T(8,128)(2,1)S(1)}, bf16[16,1,64,128]{3,2,1,0:T(8,128)(2,1)}, u32[]{:S(2)}) %copy-start) | copy-done | bytes 262168
  1.0 0.2 pack_rows.1
  1.1 3.3 %collective-permute-start = (bf16[1,20,16,128]{3,2,1,0:T(8,128)(2,1)S(1)}, bf16[1,20,16,128]{3,2,1,0:T(8,128)(2,1)S(1)}, u32[]{:S(2)}, u32[]{:S(2)}) collective-permute-start(bf16[1,20,16,128]{3,2,1,0:T(8,128)(2,1)S(1)} %get-tuple-element.16), channel_id=1, source_target_pairs={{0,2},{1,3},{2,4},{3,5},{4,6},{5,7},{6,0},{7,1},{8,10},{9,11},{10,... | collective-permute-start | bytes 245768 | tf_op jit(solution)/shard_map/ppermute | solution.py:267
  4.5 5.4 %collective-permute-start.1 = (bf16[1,20,16,128]{3,2,1,0:T(8,128)(2,1)S(1)}, bf16[1,20,16,128]{3,2,1,0:T(8,128)(2,1)S(1)}, u32[]{:S(2)}, u32[]{:S(2)}) collective-permute-start(bf16[1,20,16,128]{3,2,1,0:T(8,128)(2,1)S(1)} %get-tuple-element.17), channel_id=1, source_target_pairs={{0,4},{1,5},{2,6},{3,7},{4,0},{5,1},{6,2},{7,3},{8,12},{9,13},{10,... | collective-permute-start | bytes 245768 | tf_op jit(solution)/shard_map/ppermute | solution.py:267
  9.9 2.7 %collective-permute-start.2 = (bf16[1,20,16,128]{3,2,1,0:T(8,128)(2,1)S(1)}, bf16[1,20,16,128]{3,2,1,0:T(8,128)(2,1)S(1)}, u32[]{:S(2)}, u32[]{:S(2)}) collective-permute-start(bf16[1,20,16,128]{3,2,1,0:T(8,128)(2,1)S(1)} %get-tuple-element.18), channel_id=1, source_target_pairs={{0,6},{1,7},{2,0},{3,1},{4,2},{5,3},{6,4},{7,5},{8,14},{9,15},{10,... | collective-permute-start | bytes 245768 | tf_op jit(solution)/shard_map/ppermute | solution.py:267
  12.5 2.4 %copy.12 = bf16[3,3,3,128,128]{3,1,4,2,0:T(4,128)(2,1)S(1)} copy(bf16[3,3,3,128,128]{4,3,2,1,0:T(8,128)(2,1)} %bitcast.34) | data formatting | bytes 1769472 | tf_op jit(solution)/shard_map/reshape | solution.py:201
  15.0 0.8 %reshape.26 = bf16[3,384,384]{2,1,0:T(8,128)(2,1)S(1)} reshape(bf16[3,3,128,3,128]{4,3,2,1,0:T(4,128)(2,1)S(1)} %bitcast.27) | data formatting | bytes 1769472 | tf_op jit(solution)/shard_map/reshape | solution.py:203
  15.8 0.1 slice.42
  15.9 0.0 copy-start.1
  16.0 0.1 slice.33.refs_1_.weight_ref
  16.1 0.4 copy-done.1
  16.6 0.1 copy.13.refs_2_.bias_ref
  16.7 0.5 slice.34
  18.0 0.0 collective-permute-done
  18.0 0.0 collective-permute-done.1
  18.0 0.0 collective-permute-done.2
  18.1 0.8 %collective-permute-start.6 = (bf16[4,20,16,128]{3,2,1,0:T(8,128)(2,1)S(1)}, bf16[4,20,16,128]{3,2,1,0:T(8,128)(2,1)S(1)}, u32[]{:S(2)}, u32[]{:S(2)}) collective-permute-start(bf16[4,20,16,128]{3,2,1,0:T(8,128)(2,1)S(1)} %constant_dynamic-update-slice_fusion.kept_ref), channel_id=1, source_target_pairs={{0,8},{8,0},{16,24},{24,16},{32,40},{40,32},{48,56},{56,48},{64,72... | collective-permute-start | bytes 983048 | tf_op jit(solution)/shard_map/ppermute | solution.py:275
  18.9 0.1 collective-permute-start.4
  19.0 1.5 %collective-permute-start.3 = (bf16[4,20,16,128]{3,2,1,0:T(8,128)(2,1)S(1)}, bf16[4,20,16,128]{3,2,1,0:T(8,128)(2,1)S(1)}, u32[]{:S(2)}, u32[]{:S(2)}) collective-permute-start(bf16[4,20,16,128]{3,2,1,0:T(8,128)(2,1)S(1)} %constant_dynamic-update-slice_fusion.kept_ref), channel_id=1, source_target_pairs={{0,1},{1,0},{2,3},{3,2},{4,5},{5,4},{6,7},{7,6},{8,16},{9,17},{10,... | collective-permute-start | bytes 983048 | tf_op jit(solution)/shard_map/ppermute | solution.py:275
  20.5 0.0 collective-permute-done.4.other_ref
  20.5 0.8 %first_own.1 = (f32[10,128,128]{2,1,0:T(8,128)S(1)}, s32[8,128]{1,0:T(8,128)S(1)}) custom-call(bf16[4,20,16,128]{3,2,1,0:T(8,128)(2,1)S(1)} %constant_dynamic-update-slice_fusion.kept_ref, bf16[4,12,16,128]{3,2,1,0:T(8,128)(2,1)S(1)} %collective-permute-done.4.other_ref, bf16[384,384]{1,0:T(8,128)(2,1)S(1)} %bitcast.22), custom_call_target="tpu_custom_call" | custom-call | flops 377487360 | bytes 4000000 | tf_op jit(solution)/shard_map/first_own/pallas_call | solution.py:235
  21.3 0.5 slice.35
  22.5 5.2 %collective-permute-done.6.kept_ref = bf16[4,20,16,128]{3,2,1,0:T(8,128)(2,1)S(1)} collective-permute-done((bf16[4,20,16,128]{3,2,1,0:T(8,128)(2,1)S(1)}, bf16[4,20,16,128]{3,2,1,0:T(8,128)(2,1)S(1)}, u32[]{:S(2)}, u32[]{:S(2)}) %collective-permute-start.6) | collective-permute-done | bytes 327712 | tf_op jit(solution)/shard_map/ppermute | solution.py:275
  27.8 0.1 collective-permute-start.7
  27.9 5.5 %collective-permute-done.3.kept_ref = bf16[4,20,16,128]{3,2,1,0:T(8,128)(2,1)S(1)} collective-permute-done((bf16[4,20,16,128]{3,2,1,0:T(8,128)(2,1)S(1)}, bf16[4,20,16,128]{3,2,1,0:T(8,128)(2,1)S(1)}, u32[]{:S(2)}, u32[]{:S(2)}) %collective-permute-start.3) | collective-permute-done | bytes 327712 | tf_op jit(solution)/shard_map/ppermute | solution.py:275
  33.4 0.1 collective-permute-start.5
  33.5 0.0 collective-permute-done.7.other_ref
  33.5 0.8 %first_near.1.before_ref = f32[10,128,128]{2,1,0:T(8,128)S(1)} custom-call(bf16[4,20,16,128]{3,2,1,0:T(8,128)(2,1)S(1)} %collective-permute-done.6.kept_ref, bf16[4,12,16,128]{3,2,1,0:T(8,128)(2,1)S(1)} %collective-permute-done.7.other_ref, bf16[2,384,384]{2,1,0:T(8,128)(2,1)S(1)} %slice.33.refs_1_.weight_ref, f32[10,128,128]{2,1,0:T(8,128)S(1)} %get-tuple-element.20.before_ref), custom_call_target="tpu_custom_call" | custom-call | flops 377487360 | bytes 4000000 | tf_op jit(solution)/shard_map/first_near/pallas_call | solution.py:235
  34.3 0.6 collective-permute-done.5.other_ref
  34.9 0.8 %first_far.1.plane_ref = bf16[10,128,128]{2,1,0:T(8,128)(2,1)S(1)} custom-call(bf16[4,20,16,128]{3,2,1,0:T(8,128)(2,1)S(1)} %collective-permute-done.3.kept_ref, bf16[4,12,16,128]{3,2,1,0:T(8,128)(2,1)S(1)} %collective-permute-done.5.other_ref, bf16[2,384,384]{2,1,0:T(8,128)(2,1)S(1)} %slice.33.refs_1_.weight_ref, f32[10,128,128]{2,1,0:T(8,128)S(1)} %first_near.1.before_ref, ...), custom_call_target="tpu_custom_call" | custom-call | flops 377487360 | bytes 4000000 | tf_op jit(solution)/shard_map/first_far/pallas_call | solution.py:235
  35.7 0.1 collective-permute-start.9
  35.8 1.5 %collective-permute-start.8 = (bf16[10,128,128]{2,1,0:T(8,128)(2,1)S(1)}, bf16[10,128,128]{2,1,0:T(8,128)(2,1)S(1)}, u32[]{:S(2)}, u32[]{:S(2)}) collective-permute-start(bf16[10,128,128]{2,1,0:T(8,128)(2,1)S(1)} %first_far.1.plane_ref), channel_id=1, source_target_pairs={{0,1},{1,0},{2,3},{3,2},{4,5},{5,4},{6,7},{7,6},{8,16},{9,17},{10,... | collective-permute-start | bytes 983048 | tf_op jit(solution)/shard_map/ppermute | solution.py:275
  37.4 2.4 %copy.15 = bf16[3,3,3,128,128]{3,1,4,2,0:T(4,128)(2,1)S(1)} copy(bf16[3,3,3,128,128]{4,3,2,1,0:T(8,128)(2,1)} %bitcast.35) | data formatting | bytes 1769472 | tf_op jit(solution)/shard_map/reshape | solution.py:201
  39.8 0.8 %reshape.28 = bf16[3,3,4,2,16,384]{5,4,3,2,1,0:T(8,128)(2,1)S(1)} reshape(bf16[3,3,128,3,128]{4,3,2,1,0:T(4,128)(2,1)S(1)} %bitcast.31) | data formatting | bytes 1769472 | tf_op jit(solution)/shard_map/reshape | solution.py:205
  40.6 0.1 copy.16
  40.8 0.0 copy-start.2
  40.8 0.1 slice.36.weight_ref
  40.9 0.5 copy-done.2
  41.4 0.1 reshape.30
  41.5 0.1 reshape.32.bias_ref
  41.6 0.7 second_own.1.before_ref
  42.3 3.3 %collective-permute-done.9.plane_ref = bf16[10,128,128]{2,1,0:T(8,128)(2,1)S(1)} collective-permute-done((bf16[10,128,128]{2,1,0:T(8,128)(2,1)S(1)}, bf16[10,128,128]{2,1,0:T(8,128)(2,1)S(1)}, u32[]{:S(2)}, u32[]{:S(2)}) %collective-permute-start.9) | collective-permute-done | bytes 327712 | tf_op jit(solution)/shard_map/ppermute | solution.py:275
  45.6 0.7 second_near.1.before_ref
  46.2 5.1 %collective-permute-done.8.plane_ref = bf16[10,128,128]{2,1,0:T(8,128)(2,1)S(1)} collective-permute-done((bf16[10,128,128]{2,1,0:T(8,128)(2,1)S(1)}, bf16[10,128,128]{2,1,0:T(8,128)(2,1)S(1)}, u32[]{:S(2)}, u32[]{:S(2)}) %collective-permute-start.8) | collective-permute-done | bytes 327712 | tf_op jit(solution)/shard_map/ppermute | solution.py:275
  51.3 0.5 second_far_other.1
  51.8 0.3 collective-permute-start.10
  52.1 0.5 second_far_own.1
  52.6 0.8 %collective-permute-done.10 = bf16[4,8,16,128]{3,2,1,0:T(8,128)(2,1)S(1)} collective-permute-done((bf16[4,8,16,128]{3,2,1,0:T(8,128)(2,1)S(1)}, bf16[4,8,16,128]{3,2,1,0:T(8,128)(2,1)S(1)}, u32[]{:S(2)}, u32[]{:S(2)}) %collective-permute-start.10) | collective-permute-done | bytes 131104 | tf_op jit(solution)/shard_map/ppermute | solution.py:331
  53.4 3.5 %collective-permute-start.13 = (bf16[2,8,16,128]{3,2,1,0:T(8,128)(2,1)S(1)}, bf16[2,8,16,128]{3,2,1,0:T(8,128)(2,1)S(1)}, u32[]{:S(2)}, u32[]{:S(2)}) collective-permute-start(bf16[2,8,16,128]{3,2,1,0:T(8,128)(2,1)S(1)} %pad_maximum_fusion.3), channel_id=1, source_target_pairs={{0,6},{1,7},{2,0},{3,1},{4,2},{5,3},{6,4},{7,5},{8,14},{9,15},{10,... | collective-permute-start | bytes 196616 | tf_op jit(solution)/shard_map/ppermute | solution.py:333
  56.9 2.2 %collective-permute-start.12 = (bf16[2,8,16,128]{3,2,1,0:T(8,128)(2,1)S(1)}, bf16[2,8,16,128]{3,2,1,0:T(8,128)(2,1)S(1)}, u32[]{:S(2)}, u32[]{:S(2)}) collective-permute-start(bf16[2,8,16,128]{3,2,1,0:T(8,128)(2,1)S(1)} %pad_maximum_fusion.2), channel_id=1, source_target_pairs={{0,4},{1,5},{2,6},{3,7},{4,0},{5,1},{6,2},{7,3},{8,12},{9,13},{10,... | collective-permute-start | bytes 196616 | tf_op jit(solution)/shard_map/ppermute | solution.py:333
  59.1 1.5 %collective-permute-start.11 = (bf16[2,8,16,128]{3,2,1,0:T(8,128)(2,1)S(1)}, bf16[2,8,16,128]{3,2,1,0:T(8,128)(2,1)S(1)}, u32[]{:S(2)}, u32[]{:S(2)}) collective-permute-start(bf16[2,8,16,128]{3,2,1,0:T(8,128)(2,1)S(1)} %pad_maximum_fusion.1), channel_id=1, source_target_pairs={{0,2},{1,3},{2,4},{3,5},{4,6},{5,7},{6,0},{7,1},{8,10},{9,11},{10,... | collective-permute-start | bytes 196616 | tf_op jit(solution)/shard_map/ppermute | solution.py:333
  60.6 0.0 collective-permute-done.13.refs_3_
  60.6 6.2 %collective-permute-done.12.refs_2_ = bf16[2,8,16,128]{3,2,1,0:T(8,128)(2,1)S(1)} collective-permute-done((bf16[2,8,16,128]{3,2,1,0:T(8,128)(2,1)S(1)}, bf16[2,8,16,128]{3,2,1,0:T(8,128)(2,1)S(1)}, u32[]{:S(2)}, u32[]{:S(2)}) %collective-permute-start.12) | collective-permute-done | bytes 65568 | tf_op jit(solution)/shard_map/ppermute | solution.py:333
  66.9 0.0 collective-permute-done.11.refs_1_
  66.9 0.9 %unpack_rows.1 = bf16[16,1,64,128]{3,2,1,0:T(8,128)(2,1)} custom-call(bf16[2,8,16,128]{3,2,1,0:T(8,128)(2,1)S(1)} %pad_maximum_fusion.refs_0_, bf16[2,8,16,128]{3,2,1,0:T(8,128)(2,1)S(1)} %collective-permute-done.11.refs_1_, bf16[2,8,16,128]{3,2,1,0:T(8,128)(2,1)S(1)} %collective-permute-done.12.refs_2_, ...), custom_call_target="tpu_custom_call" | custom-call | tf_op jit(solution)/shard_map/unpack_rows/pallas_call | solution.py:235
  (18 shorter events, 0.3 us)
Async XLA Ops:
  0.0 0.9 %copy-start = (bf16[16,1,64,128]{3,2,1,0:T(8,128)(2,1)S(1)}, bf16[16,1,64,128]{3,2,1,0:T(8,128)(2,1)}, u32[]{:S(2)}) copy-start(bf16[16,1,64,128]{3,2,1,0:T(8,128)(2,1)} %volume_ref.1) | copy-start | bytes 786436
  1.1 16.8 %collective-permute-start = (bf16[1,20,16,128]{3,2,1,0:T(8,128)(2,1)S(1)}, bf16[1,20,16,128]{3,2,1,0:T(8,128)(2,1)S(1)}, u32[]{:S(2)}, u32[]{:S(2)}) collective-permute-start(bf16[1,20,16,128]{3,2,1,0:T(8,128)(2,1)S(1)} %get-tuple-element.16), channel_id=1, source_target_pairs={{0,2},{1,3},{2,4},{3,5},{4,6},{5,7},{6,0},{7,1},{8,10},{9,11},{10,... | collective-permute-start | bytes 245768 | tf_op jit(solution)/shard_map/ppermute | solution.py:267
  4.5 13.5 %collective-permute-start.1 = (bf16[1,20,16,128]{3,2,1,0:T(8,128)(2,1)S(1)}, bf16[1,20,16,128]{3,2,1,0:T(8,128)(2,1)S(1)}, u32[]{:S(2)}, u32[]{:S(2)}) collective-permute-start(bf16[1,20,16,128]{3,2,1,0:T(8,128)(2,1)S(1)} %get-tuple-element.17), channel_id=1, source_target_pairs={{0,4},{1,5},{2,6},{3,7},{4,0},{5,1},{6,2},{7,3},{8,12},{9,13},{10,... | collective-permute-start | bytes 245768 | tf_op jit(solution)/shard_map/ppermute | solution.py:267
  9.9 8.2 %collective-permute-start.2 = (bf16[1,20,16,128]{3,2,1,0:T(8,128)(2,1)S(1)}, bf16[1,20,16,128]{3,2,1,0:T(8,128)(2,1)S(1)}, u32[]{:S(2)}, u32[]{:S(2)}) collective-permute-start(bf16[1,20,16,128]{3,2,1,0:T(8,128)(2,1)S(1)} %get-tuple-element.18), channel_id=1, source_target_pairs={{0,6},{1,7},{2,0},{3,1},{4,2},{5,3},{6,4},{7,5},{8,14},{9,15},{10,... | collective-permute-start | bytes 245768 | tf_op jit(solution)/shard_map/ppermute | solution.py:267
  15.9 0.7 copy-start.1
  18.1 9.7 %collective-permute-start.6 = (bf16[4,20,16,128]{3,2,1,0:T(8,128)(2,1)S(1)}, bf16[4,20,16,128]{3,2,1,0:T(8,128)(2,1)S(1)}, u32[]{:S(2)}, u32[]{:S(2)}) collective-permute-start(bf16[4,20,16,128]{3,2,1,0:T(8,128)(2,1)S(1)} %constant_dynamic-update-slice_fusion.kept_ref), channel_id=1, source_target_pairs={{0,8},{8,0},{16,24},{24,16},{32,40},{40,32},{48,56},{56,48},{64,72... | collective-permute-start | bytes 983048 | tf_op jit(solution)/shard_map/ppermute | solution.py:275
  18.9 1.6 %collective-permute-start.4 = (bf16[4,12,16,128]{3,2,1,0:T(8,128)(2,1)S(1)}, bf16[4,12,16,128]{3,2,1,0:T(8,128)(2,1)S(1)}, u32[]{:S(2)}, u32[]{:S(2)}) collective-permute-start(bf16[4,12,16,128]{3,2,1,0:T(8,128)(2,1)S(1)} %constant_dynamic-slice_fusion.2), channel_id=1, source_target_pairs={{0,1},{1,0},{2,3},{3,2},{4,5},{5,4},{6,7},{7,6},{8,9},{9,8},{10,11... | collective-permute-start | bytes 589832 | tf_op jit(solution)/shard_map/ppermute | solution.py:272
  19.0 14.4 %collective-permute-start.3 = (bf16[4,20,16,128]{3,2,1,0:T(8,128)(2,1)S(1)}, bf16[4,20,16,128]{3,2,1,0:T(8,128)(2,1)S(1)}, u32[]{:S(2)}, u32[]{:S(2)}) collective-permute-start(bf16[4,20,16,128]{3,2,1,0:T(8,128)(2,1)S(1)} %constant_dynamic-update-slice_fusion.kept_ref), channel_id=1, source_target_pairs={{0,1},{1,0},{2,3},{3,2},{4,5},{5,4},{6,7},{7,6},{8,16},{9,17},{10,... | collective-permute-start | bytes 983048 | tf_op jit(solution)/shard_map/ppermute | solution.py:275
  27.8 5.7 %collective-permute-start.7 = (bf16[4,12,16,128]{3,2,1,0:T(8,128)(2,1)S(1)}, bf16[4,12,16,128]{3,2,1,0:T(8,128)(2,1)S(1)}, u32[]{:S(2)}, u32[]{:S(2)}) collective-permute-start(bf16[4,12,16,128]{3,2,1,0:T(8,128)(2,1)S(1)} %constant_dynamic-slice_fusion), channel_id=1, source_target_pairs={{0,1},{1,0},{2,3},{3,2},{4,5},{5,4},{6,7},{7,6},{8,9},{9,8},{10,11... | collective-permute-start | bytes 589832 | tf_op jit(solution)/shard_map/ppermute | solution.py:272
  33.4 1.5 %collective-permute-start.5 = (bf16[4,12,16,128]{3,2,1,0:T(8,128)(2,1)S(1)}, bf16[4,12,16,128]{3,2,1,0:T(8,128)(2,1)S(1)}, u32[]{:S(2)}, u32[]{:S(2)}) collective-permute-start(bf16[4,12,16,128]{3,2,1,0:T(8,128)(2,1)S(1)} %constant_dynamic-slice_fusion.1), channel_id=1, source_target_pairs={{0,1},{1,0},{2,3},{3,2},{4,5},{5,4},{6,7},{7,6},{8,9},{9,8},{10,11... | collective-permute-start | bytes 589832 | tf_op jit(solution)/shard_map/ppermute | solution.py:272
  35.7 9.8 %collective-permute-start.9 = (bf16[10,128,128]{2,1,0:T(8,128)(2,1)S(1)}, bf16[10,128,128]{2,1,0:T(8,128)(2,1)S(1)}, u32[]{:S(2)}, u32[]{:S(2)}) collective-permute-start(bf16[10,128,128]{2,1,0:T(8,128)(2,1)S(1)} %first_far.1.plane_ref), channel_id=1, source_target_pairs={{0,8},{8,0},{16,24},{24,16},{32,40},{40,32},{48,56},{56,48},{64,72... | collective-permute-start | bytes 983048 | tf_op jit(solution)/shard_map/ppermute | solution.py:275
  35.8 15.5 %collective-permute-start.8 = (bf16[10,128,128]{2,1,0:T(8,128)(2,1)S(1)}, bf16[10,128,128]{2,1,0:T(8,128)(2,1)S(1)}, u32[]{:S(2)}, u32[]{:S(2)}) collective-permute-start(bf16[10,128,128]{2,1,0:T(8,128)(2,1)S(1)} %first_far.1.plane_ref), channel_id=1, source_target_pairs={{0,1},{1,0},{2,3},{3,2},{4,5},{5,4},{6,7},{7,6},{8,16},{9,17},{10,... | collective-permute-start | bytes 983048 | tf_op jit(solution)/shard_map/ppermute | solution.py:275
  40.8 0.7 copy-start.2
  51.8 1.6 %collective-permute-start.10 = (bf16[4,8,16,128]{3,2,1,0:T(8,128)(2,1)S(1)}, bf16[4,8,16,128]{3,2,1,0:T(8,128)(2,1)S(1)}, u32[]{:S(2)}, u32[]{:S(2)}) collective-permute-start(bf16[4,8,16,128]{3,2,1,0:T(8,128)(2,1)S(1)} %second_far_other.1), channel_id=1, source_target_pairs={{0,1},{1,0},{2,3},{3,2},{4,5},{5,4},{6,7},{7,6},{8,9},{9,8},{10,11... | collective-permute-start | bytes 393224 | tf_op jit(solution)/shard_map/ppermute | solution.py:331
  53.4 7.2 %collective-permute-start.13 = (bf16[2,8,16,128]{3,2,1,0:T(8,128)(2,1)S(1)}, bf16[2,8,16,128]{3,2,1,0:T(8,128)(2,1)S(1)}, u32[]{:S(2)}, u32[]{:S(2)}) collective-permute-start(bf16[2,8,16,128]{3,2,1,0:T(8,128)(2,1)S(1)} %pad_maximum_fusion.3), channel_id=1, source_target_pairs={{0,6},{1,7},{2,0},{3,1},{4,2},{5,3},{6,4},{7,5},{8,14},{9,15},{10,... | collective-permute-start | bytes 196616 | tf_op jit(solution)/shard_map/ppermute | solution.py:333
  56.9 10.0 %collective-permute-start.12 = (bf16[2,8,16,128]{3,2,1,0:T(8,128)(2,1)S(1)}, bf16[2,8,16,128]{3,2,1,0:T(8,128)(2,1)S(1)}, u32[]{:S(2)}, u32[]{:S(2)}) collective-permute-start(bf16[2,8,16,128]{3,2,1,0:T(8,128)(2,1)S(1)} %pad_maximum_fusion.2), channel_id=1, source_target_pairs={{0,4},{1,5},{2,6},{3,7},{4,0},{5,1},{6,2},{7,3},{8,12},{9,13},{10,... | collective-permute-start | bytes 196616 | tf_op jit(solution)/shard_map/ppermute | solution.py:333
  59.1 7.7 %collective-permute-start.11 = (bf16[2,8,16,128]{3,2,1,0:T(8,128)(2,1)S(1)}, bf16[2,8,16,128]{3,2,1,0:T(8,128)(2,1)S(1)}, u32[]{:S(2)}, u32[]{:S(2)}) collective-permute-start(bf16[2,8,16,128]{3,2,1,0:T(8,128)(2,1)S(1)} %pad_maximum_fusion.1), channel_id=1, source_target_pairs={{0,2},{1,3},{2,4},{3,5},{4,6},{5,7},{6,0},{7,1},{8,10},{9,11},{10,... | collective-permute-start | bytes 196616 | tf_op jit(solution)/shard_map/ppermute | solution.py:333

commit v9 on v7

--- a/solution.py
+++ b/solution.py
@@ -1,3 +1,5 @@
+import functools
+
 import jax
 import jax.numpy as jnp
 from jax import lax
@@ -9,6 +11,8 @@
 F32 = jnp.float32
 CORES = 2
 RIM = 2
+FIRST = True
+SECOND = True
 PARAMS = pltpu.CompilerParams(vmem_limit_bytes=24 * 1024 * 1024)
 VMEM = pl.BlockSpec(memory_space=pltpu.VMEM)
 
@@ -86,6 +90,11 @@
     return get
 
 
+def side_of(far):
+    odd = lax.axis_index("space") % 2
+    return odd if far else 1 - odd
+
+
 def own_kernel(plane_ref, weight_ref, out_ref):
     rows, _, lanes = out_ref.shape
 
@@ -95,14 +104,13 @@
     conv_rows(rows_of(plane_ref, False), 1, weight_ref[...], store, rows, lanes)
 
 
-def near_kernel(plane_ref, weight_ref, before_ref, out_ref):
+def add_kernel(far, plane_ref, weight_ref, before_ref, out_ref):
     rows, _, lanes = out_ref.shape
 
     def store(row, value):
         out_ref[row] = before_ref[row] + value
 
-    weight = weight_ref[1 - lax.axis_index("space") % 2]
-    conv_rows(rows_of(plane_ref, False), 1, weight, store, rows, lanes)
+    conv_rows(rows_of(plane_ref, far), 1, weight_ref[side_of(far)], store, rows, lanes)
 
 
 def first_own_kernel(kept_ref, other_ref, weight_ref, later_ref, bias_ref, out_ref, zero_ref, joined_ref):
@@ -111,12 +119,12 @@
     zero_ref[...] = jnp.zeros_like(zero_ref)
 
 
-def first_near_kernel(kept_ref, other_ref, weight_ref, before_ref, out_ref, joined_ref):
+def first_add_kernel(far, kept_ref, other_ref, weight_ref, before_ref, out_ref, joined_ref):
     gather_rows(kept_ref, other_ref, joined_ref)
-    near_kernel(joined_ref, weight_ref, before_ref, out_ref)
-
-
-def first_far_kernel(kept_ref, other_ref, weight_ref, before_ref, bias_ref, out_ref, joined_ref):
+    add_kernel(far, joined_ref, weight_ref, before_ref, out_ref)
+
+
+def first_kernel(far, kept_ref, other_ref, weight_ref, before_ref, bias_ref, out_ref, joined_ref):
     gather_rows(kept_ref, other_ref, joined_ref)
     rows, _, lanes = out_ref.shape
     block = lax.axis_index("chan")
@@ -130,11 +138,10 @@
             value = jnp.where(block == lax.axis_size("chan") - 1, 0.0, value)
         out_ref[row] = value.astype(BF16)
 
-    weight = weight_ref[lax.axis_index("space") % 2]
-    conv_rows(rows_of(joined_ref, True), 1, weight, store, rows, lanes)
-
-
-def second_kernel(plane_ref, weight_ref, before_ref, bias_ref, *refs):
+    conv_rows(rows_of(joined_ref, far), 1, weight_ref[side_of(far)], store, rows, lanes)
+
+
+def second_kernel(far, plane_ref, weight_ref, before_ref, bias_ref, *refs):
     outs, all_ref = refs[:-1], refs[-1]
     groups, cores, rows, width, lanes = all_ref.shape
     bias = bias_ref[...]
@@ -146,8 +153,7 @@
                 at = (g * cores + c) * width
                 all_ref[g, c, row] = value[at : at + width]
 
-    weight = weight_ref[lax.axis_index("space") % 2]
-    conv_rows(rows_of(plane_ref, True), 1, weight, store, rows, lanes)
+    conv_rows(rows_of(plane_ref, far), 1, weight_ref[side_of(far)], store, rows, lanes)
     for k in range(groups):
         outs[k][...] = all_ref[lax.rem(my_group() + k, groups)]
 
@@ -237,13 +243,15 @@
             sent = lax.dynamic_slice_in_dim(array, (1 - core) * rows, rows + 2 * RIM, 1)
             return lax.ppermute(sent, "chan", swap)
 
-        def halo(array):
-            return lax.ppermute(array, ("space", "chan"), far), lax.ppermute(array, "space", near)
+        def halo(array, far_first):
+            far_plane = lax.ppermute(array, ("space", "chan"), far)
+            near_plane = lax.ppermute(array, "space", near)
+            return (far_plane, near_plane) if far_first else (near_plane, far_plane)
 
         partial = jax.ShapeDtypeStruct((rows + RIM, full, lanes), F32)
         joined = [pltpu.VMEM((rows + 2 * RIM, full, lanes), BF16)]
         work = cost(rows + RIM, 1, full, lanes)
-        far_plane, near_plane = halo(kept)
+        planes = halo(kept, FIRST)
         total, zero = call(
             first_own_kernel,
             [partial, jax.ShapeDtypeStruct((8, 128), jnp.int32)],
@@ -254,34 +262,36 @@
         )
         later_core = core + zero[0, 0]
         total = call(
-            first_near_kernel,
+            functools.partial(first_add_kernel, FIRST),
             partial,
-            [near_plane, from_other_core(near_plane, later_core), beside_one, total],
+            [planes[0], from_other_core(planes[0], later_core), beside_one, total],
             joined,
             cost_estimate=work,
-            name="first_near",
+            name="first_add",
         )
         hidden = call(
-            first_far_kernel,
+            functools.partial(first_kernel, not FIRST),
             jax.ShapeDtypeStruct((rows + RIM, full, lanes), BF16),
-            [far_plane, from_other_core(far_plane, later_core), beside_one, total, bias_one[:, None]],
+            [planes[1], from_other_core(planes[1], later_core), beside_one, total, bias_one[:, None]],
             joined,
             cost_estimate=work,
-            name="first_far",
+            name="first_last",
         )
 
         partial = jax.ShapeDtypeStruct((rows, full, lanes), F32)
         work = cost(rows, 1, full, lanes)
-        far_plane, near_plane = halo(hidden)
+        planes = halo(hidden, SECOND)
         total = call(own_kernel, partial, [hidden, own_two], cost_estimate=work, name="second_own")
-        total = call(near_kernel, partial, [near_plane, beside_two, total], cost_estimate=work, name="second_near")
+        total = call(
+            functools.partial(add_kernel, SECOND), partial, [planes[0], beside_two, total], cost_estimate=work, name="second_add"
+        )
         blocks = call(
-            second_kernel,
+            functools.partial(second_kernel, not SECOND),
             [jax.ShapeDtypeStruct((CORES, rows, width, lanes), BF16)] * groups,
-            [far_plane, beside_two, total, bias_two[:, None]],
+            [planes[1], beside_two, total, bias_two[:, None]],
             [pltpu.VMEM((groups, CORES, rows, width, lanes), BF16)],
             cost_estimate=work,
-            name="second_far",
+            name="second_last",
         )
 
         blocks = [blocks[0]] + [lax.ppermute(blocks[k], "chan", ahead(k)) for k in range(1, groups)]

time: 65.5 us -> 66.2 us (1.011)
  the two profiles are of different devices: /device:TPU:31 before, /device:TPU:33 now
where the time goes in v9:
time: 66.2 us; the launch traced here: 66 us
  starting transfers between devices  33.6 us (51%)
  waiting for transfers between devices  17.2 us (26%)
  local copies, waits for them, and re-layouts  8.79 us (13%)
  Pallas kernels  5.48 us (8%)
  between operations  0.88 us (1%)
    ppermute x2, starting transfers between devices, halo(): far_plane = lax.ppermute(array, ('space', 'chan'), far)  11.8 us
    ppermute x3, starting transfers between devices, per_device(): got = lax.ppermute(pieces[k], 'chan', ahead(k))  9.66 us
    ppermute x3, starting transfers between devices, per_device(): lax.ppermute(blocks[k], 'chan', ahead(k))  6.73 us
    ppermute x2, waiting for transfers between devices, halo(): far_plane = lax.ppermute(array, ('space', 'chan'), far)  6.5 us
    pallas_call x8, Pallas kernels, call(): pl.pallas_call(kernel, out_shape=shapes, in_specs=[VMEM] * len(inputs), o...  5.48 us
    ppermute x3, waiting for transfers between devices, per_device(): got = lax.ppermute(pieces[k], 'chan', ahead(k))  4.29 us
    ppermute x3, waiting for transfers between devices, per_device(): lax.ppermute(blocks[k], 'chan', ahead(k))  3.77 us
    unnamed x14, local copies, waits for them, and re-layouts  3.57 us
  transfers between devices with their start and end apart: 14, of which 9 were waited for; matrix products, arithmetic and copies ran while one was open for 8% of the time, Pallas kernels for 5%

profile of v9, /device:TPU:33, one launch (start us, length us, event | category | flops | bytes accessed | tf_op | source)
XLA Modules:
  0.0 66.0 jit_solution(4300889452045147219)
XLA Ops:
  0.0 0.0 copy-start
  0.0 0.9 %copy-done = bf16[16,1,64,128]{3,2,1,0:T(8,128)(2,1)S(1)} copy-done((bf16[16,1,64,128]{3,2,1,0:T(8,128)(2,1)S(1)}, bf16[16,1,64,128]{3,2,1,0:T(8,128)(2,1)}, u32[]{:S(2)}) %copy-start) | copy-done | bytes 262168
  1.0 0.0 copy-start.2
  1.0 0.2 pack_rows.1
  1.1 3.1 %collective-permute-start = (bf16[1,20,16,128]{3,2,1,0:T(8,128)(2,1)S(1)}, bf16[1,20,16,128]{3,2,1,0:T(8,128)(2,1)S(1)}, u32[]{:S(2)}, u32[]{:S(2)}) collective-permute-start(bf16[1,20,16,128]{3,2,1,0:T(8,128)(2,1)S(1)} %get-tuple-element.16), channel_id=1, source_target_pairs={{0,2},{1,3},{2,4},{3,5},{4,6},{5,7},{6,0},{7,1},{8,10},{9,11},{10,... | collective-permute-start | bytes 245768 | tf_op jit(solution)/shard_map/ppermute | solution.py:239
  4.2 4.2 %collective-permute-start.1 = (bf16[1,20,16,128]{3,2,1,0:T(8,128)(2,1)S(1)}, bf16[1,20,16,128]{3,2,1,0:T(8,128)(2,1)S(1)}, u32[]{:S(2)}, u32[]{:S(2)}) collective-permute-start(bf16[1,20,16,128]{3,2,1,0:T(8,128)(2,1)S(1)} %get-tuple-element.17), channel_id=1, source_target_pairs={{0,4},{1,5},{2,6},{3,7},{4,0},{5,1},{6,2},{7,3},{8,12},{9,13},{10,... | collective-permute-start | bytes 245768 | tf_op jit(solution)/shard_map/ppermute | solution.py:239
  8.4 2.4 %collective-permute-start.2 = (bf16[1,20,16,128]{3,2,1,0:T(8,128)(2,1)S(1)}, bf16[1,20,16,128]{3,2,1,0:T(8,128)(2,1)S(1)}, u32[]{:S(2)}, u32[]{:S(2)}) collective-permute-start(bf16[1,20,16,128]{3,2,1,0:T(8,128)(2,1)S(1)} %get-tuple-element.18), channel_id=1, source_target_pairs={{0,6},{1,7},{2,0},{3,1},{4,2},{5,3},{6,4},{7,5},{8,14},{9,15},{10,... | collective-permute-start | bytes 245768 | tf_op jit(solution)/shard_map/ppermute | solution.py:239
  10.9 0.0 collective-permute-done
  10.9 0.6 collective-permute-done.1
  11.5 3.7 %collective-permute-done.2 = bf16[1,20,16,128]{3,2,1,0:T(8,128)(2,1)S(1)} collective-permute-done((bf16[1,20,16,128]{3,2,1,0:T(8,128)(2,1)S(1)}, bf16[1,20,16,128]{3,2,1,0:T(8,128)(2,1)S(1)}, u32[]{:S(2)}, u32[]{:S(2)}) %collective-permute-start.2) | collective-permute-done | bytes 81952 | tf_op jit(solution)/shard_map/ppermute | solution.py:239
  15.2 7.6 %collective-permute-start.6 = (bf16[4,20,16,128]{3,2,1,0:T(8,128)(2,1)S(1)}, bf16[4,20,16,128]{3,2,1,0:T(8,128)(2,1)S(1)}, u32[]{:S(2)}, u32[]{:S(2)}) collective-permute-start(bf16[4,20,16,128]{3,2,1,0:T(8,128)(2,1)S(1)} %constant_dynamic-update-slice_fusion.kept_ref), channel_id=1, source_target_pairs={{0,1},{1,0},{2,3},{3,2},{4,5},{5,4},{6,7},{7,6},{8,16},{9,17},{10,... | collective-permute-start | bytes 983048 | tf_op jit(solution)/shard_map/ppermute | solution.py:247
  22.8 0.9 %collective-permute-start.4 = (bf16[4,12,16,128]{3,2,1,0:T(8,128)(2,1)S(1)}, bf16[4,12,16,128]{3,2,1,0:T(8,128)(2,1)S(1)}, u32[]{:S(2)}, u32[]{:S(2)}) collective-permute-start(bf16[4,12,16,128]{3,2,1,0:T(8,128)(2,1)S(1)} %constant_dynamic-slice_fusion.6), channel_id=1, source_target_pairs={{0,1},{1,0},{2,3},{3,2},{4,5},{5,4},{6,7},{7,6},{8,9},{9,8},{10,11... | collective-permute-start | bytes 589832 | tf_op jit(solution)/shard_map/ppermute | solution.py:244
  23.7 0.0 collective-permute-start.3
  23.7 0.0 copy-done.2
  23.7 0.7 %slice.17 = bf16[9,128,128]{2,1,0:T(8,128)(2,1)} slice(bf16[27,128,128]{2,1,0:T(8,128)(2,1)S(1)} %copy-done.2), slice={[9:18], [0:128], [0:128]} | slice | bytes 589824 | tf_op jit(solution)/shard_map/slice | solution.py:178
  24.5 0.6 copy.20
  25.0 0.5 reshape.24.later_ref.weight_ref
  25.6 0.0 copy-start.3
  25.6 0.6 copy-done.3
  26.3 0.1 copy.15.bias_ref
  26.4 1.2 %copy.13 = bf16[3,3,128,128]{2,0,3,1:T(4,128)(2,1)S(1)} copy(bf16[3,3,128,128]{3,2,1,0:T(8,128)(2,1)} %bitcast.27) | data formatting | bytes 589824 | tf_op jit(solution)/shard_map/squeeze | solution.py:178
  27.6 0.0 collective-permute-done.4.other_ref
  27.6 0.8 %first_own.1 = (f32[10,128,128]{2,1,0:T(8,128)S(1)}, s32[8,128]{1,0:T(8,128)S(1)}) custom-call(bf16[4,20,16,128]{3,2,1,0:T(8,128)(2,1)S(1)} %constant_dynamic-update-slice_fusion.kept_ref, bf16[4,12,16,128]{3,2,1,0:T(8,128)(2,1)S(1)} %collective-permute-done.4.other_ref, bf16[384,384]{1,0:T(8,128)(2,1)S(1)} %bitcast.22, ...), custom_call_target="tpu_custom_call" | custom-call | flops 377487360 | bytes 4000000 | tf_op jit(solution)/shard_map/first_own/pallas_call | solution.py:208
  28.5 0.5 slice.19
  29.6 0.8 %collective-permute-done.6.kept_ref = bf16[4,20,16,128]{3,2,1,0:T(8,128)(2,1)S(1)} collective-permute-done((bf16[4,20,16,128]{3,2,1,0:T(8,128)(2,1)S(1)}, bf16[4,20,16,128]{3,2,1,0:T(8,128)(2,1)S(1)}, u32[]{:S(2)}, u32[]{:S(2)}) %collective-permute-start.6) | collective-permute-done | bytes 327712 | tf_op jit(solution)/shard_map/ppermute | solution.py:247
  30.4 1.1 %collective-permute-start.7 = (bf16[4,12,16,128]{3,2,1,0:T(8,128)(2,1)S(1)}, bf16[4,12,16,128]{3,2,1,0:T(8,128)(2,1)S(1)}, u32[]{:S(2)}, u32[]{:S(2)}) collective-permute-start(bf16[4,12,16,128]{3,2,1,0:T(8,128)(2,1)S(1)} %constant_dynamic-slice_fusion.4), channel_id=1, source_target_pairs={{0,1},{1,0},{2,3},{3,2},{4,5},{5,4},{6,7},{7,6},{8,9},{9,8},{10,11... | collective-permute-start | bytes 589832 | tf_op jit(solution)/shard_map/ppermute | solution.py:244
  31.6 1.4 %collective-permute-done.3.kept_ref = bf16[4,20,16,128]{3,2,1,0:T(8,128)(2,1)S(1)} collective-permute-done((bf16[4,20,16,128]{3,2,1,0:T(8,128)(2,1)S(1)}, bf16[4,20,16,128]{3,2,1,0:T(8,128)(2,1)S(1)}, u32[]{:S(2)}, u32[]{:S(2)}) %collective-permute-start.3) | collective-permute-done | bytes 327712 | tf_op jit(solution)/shard_map/ppermute | solution.py:248
  32.9 1.0 %collective-permute-start.5 = (bf16[4,12,16,128]{3,2,1,0:T(8,128)(2,1)S(1)}, bf16[4,12,16,128]{3,2,1,0:T(8,128)(2,1)S(1)}, u32[]{:S(2)}, u32[]{:S(2)}) collective-permute-start(bf16[4,12,16,128]{3,2,1,0:T(8,128)(2,1)S(1)} %constant_dynamic-slice_fusion.5), channel_id=1, source_target_pairs={{0,1},{1,0},{2,3},{3,2},{4,5},{5,4},{6,7},{7,6},{8,9},{9,8},{10,11... | collective-permute-start | bytes 589832 | tf_op jit(solution)/shard_map/ppermute | solution.py:244
  33.9 0.0 collective-permute-done.7.other_ref
  33.9 0.8 %first_add.1.before_ref = f32[10,128,128]{2,1,0:T(8,128)S(1)} custom-call(bf16[4,20,16,128]{3,2,1,0:T(8,128)(2,1)S(1)} %collective-permute-done.6.kept_ref, bf16[4,12,16,128]{3,2,1,0:T(8,128)(2,1)S(1)} %collective-permute-done.7.other_ref, bf16[2,384,384]{2,1,0:T(8,128)(2,1)S(1)} %reshape.24.later_ref.weight_ref, ...), custom_call_target="tpu_custom_call" | custom-call | flops 377487360 | bytes 4000000 | tf_op jit(solution)/shard_map/first_add/pallas_call | solution.py:208
  34.7 0.2 collective-permute-done.5.other_ref
  35.0 0.8 %first_last.1.plane_ref = bf16[10,128,128]{2,1,0:T(8,128)(2,1)S(1)} custom-call(bf16[4,20,16,128]{3,2,1,0:T(8,128)(2,1)S(1)} %collective-permute-done.3.kept_ref, bf16[4,12,16,128]{3,2,1,0:T(8,128)(2,1)S(1)} %collective-permute-done.5.other_ref, bf16[2,384,384]{2,1,0:T(8,128)(2,1)S(1)} %reshape.24.later_ref.weight_ref, ...), custom_call_target="tpu_custom_call" | custom-call | flops 377487360 | bytes 4000000 | tf_op jit(solution)/shard_map/first_last/pallas_call | solution.py:208
  35.8 4.3 %collective-permute-start.9 = (bf16[10,128,128]{2,1,0:T(8,128)(2,1)S(1)}, bf16[10,128,128]{2,1,0:T(8,128)(2,1)S(1)}, u32[]{:S(2)}, u32[]{:S(2)}) collective-permute-start(bf16[10,128,128]{2,1,0:T(8,128)(2,1)S(1)} %first_last.1.plane_ref), channel_id=1, source_target_pairs={{0,1},{1,0},{2,3},{3,2},{4,5},{5,4},{6,7},{7,6},{8,16},{9,17},{10,... | collective-permute-start | bytes 983048 | tf_op jit(solution)/shard_map/ppermute | solution.py:247
  40.0 0.0 collective-permute-start.8
  40.0 0.0 slice-start
  40.0 0.0 copy-start.1
  40.0 1.0 %slice-done = bf16[9,128,128]{2,1,0:T(8,128)(2,1)S(1)} async-done(((bf16[27,128,128]{2,1,0:T(8,128)(2,1)}), bf16[9,128,128]{2,1,0:T(8,128)(2,1)S(1)}, s32[]{:S(2)}) %slice-start) | async-done | bytes 294936 | tf_op jit(solution)/shard_map/slice | solution.py:178
  41.0 0.2 copy.18
  41.3 0.1 copy-done.1
  41.4 0.6 copy.21
  42.0 0.5 reshape.26.weight_ref
  42.6 0.0 copy-start.4
  42.6 0.6 copy-done.4
  43.2 0.1 copy.19.bias_ref
  43.3 0.7 %second_own.1.before_ref = f32[8,128,128]{2,1,0:T(8,128)S(1)} custom-call(bf16[10,128,128]{2,1,0:T(8,128)(2,1)S(1)} %first_last.1.plane_ref, bf16[384,384]{1,0:T(8,128)(2,1)S(1)} %bitcast.21), custom_call_target="tpu_custom_call" | custom-call | flops 301989888 | bytes 4000000 | tf_op jit(solution)/shard_map/second_own/pallas_call | solution.py:208
  44.0 5.7 %collective-permute-done.9.plane_ref = bf16[10,128,128]{2,1,0:T(8,128)(2,1)S(1)} collective-permute-done((bf16[10,128,128]{2,1,0:T(8,128)(2,1)S(1)}, bf16[10,128,128]{2,1,0:T(8,128)(2,1)S(1)}, u32[]{:S(2)}, u32[]{:S(2)}) %collective-permute-start.9) | collective-permute-done | bytes 327712 | tf_op jit(solution)/shard_map/ppermute | solution.py:247
  49.7 0.7 %second_add.1.before_ref = f32[8,128,128]{2,1,0:T(8,128)S(1)} custom-call(bf16[10,128,128]{2,1,0:T(8,128)(2,1)S(1)} %collective-permute-done.9.plane_ref, bf16[2,384,384]{2,1,0:T(8,128)(2,1)S(1)} %reshape.26.weight_ref, f32[8,128,128]{2,1,0:T(8,128)S(1)} %second_own.1.before_ref), custom_call_target="tpu_custom_call" | custom-call | flops 301989888 | bytes 4000000 | tf_op jit(solution)/shard_map/second_add/pallas_call | solution.py:208
  50.4 0.0 collective-permute-done.8.plane_ref
  50.4 0.7 %second_last.1 = (bf16[2,8,16,128]{3,2,1,0:T(8,128)(2,1)S(1)}, bf16[2,8,16,128]{3,2,1,0:T(8,128)(2,1)S(1)}, bf16[2,8,16,128]{3,2,1,0:T(8,128)(2,1)S(1)}, bf16[2,8,16,128]{3,2,1,0:T(8,128)(2,1)S(1)}) custom-call(bf16[10,128,128]{2,1,0:T(8,128)(2,1)S(1)} %collective-permute-done.8.plane_ref, bf16[2,384,384]{2,1,0:T(8,128)(2,1)S(1)} %reshape.26.weight_ref, ...), custom_call_target="tpu_custom_call" | custom-call | flops 301989888 | bytes 4000000 | tf_op jit(solution)/shard_map/second_last/pallas_call | solution.py:208
  51.1 1.8 %collective-permute-start.10 = (bf16[2,8,16,128]{3,2,1,0:T(8,128)(2,1)S(1)}, bf16[2,8,16,128]{3,2,1,0:T(8,128)(2,1)S(1)}, u32[]{:S(2)}, u32[]{:S(2)}) collective-permute-start(bf16[2,8,16,128]{3,2,1,0:T(8,128)(2,1)S(1)} %get-tuple-element.22), channel_id=1, source_target_pairs={{0,2},{1,3},{2,4},{3,5},{4,6},{5,7},{6,0},{7,1},{8,10},{9,11},{10,... | collective-permute-start | bytes 196616 | tf_op jit(solution)/shard_map/ppermute | solution.py:297
  52.9 4.2 %collective-permute-start.11 = (bf16[2,8,16,128]{3,2,1,0:T(8,128)(2,1)S(1)}, bf16[2,8,16,128]{3,2,1,0:T(8,128)(2,1)S(1)}, u32[]{:S(2)}, u32[]{:S(2)}) collective-permute-start(bf16[2,8,16,128]{3,2,1,0:T(8,128)(2,1)S(1)} %get-tuple-element.23), channel_id=1, source_target_pairs={{0,4},{1,5},{2,6},{3,7},{4,0},{5,1},{6,2},{7,3},{8,12},{9,13},{10,... | collective-permute-start | bytes 196616 | tf_op jit(solution)/shard_map/ppermute | solution.py:297
  57.1 0.7 %collective-permute-start.12 = (bf16[2,8,16,128]{3,2,1,0:T(8,128)(2,1)S(1)}, bf16[2,8,16,128]{3,2,1,0:T(8,128)(2,1)S(1)}, u32[]{:S(2)}, u32[]{:S(2)}) collective-permute-start(bf16[2,8,16,128]{3,2,1,0:T(8,128)(2,1)S(1)} %get-tuple-element.24), channel_id=1, source_target_pairs={{0,6},{1,7},{2,0},{3,1},{4,2},{5,3},{6,4},{7,5},{8,14},{9,15},{10,... | collective-permute-start | bytes 196616 | tf_op jit(solution)/shard_map/ppermute | solution.py:297
  57.9 0.0 collective-permute-done.10.refs_1_
  57.9 2.1 %collective-permute-done.11.refs_2_ = bf16[2,8,16,128]{3,2,1,0:T(8,128)(2,1)S(1)} collective-permute-done((bf16[2,8,16,128]{3,2,1,0:T(8,128)(2,1)S(1)}, bf16[2,8,16,128]{3,2,1,0:T(8,128)(2,1)S(1)}, u32[]{:S(2)}, u32[]{:S(2)}) %collective-permute-start.11) | collective-permute-done | bytes 65568 | tf_op jit(solution)/shard_map/ppermute | solution.py:297
  59.9 1.7 %collective-permute-done.12.refs_3_ = bf16[2,8,16,128]{3,2,1,0:T(8,128)(2,1)S(1)} collective-permute-done((bf16[2,8,16,128]{3,2,1,0:T(8,128)(2,1)S(1)}, bf16[2,8,16,128]{3,2,1,0:T(8,128)(2,1)S(1)}, u32[]{:S(2)}, u32[]{:S(2)}) %collective-permute-start.12) | collective-permute-done | bytes 65568 | tf_op jit(solution)/shard_map/ppermute | solution.py:297
  61.7 2.5 %collective-permute-start.13 = (bf16[4,8,16,128]{3,2,1,0:T(8,128)(2,1)S(1)}, bf16[4,8,16,128]{3,2,1,0:T(8,128)(2,1)S(1)}, u32[]{:S(2)}, u32[]{:S(2)}) collective-permute-start(bf16[4,8,16,128]{3,2,1,0:T(8,128)(2,1)S(1)} %pad_maximum_fusion), channel_id=1, source_target_pairs={{0,1},{1,0},{2,3},{3,2},{4,5},{5,4},{6,7},{7,6},{8,9},{9,8},{10,11... | collective-permute-start | bytes 393224 | tf_op jit(solution)/shard_map/ppermute | solution.py:299
  64.2 1.0 %collective-permute-done.13.swapped_ref = bf16[4,8,16,128]{3,2,1,0:T(8,128)(2,1)S(1)} collective-permute-done((bf16[4,8,16,128]{3,2,1,0:T(8,128)(2,1)S(1)}, bf16[4,8,16,128]{3,2,1,0:T(8,128)(2,1)S(1)}, u32[]{:S(2)}, u32[]{:S(2)}) %collective-permute-start.13) | collective-permute-done | bytes 131104 | tf_op jit(solution)/shard_map/ppermute | solution.py:299
  65.1 0.8 %unpack_rows.1 = bf16[16,1,64,128]{3,2,1,0:T(8,128)(2,1)} custom-call(bf16[4,8,16,128]{3,2,1,0:T(8,128)(2,1)S(1)} %collective-permute-done.13.swapped_ref, bf16[2,8,16,128]{3,2,1,0:T(8,128)(2,1)S(1)} %get-tuple-element.21.refs_0_, bf16[2,8,16,128]{3,2,1,0:T(8,128)(2,1)S(1)} %collective-permute-done.10.refs_1_, ...), custom_call_target="tpu_custom_call" | custom-call | tf_op jit(solution)/shard_map/unpack_rows/pallas_call | solution.py:208
  (17 shorter events, 0.4 us)
Async XLA Ops:
  0.0 0.9 %copy-start = (bf16[16,1,64,128]{3,2,1,0:T(8,128)(2,1)S(1)}, bf16[16,1,64,128]{3,2,1,0:T(8,128)(2,1)}, u32[]{:S(2)}) copy-start(bf16[16,1,64,128]{3,2,1,0:T(8,128)(2,1)} %volume_ref.1) | copy-start | bytes 786436
  1.0 22.7 %copy-start.2 = (bf16[27,128,128]{2,1,0:T(8,128)(2,1)S(1)}, bf16[27,128,128]{2,1,0:T(8,128)(2,1)}, u32[]{:S(2)}) copy-start(bf16[27,128,128]{2,1,0:T(8,128)(2,1)} %param.6) | copy-start | bytes 2654212
  1.1 9.7 %collective-permute-start = (bf16[1,20,16,128]{3,2,1,0:T(8,128)(2,1)S(1)}, bf16[1,20,16,128]{3,2,1,0:T(8,128)(2,1)S(1)}, u32[]{:S(2)}, u32[]{:S(2)}) collective-permute-start(bf16[1,20,16,128]{3,2,1,0:T(8,128)(2,1)S(1)} %get-tuple-element.16), channel_id=1, source_target_pairs={{0,2},{1,3},{2,4},{3,5},{4,6},{5,7},{6,0},{7,1},{8,10},{9,11},{10,... | collective-permute-start | bytes 245768 | tf_op jit(solution)/shard_map/ppermute | solution.py:239
  4.2 7.3 %collective-permute-start.1 = (bf16[1,20,16,128]{3,2,1,0:T(8,128)(2,1)S(1)}, bf16[1,20,16,128]{3,2,1,0:T(8,128)(2,1)S(1)}, u32[]{:S(2)}, u32[]{:S(2)}) collective-permute-start(bf16[1,20,16,128]{3,2,1,0:T(8,128)(2,1)S(1)} %get-tuple-element.17), channel_id=1, source_target_pairs={{0,4},{1,5},{2,6},{3,7},{4,0},{5,1},{6,2},{7,3},{8,12},{9,13},{10,... | collective-permute-start | bytes 245768 | tf_op jit(solution)/shard_map/ppermute | solution.py:239
  8.4 6.8 %collective-permute-start.2 = (bf16[1,20,16,128]{3,2,1,0:T(8,128)(2,1)S(1)}, bf16[1,20,16,128]{3,2,1,0:T(8,128)(2,1)S(1)}, u32[]{:S(2)}, u32[]{:S(2)}) collective-permute-start(bf16[1,20,16,128]{3,2,1,0:T(8,128)(2,1)S(1)} %get-tuple-element.18), channel_id=1, source_target_pairs={{0,6},{1,7},{2,0},{3,1},{4,2},{5,3},{6,4},{7,5},{8,14},{9,15},{10,... | collective-permute-start | bytes 245768 | tf_op jit(solution)/shard_map/ppermute | solution.py:239
  15.2 15.2 %collective-permute-start.6 = (bf16[4,20,16,128]{3,2,1,0:T(8,128)(2,1)S(1)}, bf16[4,20,16,128]{3,2,1,0:T(8,128)(2,1)S(1)}, u32[]{:S(2)}, u32[]{:S(2)}) collective-permute-start(bf16[4,20,16,128]{3,2,1,0:T(8,128)(2,1)S(1)} %constant_dynamic-update-slice_fusion.kept_ref), channel_id=1, source_target_pairs={{0,1},{1,0},{2,3},{3,2},{4,5},{5,4},{6,7},{7,6},{8,16},{9,17},{10,... | collective-permute-start | bytes 983048 | tf_op jit(solution)/shard_map/ppermute | solution.py:247
  22.8 4.8 %collective-permute-start.4 = (bf16[4,12,16,128]{3,2,1,0:T(8,128)(2,1)S(1)}, bf16[4,12,16,128]{3,2,1,0:T(8,128)(2,1)S(1)}, u32[]{:S(2)}, u32[]{:S(2)}) collective-permute-start(bf16[4,12,16,128]{3,2,1,0:T(8,128)(2,1)S(1)} %constant_dynamic-slice_fusion.6), channel_id=1, source_target_pairs={{0,1},{1,0},{2,3},{3,2},{4,5},{5,4},{6,7},{7,6},{8,9},{9,8},{10,11... | collective-permute-start | bytes 589832 | tf_op jit(solution)/shard_map/ppermute | solution.py:244
  23.7 9.3 %collective-permute-start.3 = (bf16[4,20,16,128]{3,2,1,0:T(8,128)(2,1)S(1)}, bf16[4,20,16,128]{3,2,1,0:T(8,128)(2,1)S(1)}, u32[]{:S(2)}, u32[]{:S(2)}) collective-permute-start(bf16[4,20,16,128]{3,2,1,0:T(8,128)(2,1)S(1)} %constant_dynamic-update-slice_fusion.kept_ref), channel_id=1, source_target_pairs={{0,8},{8,0},{16,24},{24,16},{32,40},{40,32},{48,56},{56,48},{64,72... | collective-permute-start | bytes 983048 | tf_op jit(solution)/shard_map/ppermute | solution.py:248
  25.6 0.7 copy-start.3
  30.4 3.5 %collective-permute-start.7 = (bf16[4,12,16,128]{3,2,1,0:T(8,128)(2,1)S(1)}, bf16[4,12,16,128]{3,2,1,0:T(8,128)(2,1)S(1)}, u32[]{:S(2)}, u32[]{:S(2)}) collective-permute-start(bf16[4,12,16,128]{3,2,1,0:T(8,128)(2,1)S(1)} %constant_dynamic-slice_fusion.4), channel_id=1, source_target_pairs={{0,1},{1,0},{2,3},{3,2},{4,5},{5,4},{6,7},{7,6},{8,9},{9,8},{10,11... | collective-permute-start | bytes 589832 | tf_op jit(solution)/shard_map/ppermute | solution.py:244
  32.9 2.0 %collective-permute-start.5 = (bf16[4,12,16,128]{3,2,1,0:T(8,128)(2,1)S(1)}, bf16[4,12,16,128]{3,2,1,0:T(8,128)(2,1)S(1)}, u32[]{:S(2)}, u32[]{:S(2)}) collective-permute-start(bf16[4,12,16,128]{3,2,1,0:T(8,128)(2,1)S(1)} %constant_dynamic-slice_fusion.5), channel_id=1, source_target_pairs={{0,1},{1,0},{2,3},{3,2},{4,5},{5,4},{6,7},{7,6},{8,9},{9,8},{10,11... | collective-permute-start | bytes 589832 | tf_op jit(solution)/shard_map/ppermute | solution.py:244
  35.8 13.9 %collective-permute-start.9 = (bf16[10,128,128]{2,1,0:T(8,128)(2,1)S(1)}, bf16[10,128,128]{2,1,0:T(8,128)(2,1)S(1)}, u32[]{:S(2)}, u32[]{:S(2)}) collective-permute-start(bf16[10,128,128]{2,1,0:T(8,128)(2,1)S(1)} %first_last.1.plane_ref), channel_id=1, source_target_pairs={{0,1},{1,0},{2,3},{3,2},{4,5},{5,4},{6,7},{7,6},{8,16},{9,17},{10,... | collective-permute-start | bytes 983048 | tf_op jit(solution)/shard_map/ppermute | solution.py:247
  40.0 10.4 %collective-permute-start.8 = (bf16[10,128,128]{2,1,0:T(8,128)(2,1)S(1)}, bf16[10,128,128]{2,1,0:T(8,128)(2,1)S(1)}, u32[]{:S(2)}, u32[]{:S(2)}) collective-permute-start(bf16[10,128,128]{2,1,0:T(8,128)(2,1)S(1)} %first_last.1.plane_ref), channel_id=1, source_target_pairs={{0,8},{8,0},{16,24},{24,16},{32,40},{40,32},{48,56},{56,48},{64,72... | collective-permute-start | bytes 983048 | tf_op jit(solution)/shard_map/ppermute | solution.py:248
  40.0 1.0 %slice-start = ((bf16[27,128,128]{2,1,0:T(8,128)(2,1)}), bf16[9,128,128]{2,1,0:T(8,128)(2,1)S(1)}, s32[]{:S(2)}) async-start(bf16[27,128,128]{2,1,0:T(8,128)(2,1)} %param.8), calls=%async_computation | async-start | bytes 589824 | tf_op jit(solution)/shard_map/slice | solution.py:178
  40.0 1.3 %copy-start.1 = (bf16[27,128,128]{2,1,0:T(8,128)(2,1)S(1)}, bf16[27,128,128]{2,1,0:T(8,128)(2,1)}, u32[]{:S(2)}) copy-start(bf16[27,128,128]{2,1,0:T(8,128)(2,1)} %param.8) | copy-start | bytes 2654212
  42.6 0.7 copy-start.4
  51.1 6.7 %collective-permute-start.10 = (bf16[2,8,16,128]{3,2,1,0:T(8,128)(2,1)S(1)}, bf16[2,8,16,128]{3,2,1,0:T(8,128)(2,1)S(1)}, u32[]{:S(2)}, u32[]{:S(2)}) collective-permute-start(bf16[2,8,16,128]{3,2,1,0:T(8,128)(2,1)S(1)} %get-tuple-element.22), channel_id=1, source_target_pairs={{0,2},{1,3},{2,4},{3,5},{4,6},{5,7},{6,0},{7,1},{8,10},{9,11},{10,... | collective-permute-start | bytes 196616 | tf_op jit(solution)/shard_map/ppermute | solution.py:297
  52.9 7.0 %collective-permute-start.11 = (bf16[2,8,16,128]{3,2,1,0:T(8,128)(2,1)S(1)}, bf16[2,8,16,128]{3,2,1,0:T(8,128)(2,1)S(1)}, u32[]{:S(2)}, u32[]{:S(2)}) collective-permute-start(bf16[2,8,16,128]{3,2,1,0:T(8,128)(2,1)S(1)} %get-tuple-element.23), channel_id=1, source_target_pairs={{0,4},{1,5},{2,6},{3,7},{4,0},{5,1},{6,2},{7,3},{8,12},{9,13},{10,... | collective-permute-start | bytes 196616 | tf_op jit(solution)/shard_map/ppermute | solution.py:297
  57.1 4.5 %collective-permute-start.12 = (bf16[2,8,16,128]{3,2,1,0:T(8,128)(2,1)S(1)}, bf16[2,8,16,128]{3,2,1,0:T(8,128)(2,1)S(1)}, u32[]{:S(2)}, u32[]{:S(2)}) collective-permute-start(bf16[2,8,16,128]{3,2,1,0:T(8,128)(2,1)S(1)} %get-tuple-element.24), channel_id=1, source_target_pairs={{0,6},{1,7},{2,0},{3,1},{4,2},{5,3},{6,4},{7,5},{8,14},{9,15},{10,... | collective-permute-start | bytes 196616 | tf_op jit(solution)/shard_map/ppermute | solution.py:297
  61.7 3.5 %collective-permute-start.13 = (bf16[4,8,16,128]{3,2,1,0:T(8,128)(2,1)S(1)}, bf16[4,8,16,128]{3,2,1,0:T(8,128)(2,1)S(1)}, u32[]{:S(2)}, u32[]{:S(2)}) collective-permute-start(bf16[4,8,16,128]{3,2,1,0:T(8,128)(2,1)S(1)} %pad_maximum_fusion), channel_id=1, source_target_pairs={{0,1},{1,0},{2,3},{3,2},{4,5},{5,4},{6,7},{7,6},{8,9},{9,8},{10,11... | collective-permute-start | bytes 393224 | tf_op jit(solution)/shard_map/ppermute | solution.py:299

commit v10 on v7

--- a/solution.py
+++ b/solution.py
@@ -1,3 +1,5 @@
+import functools
+
 import jax
 import jax.numpy as jnp
 from jax import lax
@@ -105,7 +107,8 @@
     conv_rows(rows_of(plane_ref, False), 1, weight, store, rows, lanes)
 
 
-def first_own_kernel(kept_ref, other_ref, weight_ref, later_ref, bias_ref, out_ref, zero_ref, joined_ref):
+def first_own_kernel(kept_ref, other_ref, weight_ref, *refs):
+    out_ref, zero_ref, joined_ref = refs[-3:]
     gather_rows(kept_ref, other_ref, joined_ref)
     own_kernel(joined_ref, weight_ref, out_ref)
     zero_ref[...] = jnp.zeros_like(zero_ref)
@@ -134,20 +137,35 @@
     conv_rows(rows_of(joined_ref, True), 1, weight, store, rows, lanes)
 
 
-def second_kernel(plane_ref, weight_ref, before_ref, bias_ref, *refs):
+def share_kernel(far, plane_ref, weight_ref, *refs):
+    out_ref = refs[-1]
+    rows, _, lanes = out_ref.shape
+    odd = lax.axis_index("space") % 2
+
+    def store(row, value):
+        out_ref[row] = value.astype(BF16)
+
+    weight = weight_ref[1 - odd if far else odd]
+    conv_rows(rows_of(plane_ref, False), 1, weight, store, rows, lanes)
+
+
+def sum_kernel(far_ref, own_ref, out_ref):
+    far = rows_of(far_ref, True)
+    for row in range(out_ref.shape[0]):
+        out_ref[row] = own_ref[row] + far(0, row).astype(F32)
+
+
+def second_kernel(near_ref, own_ref, bias_ref, *refs):
     outs, all_ref = refs[:-1], refs[-1]
-    groups, cores, rows, width, lanes = all_ref.shape
+    groups, cores, rows, width, _ = all_ref.shape
     bias = bias_ref[...]
-
-    def store(row, value):
-        value = jnp.maximum(value + before_ref[row] + bias, 0.0).astype(BF16)
+    for row in range(rows):
+        value = own_ref[row] + near_ref[row].astype(F32)
+        value = jnp.maximum(value + bias, 0.0).astype(BF16)
         for g in range(groups):
             for c in range(cores):
                 at = (g * cores + c) * width
                 all_ref[g, c, row] = value[at : at + width]
-
-    weight = weight_ref[lax.axis_index("space") % 2]
-    conv_rows(rows_of(plane_ref, True), 1, weight, store, rows, lanes)
     for k in range(groups):
         outs[k][...] = all_ref[lax.rem(my_group() + k, groups)]
 
@@ -237,17 +255,15 @@
             sent = lax.dynamic_slice_in_dim(array, (1 - core) * rows, rows + 2 * RIM, 1)
             return lax.ppermute(sent, "chan", swap)
 
-        def halo(array):
-            return lax.ppermute(array, ("space", "chan"), far), lax.ppermute(array, "space", near)
-
         partial = jax.ShapeDtypeStruct((rows + RIM, full, lanes), F32)
         joined = [pltpu.VMEM((rows + 2 * RIM, full, lanes), BF16)]
         work = cost(rows + RIM, 1, full, lanes)
-        far_plane, near_plane = halo(kept)
+        far_plane = lax.ppermute(kept, ("space", "chan"), far)
+        near_plane = lax.ppermute(kept, "space", near)
         total, zero = call(
             first_own_kernel,
             [partial, jax.ShapeDtypeStruct((8, 128), jnp.int32)],
-            [kept, from_other_core(kept, core), own_one, beside_one, bias_one[:, None]],
+            [kept, from_other_core(kept, core), own_one, beside_one, bias_one[:, None], beside_two],
             joined,
             cost_estimate=work,
             name="first_own",
@@ -270,18 +286,29 @@
             name="first_far",
         )
 
+        work = cost(rows, 1, full, lanes)
+        sent = jax.ShapeDtypeStruct((rows, full, lanes), BF16)
+        far_share = call(
+            functools.partial(share_kernel, True), sent, [hidden, beside_two], cost_estimate=work, name="far_share"
+        )
+        near_share = call(
+            functools.partial(share_kernel, False),
+            sent,
+            [hidden, beside_two, far_share],
+            cost_estimate=work,
+            name="near_share",
+        )
+        far_share = lax.ppermute(far_share, ("space", "chan"), far)
+        near_share = lax.ppermute(near_share, "space", near)
         partial = jax.ShapeDtypeStruct((rows, full, lanes), F32)
-        work = cost(rows, 1, full, lanes)
-        far_plane, near_plane = halo(hidden)
         total = call(own_kernel, partial, [hidden, own_two], cost_estimate=work, name="second_own")
-        total = call(near_kernel, partial, [near_plane, beside_two, total], cost_estimate=work, name="second_near")
+        total = call(sum_kernel, partial, [far_share, total], name="second_far")
         blocks = call(
             second_kernel,
             [jax.ShapeDtypeStruct((CORES, rows, width, lanes), BF16)] * groups,
-            [far_plane, beside_two, total, bias_two[:, None]],
+            [near_share, total, bias_two[:, None]],
             [pltpu.VMEM((groups, CORES, rows, width, lanes), BF16)],
-            cost_estimate=work,
-            name="second_far",
+            name="second_sum",
         )
 
         blocks = [blocks[0]] + [lax.ppermute(blocks[k], "chan", ahead(k)) for k in range(1, groups)]

time: 65.5 us -> 65.5 us (level)
  the two profiles are of different devices: /device:TPU:31 before, /device:TPU:33 now
where the time goes in v10:
time: 65.5 us; the launch traced here: 65.2 us
  starting transfers between devices  36.1 us (55%)
  waiting for transfers between devices  12.7 us (19%)
  local copies, waits for them, and re-layouts  9.79 us (15%)
  Pallas kernels  5.66 us (9%)
  between operations  0.92 us (1%)
    ppermute x3, starting transfers between devices, per_device(): got = lax.ppermute(pieces[k], 'chan', ahead(k))  9.66 us
    ppermute x3, starting transfers between devices, per_device(): lax.ppermute(blocks[k], 'chan', ahead(k))  7.43 us
    ppermute x1, starting transfers between devices, per_device(): far_plane = lax.ppermute(kept, ('space', 'chan'), far)  6.2 us
    ppermute x1, starting transfers between devices, per_device(): far_share = lax.ppermute(far_share, ('space', 'chan'), far)  5.71 us
    pallas_call x10, Pallas kernels, call(): pl.pallas_call(kernel, out_shape=shapes, in_specs=[VMEM] * len(inputs), o...  5.66 us
    ppermute x3, waiting for transfers between devices, per_device(): got = lax.ppermute(pieces[k], 'chan', ahead(k))  4.27 us
    unnamed x12, local copies, waits for them, and re-layouts  3.51 us
    ppermute x1, starting transfers between devices, per_device(): swapped = lax.ppermute(theirs, 'chan', swap)  3.2 us
  transfers between devices with their start and end apart: 14, of which 9 were waited for; matrix products, arithmetic and copies ran while one was open for 12% of the time, Pallas kernels for 5%

profile of v10, /device:TPU:33, one launch (start us, length us, event | category | flops | bytes accessed | tf_op | source)
XLA Modules:
  0.0 65.2 jit_solution(11480250571647232671)
XLA Ops:
  0.0 0.0 copy-start
  0.0 0.9 %copy-done = bf16[16,1,64,128]{3,2,1,0:T(8,128)(2,1)S(1)} copy-done((bf16[16,1,64,128]{3,2,1,0:T(8,128)(2,1)S(1)}, bf16[16,1,64,128]{3,2,1,0:T(8,128)(2,1)}, u32[]{:S(2)}) %copy-start) | copy-done | bytes 262168
  1.0 0.2 pack_rows.1
  1.1 3.1 %collective-permute-start = (bf16[1,20,16,128]{3,2,1,0:T(8,128)(2,1)S(1)}, bf16[1,20,16,128]{3,2,1,0:T(8,128)(2,1)S(1)}, u32[]{:S(2)}, u32[]{:S(2)}) collective-permute-start(bf16[1,20,16,128]{3,2,1,0:T(8,128)(2,1)S(1)} %get-tuple-element.16), channel_id=1, source_target_pairs={{0,2},{1,3},{2,4},{3,5},{4,6},{5,7},{6,0},{7,1},{8,10},{9,11},{10,... | collective-permute-start | bytes 245768 | tf_op jit(solution)/shard_map/ppermute | solution.py:251
  4.2 4.2 %collective-permute-start.1 = (bf16[1,20,16,128]{3,2,1,0:T(8,128)(2,1)S(1)}, bf16[1,20,16,128]{3,2,1,0:T(8,128)(2,1)S(1)}, u32[]{:S(2)}, u32[]{:S(2)}) collective-permute-start(bf16[1,20,16,128]{3,2,1,0:T(8,128)(2,1)S(1)} %get-tuple-element.17), channel_id=1, source_target_pairs={{0,4},{1,5},{2,6},{3,7},{4,0},{5,1},{6,2},{7,3},{8,12},{9,13},{10,... | collective-permute-start | bytes 245768 | tf_op jit(solution)/shard_map/ppermute | solution.py:251
  8.4 2.4 %collective-permute-start.2 = (bf16[1,20,16,128]{3,2,1,0:T(8,128)(2,1)S(1)}, bf16[1,20,16,128]{3,2,1,0:T(8,128)(2,1)S(1)}, u32[]{:S(2)}, u32[]{:S(2)}) collective-permute-start(bf16[1,20,16,128]{3,2,1,0:T(8,128)(2,1)S(1)} %get-tuple-element.18), channel_id=1, source_target_pairs={{0,6},{1,7},{2,0},{3,1},{4,2},{5,3},{6,4},{7,5},{8,14},{9,15},{10,... | collective-permute-start | bytes 245768 | tf_op jit(solution)/shard_map/ppermute | solution.py:251
  10.8 0.0 copy-start.1
  10.9 0.0 collective-permute-done
  10.9 0.6 collective-permute-done.1
  11.5 3.7 %collective-permute-done.2 = bf16[1,20,16,128]{3,2,1,0:T(8,128)(2,1)S(1)} collective-permute-done((bf16[1,20,16,128]{3,2,1,0:T(8,128)(2,1)S(1)}, bf16[1,20,16,128]{3,2,1,0:T(8,128)(2,1)S(1)}, u32[]{:S(2)}, u32[]{:S(2)}) %collective-permute-start.2) | collective-permute-done | bytes 81952 | tf_op jit(solution)/shard_map/ppermute | solution.py:251
  15.2 1.4 %collective-permute-start.6 = (bf16[4,20,16,128]{3,2,1,0:T(8,128)(2,1)S(1)}, bf16[4,20,16,128]{3,2,1,0:T(8,128)(2,1)S(1)}, u32[]{:S(2)}, u32[]{:S(2)}) collective-permute-start(bf16[4,20,16,128]{3,2,1,0:T(8,128)(2,1)S(1)} %constant_dynamic-update-slice_fusion.kept_ref), channel_id=1, source_target_pairs={{0,8},{8,0},{16,24},{24,16},{32,40},{40,32},{48,56},{56,48},{64,72... | collective-permute-start | bytes 983048 | tf_op jit(solution)/shard_map/ppermute | solution.py:262
  16.6 0.7 %constant_dynamic-slice_fusion.6 = bf16[4,12,16,128]{3,2,1,0:T(8,128)(2,1)} fusion(bf16[4,20,16,128]{3,2,1,0:T(8,128)(2,1)S(1)} %constant_dynamic-update-slice_fusion.kept_ref, s32[]{:T(128)S(6)} %select_n.58), kind=kLoop, calls=%fused_computation.9 | loop fusion | bytes 393220 | tf_op jit(solution)/shard_map/dynamic_slice | solution.py:255
  17.3 1.2 %collective-permute-start.4 = (bf16[4,12,16,128]{3,2,1,0:T(8,128)(2,1)}, bf16[4,12,16,128]{3,2,1,0:T(8,128)(2,1)S(1)}, u32[]{:S(2)}, u32[]{:S(2)}) collective-permute-start(bf16[4,12,16,128]{3,2,1,0:T(8,128)(2,1)} %constant_dynamic-slice_fusion.6), channel_id=1, source_target_pairs={{0,1},{1,0},{2,3},{3,2},{4,5},{5,4},{6,7},{7,6},{8,9},{9,8},{10,11... | collective-permute-start | bytes 589832 | tf_op jit(solution)/shard_map/ppermute | solution.py:256
  18.5 6.2 %collective-permute-start.3 = (bf16[4,20,16,128]{3,2,1,0:T(8,128)(2,1)S(1)}, bf16[4,20,16,128]{3,2,1,0:T(8,128)(2,1)S(1)}, u32[]{:S(2)}, u32[]{:S(2)}) collective-permute-start(bf16[4,20,16,128]{3,2,1,0:T(8,128)(2,1)S(1)} %constant_dynamic-update-slice_fusion.kept_ref), channel_id=1, source_target_pairs={{0,1},{1,0},{2,3},{3,2},{4,5},{5,4},{6,7},{7,6},{8,16},{9,17},{10,... | collective-permute-start | bytes 983048 | tf_op jit(solution)/shard_map/ppermute | solution.py:261
  24.7 1.0 %slice.17 = bf16[9,128,128]{2,1,0:T(8,128)(2,1)S(1)} slice(bf16[27,128,128]{2,1,0:T(8,128)(2,1)} %param.6), slice={[9:18], [0:128], [0:128]} | slice | bytes 589824 | tf_op jit(solution)/shard_map/slice | solution.py:190
  25.7 0.0 copy-done.1
  25.7 0.6 copy.20
  26.3 0.5 reshape.24.refs_0_.weight_ref
  26.9 1.1 %slice.19 = bf16[2,3,3,128,128]{4,3,2,1,0:T(8,128)(2,1)S(1)} slice(bf16[3,3,3,128,128]{4,3,2,1,0:T(8,128)(2,1)} %bitcast.30), slice={[0:3:2], [0:3:1], [0:3:1], [0:128:1], [0:128:1]} | slice | bytes 1179648 | tf_op jit(solution)/shard_map/slice | solution.py:191
  28.0 0.6 copy.21
  28.6 0.5 reshape.26.refs_2_.weight_ref
  29.1 0.0 copy-start.2
  29.1 0.6 copy-done.2
  29.8 0.1 copy.16.refs_1_.bias_ref
  29.9 0.2 copy.13
  30.2 0.0 collective-permute-done.4.other_ref
  30.2 0.8 %first_own.1 = (f32[10,128,128]{2,1,0:T(8,128)S(1)}, s32[8,128]{1,0:T(8,128)S(1)}) custom-call(bf16[4,20,16,128]{3,2,1,0:T(8,128)(2,1)S(1)} %constant_dynamic-update-slice_fusion.kept_ref, bf16[4,12,16,128]{3,2,1,0:T(8,128)(2,1)S(1)} %collective-permute-done.4.other_ref, bf16[384,384]{1,0:T(8,128)(2,1)S(1)} %bitcast.22, ...), custom_call_target="tpu_custom_call" | custom-call | flops 377487360 | bytes 4000000 | tf_op jit(solution)/shard_map/first_own/pallas_call | solution.py:220
  31.0 0.5 slice.20
  32.2 0.0 collective-permute-done.6.kept_ref
  32.2 0.4 collective-permute-start.7
  32.6 0.2 collective-permute-done.3.kept_ref
  32.8 0.7 %collective-permute-start.5 = (bf16[4,12,16,128]{3,2,1,0:T(8,128)(2,1)S(1)}, bf16[4,12,16,128]{3,2,1,0:T(8,128)(2,1)S(1)}, u32[]{:S(2)}, u32[]{:S(2)}) collective-permute-start(bf16[4,12,16,128]{3,2,1,0:T(8,128)(2,1)S(1)} %constant_dynamic-slice_fusion.5), channel_id=1, source_target_pairs={{0,1},{1,0},{2,3},{3,2},{4,5},{5,4},{6,7},{7,6},{8,9},{9,8},{10,11... | collective-permute-start | bytes 589832 | tf_op jit(solution)/shard_map/ppermute | solution.py:256
  33.5 0.3 collective-permute-done.7.other_ref
  33.8 0.8 %first_near.1.before_ref = f32[10,128,128]{2,1,0:T(8,128)S(1)} custom-call(bf16[4,20,16,128]{3,2,1,0:T(8,128)(2,1)S(1)} %collective-permute-done.6.kept_ref, bf16[4,12,16,128]{3,2,1,0:T(8,128)(2,1)S(1)} %collective-permute-done.7.other_ref, bf16[2,384,384]{2,1,0:T(8,128)(2,1)S(1)} %reshape.24.refs_0_.weight_ref, f32[10,128,128]{2,1,0:T(8,128)S(1)} %get-tuple-element.20.before_ref), custom_call_target="tpu_custom_call" | custom-call | flops 377487360 | bytes 4000000 | tf_op jit(solution)/shard_map/first_near/pallas_call | solution.py:220
  34.6 0.0 collective-permute-done.5.other_ref
  34.6 0.8 %first_far.1.plane_ref = bf16[10,128,128]{2,1,0:T(8,128)(2,1)S(1)} custom-call(bf16[4,20,16,128]{3,2,1,0:T(8,128)(2,1)S(1)} %collective-permute-done.3.kept_ref, bf16[4,12,16,128]{3,2,1,0:T(8,128)(2,1)S(1)} %collective-permute-done.5.other_ref, bf16[2,384,384]{2,1,0:T(8,128)(2,1)S(1)} %reshape.24.refs_0_.weight_ref, ...), custom_call_target="tpu_custom_call" | custom-call | flops 377487360 | bytes 4000000 | tf_op jit(solution)/shard_map/first_far/pallas_call | solution.py:220
  35.4 0.7 %far_share.1.refs_0_ = bf16[8,128,128]{2,1,0:T(8,128)(2,1)S(1)} custom-call(bf16[10,128,128]{2,1,0:T(8,128)(2,1)S(1)} %first_far.1.plane_ref, bf16[2,384,384]{2,1,0:T(8,128)(2,1)S(1)} %reshape.26.refs_2_.weight_ref), custom_call_target="tpu_custom_call" | custom-call | flops 301989888 | bytes 4000000 | tf_op jit(solution)/shard_map/far_share/pallas_call | solution.py:220
  36.1 5.7 %collective-permute-start.9 = (bf16[8,128,128]{2,1,0:T(8,128)(2,1)S(1)}, bf16[8,128,128]{2,1,0:T(8,128)(2,1)S(1)}, u32[]{:S(2)}, u32[]{:S(2)}) collective-permute-start(bf16[8,128,128]{2,1,0:T(8,128)(2,1)S(1)} %far_share.1.refs_0_), channel_id=1, source_target_pairs={{0,1},{1,0},{2,3},{3,2},{4,5},{5,4},{6,7},{7,6},{8,16},{9,17},{10,... | collective-permute-start | bytes 786440 | tf_op jit(solution)/shard_map/ppermute | solution.py:301
  41.8 0.7 %near_share.1 = bf16[8,128,128]{2,1,0:T(8,128)(2,1)S(1)} custom-call(bf16[10,128,128]{2,1,0:T(8,128)(2,1)S(1)} %first_far.1.plane_ref, bf16[2,384,384]{2,1,0:T(8,128)(2,1)S(1)} %reshape.26.refs_2_.weight_ref, bf16[8,128,128]{2,1,0:T(8,128)(2,1)S(1)} %far_share.1.refs_0_), custom_call_target="tpu_custom_call" | custom-call | flops 301989888 | bytes 4000000 | tf_op jit(solution)/shard_map/near_share/pallas_call | solution.py:220
  42.5 0.3 collective-permute-start.8
  42.8 1.0 %slice.21 = bf16[9,128,128]{2,1,0:T(8,128)(2,1)S(1)} slice(bf16[27,128,128]{2,1,0:T(8,128)(2,1)} %param.8), slice={[9:18], [0:128], [0:128]} | slice | bytes 589824 | tf_op jit(solution)/shard_map/slice | solution.py:190
  43.8 0.2 copy.18
  44.1 0.0 copy-start.3
  44.1 0.6 copy-done.3
  44.7 0.1 copy.19.bias_ref
  44.9 0.7 %second_own.1.own_ref = f32[8,128,128]{2,1,0:T(8,128)S(1)} custom-call(bf16[10,128,128]{2,1,0:T(8,128)(2,1)S(1)} %first_far.1.plane_ref, bf16[384,384]{1,0:T(8,128)(2,1)S(1)} %bitcast.21), custom_call_target="tpu_custom_call" | custom-call | flops 301989888 | bytes 4000000 | tf_op jit(solution)/shard_map/second_own/pallas_call | solution.py:220
  45.5 2.5 %collective-permute-done.9.far_ref = bf16[8,128,128]{2,1,0:T(8,128)(2,1)S(1)} collective-permute-done((bf16[8,128,128]{2,1,0:T(8,128)(2,1)S(1)}, bf16[8,128,128]{2,1,0:T(8,128)(2,1)S(1)}, u32[]{:S(2)}, u32[]{:S(2)}) %collective-permute-start.9) | collective-permute-done | bytes 262176 | tf_op jit(solution)/shard_map/ppermute | solution.py:301
  48.0 0.1 second_far.1.own_ref
  48.1 1.9 %collective-permute-done.8.near_ref = bf16[8,128,128]{2,1,0:T(8,128)(2,1)S(1)} collective-permute-done((bf16[8,128,128]{2,1,0:T(8,128)(2,1)S(1)}, bf16[8,128,128]{2,1,0:T(8,128)(2,1)S(1)}, u32[]{:S(2)}, u32[]{:S(2)}) %collective-permute-start.8) | collective-permute-done | bytes 262176 | tf_op jit(solution)/shard_map/ppermute | solution.py:302
  50.0 0.1 second_sum.1
  50.1 1.8 %collective-permute-start.10 = (bf16[2,8,16,128]{3,2,1,0:T(8,128)(2,1)S(1)}, bf16[2,8,16,128]{3,2,1,0:T(8,128)(2,1)S(1)}, u32[]{:S(2)}, u32[]{:S(2)}) collective-permute-start(bf16[2,8,16,128]{3,2,1,0:T(8,128)(2,1)S(1)} %get-tuple-element.22), channel_id=1, source_target_pairs={{0,2},{1,3},{2,4},{3,5},{4,6},{5,7},{6,0},{7,1},{8,10},{9,11},{10,... | collective-permute-start | bytes 196616 | tf_op jit(solution)/shard_map/ppermute | solution.py:314
  51.9 3.5 %collective-permute-start.11 = (bf16[2,8,16,128]{3,2,1,0:T(8,128)(2,1)S(1)}, bf16[2,8,16,128]{3,2,1,0:T(8,128)(2,1)S(1)}, u32[]{:S(2)}, u32[]{:S(2)}) collective-permute-start(bf16[2,8,16,128]{3,2,1,0:T(8,128)(2,1)S(1)} %get-tuple-element.23), channel_id=1, source_target_pairs={{0,4},{1,5},{2,6},{3,7},{4,0},{5,1},{6,2},{7,3},{8,12},{9,13},{10,... | collective-permute-start | bytes 196616 | tf_op jit(solution)/shard_map/ppermute | solution.py:314
  55.4 2.1 %collective-permute-start.12 = (bf16[2,8,16,128]{3,2,1,0:T(8,128)(2,1)S(1)}, bf16[2,8,16,128]{3,2,1,0:T(8,128)(2,1)S(1)}, u32[]{:S(2)}, u32[]{:S(2)}) collective-permute-start(bf16[2,8,16,128]{3,2,1,0:T(8,128)(2,1)S(1)} %get-tuple-element.24), channel_id=1, source_target_pairs={{0,6},{1,7},{2,0},{3,1},{4,2},{5,3},{6,4},{7,5},{8,14},{9,15},{10,... | collective-permute-start | bytes 196616 | tf_op jit(solution)/shard_map/ppermute | solution.py:314
  57.5 0.0 collective-permute-done.10.refs_1_
  57.6 1.4 %collective-permute-done.11.refs_2_ = bf16[2,8,16,128]{3,2,1,0:T(8,128)(2,1)S(1)} collective-permute-done((bf16[2,8,16,128]{3,2,1,0:T(8,128)(2,1)S(1)}, bf16[2,8,16,128]{3,2,1,0:T(8,128)(2,1)S(1)}, u32[]{:S(2)}, u32[]{:S(2)}) %collective-permute-start.11) | collective-permute-done | bytes 65568 | tf_op jit(solution)/shard_map/ppermute | solution.py:314
  58.9 1.2 %collective-permute-done.12.refs_3_ = bf16[2,8,16,128]{3,2,1,0:T(8,128)(2,1)S(1)} collective-permute-done((bf16[2,8,16,128]{3,2,1,0:T(8,128)(2,1)S(1)}, bf16[2,8,16,128]{3,2,1,0:T(8,128)(2,1)S(1)}, u32[]{:S(2)}, u32[]{:S(2)}) %collective-permute-start.12) | collective-permute-done | bytes 65568 | tf_op jit(solution)/shard_map/ppermute | solution.py:314
  60.2 3.2 %collective-permute-start.13 = (bf16[4,8,16,128]{3,2,1,0:T(8,128)(2,1)S(1)}, bf16[4,8,16,128]{3,2,1,0:T(8,128)(2,1)S(1)}, u32[]{:S(2)}, u32[]{:S(2)}) collective-permute-start(bf16[4,8,16,128]{3,2,1,0:T(8,128)(2,1)S(1)} %pad_maximum_fusion), channel_id=1, source_target_pairs={{0,1},{1,0},{2,3},{3,2},{4,5},{5,4},{6,7},{7,6},{8,9},{9,8},{10,11... | collective-permute-start | bytes 393224 | tf_op jit(solution)/shard_map/ppermute | solution.py:316
  63.4 1.0 %collective-permute-done.13.swapped_ref = bf16[4,8,16,128]{3,2,1,0:T(8,128)(2,1)S(1)} collective-permute-done((bf16[4,8,16,128]{3,2,1,0:T(8,128)(2,1)S(1)}, bf16[4,8,16,128]{3,2,1,0:T(8,128)(2,1)S(1)}, u32[]{:S(2)}, u32[]{:S(2)}) %collective-permute-start.13) | collective-permute-done | bytes 131104 | tf_op jit(solution)/shard_map/ppermute | solution.py:316
  64.4 0.8 %unpack_rows.1 = bf16[16,1,64,128]{3,2,1,0:T(8,128)(2,1)} custom-call(bf16[4,8,16,128]{3,2,1,0:T(8,128)(2,1)S(1)} %collective-permute-done.13.swapped_ref, bf16[2,8,16,128]{3,2,1,0:T(8,128)(2,1)S(1)} %get-tuple-element.21.refs_0_, bf16[2,8,16,128]{3,2,1,0:T(8,128)(2,1)S(1)} %collective-permute-done.10.refs_1_, ...), custom_call_target="tpu_custom_call" | custom-call | tf_op jit(solution)/shard_map/unpack_rows/pallas_call | solution.py:220
  (15 shorter events, 0.3 us)
Async XLA Ops:
  0.0 0.9 %copy-start = (bf16[16,1,64,128]{3,2,1,0:T(8,128)(2,1)S(1)}, bf16[16,1,64,128]{3,2,1,0:T(8,128)(2,1)}, u32[]{:S(2)}) copy-start(bf16[16,1,64,128]{3,2,1,0:T(8,128)(2,1)} %volume_ref.1) | copy-start | bytes 786436
  1.1 9.8 %collective-permute-start = (bf16[1,20,16,128]{3,2,1,0:T(8,128)(2,1)S(1)}, bf16[1,20,16,128]{3,2,1,0:T(8,128)(2,1)S(1)}, u32[]{:S(2)}, u32[]{:S(2)}) collective-permute-start(bf16[1,20,16,128]{3,2,1,0:T(8,128)(2,1)S(1)} %get-tuple-element.16), channel_id=1, source_target_pairs={{0,2},{1,3},{2,4},{3,5},{4,6},{5,7},{6,0},{7,1},{8,10},{9,11},{10,... | collective-permute-start | bytes 245768 | tf_op jit(solution)/shard_map/ppermute | solution.py:251
  4.2 7.3 %collective-permute-start.1 = (bf16[1,20,16,128]{3,2,1,0:T(8,128)(2,1)S(1)}, bf16[1,20,16,128]{3,2,1,0:T(8,128)(2,1)S(1)}, u32[]{:S(2)}, u32[]{:S(2)}) collective-permute-start(bf16[1,20,16,128]{3,2,1,0:T(8,128)(2,1)S(1)} %get-tuple-element.17), channel_id=1, source_target_pairs={{0,4},{1,5},{2,6},{3,7},{4,0},{5,1},{6,2},{7,3},{8,12},{9,13},{10,... | collective-permute-start | bytes 245768 | tf_op jit(solution)/shard_map/ppermute | solution.py:251
  8.4 6.8 %collective-permute-start.2 = (bf16[1,20,16,128]{3,2,1,0:T(8,128)(2,1)S(1)}, bf16[1,20,16,128]{3,2,1,0:T(8,128)(2,1)S(1)}, u32[]{:S(2)}, u32[]{:S(2)}) collective-permute-start(bf16[1,20,16,128]{3,2,1,0:T(8,128)(2,1)S(1)} %get-tuple-element.18), channel_id=1, source_target_pairs={{0,6},{1,7},{2,0},{3,1},{4,2},{5,3},{6,4},{7,5},{8,14},{9,15},{10,... | collective-permute-start | bytes 245768 | tf_op jit(solution)/shard_map/ppermute | solution.py:251
  10.8 14.9 %copy-start.1 = (bf16[27,128,128]{2,1,0:T(8,128)(2,1)S(1)}, bf16[27,128,128]{2,1,0:T(8,128)(2,1)}, u32[]{:S(2)}) copy-start(bf16[27,128,128]{2,1,0:T(8,128)(2,1)} %param.6) | copy-start | bytes 2654212
  15.2 17.0 %collective-permute-start.6 = (bf16[4,20,16,128]{3,2,1,0:T(8,128)(2,1)S(1)}, bf16[4,20,16,128]{3,2,1,0:T(8,128)(2,1)S(1)}, u32[]{:S(2)}, u32[]{:S(2)}) collective-permute-start(bf16[4,20,16,128]{3,2,1,0:T(8,128)(2,1)S(1)} %constant_dynamic-update-slice_fusion.kept_ref), channel_id=1, source_target_pairs={{0,8},{8,0},{16,24},{24,16},{32,40},{40,32},{48,56},{56,48},{64,72... | collective-permute-start | bytes 983048 | tf_op jit(solution)/shard_map/ppermute | solution.py:262
  17.3 12.9 %collective-permute-start.4 = (bf16[4,12,16,128]{3,2,1,0:T(8,128)(2,1)}, bf16[4,12,16,128]{3,2,1,0:T(8,128)(2,1)S(1)}, u32[]{:S(2)}, u32[]{:S(2)}) collective-permute-start(bf16[4,12,16,128]{3,2,1,0:T(8,128)(2,1)} %constant_dynamic-slice_fusion.6), channel_id=1, source_target_pairs={{0,1},{1,0},{2,3},{3,2},{4,5},{5,4},{6,7},{7,6},{8,9},{9,8},{10,11... | collective-permute-start | bytes 589832 | tf_op jit(solution)/shard_map/ppermute | solution.py:256
  18.5 14.3 %collective-permute-start.3 = (bf16[4,20,16,128]{3,2,1,0:T(8,128)(2,1)S(1)}, bf16[4,20,16,128]{3,2,1,0:T(8,128)(2,1)S(1)}, u32[]{:S(2)}, u32[]{:S(2)}) collective-permute-start(bf16[4,20,16,128]{3,2,1,0:T(8,128)(2,1)S(1)} %constant_dynamic-update-slice_fusion.kept_ref), channel_id=1, source_target_pairs={{0,1},{1,0},{2,3},{3,2},{4,5},{5,4},{6,7},{7,6},{8,16},{9,17},{10,... | collective-permute-start | bytes 983048 | tf_op jit(solution)/shard_map/ppermute | solution.py:261
  29.1 0.7 %copy-start.2 = (f32[128]{0:T(128)S(1)}, f32[128]{0:T(128)}, u32[]{:S(2)}) copy-start(f32[128]{0:T(128)} %param.7) | copy-start | bytes 1540
  32.2 1.5 %collective-permute-start.7 = (bf16[4,12,16,128]{3,2,1,0:T(8,128)(2,1)S(1)}, bf16[4,12,16,128]{3,2,1,0:T(8,128)(2,1)S(1)}, u32[]{:S(2)}, u32[]{:S(2)}) collective-permute-start(bf16[4,12,16,128]{3,2,1,0:T(8,128)(2,1)S(1)} %constant_dynamic-slice_fusion.4), channel_id=1, source_target_pairs={{0,1},{1,0},{2,3},{3,2},{4,5},{5,4},{6,7},{7,6},{8,9},{9,8},{10,11... | collective-permute-start | bytes 589832 | tf_op jit(solution)/shard_map/ppermute | solution.py:256
  32.8 1.8 %collective-permute-start.5 = (bf16[4,12,16,128]{3,2,1,0:T(8,128)(2,1)S(1)}, bf16[4,12,16,128]{3,2,1,0:T(8,128)(2,1)S(1)}, u32[]{:S(2)}, u32[]{:S(2)}) collective-permute-start(bf16[4,12,16,128]{3,2,1,0:T(8,128)(2,1)S(1)} %constant_dynamic-slice_fusion.5), channel_id=1, source_target_pairs={{0,1},{1,0},{2,3},{3,2},{4,5},{5,4},{6,7},{7,6},{8,9},{9,8},{10,11... | collective-permute-start | bytes 589832 | tf_op jit(solution)/shard_map/ppermute | solution.py:256
  36.1 11.9 %collective-permute-start.9 = (bf16[8,128,128]{2,1,0:T(8,128)(2,1)S(1)}, bf16[8,128,128]{2,1,0:T(8,128)(2,1)S(1)}, u32[]{:S(2)}, u32[]{:S(2)}) collective-permute-start(bf16[8,128,128]{2,1,0:T(8,128)(2,1)S(1)} %far_share.1.refs_0_), channel_id=1, source_target_pairs={{0,1},{1,0},{2,3},{3,2},{4,5},{5,4},{6,7},{7,6},{8,16},{9,17},{10,... | collective-permute-start | bytes 786440 | tf_op jit(solution)/shard_map/ppermute | solution.py:301
  42.5 7.5 %collective-permute-start.8 = (bf16[8,128,128]{2,1,0:T(8,128)(2,1)S(1)}, bf16[8,128,128]{2,1,0:T(8,128)(2,1)S(1)}, u32[]{:S(2)}, u32[]{:S(2)}) collective-permute-start(bf16[8,128,128]{2,1,0:T(8,128)(2,1)S(1)} %near_share.1), channel_id=1, source_target_pairs={{0,8},{8,0},{16,24},{24,16},{32,40},{40,32},{48,56},{56,48},{64,72... | collective-permute-start | bytes 786440 | tf_op jit(solution)/shard_map/ppermute | solution.py:302
  44.1 0.7 %copy-start.3 = (f32[128]{0:T(128)S(1)}, f32[128]{0:T(128)}, u32[]{:S(2)}) copy-start(f32[128]{0:T(128)} %param.9) | copy-start | bytes 1540
  50.1 7.4 %collective-permute-start.10 = (bf16[2,8,16,128]{3,2,1,0:T(8,128)(2,1)S(1)}, bf16[2,8,16,128]{3,2,1,0:T(8,128)(2,1)S(1)}, u32[]{:S(2)}, u32[]{:S(2)}) collective-permute-start(bf16[2,8,16,128]{3,2,1,0:T(8,128)(2,1)S(1)} %get-tuple-element.22), channel_id=1, source_target_pairs={{0,2},{1,3},{2,4},{3,5},{4,6},{5,7},{6,0},{7,1},{8,10},{9,11},{10,... | collective-permute-start | bytes 196616 | tf_op jit(solution)/shard_map/ppermute | solution.py:314
  51.9 7.0 %collective-permute-start.11 = (bf16[2,8,16,128]{3,2,1,0:T(8,128)(2,1)S(1)}, bf16[2,8,16,128]{3,2,1,0:T(8,128)(2,1)S(1)}, u32[]{:S(2)}, u32[]{:S(2)}) collective-permute-start(bf16[2,8,16,128]{3,2,1,0:T(8,128)(2,1)S(1)} %get-tuple-element.23), channel_id=1, source_target_pairs={{0,4},{1,5},{2,6},{3,7},{4,0},{5,1},{6,2},{7,3},{8,12},{9,13},{10,... | collective-permute-start | bytes 196616 | tf_op jit(solution)/shard_map/ppermute | solution.py:314
  55.4 4.7 %collective-permute-start.12 = (bf16[2,8,16,128]{3,2,1,0:T(8,128)(2,1)S(1)}, bf16[2,8,16,128]{3,2,1,0:T(8,128)(2,1)S(1)}, u32[]{:S(2)}, u32[]{:S(2)}) collective-permute-start(bf16[2,8,16,128]{3,2,1,0:T(8,128)(2,1)S(1)} %get-tuple-element.24), channel_id=1, source_target_pairs={{0,6},{1,7},{2,0},{3,1},{4,2},{5,3},{6,4},{7,5},{8,14},{9,15},{10,... | collective-permute-start | bytes 196616 | tf_op jit(solution)/shard_map/ppermute | solution.py:314
  60.2 4.2 %collective-permute-start.13 = (bf16[4,8,16,128]{3,2,1,0:T(8,128)(2,1)S(1)}, bf16[4,8,16,128]{3,2,1,0:T(8,128)(2,1)S(1)}, u32[]{:S(2)}, u32[]{:S(2)}) collective-permute-start(bf16[4,8,16,128]{3,2,1,0:T(8,128)(2,1)S(1)} %pad_maximum_fusion), channel_id=1, source_target_pairs={{0,1},{1,0},{2,3},{3,2},{4,5},{5,4},{6,7},{7,6},{8,9},{9,8},{10,11... | collective-permute-start | bytes 393224 | tf_op jit(solution)/shard_map/ppermute | solution.py:316

commit v11 on v7

--- a/solution.py
+++ b/solution.py
@@ -229,7 +229,7 @@
         )
         kept = jnp.zeros((groups, tall, width, lanes), BF16)
         kept = lax.dynamic_update_slice_in_dim(kept, pieces[0], group, 0)
-        for k in range(1, groups):
+        for k in sorted(range(1, groups), key=lambda k: abs(k - groups // 2)):
             got = lax.ppermute(pieces[k], "chan", ahead(k))
             kept = lax.dynamic_update_slice_in_dim(kept, got, (group + groups - k) % groups, 0)
 

time: 65.5 us -> 64.7 us (0.988)
  waiting for transfers between devices: 23.5 us -> 21.4 us
  starting transfers between devices: 25.7 us -> 27.3 us
    ppermute x3, waiting for transfers between devices: 6.4 us -> 4.6 us  [per_device(): got = lax.ppermute(pieces[k], 'chan', ahead(k))]
    ppermute x2, waiting for transfers between devices: 6.12 us -> 4.79 us  [halo(): lax.ppermute(array, 'space', near)]
    ppermute x3, starting transfers between devices: 3.24 us -> 4.26 us  [from_other_core(): return lax.ppermute(sent, 'chan', swap)]
where the time goes in v11:
time: 64.7 us; the launch traced here: 63.8 us
  starting transfers between devices  27.3 us (42%)
  waiting for transfers between devices  21.4 us (33%)
  local copies, waits for them, and re-layouts  8.79 us (14%)
  Pallas kernels  5.48 us (8%)
  between operations  0.88 us (1%)
    ppermute x3, starting transfers between devices, per_device(): got = lax.ppermute(pieces[k], 'chan', ahead(k))  10.6 us
    ppermute x2, waiting for transfers between devices, halo(): lax.ppermute(array, ('space', 'chan'), far)  8.9 us
    ppermute x3, starting transfers between devices, per_device(): lax.ppermute(blocks[k], 'chan', ahead(k))  8.32 us
    pallas_call x8, Pallas kernels, call(): pl.pallas_call(kernel, out_shape=shapes, in_specs=[VMEM] * len(inputs), o...  5.48 us
    ppermute x2, waiting for transfers between devices, halo(): lax.ppermute(array, 'space', near)  4.79 us
    ppermute x3, waiting for transfers between devices, per_device(): got = lax.ppermute(pieces[k], 'chan', ahead(k))  4.6 us
    ppermute x3, starting transfers between devices, from_other_core(): return lax.ppermute(sent, 'chan', swap)  4.26 us
    unnamed x14, local copies, waits for them, and re-layouts  3.57 us
  transfers between devices with their start and end apart: 14, of which 10 were waited for; matrix products, arithmetic and copies ran while one was open for 9% of the time, Pallas kernels for 5%

profile of v11, /device:TPU:31, one launch (start us, length us, event | category | flops | bytes accessed | tf_op | source)
XLA Modules:
  0.0 63.8 jit_solution(14904340697883270287)
XLA Ops:
  0.0 0.0 copy-start
  0.0 0.9 %copy-done = bf16[16,1,64,128]{3,2,1,0:T(8,128)(2,1)S(1)} copy-done((bf16[16,1,64,128]{3,2,1,0:T(8,128)(2,1)S(1)}, bf16[16,1,64,128]{3,2,1,0:T(8,128)(2,1)}, u32[]{:S(2)}) %copy-start) | copy-done | bytes 262168
  1.0 0.0 copy-start.2
  1.0 0.2 pack_rows.1
  1.1 7.0 %collective-permute-start = (bf16[1,20,16,128]{3,2,1,0:T(8,128)(2,1)S(1)}, bf16[1,20,16,128]{3,2,1,0:T(8,128)(2,1)S(1)}, u32[]{:S(2)}, u32[]{:S(2)}) collective-permute-start(bf16[1,20,16,128]{3,2,1,0:T(8,128)(2,1)S(1)} %get-tuple-element.16), channel_id=1, source_target_pairs={{0,4},{1,5},{2,6},{3,7},{4,0},{5,1},{6,2},{7,3},{8,12},{9,13},{10,... | collective-permute-start | bytes 245768 | tf_op jit(solution)/shard_map/ppermute | solution.py:233
  8.1 1.2 %collective-permute-start.1 = (bf16[1,20,16,128]{3,2,1,0:T(8,128)(2,1)S(1)}, bf16[1,20,16,128]{3,2,1,0:T(8,128)(2,1)S(1)}, u32[]{:S(2)}, u32[]{:S(2)}) collective-permute-start(bf16[1,20,16,128]{3,2,1,0:T(8,128)(2,1)S(1)} %get-tuple-element.17), channel_id=1, source_target_pairs={{0,2},{1,3},{2,4},{3,5},{4,6},{5,7},{6,0},{7,1},{8,10},{9,11},{10,... | collective-permute-start | bytes 245768 | tf_op jit(solution)/shard_map/ppermute | solution.py:233
  9.3 2.4 %collective-permute-start.2 = (bf16[1,20,16,128]{3,2,1,0:T(8,128)(2,1)S(1)}, bf16[1,20,16,128]{3,2,1,0:T(8,128)(2,1)S(1)}, u32[]{:S(2)}, u32[]{:S(2)}) collective-permute-start(bf16[1,20,16,128]{3,2,1,0:T(8,128)(2,1)S(1)} %get-tuple-element.18), channel_id=1, source_target_pairs={{0,6},{1,7},{2,0},{3,1},{4,2},{5,3},{6,4},{7,5},{8,14},{9,15},{10,... | collective-permute-start | bytes 245768 | tf_op jit(solution)/shard_map/ppermute | solution.py:233
  11.8 0.0 collective-permute-done
  11.8 2.3 %collective-permute-done.1 = bf16[1,20,16,128]{3,2,1,0:T(8,128)(2,1)S(1)} collective-permute-done((bf16[1,20,16,128]{3,2,1,0:T(8,128)(2,1)S(1)}, bf16[1,20,16,128]{3,2,1,0:T(8,128)(2,1)S(1)}, u32[]{:S(2)}, u32[]{:S(2)}) %collective-permute-start.1) | collective-permute-done | bytes 81952 | tf_op jit(solution)/shard_map/ppermute | solution.py:233
  14.1 2.3 %collective-permute-done.2 = bf16[1,20,16,128]{3,2,1,0:T(8,128)(2,1)S(1)} collective-permute-done((bf16[1,20,16,128]{3,2,1,0:T(8,128)(2,1)S(1)}, bf16[1,20,16,128]{3,2,1,0:T(8,128)(2,1)S(1)}, u32[]{:S(2)}, u32[]{:S(2)}) %collective-permute-start.2) | collective-permute-done | bytes 81952 | tf_op jit(solution)/shard_map/ppermute | solution.py:233
  16.4 0.6 collective-permute-start.6
  17.0 1.3 %collective-permute-start.4 = (bf16[4,12,16,128]{3,2,1,0:T(8,128)(2,1)S(1)}, bf16[4,12,16,128]{3,2,1,0:T(8,128)(2,1)S(1)}, u32[]{:S(2)}, u32[]{:S(2)}) collective-permute-start(bf16[4,12,16,128]{3,2,1,0:T(8,128)(2,1)S(1)} %constant_dynamic-slice_fusion.6), channel_id=1, source_target_pairs={{0,1},{1,0},{2,3},{3,2},{4,5},{5,4},{6,7},{7,6},{8,9},{9,8},{10,11... | collective-permute-start | bytes 589832 | tf_op jit(solution)/shard_map/ppermute | solution.py:238
  18.3 0.2 collective-permute-start.3
  18.5 0.0 copy-done.2
  18.5 0.7 %slice.17 = bf16[9,128,128]{2,1,0:T(8,128)(2,1)} slice(bf16[27,128,128]{2,1,0:T(8,128)(2,1)S(1)} %copy-done.2), slice={[9:18], [0:128], [0:128]} | slice | bytes 589824 | tf_op jit(solution)/shard_map/slice | solution.py:172
  19.3 0.6 copy.20
  19.9 0.5 reshape.24.later_ref.weight_ref
  20.4 0.0 copy-start.3
  20.5 0.6 %copy-done.3 = f32[128]{0:T(128)S(1)} copy-done((f32[128]{0:T(128)S(1)}, f32[128]{0:T(128)}, u32[]{:S(2)}) %copy-start.3) | copy-done | bytes 536
  21.1 0.1 copy.15.bias_ref
  21.2 1.2 %copy.13 = bf16[3,3,128,128]{2,0,3,1:T(4,128)(2,1)S(1)} copy(bf16[3,3,128,128]{3,2,1,0:T(8,128)(2,1)} %bitcast.27) | data formatting | bytes 589824 | tf_op jit(solution)/shard_map/squeeze | solution.py:172
  22.5 0.0 collective-permute-done.4.other_ref
  22.5 0.8 %first_own.1 = (f32[10,128,128]{2,1,0:T(8,128)S(1)}, s32[8,128]{1,0:T(8,128)S(1)}) custom-call(bf16[4,20,16,128]{3,2,1,0:T(8,128)(2,1)S(1)} %constant_dynamic-update-slice_fusion.kept_ref, bf16[4,12,16,128]{3,2,1,0:T(8,128)(2,1)S(1)} %collective-permute-done.4.other_ref, bf16[384,384]{1,0:T(8,128)(2,1)S(1)} %bitcast.22, ...), custom_call_target="tpu_custom_call" | custom-call | flops 377487360 | bytes 4000000 | tf_op jit(solution)/shard_map/first_own/pallas_call | solution.py:202
  23.3 0.5 slice.19
  24.5 0.3 collective-permute-done.6.kept_ref
  24.8 2.0 %collective-permute-start.7 = (bf16[4,12,16,128]{3,2,1,0:T(8,128)(2,1)S(1)}, bf16[4,12,16,128]{3,2,1,0:T(8,128)(2,1)S(1)}, u32[]{:S(2)}, u32[]{:S(2)}) collective-permute-start(bf16[4,12,16,128]{3,2,1,0:T(8,128)(2,1)S(1)} %constant_dynamic-slice_fusion.4), channel_id=1, source_target_pairs={{0,1},{1,0},{2,3},{3,2},{4,5},{5,4},{6,7},{7,6},{8,9},{9,8},{10,11... | collective-permute-start | bytes 589832 | tf_op jit(solution)/shard_map/ppermute | solution.py:238
  26.7 5.1 %collective-permute-done.3.kept_ref = bf16[4,20,16,128]{3,2,1,0:T(8,128)(2,1)S(1)} collective-permute-done((bf16[4,20,16,128]{3,2,1,0:T(8,128)(2,1)S(1)}, bf16[4,20,16,128]{3,2,1,0:T(8,128)(2,1)S(1)}, u32[]{:S(2)}, u32[]{:S(2)}) %collective-permute-start.3) | collective-permute-done | bytes 327712 | tf_op jit(solution)/shard_map/ppermute | solution.py:241
  31.8 1.0 %collective-permute-start.5 = (bf16[4,12,16,128]{3,2,1,0:T(8,128)(2,1)S(1)}, bf16[4,12,16,128]{3,2,1,0:T(8,128)(2,1)S(1)}, u32[]{:S(2)}, u32[]{:S(2)}) collective-permute-start(bf16[4,12,16,128]{3,2,1,0:T(8,128)(2,1)S(1)} %constant_dynamic-slice_fusion.5), channel_id=1, source_target_pairs={{0,1},{1,0},{2,3},{3,2},{4,5},{5,4},{6,7},{7,6},{8,9},{9,8},{10,11... | collective-permute-start | bytes 589832 | tf_op jit(solution)/shard_map/ppermute | solution.py:238
  32.8 0.0 collective-permute-done.7.other_ref
  32.8 0.8 %first_near.1.before_ref = f32[10,128,128]{2,1,0:T(8,128)S(1)} custom-call(bf16[4,20,16,128]{3,2,1,0:T(8,128)(2,1)S(1)} %collective-permute-done.6.kept_ref, bf16[4,12,16,128]{3,2,1,0:T(8,128)(2,1)S(1)} %collective-permute-done.7.other_ref, bf16[2,384,384]{2,1,0:T(8,128)(2,1)S(1)} %reshape.24.later_ref.weight_ref, ...), custom_call_target="tpu_custom_call" | custom-call | flops 377487360 | bytes 4000000 | tf_op jit(solution)/shard_map/first_near/pallas_call | solution.py:202
  33.6 0.3 collective-permute-done.5.other_ref
  33.9 0.8 %first_far.1.plane_ref = bf16[10,128,128]{2,1,0:T(8,128)(2,1)S(1)} custom-call(bf16[4,20,16,128]{3,2,1,0:T(8,128)(2,1)S(1)} %collective-permute-done.3.kept_ref, bf16[4,12,16,128]{3,2,1,0:T(8,128)(2,1)S(1)} %collective-permute-done.5.other_ref, bf16[2,384,384]{2,1,0:T(8,128)(2,1)S(1)} %reshape.24.later_ref.weight_ref, ...), custom_call_target="tpu_custom_call" | custom-call | flops 377487360 | bytes 4000000 | tf_op jit(solution)/shard_map/first_far/pallas_call | solution.py:202
  34.7 0.1 collective-permute-start.9
  34.8 0.4 collective-permute-start.8
  35.2 0.0 slice-start
  35.2 0.0 copy-start.1
  35.2 1.0 %slice-done = bf16[9,128,128]{2,1,0:T(8,128)(2,1)S(1)} async-done(((bf16[27,128,128]{2,1,0:T(8,128)(2,1)}), bf16[9,128,128]{2,1,0:T(8,128)(2,1)S(1)}, s32[]{:S(2)}) %slice-start) | async-done | bytes 294936 | tf_op jit(solution)/shard_map/slice | solution.py:172
  36.2 0.2 copy.18
  36.5 0.1 copy-done.1
  36.6 0.6 copy.21
  37.2 0.5 reshape.26.weight_ref
  37.7 0.0 copy-start.4
  37.8 0.6 %copy-done.4 = f32[128]{0:T(128)S(1)} copy-done((f32[128]{0:T(128)S(1)}, f32[128]{0:T(128)}, u32[]{:S(2)}) %copy-start.4) | copy-done | bytes 536
  38.4 0.1 copy.19.bias_ref
  38.5 0.7 %second_own.1.before_ref = f32[8,128,128]{2,1,0:T(8,128)S(1)} custom-call(bf16[10,128,128]{2,1,0:T(8,128)(2,1)S(1)} %first_far.1.plane_ref, bf16[384,384]{1,0:T(8,128)(2,1)S(1)} %bitcast.21), custom_call_target="tpu_custom_call" | custom-call | flops 301989888 | bytes 4000000 | tf_op jit(solution)/shard_map/second_own/pallas_call | solution.py:202
  39.2 4.5 %collective-permute-done.9.plane_ref = bf16[10,128,128]{2,1,0:T(8,128)(2,1)S(1)} collective-permute-done((bf16[10,128,128]{2,1,0:T(8,128)(2,1)S(1)}, bf16[10,128,128]{2,1,0:T(8,128)(2,1)S(1)}, u32[]{:S(2)}, u32[]{:S(2)}) %collective-permute-start.9) | collective-permute-done | bytes 327712 | tf_op jit(solution)/shard_map/ppermute | solution.py:241
  43.7 0.7 %second_near.1.before_ref = f32[8,128,128]{2,1,0:T(8,128)S(1)} custom-call(bf16[10,128,128]{2,1,0:T(8,128)(2,1)S(1)} %collective-permute-done.9.plane_ref, bf16[2,384,384]{2,1,0:T(8,128)(2,1)S(1)} %reshape.26.weight_ref, f32[8,128,128]{2,1,0:T(8,128)S(1)} %second_own.1.before_ref), custom_call_target="tpu_custom_call" | custom-call | flops 301989888 | bytes 4000000 | tf_op jit(solution)/shard_map/second_near/pallas_call | solution.py:202
  44.4 3.8 %collective-permute-done.8.plane_ref = bf16[10,128,128]{2,1,0:T(8,128)(2,1)S(1)} collective-permute-done((bf16[10,128,128]{2,1,0:T(8,128)(2,1)S(1)}, bf16[10,128,128]{2,1,0:T(8,128)(2,1)S(1)}, u32[]{:S(2)}, u32[]{:S(2)}) %collective-permute-start.8) | collective-permute-done | bytes 327712 | tf_op jit(solution)/shard_map/ppermute | solution.py:241
  48.2 0.7 %second_far.1 = (bf16[2,8,16,128]{3,2,1,0:T(8,128)(2,1)S(1)}, bf16[2,8,16,128]{3,2,1,0:T(8,128)(2,1)S(1)}, bf16[2,8,16,128]{3,2,1,0:T(8,128)(2,1)S(1)}, bf16[2,8,16,128]{3,2,1,0:T(8,128)(2,1)S(1)}) custom-call(bf16[10,128,128]{2,1,0:T(8,128)(2,1)S(1)} %collective-permute-done.8.plane_ref, bf16[2,384,384]{2,1,0:T(8,128)(2,1)S(1)} %reshape.26.weight_ref, ...), custom_call_target="tpu_custom_call" | custom-call | flops 301989888 | bytes 4000000 | tf_op jit(solution)/shard_map/second_far/pallas_call | solution.py:202
  48.9 1.4 %collective-permute-start.10 = (bf16[2,8,16,128]{3,2,1,0:T(8,128)(2,1)S(1)}, bf16[2,8,16,128]{3,2,1,0:T(8,128)(2,1)S(1)}, u32[]{:S(2)}, u32[]{:S(2)}) collective-permute-start(bf16[2,8,16,128]{3,2,1,0:T(8,128)(2,1)S(1)} %get-tuple-element.22), channel_id=1, source_target_pairs={{0,2},{1,3},{2,4},{3,5},{4,6},{5,7},{6,0},{7,1},{8,10},{9,11},{10,... | collective-permute-start | bytes 196616 | tf_op jit(solution)/shard_map/ppermute | solution.py:287
  50.3 4.5 %collective-permute-start.11 = (bf16[2,8,16,128]{3,2,1,0:T(8,128)(2,1)S(1)}, bf16[2,8,16,128]{3,2,1,0:T(8,128)(2,1)S(1)}, u32[]{:S(2)}, u32[]{:S(2)}) collective-permute-start(bf16[2,8,16,128]{3,2,1,0:T(8,128)(2,1)S(1)} %get-tuple-element.23), channel_id=1, source_target_pairs={{0,4},{1,5},{2,6},{3,7},{4,0},{5,1},{6,2},{7,3},{8,12},{9,13},{10,... | collective-permute-start | bytes 196616 | tf_op jit(solution)/shard_map/ppermute | solution.py:287
  54.8 2.5 %collective-permute-start.12 = (bf16[2,8,16,128]{3,2,1,0:T(8,128)(2,1)S(1)}, bf16[2,8,16,128]{3,2,1,0:T(8,128)(2,1)S(1)}, u32[]{:S(2)}, u32[]{:S(2)}) collective-permute-start(bf16[2,8,16,128]{3,2,1,0:T(8,128)(2,1)S(1)} %get-tuple-element.24), channel_id=1, source_target_pairs={{0,6},{1,7},{2,0},{3,1},{4,2},{5,3},{6,4},{7,5},{8,14},{9,15},{10,... | collective-permute-start | bytes 196616 | tf_op jit(solution)/shard_map/ppermute | solution.py:287
  57.2 0.0 collective-permute-done.10.refs_1_
  57.2 0.1 collective-permute-done.11.refs_2_
  57.3 1.7 %collective-permute-done.12.refs_3_ = bf16[2,8,16,128]{3,2,1,0:T(8,128)(2,1)S(1)} collective-permute-done((bf16[2,8,16,128]{3,2,1,0:T(8,128)(2,1)S(1)}, bf16[2,8,16,128]{3,2,1,0:T(8,128)(2,1)S(1)}, u32[]{:S(2)}, u32[]{:S(2)}) %collective-permute-start.12) | collective-permute-done | bytes 65568 | tf_op jit(solution)/shard_map/ppermute | solution.py:287
  59.1 2.9 %collective-permute-start.13 = (bf16[4,8,16,128]{3,2,1,0:T(8,128)(2,1)S(1)}, bf16[4,8,16,128]{3,2,1,0:T(8,128)(2,1)S(1)}, u32[]{:S(2)}, u32[]{:S(2)}) collective-permute-start(bf16[4,8,16,128]{3,2,1,0:T(8,128)(2,1)S(1)} %pad_maximum_fusion), channel_id=1, source_target_pairs={{0,1},{1,0},{2,3},{3,2},{4,5},{5,4},{6,7},{7,6},{8,9},{9,8},{10,11... | collective-permute-start | bytes 393224 | tf_op jit(solution)/shard_map/ppermute | solution.py:289
  62.0 1.0 %collective-permute-done.13.swapped_ref = bf16[4,8,16,128]{3,2,1,0:T(8,128)(2,1)S(1)} collective-permute-done((bf16[4,8,16,128]{3,2,1,0:T(8,128)(2,1)S(1)}, bf16[4,8,16,128]{3,2,1,0:T(8,128)(2,1)S(1)}, u32[]{:S(2)}, u32[]{:S(2)}) %collective-permute-start.13) | collective-permute-done | bytes 131104 | tf_op jit(solution)/shard_map/ppermute | solution.py:289
  63.0 0.8 %unpack_rows.1 = bf16[16,1,64,128]{3,2,1,0:T(8,128)(2,1)} custom-call(bf16[4,8,16,128]{3,2,1,0:T(8,128)(2,1)S(1)} %collective-permute-done.13.swapped_ref, bf16[2,8,16,128]{3,2,1,0:T(8,128)(2,1)S(1)} %get-tuple-element.21.refs_0_, bf16[2,8,16,128]{3,2,1,0:T(8,128)(2,1)S(1)} %collective-permute-done.10.refs_1_, ...), custom_call_target="tpu_custom_call" | custom-call | tf_op jit(solution)/shard_map/unpack_rows/pallas_call | solution.py:202
  (17 shorter events, 0.4 us)
Async XLA Ops:
  0.0 0.9 %copy-start = (bf16[16,1,64,128]{3,2,1,0:T(8,128)(2,1)S(1)}, bf16[16,1,64,128]{3,2,1,0:T(8,128)(2,1)}, u32[]{:S(2)}) copy-start(bf16[16,1,64,128]{3,2,1,0:T(8,128)(2,1)} %volume_ref.1) | copy-start | bytes 786436
  1.0 17.6 %copy-start.2 = (bf16[27,128,128]{2,1,0:T(8,128)(2,1)S(1)}, bf16[27,128,128]{2,1,0:T(8,128)(2,1)}, u32[]{:S(2)}) copy-start(bf16[27,128,128]{2,1,0:T(8,128)(2,1)} %param.6) | copy-start | bytes 2654212
  1.1 10.6 %collective-permute-start = (bf16[1,20,16,128]{3,2,1,0:T(8,128)(2,1)S(1)}, bf16[1,20,16,128]{3,2,1,0:T(8,128)(2,1)S(1)}, u32[]{:S(2)}, u32[]{:S(2)}) collective-permute-start(bf16[1,20,16,128]{3,2,1,0:T(8,128)(2,1)S(1)} %get-tuple-element.16), channel_id=1, source_target_pairs={{0,4},{1,5},{2,6},{3,7},{4,0},{5,1},{6,2},{7,3},{8,12},{9,13},{10,... | collective-permute-start | bytes 245768 | tf_op jit(solution)/shard_map/ppermute | solution.py:233
  8.1 6.0 %collective-permute-start.1 = (bf16[1,20,16,128]{3,2,1,0:T(8,128)(2,1)S(1)}, bf16[1,20,16,128]{3,2,1,0:T(8,128)(2,1)S(1)}, u32[]{:S(2)}, u32[]{:S(2)}) collective-permute-start(bf16[1,20,16,128]{3,2,1,0:T(8,128)(2,1)S(1)} %get-tuple-element.17), channel_id=1, source_target_pairs={{0,2},{1,3},{2,4},{3,5},{4,6},{5,7},{6,0},{7,1},{8,10},{9,11},{10,... | collective-permute-start | bytes 245768 | tf_op jit(solution)/shard_map/ppermute | solution.py:233
  9.3 7.1 %collective-permute-start.2 = (bf16[1,20,16,128]{3,2,1,0:T(8,128)(2,1)S(1)}, bf16[1,20,16,128]{3,2,1,0:T(8,128)(2,1)S(1)}, u32[]{:S(2)}, u32[]{:S(2)}) collective-permute-start(bf16[1,20,16,128]{3,2,1,0:T(8,128)(2,1)S(1)} %get-tuple-element.18), channel_id=1, source_target_pairs={{0,6},{1,7},{2,0},{3,1},{4,2},{5,3},{6,4},{7,5},{8,14},{9,15},{10,... | collective-permute-start | bytes 245768 | tf_op jit(solution)/shard_map/ppermute | solution.py:233
  16.4 8.3 %collective-permute-start.6 = (bf16[4,20,16,128]{3,2,1,0:T(8,128)(2,1)S(1)}, bf16[4,20,16,128]{3,2,1,0:T(8,128)(2,1)S(1)}, u32[]{:S(2)}, u32[]{:S(2)}) collective-permute-start(bf16[4,20,16,128]{3,2,1,0:T(8,128)(2,1)S(1)} %constant_dynamic-update-slice_fusion.kept_ref), channel_id=1, source_target_pairs={{0,8},{8,0},{16,24},{24,16},{32,40},{40,32},{48,56},{56,48},{64,72... | collective-permute-start | bytes 983048 | tf_op jit(solution)/shard_map/ppermute | solution.py:241
  17.0 5.5 %collective-permute-start.4 = (bf16[4,12,16,128]{3,2,1,0:T(8,128)(2,1)S(1)}, bf16[4,12,16,128]{3,2,1,0:T(8,128)(2,1)S(1)}, u32[]{:S(2)}, u32[]{:S(2)}) collective-permute-start(bf16[4,12,16,128]{3,2,1,0:T(8,128)(2,1)S(1)} %constant_dynamic-slice_fusion.6), channel_id=1, source_target_pairs={{0,1},{1,0},{2,3},{3,2},{4,5},{5,4},{6,7},{7,6},{8,9},{9,8},{10,11... | collective-permute-start | bytes 589832 | tf_op jit(solution)/shard_map/ppermute | solution.py:238
  18.3 13.5 %collective-permute-start.3 = (bf16[4,20,16,128]{3,2,1,0:T(8,128)(2,1)S(1)}, bf16[4,20,16,128]{3,2,1,0:T(8,128)(2,1)S(1)}, u32[]{:S(2)}, u32[]{:S(2)}) collective-permute-start(bf16[4,20,16,128]{3,2,1,0:T(8,128)(2,1)S(1)} %constant_dynamic-update-slice_fusion.kept_ref), channel_id=1, source_target_pairs={{0,1},{1,0},{2,3},{3,2},{4,5},{5,4},{6,7},{7,6},{8,16},{9,17},{10,... | collective-permute-start | bytes 983048 | tf_op jit(solution)/shard_map/ppermute | solution.py:241
  20.4 0.7 %copy-start.3 = (f32[128]{0:T(128)S(1)}, f32[128]{0:T(128)}, u32[]{:S(2)}) copy-start(f32[128]{0:T(128)} %param.7) | copy-start | bytes 1540
  24.8 8.0 %collective-permute-start.7 = (bf16[4,12,16,128]{3,2,1,0:T(8,128)(2,1)S(1)}, bf16[4,12,16,128]{3,2,1,0:T(8,128)(2,1)S(1)}, u32[]{:S(2)}, u32[]{:S(2)}) collective-permute-start(bf16[4,12,16,128]{3,2,1,0:T(8,128)(2,1)S(1)} %constant_dynamic-slice_fusion.4), channel_id=1, source_target_pairs={{0,1},{1,0},{2,3},{3,2},{4,5},{5,4},{6,7},{7,6},{8,9},{9,8},{10,11... | collective-permute-start | bytes 589832 | tf_op jit(solution)/shard_map/ppermute | solution.py:238
  31.8 2.0 %collective-permute-start.5 = (bf16[4,12,16,128]{3,2,1,0:T(8,128)(2,1)S(1)}, bf16[4,12,16,128]{3,2,1,0:T(8,128)(2,1)S(1)}, u32[]{:S(2)}, u32[]{:S(2)}) collective-permute-start(bf16[4,12,16,128]{3,2,1,0:T(8,128)(2,1)S(1)} %constant_dynamic-slice_fusion.5), channel_id=1, source_target_pairs={{0,1},{1,0},{2,3},{3,2},{4,5},{5,4},{6,7},{7,6},{8,9},{9,8},{10,11... | collective-permute-start | bytes 589832 | tf_op jit(solution)/shard_map/ppermute | solution.py:238
  34.7 9.0 %collective-permute-start.9 = (bf16[10,128,128]{2,1,0:T(8,128)(2,1)S(1)}, bf16[10,128,128]{2,1,0:T(8,128)(2,1)S(1)}, u32[]{:S(2)}, u32[]{:S(2)}) collective-permute-start(bf16[10,128,128]{2,1,0:T(8,128)(2,1)S(1)} %first_far.1.plane_ref), channel_id=1, source_target_pairs={{0,8},{8,0},{16,24},{24,16},{32,40},{40,32},{48,56},{56,48},{64,72... | collective-permute-start | bytes 983048 | tf_op jit(solution)/shard_map/ppermute | solution.py:241
  34.8 13.4 %collective-permute-start.8 = (bf16[10,128,128]{2,1,0:T(8,128)(2,1)S(1)}, bf16[10,128,128]{2,1,0:T(8,128)(2,1)S(1)}, u32[]{:S(2)}, u32[]{:S(2)}) collective-permute-start(bf16[10,128,128]{2,1,0:T(8,128)(2,1)S(1)} %first_far.1.plane_ref), channel_id=1, source_target_pairs={{0,1},{1,0},{2,3},{3,2},{4,5},{5,4},{6,7},{7,6},{8,16},{9,17},{10,... | collective-permute-start | bytes 983048 | tf_op jit(solution)/shard_map/ppermute | solution.py:241
  35.2 1.0 %slice-start = ((bf16[27,128,128]{2,1,0:T(8,128)(2,1)}), bf16[9,128,128]{2,1,0:T(8,128)(2,1)S(1)}, s32[]{:S(2)}) async-start(bf16[27,128,128]{2,1,0:T(8,128)(2,1)} %param.8), calls=%async_computation | async-start | bytes 589824 | tf_op jit(solution)/shard_map/slice | solution.py:172
  35.2 1.3 %copy-start.1 = (bf16[27,128,128]{2,1,0:T(8,128)(2,1)S(1)}, bf16[27,128,128]{2,1,0:T(8,128)(2,1)}, u32[]{:S(2)}) copy-start(bf16[27,128,128]{2,1,0:T(8,128)(2,1)} %param.8) | copy-start | bytes 2654212
  37.7 0.7 %copy-start.4 = (f32[128]{0:T(128)S(1)}, f32[128]{0:T(128)}, u32[]{:S(2)}) copy-start(f32[128]{0:T(128)} %param.9) | copy-start | bytes 1540
  48.9 8.3 %collective-permute-start.10 = (bf16[2,8,16,128]{3,2,1,0:T(8,128)(2,1)S(1)}, bf16[2,8,16,128]{3,2,1,0:T(8,128)(2,1)S(1)}, u32[]{:S(2)}, u32[]{:S(2)}) collective-permute-start(bf16[2,8,16,128]{3,2,1,0:T(8,128)(2,1)S(1)} %get-tuple-element.22), channel_id=1, source_target_pairs={{0,2},{1,3},{2,4},{3,5},{4,6},{5,7},{6,0},{7,1},{8,10},{9,11},{10,... | collective-permute-start | bytes 196616 | tf_op jit(solution)/shard_map/ppermute | solution.py:287
  50.3 7.0 %collective-permute-start.11 = (bf16[2,8,16,128]{3,2,1,0:T(8,128)(2,1)S(1)}, bf16[2,8,16,128]{3,2,1,0:T(8,128)(2,1)S(1)}, u32[]{:S(2)}, u32[]{:S(2)}) collective-permute-start(bf16[2,8,16,128]{3,2,1,0:T(8,128)(2,1)S(1)} %get-tuple-element.23), channel_id=1, source_target_pairs={{0,4},{1,5},{2,6},{3,7},{4,0},{5,1},{6,2},{7,3},{8,12},{9,13},{10,... | collective-permute-start | bytes 196616 | tf_op jit(solution)/shard_map/ppermute | solution.py:287
  54.8 4.3 %collective-permute-start.12 = (bf16[2,8,16,128]{3,2,1,0:T(8,128)(2,1)S(1)}, bf16[2,8,16,128]{3,2,1,0:T(8,128)(2,1)S(1)}, u32[]{:S(2)}, u32[]{:S(2)}) collective-permute-start(bf16[2,8,16,128]{3,2,1,0:T(8,128)(2,1)S(1)} %get-tuple-element.24), channel_id=1, source_target_pairs={{0,6},{1,7},{2,0},{3,1},{4,2},{5,3},{6,4},{7,5},{8,14},{9,15},{10,... | collective-permute-start | bytes 196616 | tf_op jit(solution)/shard_map/ppermute | solution.py:287
  59.1 3.9 %collective-permute-start.13 = (bf16[4,8,16,128]{3,2,1,0:T(8,128)(2,1)S(1)}, bf16[4,8,16,128]{3,2,1,0:T(8,128)(2,1)S(1)}, u32[]{:S(2)}, u32[]{:S(2)}) collective-permute-start(bf16[4,8,16,128]{3,2,1,0:T(8,128)(2,1)S(1)} %pad_maximum_fusion), channel_id=1, source_target_pairs={{0,1},{1,0},{2,3},{3,2},{4,5},{5,4},{6,7},{7,6},{8,9},{9,8},{10,11... | collective-permute-start | bytes 393224 | tf_op jit(solution)/shard_map/ppermute | solution.py:289

commit v12 on v11

--- a/solution.py
+++ b/solution.py
@@ -194,6 +194,8 @@
 
     far = [(i * chan + j, far_partner(i, j)) for i in range(space) for j in range(chan)]
 
+    order = sorted(range(1, groups), key=lambda k: abs(k - groups // 2))
+
     def ahead(k):
         return [(i, (i + CORES * k) % chan) for i in range(chan)]
 
@@ -229,7 +231,7 @@
         )
         kept = jnp.zeros((groups, tall, width, lanes), BF16)
         kept = lax.dynamic_update_slice_in_dim(kept, pieces[0], group, 0)
-        for k in sorted(range(1, groups), key=lambda k: abs(k - groups // 2)):
+        for k in order:
             got = lax.ppermute(pieces[k], "chan", ahead(k))
             kept = lax.dynamic_update_slice_in_dim(kept, got, (group + groups - k) % groups, 0)
 
@@ -284,8 +286,13 @@
             name="second_far",
         )
 
-        blocks = [blocks[0]] + [lax.ppermute(blocks[k], "chan", ahead(k)) for k in range(1, groups)]
-        theirs = jnp.stack([lax.dynamic_index_in_dim(b, 1 - core, 0, keepdims=False) for b in blocks])
+        blocks = list(blocks)
+        theirs = jnp.zeros((groups, rows, width, lanes), BF16)
+        for k in [0, *order]:
+            if k:
+                blocks[k] = lax.ppermute(blocks[k], "chan", ahead(k))
+            sent = lax.dynamic_index_in_dim(blocks[k], 1 - core, 0)
+            theirs = lax.dynamic_update_slice_in_dim(theirs, sent, k, 0)
         swapped = lax.ppermute(theirs, "chan", swap)
         return call(
             unpack_kernel,

time: 64.7 us -> 63.9 us (0.988)
  transfers between devices with their start and end apart: 14 -> 14, of which waited for: 10 -> 9; matrix products, arithmetic and copies ran while one was open for 9% -> 9% of each run, Pallas kernels for 5% -> 5%
where the time goes in v12:
time: 63.9 us; the launch traced here: 63.7 us
  starting transfers between devices  27.3 us (43%)
  waiting for transfers between devices  21.2 us (33%)
  local copies, waits for them, and re-layouts  8.83 us (14%)
  Pallas kernels  5.48 us (9%)
  between operations  0.88 us (1%)
    ppermute x3, starting transfers between devices, per_device(): got = lax.ppermute(pieces[k], 'chan', ahead(k))  10.6 us
    ppermute x2, waiting for transfers between devices, halo(): lax.ppermute(array, ('space', 'chan'), far)  8.9 us
    ppermute x3, starting transfers between devices, per_device(): blocks[k] = lax.ppermute(blocks[k], 'chan', ahead(k))  8.41 us
    pallas_call x8, Pallas kernels, call(): pl.pallas_call(kernel, out_shape=shapes, in_specs=[VMEM] * len(inputs), o...  5.48 us
    ppermute x2, waiting for transfers between devices, halo(): lax.ppermute(array, 'space', near)  4.79 us
    ppermute x3, waiting for transfers between devices, per_device(): got = lax.ppermute(pieces[k], 'chan', ahead(k))  4.6 us
    ppermute x3, starting transfers between devices, from_other_core(): return lax.ppermute(sent, 'chan', swap)  4.26 us
    unnamed x14, local copies, waits for them, and re-layouts  3.57 us
  transfers between devices with their start and end apart: 14, of which 9 were waited for; matrix products, arithmetic and copies ran while one was open for 9% of the time, Pallas kernels for 5%

profile of v12, /device:TPU:31, one launch (start us, length us, event | category | flops | bytes accessed | tf_op | source)
XLA Modules:
  0.0 63.7 jit_solution(1267755973729513896)
XLA Ops:
  0.0 0.0 copy-start
  0.0 0.9 %copy-done = bf16[16,1,64,128]{3,2,1,0:T(8,128)(2,1)S(1)} copy-done((bf16[16,1,64,128]{3,2,1,0:T(8,128)(2,1)S(1)}, bf16[16,1,64,128]{3,2,1,0:T(8,128)(2,1)}, u32[]{:S(2)}) %copy-start) | copy-done | bytes 262168
  1.0 0.0 copy-start.2
  1.0 0.2 pack_rows.1
  1.1 7.0 %collective-permute-start = (bf16[1,20,16,128]{3,2,1,0:T(8,128)(2,1)S(1)}, bf16[1,20,16,128]{3,2,1,0:T(8,128)(2,1)S(1)}, u32[]{:S(2)}, u32[]{:S(2)}) collective-permute-start(bf16[1,20,16,128]{3,2,1,0:T(8,128)(2,1)S(1)} %get-tuple-element.16), channel_id=1, source_target_pairs={{0,4},{1,5},{2,6},{3,7},{4,0},{5,1},{6,2},{7,3},{8,12},{9,13},{10,... | collective-permute-start | bytes 245768 | tf_op jit(solution)/shard_map/ppermute | solution.py:235
  8.1 1.2 %collective-permute-start.1 = (bf16[1,20,16,128]{3,2,1,0:T(8,128)(2,1)S(1)}, bf16[1,20,16,128]{3,2,1,0:T(8,128)(2,1)S(1)}, u32[]{:S(2)}, u32[]{:S(2)}) collective-permute-start(bf16[1,20,16,128]{3,2,1,0:T(8,128)(2,1)S(1)} %get-tuple-element.17), channel_id=1, source_target_pairs={{0,2},{1,3},{2,4},{3,5},{4,6},{5,7},{6,0},{7,1},{8,10},{9,11},{10,... | collective-permute-start | bytes 245768 | tf_op jit(solution)/shard_map/ppermute | solution.py:235
  9.3 2.4 %collective-permute-start.2 = (bf16[1,20,16,128]{3,2,1,0:T(8,128)(2,1)S(1)}, bf16[1,20,16,128]{3,2,1,0:T(8,128)(2,1)S(1)}, u32[]{:S(2)}, u32[]{:S(2)}) collective-permute-start(bf16[1,20,16,128]{3,2,1,0:T(8,128)(2,1)S(1)} %get-tuple-element.18), channel_id=1, source_target_pairs={{0,6},{1,7},{2,0},{3,1},{4,2},{5,3},{6,4},{7,5},{8,14},{9,15},{10,... | collective-permute-start | bytes 245768 | tf_op jit(solution)/shard_map/ppermute | solution.py:235
  11.8 0.0 collective-permute-done
  11.8 2.3 %collective-permute-done.1 = bf16[1,20,16,128]{3,2,1,0:T(8,128)(2,1)S(1)} collective-permute-done((bf16[1,20,16,128]{3,2,1,0:T(8,128)(2,1)S(1)}, bf16[1,20,16,128]{3,2,1,0:T(8,128)(2,1)S(1)}, u32[]{:S(2)}, u32[]{:S(2)}) %collective-permute-start.1) | collective-permute-done | bytes 81952 | tf_op jit(solution)/shard_map/ppermute | solution.py:235
  14.1 2.3 %collective-permute-done.2 = bf16[1,20,16,128]{3,2,1,0:T(8,128)(2,1)S(1)} collective-permute-done((bf16[1,20,16,128]{3,2,1,0:T(8,128)(2,1)S(1)}, bf16[1,20,16,128]{3,2,1,0:T(8,128)(2,1)S(1)}, u32[]{:S(2)}, u32[]{:S(2)}) %collective-permute-start.2) | collective-permute-done | bytes 81952 | tf_op jit(solution)/shard_map/ppermute | solution.py:235
  16.4 0.6 collective-permute-start.6
  17.0 1.3 %collective-permute-start.4 = (bf16[4,12,16,128]{3,2,1,0:T(8,128)(2,1)S(1)}, bf16[4,12,16,128]{3,2,1,0:T(8,128)(2,1)S(1)}, u32[]{:S(2)}, u32[]{:S(2)}) collective-permute-start(bf16[4,12,16,128]{3,2,1,0:T(8,128)(2,1)S(1)} %constant_dynamic-slice_fusion.3), channel_id=1, source_target_pairs={{0,1},{1,0},{2,3},{3,2},{4,5},{5,4},{6,7},{7,6},{8,9},{9,8},{10,11... | collective-permute-start | bytes 589832 | tf_op jit(solution)/shard_map/ppermute | solution.py:240
  18.3 0.2 collective-permute-start.3
  18.5 0.0 copy-done.2
  18.5 0.7 %slice.17 = bf16[9,128,128]{2,1,0:T(8,128)(2,1)} slice(bf16[27,128,128]{2,1,0:T(8,128)(2,1)S(1)} %copy-done.2), slice={[9:18], [0:128], [0:128]} | slice | bytes 589824 | tf_op jit(solution)/shard_map/slice | solution.py:172
  19.3 0.6 copy.20
  19.9 0.5 reshape.24.later_ref.weight_ref
  20.4 0.0 copy-start.3
  20.5 0.6 %copy-done.3 = f32[128]{0:T(128)S(1)} copy-done((f32[128]{0:T(128)S(1)}, f32[128]{0:T(128)}, u32[]{:S(2)}) %copy-start.3) | copy-done | bytes 536
  21.1 0.1 copy.15.bias_ref
  21.2 1.2 %copy.13 = bf16[3,3,128,128]{2,0,3,1:T(4,128)(2,1)S(1)} copy(bf16[3,3,128,128]{3,2,1,0:T(8,128)(2,1)} %bitcast.27) | data formatting | bytes 589824 | tf_op jit(solution)/shard_map/squeeze | solution.py:172
  22.5 0.0 collective-permute-done.4.other_ref
  22.5 0.8 %first_own.1 = (f32[10,128,128]{2,1,0:T(8,128)S(1)}, s32[8,128]{1,0:T(8,128)S(1)}) custom-call(bf16[4,20,16,128]{3,2,1,0:T(8,128)(2,1)S(1)} %constant_dynamic-update-slice_fusion.kept_ref, bf16[4,12,16,128]{3,2,1,0:T(8,128)(2,1)S(1)} %collective-permute-done.4.other_ref, bf16[384,384]{1,0:T(8,128)(2,1)S(1)} %bitcast.22, ...), custom_call_target="tpu_custom_call" | custom-call | flops 377487360 | bytes 4000000 | tf_op jit(solution)/shard_map/first_own/pallas_call | solution.py:204
  23.3 0.5 slice.19
  24.5 0.3 collective-permute-done.6.kept_ref
  24.8 2.0 %collective-permute-start.7 = (bf16[4,12,16,128]{3,2,1,0:T(8,128)(2,1)S(1)}, bf16[4,12,16,128]{3,2,1,0:T(8,128)(2,1)S(1)}, u32[]{:S(2)}, u32[]{:S(2)}) collective-permute-start(bf16[4,12,16,128]{3,2,1,0:T(8,128)(2,1)S(1)} %constant_dynamic-slice_fusion.1), channel_id=1, source_target_pairs={{0,1},{1,0},{2,3},{3,2},{4,5},{5,4},{6,7},{7,6},{8,9},{9,8},{10,11... | collective-permute-start | bytes 589832 | tf_op jit(solution)/shard_map/ppermute | solution.py:240
  26.7 5.1 %collective-permute-done.3.kept_ref = bf16[4,20,16,128]{3,2,1,0:T(8,128)(2,1)S(1)} collective-permute-done((bf16[4,20,16,128]{3,2,1,0:T(8,128)(2,1)S(1)}, bf16[4,20,16,128]{3,2,1,0:T(8,128)(2,1)S(1)}, u32[]{:S(2)}, u32[]{:S(2)}) %collective-permute-start.3) | collective-permute-done | bytes 327712 | tf_op jit(solution)/shard_map/ppermute | solution.py:243
  31.8 1.0 %collective-permute-start.5 = (bf16[4,12,16,128]{3,2,1,0:T(8,128)(2,1)S(1)}, bf16[4,12,16,128]{3,2,1,0:T(8,128)(2,1)S(1)}, u32[]{:S(2)}, u32[]{:S(2)}) collective-permute-start(bf16[4,12,16,128]{3,2,1,0:T(8,128)(2,1)S(1)} %constant_dynamic-slice_fusion.2), channel_id=1, source_target_pairs={{0,1},{1,0},{2,3},{3,2},{4,5},{5,4},{6,7},{7,6},{8,9},{9,8},{10,11... | collective-permute-start | bytes 589832 | tf_op jit(solution)/shard_map/ppermute | solution.py:240
  32.8 0.0 collective-permute-done.7.other_ref
  32.8 0.8 %first_near.1.before_ref = f32[10,128,128]{2,1,0:T(8,128)S(1)} custom-call(bf16[4,20,16,128]{3,2,1,0:T(8,128)(2,1)S(1)} %collective-permute-done.6.kept_ref, bf16[4,12,16,128]{3,2,1,0:T(8,128)(2,1)S(1)} %collective-permute-done.7.other_ref, bf16[2,384,384]{2,1,0:T(8,128)(2,1)S(1)} %reshape.24.later_ref.weight_ref, ...), custom_call_target="tpu_custom_call" | custom-call | flops 377487360 | bytes 4000000 | tf_op jit(solution)/shard_map/first_near/pallas_call | solution.py:204
  33.6 0.3 collective-permute-done.5.other_ref
  33.9 0.8 %first_far.1.plane_ref = bf16[10,128,128]{2,1,0:T(8,128)(2,1)S(1)} custom-call(bf16[4,20,16,128]{3,2,1,0:T(8,128)(2,1)S(1)} %collective-permute-done.3.kept_ref, bf16[4,12,16,128]{3,2,1,0:T(8,128)(2,1)S(1)} %collective-permute-done.5.other_ref, bf16[2,384,384]{2,1,0:T(8,128)(2,1)S(1)} %reshape.24.later_ref.weight_ref, ...), custom_call_target="tpu_custom_call" | custom-call | flops 377487360 | bytes 4000000 | tf_op jit(solution)/shard_map/first_far/pallas_call | solution.py:204
  34.7 0.1 collective-permute-start.9
  34.8 0.4 collective-permute-start.8
  35.2 0.0 slice-start
  35.2 0.0 copy-start.1
  35.2 1.0 %slice-done = bf16[9,128,128]{2,1,0:T(8,128)(2,1)S(1)} async-done(((bf16[27,128,128]{2,1,0:T(8,128)(2,1)}), bf16[9,128,128]{2,1,0:T(8,128)(2,1)S(1)}, s32[]{:S(2)}) %slice-start) | async-done | bytes 294936 | tf_op jit(solution)/shard_map/slice | solution.py:172
  36.2 0.2 copy.18
  36.5 0.1 copy-done.1
  36.6 0.6 copy.21
  37.2 0.5 reshape.26.weight_ref
  37.7 0.0 copy-start.4
  37.8 0.6 %copy-done.4 = f32[128]{0:T(128)S(1)} copy-done((f32[128]{0:T(128)S(1)}, f32[128]{0:T(128)}, u32[]{:S(2)}) %copy-start.4) | copy-done | bytes 536
  38.4 0.1 copy.19.bias_ref
  38.5 0.7 %second_own.1.before_ref = f32[8,128,128]{2,1,0:T(8,128)S(1)} custom-call(bf16[10,128,128]{2,1,0:T(8,128)(2,1)S(1)} %first_far.1.plane_ref, bf16[384,384]{1,0:T(8,128)(2,1)S(1)} %bitcast.21), custom_call_target="tpu_custom_call" | custom-call | flops 301989888 | bytes 4000000 | tf_op jit(solution)/shard_map/second_own/pallas_call | solution.py:204
  39.2 4.5 %collective-permute-done.9.plane_ref = bf16[10,128,128]{2,1,0:T(8,128)(2,1)S(1)} collective-permute-done((bf16[10,128,128]{2,1,0:T(8,128)(2,1)S(1)}, bf16[10,128,128]{2,1,0:T(8,128)(2,1)S(1)}, u32[]{:S(2)}, u32[]{:S(2)}) %collective-permute-start.9) | collective-permute-done | bytes 327712 | tf_op jit(solution)/shard_map/ppermute | solution.py:243
  43.7 0.7 %second_near.1.before_ref = f32[8,128,128]{2,1,0:T(8,128)S(1)} custom-call(bf16[10,128,128]{2,1,0:T(8,128)(2,1)S(1)} %collective-permute-done.9.plane_ref, bf16[2,384,384]{2,1,0:T(8,128)(2,1)S(1)} %reshape.26.weight_ref, f32[8,128,128]{2,1,0:T(8,128)S(1)} %second_own.1.before_ref), custom_call_target="tpu_custom_call" | custom-call | flops 301989888 | bytes 4000000 | tf_op jit(solution)/shard_map/second_near/pallas_call | solution.py:204
  44.4 3.8 %collective-permute-done.8.plane_ref = bf16[10,128,128]{2,1,0:T(8,128)(2,1)S(1)} collective-permute-done((bf16[10,128,128]{2,1,0:T(8,128)(2,1)S(1)}, bf16[10,128,128]{2,1,0:T(8,128)(2,1)S(1)}, u32[]{:S(2)}, u32[]{:S(2)}) %collective-permute-start.8) | collective-permute-done | bytes 327712 | tf_op jit(solution)/shard_map/ppermute | solution.py:243
  48.2 0.7 %second_far.1 = (bf16[2,8,16,128]{3,2,1,0:T(8,128)(2,1)S(1)}, bf16[2,8,16,128]{3,2,1,0:T(8,128)(2,1)S(1)}, bf16[2,8,16,128]{3,2,1,0:T(8,128)(2,1)S(1)}, bf16[2,8,16,128]{3,2,1,0:T(8,128)(2,1)S(1)}) custom-call(bf16[10,128,128]{2,1,0:T(8,128)(2,1)S(1)} %collective-permute-done.8.plane_ref, bf16[2,384,384]{2,1,0:T(8,128)(2,1)S(1)} %reshape.26.weight_ref, ...), custom_call_target="tpu_custom_call" | custom-call | flops 301989888 | bytes 4000000 | tf_op jit(solution)/shard_map/second_far/pallas_call | solution.py:204
  48.9 4.8 %collective-permute-start.10 = (bf16[2,8,16,128]{3,2,1,0:T(8,128)(2,1)S(1)}, bf16[2,8,16,128]{3,2,1,0:T(8,128)(2,1)S(1)}, u32[]{:S(2)}, u32[]{:S(2)}) collective-permute-start(bf16[2,8,16,128]{3,2,1,0:T(8,128)(2,1)S(1)} %get-tuple-element.22), channel_id=1, source_target_pairs={{0,4},{1,5},{2,6},{3,7},{4,0},{5,1},{6,2},{7,3},{8,12},{9,13},{10,... | collective-permute-start | bytes 196616 | tf_op jit(solution)/shard_map/ppermute | solution.py:293
  53.7 1.2 %collective-permute-start.11 = (bf16[2,8,16,128]{3,2,1,0:T(8,128)(2,1)S(1)}, bf16[2,8,16,128]{3,2,1,0:T(8,128)(2,1)S(1)}, u32[]{:S(2)}, u32[]{:S(2)}) collective-permute-start(bf16[2,8,16,128]{3,2,1,0:T(8,128)(2,1)S(1)} %get-tuple-element.23), channel_id=1, source_target_pairs={{0,2},{1,3},{2,4},{3,5},{4,6},{5,7},{6,0},{7,1},{8,10},{9,11},{10,... | collective-permute-start | bytes 196616 | tf_op jit(solution)/shard_map/ppermute | solution.py:293
  54.9 2.5 %collective-permute-start.12 = (bf16[2,8,16,128]{3,2,1,0:T(8,128)(2,1)S(1)}, bf16[2,8,16,128]{3,2,1,0:T(8,128)(2,1)S(1)}, u32[]{:S(2)}, u32[]{:S(2)}) collective-permute-start(bf16[2,8,16,128]{3,2,1,0:T(8,128)(2,1)S(1)} %get-tuple-element.24), channel_id=1, source_target_pairs={{0,6},{1,7},{2,0},{3,1},{4,2},{5,3},{6,4},{7,5},{8,14},{9,15},{10,... | collective-permute-start | bytes 196616 | tf_op jit(solution)/shard_map/ppermute | solution.py:293
  57.3 0.0 collective-permute-done.10.refs_2_
  57.4 1.6 %collective-permute-done.11.refs_1_ = bf16[2,8,16,128]{3,2,1,0:T(8,128)(2,1)S(1)} collective-permute-done((bf16[2,8,16,128]{3,2,1,0:T(8,128)(2,1)S(1)}, bf16[2,8,16,128]{3,2,1,0:T(8,128)(2,1)S(1)}, u32[]{:S(2)}, u32[]{:S(2)}) %collective-permute-start.11) | collective-permute-done | bytes 65568 | tf_op jit(solution)/shard_map/ppermute | solution.py:293
  59.0 0.0 collective-permute-done.12.refs_3_
  59.0 2.8 %collective-permute-start.13 = (bf16[4,8,16,128]{3,2,1,0:T(8,128)(2,1)S(1)}, bf16[4,8,16,128]{3,2,1,0:T(8,128)(2,1)S(1)}, u32[]{:S(2)}, u32[]{:S(2)}) collective-permute-start(bf16[4,8,16,128]{3,2,1,0:T(8,128)(2,1)S(1)} %dynamic-slice_dynamic-update-slice_fusion), channel_id=1, source_target_pairs={{0,1},{1,0},{2,3},{3,2},{4,5},{5,4},{6,7},{7,6},{8,9},{9,8},{10,11... | collective-permute-start | bytes 393224 | tf_op jit(solution)/shard_map/ppermute | solution.py:296
  61.8 1.0 %collective-permute-done.13.swapped_ref = bf16[4,8,16,128]{3,2,1,0:T(8,128)(2,1)S(1)} collective-permute-done((bf16[4,8,16,128]{3,2,1,0:T(8,128)(2,1)S(1)}, bf16[4,8,16,128]{3,2,1,0:T(8,128)(2,1)S(1)}, u32[]{:S(2)}, u32[]{:S(2)}) %collective-permute-start.13) | collective-permute-done | bytes 131104 | tf_op jit(solution)/shard_map/ppermute | solution.py:296
  62.8 0.8 %unpack_rows.1 = bf16[16,1,64,128]{3,2,1,0:T(8,128)(2,1)} custom-call(bf16[4,8,16,128]{3,2,1,0:T(8,128)(2,1)S(1)} %collective-permute-done.13.swapped_ref, bf16[2,8,16,128]{3,2,1,0:T(8,128)(2,1)S(1)} %get-tuple-element.21.refs_0_, bf16[2,8,16,128]{3,2,1,0:T(8,128)(2,1)S(1)} %collective-permute-done.11.refs_1_, ...), custom_call_target="tpu_custom_call" | custom-call | tf_op jit(solution)/shard_map/unpack_rows/pallas_call | solution.py:204
  (17 shorter events, 0.4 us)
Async XLA Ops:
  0.0 0.9 %copy-start = (bf16[16,1,64,128]{3,2,1,0:T(8,128)(2,1)S(1)}, bf16[16,1,64,128]{3,2,1,0:T(8,128)(2,1)}, u32[]{:S(2)}) copy-start(bf16[16,1,64,128]{3,2,1,0:T(8,128)(2,1)} %volume_ref.1) | copy-start | bytes 786436
  1.0 17.6 %copy-start.2 = (bf16[27,128,128]{2,1,0:T(8,128)(2,1)S(1)}, bf16[27,128,128]{2,1,0:T(8,128)(2,1)}, u32[]{:S(2)}) copy-start(bf16[27,128,128]{2,1,0:T(8,128)(2,1)} %param.6) | copy-start | bytes 2654212
  1.1 10.6 %collective-permute-start = (bf16[1,20,16,128]{3,2,1,0:T(8,128)(2,1)S(1)}, bf16[1,20,16,128]{3,2,1,0:T(8,128)(2,1)S(1)}, u32[]{:S(2)}, u32[]{:S(2)}) collective-permute-start(bf16[1,20,16,128]{3,2,1,0:T(8,128)(2,1)S(1)} %get-tuple-element.16), channel_id=1, source_target_pairs={{0,4},{1,5},{2,6},{3,7},{4,0},{5,1},{6,2},{7,3},{8,12},{9,13},{10,... | collective-permute-start | bytes 245768 | tf_op jit(solution)/shard_map/ppermute | solution.py:235
  8.1 6.0 %collective-permute-start.1 = (bf16[1,20,16,128]{3,2,1,0:T(8,128)(2,1)S(1)}, bf16[1,20,16,128]{3,2,1,0:T(8,128)(2,1)S(1)}, u32[]{:S(2)}, u32[]{:S(2)}) collective-permute-start(bf16[1,20,16,128]{3,2,1,0:T(8,128)(2,1)S(1)} %get-tuple-element.17), channel_id=1, source_target_pairs={{0,2},{1,3},{2,4},{3,5},{4,6},{5,7},{6,0},{7,1},{8,10},{9,11},{10,... | collective-permute-start | bytes 245768 | tf_op jit(solution)/shard_map/ppermute | solution.py:235
  9.3 7.1 %collective-permute-start.2 = (bf16[1,20,16,128]{3,2,1,0:T(8,128)(2,1)S(1)}, bf16[1,20,16,128]{3,2,1,0:T(8,128)(2,1)S(1)}, u32[]{:S(2)}, u32[]{:S(2)}) collective-permute-start(bf16[1,20,16,128]{3,2,1,0:T(8,128)(2,1)S(1)} %get-tuple-element.18), channel_id=1, source_target_pairs={{0,6},{1,7},{2,0},{3,1},{4,2},{5,3},{6,4},{7,5},{8,14},{9,15},{10,... | collective-permute-start | bytes 245768 | tf_op jit(solution)/shard_map/ppermute | solution.py:235
  16.4 8.3 %collective-permute-start.6 = (bf16[4,20,16,128]{3,2,1,0:T(8,128)(2,1)S(1)}, bf16[4,20,16,128]{3,2,1,0:T(8,128)(2,1)S(1)}, u32[]{:S(2)}, u32[]{:S(2)}) collective-permute-start(bf16[4,20,16,128]{3,2,1,0:T(8,128)(2,1)S(1)} %constant_dynamic-update-slice_fusion.kept_ref), channel_id=1, source_target_pairs={{0,8},{8,0},{16,24},{24,16},{32,40},{40,32},{48,56},{56,48},{64,72... | collective-permute-start | bytes 983048 | tf_op jit(solution)/shard_map/ppermute | solution.py:243
  17.0 5.5 %collective-permute-start.4 = (bf16[4,12,16,128]{3,2,1,0:T(8,128)(2,1)S(1)}, bf16[4,12,16,128]{3,2,1,0:T(8,128)(2,1)S(1)}, u32[]{:S(2)}, u32[]{:S(2)}) collective-permute-start(bf16[4,12,16,128]{3,2,1,0:T(8,128)(2,1)S(1)} %constant_dynamic-slice_fusion.3), channel_id=1, source_target_pairs={{0,1},{1,0},{2,3},{3,2},{4,5},{5,4},{6,7},{7,6},{8,9},{9,8},{10,11... | collective-permute-start | bytes 589832 | tf_op jit(solution)/shard_map/ppermute | solution.py:240
  18.3 13.5 %collective-permute-start.3 = (bf16[4,20,16,128]{3,2,1,0:T(8,128)(2,1)S(1)}, bf16[4,20,16,128]{3,2,1,0:T(8,128)(2,1)S(1)}, u32[]{:S(2)}, u32[]{:S(2)}) collective-permute-start(bf16[4,20,16,128]{3,2,1,0:T(8,128)(2,1)S(1)} %constant_dynamic-update-slice_fusion.kept_ref), channel_id=1, source_target_pairs={{0,1},{1,0},{2,3},{3,2},{4,5},{5,4},{6,7},{7,6},{8,16},{9,17},{10,... | collective-permute-start | bytes 983048 | tf_op jit(solution)/shard_map/ppermute | solution.py:243
  20.4 0.7 %copy-start.3 = (f32[128]{0:T(128)S(1)}, f32[128]{0:T(128)}, u32[]{:S(2)}) copy-start(f32[128]{0:T(128)} %param.7) | copy-start | bytes 1540
  24.8 8.0 %collective-permute-start.7 = (bf16[4,12,16,128]{3,2,1,0:T(8,128)(2,1)S(1)}, bf16[4,12,16,128]{3,2,1,0:T(8,128)(2,1)S(1)}, u32[]{:S(2)}, u32[]{:S(2)}) collective-permute-start(bf16[4,12,16,128]{3,2,1,0:T(8,128)(2,1)S(1)} %constant_dynamic-slice_fusion.1), channel_id=1, source_target_pairs={{0,1},{1,0},{2,3},{3,2},{4,5},{5,4},{6,7},{7,6},{8,9},{9,8},{10,11... | collective-permute-start | bytes 589832 | tf_op jit(solution)/shard_map/ppermute | solution.py:240
  31.8 2.0 %collective-permute-start.5 = (bf16[4,12,16,128]{3,2,1,0:T(8,128)(2,1)S(1)}, bf16[4,12,16,128]{3,2,1,0:T(8,128)(2,1)S(1)}, u32[]{:S(2)}, u32[]{:S(2)}) collective-permute-start(bf16[4,12,16,128]{3,2,1,0:T(8,128)(2,1)S(1)} %constant_dynamic-slice_fusion.2), channel_id=1, source_target_pairs={{0,1},{1,0},{2,3},{3,2},{4,5},{5,4},{6,7},{7,6},{8,9},{9,8},{10,11... | collective-permute-start | bytes 589832 | tf_op jit(solution)/shard_map/ppermute | solution.py:240
  34.7 9.0 %collective-permute-start.9 = (bf16[10,128,128]{2,1,0:T(8,128)(2,1)S(1)}, bf16[10,128,128]{2,1,0:T(8,128)(2,1)S(1)}, u32[]{:S(2)}, u32[]{:S(2)}) collective-permute-start(bf16[10,128,128]{2,1,0:T(8,128)(2,1)S(1)} %first_far.1.plane_ref), channel_id=1, source_target_pairs={{0,8},{8,0},{16,24},{24,16},{32,40},{40,32},{48,56},{56,48},{64,72... | collective-permute-start | bytes 983048 | tf_op jit(solution)/shard_map/ppermute | solution.py:243
  34.8 13.4 %collective-permute-start.8 = (bf16[10,128,128]{2,1,0:T(8,128)(2,1)S(1)}, bf16[10,128,128]{2,1,0:T(8,128)(2,1)S(1)}, u32[]{:S(2)}, u32[]{:S(2)}) collective-permute-start(bf16[10,128,128]{2,1,0:T(8,128)(2,1)S(1)} %first_far.1.plane_ref), channel_id=1, source_target_pairs={{0,1},{1,0},{2,3},{3,2},{4,5},{5,4},{6,7},{7,6},{8,16},{9,17},{10,... | collective-permute-start | bytes 983048 | tf_op jit(solution)/shard_map/ppermute | solution.py:243
  35.2 1.0 %slice-start = ((bf16[27,128,128]{2,1,0:T(8,128)(2,1)}), bf16[9,128,128]{2,1,0:T(8,128)(2,1)S(1)}, s32[]{:S(2)}) async-start(bf16[27,128,128]{2,1,0:T(8,128)(2,1)} %param.8), calls=%async_computation | async-start | bytes 589824 | tf_op jit(solution)/shard_map/slice | solution.py:172
  35.2 1.3 %copy-start.1 = (bf16[27,128,128]{2,1,0:T(8,128)(2,1)S(1)}, bf16[27,128,128]{2,1,0:T(8,128)(2,1)}, u32[]{:S(2)}) copy-start(bf16[27,128,128]{2,1,0:T(8,128)(2,1)} %param.8) | copy-start | bytes 2654212
  37.7 0.7 %copy-start.4 = (f32[128]{0:T(128)S(1)}, f32[128]{0:T(128)}, u32[]{:S(2)}) copy-start(f32[128]{0:T(128)} %param.9) | copy-start | bytes 1540
  48.9 8.4 %collective-permute-start.10 = (bf16[2,8,16,128]{3,2,1,0:T(8,128)(2,1)S(1)}, bf16[2,8,16,128]{3,2,1,0:T(8,128)(2,1)S(1)}, u32[]{:S(2)}, u32[]{:S(2)}) collective-permute-start(bf16[2,8,16,128]{3,2,1,0:T(8,128)(2,1)S(1)} %get-tuple-element.22), channel_id=1, source_target_pairs={{0,4},{1,5},{2,6},{3,7},{4,0},{5,1},{6,2},{7,3},{8,12},{9,13},{10,... | collective-permute-start | bytes 196616 | tf_op jit(solution)/shard_map/ppermute | solution.py:293
  53.7 5.3 %collective-permute-start.11 = (bf16[2,8,16,128]{3,2,1,0:T(8,128)(2,1)S(1)}, bf16[2,8,16,128]{3,2,1,0:T(8,128)(2,1)S(1)}, u32[]{:S(2)}, u32[]{:S(2)}) collective-permute-start(bf16[2,8,16,128]{3,2,1,0:T(8,128)(2,1)S(1)} %get-tuple-element.23), channel_id=1, source_target_pairs={{0,2},{1,3},{2,4},{3,5},{4,6},{5,7},{6,0},{7,1},{8,10},{9,11},{10,... | collective-permute-start | bytes 196616 | tf_op jit(solution)/shard_map/ppermute | solution.py:293
  54.9 4.1 %collective-permute-start.12 = (bf16[2,8,16,128]{3,2,1,0:T(8,128)(2,1)S(1)}, bf16[2,8,16,128]{3,2,1,0:T(8,128)(2,1)S(1)}, u32[]{:S(2)}, u32[]{:S(2)}) collective-permute-start(bf16[2,8,16,128]{3,2,1,0:T(8,128)(2,1)S(1)} %get-tuple-element.24), channel_id=1, source_target_pairs={{0,6},{1,7},{2,0},{3,1},{4,2},{5,3},{6,4},{7,5},{8,14},{9,15},{10,... | collective-permute-start | bytes 196616 | tf_op jit(solution)/shard_map/ppermute | solution.py:293
  59.0 3.8 %collective-permute-start.13 = (bf16[4,8,16,128]{3,2,1,0:T(8,128)(2,1)S(1)}, bf16[4,8,16,128]{3,2,1,0:T(8,128)(2,1)S(1)}, u32[]{:S(2)}, u32[]{:S(2)}) collective-permute-start(bf16[4,8,16,128]{3,2,1,0:T(8,128)(2,1)S(1)} %dynamic-slice_dynamic-update-slice_fusion), channel_id=1, source_target_pairs={{0,1},{1,0},{2,3},{3,2},{4,5},{5,4},{6,7},{7,6},{8,9},{9,8},{10,11... | collective-permute-start | bytes 393224 | tf_op jit(solution)/shard_map/ppermute | solution.py:296

commit v13 on v12

--- a/solution.py
+++ b/solution.py
@@ -1,3 +1,5 @@
+import functools
+
 import jax
 import jax.numpy as jnp
 from jax import lax
@@ -152,15 +154,15 @@
         outs[k][...] = all_ref[lax.rem(my_group() + k, groups)]
 
 
-def unpack_kernel(swapped_ref, *refs):
+def unpack_kernel(order, early_ref, last_ref, *refs):
     blocks, out_ref, rows_ref = refs[:-2], refs[-2], refs[-1]
     groups = len(blocks)
     _, rows, width, lanes = blocks[0].shape
     group, core = my_group(), my_core()
-    for k in range(groups):
+    for i, k in enumerate(order):
         source = lax.rem(group + groups - k, groups) * CORES
         rows_ref[source + core] = blocks[k][core]
-        rows_ref[source + 1 - core] = swapped_ref[k]
+        rows_ref[source + 1 - core] = last_ref[0] if i == groups - 1 else early_ref[i]
     length = groups * CORES * rows
     turned = rows_ref[...].reshape(length, width, lanes).astype(F32)
     out_ref[:, 0] = jnp.swapaxes(turned, 0, 1).astype(BF16)
@@ -287,17 +289,18 @@
         )
 
         blocks = list(blocks)
-        theirs = jnp.zeros((groups, rows, width, lanes), BF16)
-        for k in [0, *order]:
+        arrival = [0, *order]
+        sent = []
+        for k in arrival:
             if k:
                 blocks[k] = lax.ppermute(blocks[k], "chan", ahead(k))
-            sent = lax.dynamic_index_in_dim(blocks[k], 1 - core, 0)
-            theirs = lax.dynamic_update_slice_in_dim(theirs, sent, k, 0)
-        swapped = lax.ppermute(theirs, "chan", swap)
+            sent.append(lax.dynamic_index_in_dim(blocks[k], 1 - core, 0))
+        early = lax.ppermute(jnp.concatenate(sent[:-1]), "chan", swap)
+        last = lax.ppermute(sent[-1], "chan", swap)
         return call(
-            unpack_kernel,
+            functools.partial(unpack_kernel, arrival),
             jax.ShapeDtypeStruct(volume.shape, BF16),
-            [swapped, *blocks],
+            [early, last, *blocks],
             [pltpu.VMEM((chan, rows, width, lanes), BF16)],
             name="unpack_rows",
         )

time: 63.9 us -> 64.6 us (1.011)
  starting transfers between devices: 27.3 us -> 28 us
    ppermute x1 -> x2, starting transfers between devices: 2.79 us -> 3.54 us  [the longest x1 3.42 us: per_device(): early = lax.ppermute(jnp.concatenate(sent[:-1]), 'chan', swap)]
  transfers between devices with their start and end apart: 14 -> 15, of which waited for: 9 -> 9; matrix products, arithmetic and copies ran while one was open for 9% -> 9% of each run, Pallas kernels for 5% -> 5%
where the time goes in v13:
time: 64.6 us; the launch traced here: 64.4 us
  starting transfers between devices  28 us (43%)
  waiting for transfers between devices  21.3 us (33%)
  local copies, waits for them, and re-layouts  8.79 us (14%)
  Pallas kernels  5.48 us (8%)
  between operations  0.88 us (1%)
    ppermute x3, starting transfers between devices, per_device(): got = lax.ppermute(pieces[k], 'chan', ahead(k))  10.6 us
    ppermute x2, waiting for transfers between devices, halo(): lax.ppermute(array, ('space', 'chan'), far)  8.9 us
    ppermute x3, starting transfers between devices, per_device(): blocks[k] = lax.ppermute(blocks[k], 'chan', ahead(k))  8.33 us
    pallas_call x8, Pallas kernels, call(): pl.pallas_call(kernel, out_shape=shapes, in_specs=[VMEM] * len(inputs), o...  5.48 us
    ppermute x2, waiting for transfers between devices, halo(): lax.ppermute(array, 'space', near)  4.8 us
    ppermute x3, waiting for transfers between devices, per_device(): got = lax.ppermute(pieces[k], 'chan', ahead(k))  4.6 us
    ppermute x3, starting transfers between devices, from_other_core(): return lax.ppermute(sent, 'chan', swap)  4.26 us
    unnamed x14, local copies, waits for them, and re-layouts  3.57 us
  transfers between devices with their start and end apart: 15, of which 9 were waited for; matrix products, arithmetic and copies ran while one was open for 9% of the time, Pallas kernels for 5%

profile of v13, /device:TPU:31, one launch (start us, length us, event | category | flops | bytes accessed | tf_op | source)
XLA Modules:
  0.0 64.4 jit_solution(12764127195788239189)
XLA Ops:
  0.0 0.0 copy-start
  0.0 0.9 %copy-done = bf16[16,1,64,128]{3,2,1,0:T(8,128)(2,1)S(1)} copy-done((bf16[16,1,64,128]{3,2,1,0:T(8,128)(2,1)S(1)}, bf16[16,1,64,128]{3,2,1,0:T(8,128)(2,1)}, u32[]{:S(2)}) %copy-start) | copy-done | bytes 262168
  1.0 0.0 copy-start.2
  1.0 0.2 pack_rows.1
  1.1 7.0 %collective-permute-start = (bf16[1,20,16,128]{3,2,1,0:T(8,128)(2,1)S(1)}, bf16[1,20,16,128]{3,2,1,0:T(8,128)(2,1)S(1)}, u32[]{:S(2)}, u32[]{:S(2)}) collective-permute-start(bf16[1,20,16,128]{3,2,1,0:T(8,128)(2,1)S(1)} %get-tuple-element.16), channel_id=1, source_target_pairs={{0,4},{1,5},{2,6},{3,7},{4,0},{5,1},{6,2},{7,3},{8,12},{9,13},{10,... | collective-permute-start | bytes 245768 | tf_op jit(solution)/shard_map/ppermute | solution.py:237
  8.1 1.2 %collective-permute-start.1 = (bf16[1,20,16,128]{3,2,1,0:T(8,128)(2,1)S(1)}, bf16[1,20,16,128]{3,2,1,0:T(8,128)(2,1)S(1)}, u32[]{:S(2)}, u32[]{:S(2)}) collective-permute-start(bf16[1,20,16,128]{3,2,1,0:T(8,128)(2,1)S(1)} %get-tuple-element.17), channel_id=1, source_target_pairs={{0,2},{1,3},{2,4},{3,5},{4,6},{5,7},{6,0},{7,1},{8,10},{9,11},{10,... | collective-permute-start | bytes 245768 | tf_op jit(solution)/shard_map/ppermute | solution.py:237
  9.3 2.4 %collective-permute-start.2 = (bf16[1,20,16,128]{3,2,1,0:T(8,128)(2,1)S(1)}, bf16[1,20,16,128]{3,2,1,0:T(8,128)(2,1)S(1)}, u32[]{:S(2)}, u32[]{:S(2)}) collective-permute-start(bf16[1,20,16,128]{3,2,1,0:T(8,128)(2,1)S(1)} %get-tuple-element.18), channel_id=1, source_target_pairs={{0,6},{1,7},{2,0},{3,1},{4,2},{5,3},{6,4},{7,5},{8,14},{9,15},{10,... | collective-permute-start | bytes 245768 | tf_op jit(solution)/shard_map/ppermute | solution.py:237
  11.8 0.0 collective-permute-done
  11.8 2.3 %collective-permute-done.1 = bf16[1,20,16,128]{3,2,1,0:T(8,128)(2,1)S(1)} collective-permute-done((bf16[1,20,16,128]{3,2,1,0:T(8,128)(2,1)S(1)}, bf16[1,20,16,128]{3,2,1,0:T(8,128)(2,1)S(1)}, u32[]{:S(2)}, u32[]{:S(2)}) %collective-permute-start.1) | collective-permute-done | bytes 81952 | tf_op jit(solution)/shard_map/ppermute | solution.py:237
  14.1 2.3 %collective-permute-done.2 = bf16[1,20,16,128]{3,2,1,0:T(8,128)(2,1)S(1)} collective-permute-done((bf16[1,20,16,128]{3,2,1,0:T(8,128)(2,1)S(1)}, bf16[1,20,16,128]{3,2,1,0:T(8,128)(2,1)S(1)}, u32[]{:S(2)}, u32[]{:S(2)}) %collective-permute-start.2) | collective-permute-done | bytes 81952 | tf_op jit(solution)/shard_map/ppermute | solution.py:237
  16.4 0.6 collective-permute-start.6
  17.0 1.3 %collective-permute-start.4 = (bf16[4,12,16,128]{3,2,1,0:T(8,128)(2,1)S(1)}, bf16[4,12,16,128]{3,2,1,0:T(8,128)(2,1)S(1)}, u32[]{:S(2)}, u32[]{:S(2)}) collective-permute-start(bf16[4,12,16,128]{3,2,1,0:T(8,128)(2,1)S(1)} %constant_dynamic-slice_fusion.6), channel_id=1, source_target_pairs={{0,1},{1,0},{2,3},{3,2},{4,5},{5,4},{6,7},{7,6},{8,9},{9,8},{10,11... | collective-permute-start | bytes 589832 | tf_op jit(solution)/shard_map/ppermute | solution.py:242
  18.3 0.2 collective-permute-start.3
  18.5 0.0 copy-done.2
  18.5 0.7 %slice.17 = bf16[9,128,128]{2,1,0:T(8,128)(2,1)} slice(bf16[27,128,128]{2,1,0:T(8,128)(2,1)S(1)} %copy-done.2), slice={[9:18], [0:128], [0:128]} | slice | bytes 589824 | tf_op jit(solution)/shard_map/slice | solution.py:174
  19.3 0.6 copy.20
  19.9 0.5 reshape.24.later_ref.weight_ref
  20.4 0.0 copy-start.3
  20.5 0.6 %copy-done.3 = f32[128]{0:T(128)S(1)} copy-done((f32[128]{0:T(128)S(1)}, f32[128]{0:T(128)}, u32[]{:S(2)}) %copy-start.3) | copy-done | bytes 536
  21.1 0.1 copy.15.bias_ref
  21.2 1.2 %copy.13 = bf16[3,3,128,128]{2,0,3,1:T(4,128)(2,1)S(1)} copy(bf16[3,3,128,128]{3,2,1,0:T(8,128)(2,1)} %bitcast.27) | data formatting | bytes 589824 | tf_op jit(solution)/shard_map/squeeze | solution.py:174
  22.5 0.0 collective-permute-done.4.other_ref
  22.5 0.8 %first_own.1 = (f32[10,128,128]{2,1,0:T(8,128)S(1)}, s32[8,128]{1,0:T(8,128)S(1)}) custom-call(bf16[4,20,16,128]{3,2,1,0:T(8,128)(2,1)S(1)} %constant_dynamic-update-slice_fusion.kept_ref, bf16[4,12,16,128]{3,2,1,0:T(8,128)(2,1)S(1)} %collective-permute-done.4.other_ref, bf16[384,384]{1,0:T(8,128)(2,1)S(1)} %bitcast.22, ...), custom_call_target="tpu_custom_call" | custom-call | flops 377487360 | bytes 4000000 | tf_op jit(solution)/shard_map/first_own/pallas_call | solution.py:206
  23.3 0.5 slice.19
  24.5 0.3 collective-permute-done.6.kept_ref
  24.8 2.0 %collective-permute-start.7 = (bf16[4,12,16,128]{3,2,1,0:T(8,128)(2,1)S(1)}, bf16[4,12,16,128]{3,2,1,0:T(8,128)(2,1)S(1)}, u32[]{:S(2)}, u32[]{:S(2)}) collective-permute-start(bf16[4,12,16,128]{3,2,1,0:T(8,128)(2,1)S(1)} %constant_dynamic-slice_fusion.4), channel_id=1, source_target_pairs={{0,1},{1,0},{2,3},{3,2},{4,5},{5,4},{6,7},{7,6},{8,9},{9,8},{10,11... | collective-permute-start | bytes 589832 | tf_op jit(solution)/shard_map/ppermute | solution.py:242
  26.7 5.1 %collective-permute-done.3.kept_ref = bf16[4,20,16,128]{3,2,1,0:T(8,128)(2,1)S(1)} collective-permute-done((bf16[4,20,16,128]{3,2,1,0:T(8,128)(2,1)S(1)}, bf16[4,20,16,128]{3,2,1,0:T(8,128)(2,1)S(1)}, u32[]{:S(2)}, u32[]{:S(2)}) %collective-permute-start.3) | collective-permute-done | bytes 327712 | tf_op jit(solution)/shard_map/ppermute | solution.py:245
  31.8 1.0 %collective-permute-start.5 = (bf16[4,12,16,128]{3,2,1,0:T(8,128)(2,1)S(1)}, bf16[4,12,16,128]{3,2,1,0:T(8,128)(2,1)S(1)}, u32[]{:S(2)}, u32[]{:S(2)}) collective-permute-start(bf16[4,12,16,128]{3,2,1,0:T(8,128)(2,1)S(1)} %constant_dynamic-slice_fusion.5), channel_id=1, source_target_pairs={{0,1},{1,0},{2,3},{3,2},{4,5},{5,4},{6,7},{7,6},{8,9},{9,8},{10,11... | collective-permute-start | bytes 589832 | tf_op jit(solution)/shard_map/ppermute | solution.py:242
  32.8 0.0 collective-permute-done.7.other_ref
  32.8 0.8 %first_near.1.before_ref = f32[10,128,128]{2,1,0:T(8,128)S(1)} custom-call(bf16[4,20,16,128]{3,2,1,0:T(8,128)(2,1)S(1)} %collective-permute-done.6.kept_ref, bf16[4,12,16,128]{3,2,1,0:T(8,128)(2,1)S(1)} %collective-permute-done.7.other_ref, bf16[2,384,384]{2,1,0:T(8,128)(2,1)S(1)} %reshape.24.later_ref.weight_ref, ...), custom_call_target="tpu_custom_call" | custom-call | flops 377487360 | bytes 4000000 | tf_op jit(solution)/shard_map/first_near/pallas_call | solution.py:206
  33.6 0.3 collective-permute-done.5.other_ref
  33.9 0.8 %first_far.1.plane_ref = bf16[10,128,128]{2,1,0:T(8,128)(2,1)S(1)} custom-call(bf16[4,20,16,128]{3,2,1,0:T(8,128)(2,1)S(1)} %collective-permute-done.3.kept_ref, bf16[4,12,16,128]{3,2,1,0:T(8,128)(2,1)S(1)} %collective-permute-done.5.other_ref, bf16[2,384,384]{2,1,0:T(8,128)(2,1)S(1)} %reshape.24.later_ref.weight_ref, ...), custom_call_target="tpu_custom_call" | custom-call | flops 377487360 | bytes 4000000 | tf_op jit(solution)/shard_map/first_far/pallas_call | solution.py:206
  34.7 0.1 collective-permute-start.9
  34.8 0.4 collective-permute-start.8
  35.2 0.0 slice-start
  35.2 0.0 copy-start.1
  35.2 1.0 %slice-done = bf16[9,128,128]{2,1,0:T(8,128)(2,1)S(1)} async-done(((bf16[27,128,128]{2,1,0:T(8,128)(2,1)}), bf16[9,128,128]{2,1,0:T(8,128)(2,1)S(1)}, s32[]{:S(2)}) %slice-start) | async-done | bytes 294936 | tf_op jit(solution)/shard_map/slice | solution.py:174
  36.2 0.2 copy.18
  36.5 0.1 copy-done.1
  36.6 0.6 copy.21
  37.2 0.5 reshape.26.weight_ref
  37.7 0.0 copy-start.4
  37.8 0.6 %copy-done.4 = f32[128]{0:T(128)S(1)} copy-done((f32[128]{0:T(128)S(1)}, f32[128]{0:T(128)}, u32[]{:S(2)}) %copy-start.4) | copy-done | bytes 536
  38.4 0.1 copy.19.bias_ref
  38.5 0.7 %second_own.1.before_ref = f32[8,128,128]{2,1,0:T(8,128)S(1)} custom-call(bf16[10,128,128]{2,1,0:T(8,128)(2,1)S(1)} %first_far.1.plane_ref, bf16[384,384]{1,0:T(8,128)(2,1)S(1)} %bitcast.21), custom_call_target="tpu_custom_call" | custom-call | flops 301989888 | bytes 4000000 | tf_op jit(solution)/shard_map/second_own/pallas_call | solution.py:206
  39.2 4.5 %collective-permute-done.9.plane_ref = bf16[10,128,128]{2,1,0:T(8,128)(2,1)S(1)} collective-permute-done((bf16[10,128,128]{2,1,0:T(8,128)(2,1)S(1)}, bf16[10,128,128]{2,1,0:T(8,128)(2,1)S(1)}, u32[]{:S(2)}, u32[]{:S(2)}) %collective-permute-start.9) | collective-permute-done | bytes 327712 | tf_op jit(solution)/shard_map/ppermute | solution.py:245
  43.7 0.7 %second_near.1.before_ref = f32[8,128,128]{2,1,0:T(8,128)S(1)} custom-call(bf16[10,128,128]{2,1,0:T(8,128)(2,1)S(1)} %collective-permute-done.9.plane_ref, bf16[2,384,384]{2,1,0:T(8,128)(2,1)S(1)} %reshape.26.weight_ref, f32[8,128,128]{2,1,0:T(8,128)S(1)} %second_own.1.before_ref), custom_call_target="tpu_custom_call" | custom-call | flops 301989888 | bytes 4000000 | tf_op jit(solution)/shard_map/second_near/pallas_call | solution.py:206
  44.4 3.8 %collective-permute-done.8.plane_ref = bf16[10,128,128]{2,1,0:T(8,128)(2,1)S(1)} collective-permute-done((bf16[10,128,128]{2,1,0:T(8,128)(2,1)S(1)}, bf16[10,128,128]{2,1,0:T(8,128)(2,1)S(1)}, u32[]{:S(2)}, u32[]{:S(2)}) %collective-permute-start.8) | collective-permute-done | bytes 327712 | tf_op jit(solution)/shard_map/ppermute | solution.py:245
  48.2 0.7 %second_far.1 = (bf16[2,8,16,128]{3,2,1,0:T(8,128)(2,1)S(1)}, bf16[2,8,16,128]{3,2,1,0:T(8,128)(2,1)S(1)}, bf16[2,8,16,128]{3,2,1,0:T(8,128)(2,1)S(1)}, bf16[2,8,16,128]{3,2,1,0:T(8,128)(2,1)S(1)}) custom-call(bf16[10,128,128]{2,1,0:T(8,128)(2,1)S(1)} %collective-permute-done.8.plane_ref, bf16[2,384,384]{2,1,0:T(8,128)(2,1)S(1)} %reshape.26.weight_ref, ...), custom_call_target="tpu_custom_call" | custom-call | flops 301989888 | bytes 4000000 | tf_op jit(solution)/shard_map/second_far/pallas_call | solution.py:206
  48.9 4.8 %collective-permute-start.10 = (bf16[2,8,16,128]{3,2,1,0:T(8,128)(2,1)S(1)}, bf16[2,8,16,128]{3,2,1,0:T(8,128)(2,1)S(1)}, u32[]{:S(2)}, u32[]{:S(2)}) collective-permute-start(bf16[2,8,16,128]{3,2,1,0:T(8,128)(2,1)S(1)} %get-tuple-element.22), channel_id=1, source_target_pairs={{0,4},{1,5},{2,6},{3,7},{4,0},{5,1},{6,2},{7,3},{8,12},{9,13},{10,... | collective-permute-start | bytes 196616 | tf_op jit(solution)/shard_map/ppermute | solution.py:296
  53.7 1.1 %collective-permute-start.11 = (bf16[2,8,16,128]{3,2,1,0:T(8,128)(2,1)S(1)}, bf16[2,8,16,128]{3,2,1,0:T(8,128)(2,1)S(1)}, u32[]{:S(2)}, u32[]{:S(2)}) collective-permute-start(bf16[2,8,16,128]{3,2,1,0:T(8,128)(2,1)S(1)} %get-tuple-element.23), channel_id=1, source_target_pairs={{0,2},{1,3},{2,4},{3,5},{4,6},{5,7},{6,0},{7,1},{8,10},{9,11},{10,... | collective-permute-start | bytes 196616 | tf_op jit(solution)/shard_map/ppermute | solution.py:296
  54.8 2.5 %collective-permute-start.13 = (bf16[2,8,16,128]{3,2,1,0:T(8,128)(2,1)S(1)}, bf16[2,8,16,128]{3,2,1,0:T(8,128)(2,1)S(1)}, u32[]{:S(2)}, u32[]{:S(2)}) collective-permute-start(bf16[2,8,16,128]{3,2,1,0:T(8,128)(2,1)S(1)} %get-tuple-element.24), channel_id=1, source_target_pairs={{0,6},{1,7},{2,0},{3,1},{4,2},{5,3},{6,4},{7,5},{8,14},{9,15},{10,... | collective-permute-start | bytes 196616 | tf_op jit(solution)/shard_map/ppermute | solution.py:296
  57.2 0.0 collective-permute-done.10.refs_2_
  57.3 1.6 %collective-permute-done.11.refs_1_ = bf16[2,8,16,128]{3,2,1,0:T(8,128)(2,1)S(1)} collective-permute-done((bf16[2,8,16,128]{3,2,1,0:T(8,128)(2,1)S(1)}, bf16[2,8,16,128]{3,2,1,0:T(8,128)(2,1)S(1)}, u32[]{:S(2)}, u32[]{:S(2)}) %collective-permute-start.11) | collective-permute-done | bytes 65568 | tf_op jit(solution)/shard_map/ppermute | solution.py:296
  58.9 3.4 %collective-permute-start.12 = (bf16[3,8,16,128]{3,2,1,0:T(8,128)(2,1)S(1)}, bf16[3,8,16,128]{3,2,1,0:T(8,128)(2,1)S(1)}, u32[]{:S(2)}, u32[]{:S(2)}) collective-permute-start(bf16[3,8,16,128]{3,2,1,0:T(8,128)(2,1)S(1)} %pad_maximum_fusion), channel_id=1, source_target_pairs={{0,1},{1,0},{2,3},{3,2},{4,5},{5,4},{6,7},{7,6},{8,9},{9,8},{10,11... | collective-permute-start | bytes 294920 | tf_op jit(solution)/shard_map/ppermute | solution.py:298
  62.3 0.0 collective-permute-done.13.refs_3_
  62.3 0.1 collective-permute-start.14
  62.5 1.1 %collective-permute-done.14.last_ref = bf16[1,8,16,128]{3,2,1,0:T(8,128)(2,1)S(1)} collective-permute-done((bf16[1,8,16,128]{3,2,1,0:T(8,128)(2,1)S(1)}, bf16[1,8,16,128]{3,2,1,0:T(8,128)(2,1)S(1)}, u32[]{:S(2)}, u32[]{:S(2)}) %collective-permute-start.14) | collective-permute-done | bytes 32800 | tf_op jit(solution)/shard_map/ppermute | solution.py:299
  63.5 0.0 collective-permute-done.12.early_ref
  63.6 0.9 %unpack_rows.1 = bf16[16,1,64,128]{3,2,1,0:T(8,128)(2,1)} custom-call(bf16[3,8,16,128]{3,2,1,0:T(8,128)(2,1)S(1)} %collective-permute-done.12.early_ref, bf16[1,8,16,128]{3,2,1,0:T(8,128)(2,1)S(1)} %collective-permute-done.14.last_ref, bf16[2,8,16,128]{3,2,1,0:T(8,128)(2,1)S(1)} %get-tuple-element.21.refs_0_, ...), custom_call_target="tpu_custom_call" | custom-call | tf_op jit(solution)/shard_map/unpack_rows/pallas_call | solution.py:206
  (17 shorter events, 0.4 us)
Async XLA Ops:
  0.0 0.9 %copy-start = (bf16[16,1,64,128]{3,2,1,0:T(8,128)(2,1)S(1)}, bf16[16,1,64,128]{3,2,1,0:T(8,128)(2,1)}, u32[]{:S(2)}) copy-start(bf16[16,1,64,128]{3,2,1,0:T(8,128)(2,1)} %volume_ref.1) | copy-start | bytes 786436
  1.0 17.6 %copy-start.2 = (bf16[27,128,128]{2,1,0:T(8,128)(2,1)S(1)}, bf16[27,128,128]{2,1,0:T(8,128)(2,1)}, u32[]{:S(2)}) copy-start(bf16[27,128,128]{2,1,0:T(8,128)(2,1)} %param.6) | copy-start | bytes 2654212
  1.1 10.6 %collective-permute-start = (bf16[1,20,16,128]{3,2,1,0:T(8,128)(2,1)S(1)}, bf16[1,20,16,128]{3,2,1,0:T(8,128)(2,1)S(1)}, u32[]{:S(2)}, u32[]{:S(2)}) collective-permute-start(bf16[1,20,16,128]{3,2,1,0:T(8,128)(2,1)S(1)} %get-tuple-element.16), channel_id=1, source_target_pairs={{0,4},{1,5},{2,6},{3,7},{4,0},{5,1},{6,2},{7,3},{8,12},{9,13},{10,... | collective-permute-start | bytes 245768 | tf_op jit(solution)/shard_map/ppermute | solution.py:237
  8.1 6.0 %collective-permute-start.1 = (bf16[1,20,16,128]{3,2,1,0:T(8,128)(2,1)S(1)}, bf16[1,20,16,128]{3,2,1,0:T(8,128)(2,1)S(1)}, u32[]{:S(2)}, u32[]{:S(2)}) collective-permute-start(bf16[1,20,16,128]{3,2,1,0:T(8,128)(2,1)S(1)} %get-tuple-element.17), channel_id=1, source_target_pairs={{0,2},{1,3},{2,4},{3,5},{4,6},{5,7},{6,0},{7,1},{8,10},{9,11},{10,... | collective-permute-start | bytes 245768 | tf_op jit(solution)/shard_map/ppermute | solution.py:237
  9.3 7.1 %collective-permute-start.2 = (bf16[1,20,16,128]{3,2,1,0:T(8,128)(2,1)S(1)}, bf16[1,20,16,128]{3,2,1,0:T(8,128)(2,1)S(1)}, u32[]{:S(2)}, u32[]{:S(2)}) collective-permute-start(bf16[1,20,16,128]{3,2,1,0:T(8,128)(2,1)S(1)} %get-tuple-element.18), channel_id=1, source_target_pairs={{0,6},{1,7},{2,0},{3,1},{4,2},{5,3},{6,4},{7,5},{8,14},{9,15},{10,... | collective-permute-start | bytes 245768 | tf_op jit(solution)/shard_map/ppermute | solution.py:237
  16.4 8.3 %collective-permute-start.6 = (bf16[4,20,16,128]{3,2,1,0:T(8,128)(2,1)S(1)}, bf16[4,20,16,128]{3,2,1,0:T(8,128)(2,1)S(1)}, u32[]{:S(2)}, u32[]{:S(2)}) collective-permute-start(bf16[4,20,16,128]{3,2,1,0:T(8,128)(2,1)S(1)} %constant_dynamic-update-slice_fusion.kept_ref), channel_id=1, source_target_pairs={{0,8},{8,0},{16,24},{24,16},{32,40},{40,32},{48,56},{56,48},{64,72... | collective-permute-start | bytes 983048 | tf_op jit(solution)/shard_map/ppermute | solution.py:245
  17.0 5.5 %collective-permute-start.4 = (bf16[4,12,16,128]{3,2,1,0:T(8,128)(2,1)S(1)}, bf16[4,12,16,128]{3,2,1,0:T(8,128)(2,1)S(1)}, u32[]{:S(2)}, u32[]{:S(2)}) collective-permute-start(bf16[4,12,16,128]{3,2,1,0:T(8,128)(2,1)S(1)} %constant_dynamic-slice_fusion.6), channel_id=1, source_target_pairs={{0,1},{1,0},{2,3},{3,2},{4,5},{5,4},{6,7},{7,6},{8,9},{9,8},{10,11... | collective-permute-start | bytes 589832 | tf_op jit(solution)/shard_map/ppermute | solution.py:242
  18.3 13.5 %collective-permute-start.3 = (bf16[4,20,16,128]{3,2,1,0:T(8,128)(2,1)S(1)}, bf16[4,20,16,128]{3,2,1,0:T(8,128)(2,1)S(1)}, u32[]{:S(2)}, u32[]{:S(2)}) collective-permute-start(bf16[4,20,16,128]{3,2,1,0:T(8,128)(2,1)S(1)} %constant_dynamic-update-slice_fusion.kept_ref), channel_id=1, source_target_pairs={{0,1},{1,0},{2,3},{3,2},{4,5},{5,4},{6,7},{7,6},{8,16},{9,17},{10,... | collective-permute-start | bytes 983048 | tf_op jit(solution)/shard_map/ppermute | solution.py:245
  20.4 0.7 %copy-start.3 = (f32[128]{0:T(128)S(1)}, f32[128]{0:T(128)}, u32[]{:S(2)}) copy-start(f32[128]{0:T(128)} %param.7) | copy-start | bytes 1540
  24.8 8.0 %collective-permute-start.7 = (bf16[4,12,16,128]{3,2,1,0:T(8,128)(2,1)S(1)}, bf16[4,12,16,128]{3,2,1,0:T(8,128)(2,1)S(1)}, u32[]{:S(2)}, u32[]{:S(2)}) collective-permute-start(bf16[4,12,16,128]{3,2,1,0:T(8,128)(2,1)S(1)} %constant_dynamic-slice_fusion.4), channel_id=1, source_target_pairs={{0,1},{1,0},{2,3},{3,2},{4,5},{5,4},{6,7},{7,6},{8,9},{9,8},{10,11... | collective-permute-start | bytes 589832 | tf_op jit(solution)/shard_map/ppermute | solution.py:242
  31.8 2.0 %collective-permute-start.5 = (bf16[4,12,16,128]{3,2,1,0:T(8,128)(2,1)S(1)}, bf16[4,12,16,128]{3,2,1,0:T(8,128)(2,1)S(1)}, u32[]{:S(2)}, u32[]{:S(2)}) collective-permute-start(bf16[4,12,16,128]{3,2,1,0:T(8,128)(2,1)S(1)} %constant_dynamic-slice_fusion.5), channel_id=1, source_target_pairs={{0,1},{1,0},{2,3},{3,2},{4,5},{5,4},{6,7},{7,6},{8,9},{9,8},{10,11... | collective-permute-start | bytes 589832 | tf_op jit(solution)/shard_map/ppermute | solution.py:242
  34.7 9.0 %collective-permute-start.9 = (bf16[10,128,128]{2,1,0:T(8,128)(2,1)S(1)}, bf16[10,128,128]{2,1,0:T(8,128)(2,1)S(1)}, u32[]{:S(2)}, u32[]{:S(2)}) collective-permute-start(bf16[10,128,128]{2,1,0:T(8,128)(2,1)S(1)} %first_far.1.plane_ref), channel_id=1, source_target_pairs={{0,8},{8,0},{16,24},{24,16},{32,40},{40,32},{48,56},{56,48},{64,72... | collective-permute-start | bytes 983048 | tf_op jit(solution)/shard_map/ppermute | solution.py:245
  34.8 13.4 %collective-permute-start.8 = (bf16[10,128,128]{2,1,0:T(8,128)(2,1)S(1)}, bf16[10,128,128]{2,1,0:T(8,128)(2,1)S(1)}, u32[]{:S(2)}, u32[]{:S(2)}) collective-permute-start(bf16[10,128,128]{2,1,0:T(8,128)(2,1)S(1)} %first_far.1.plane_ref), channel_id=1, source_target_pairs={{0,1},{1,0},{2,3},{3,2},{4,5},{5,4},{6,7},{7,6},{8,16},{9,17},{10,... | collective-permute-start | bytes 983048 | tf_op jit(solution)/shard_map/ppermute | solution.py:245
  35.2 1.0 %slice-start = ((bf16[27,128,128]{2,1,0:T(8,128)(2,1)}), bf16[9,128,128]{2,1,0:T(8,128)(2,1)S(1)}, s32[]{:S(2)}) async-start(bf16[27,128,128]{2,1,0:T(8,128)(2,1)} %param.8), calls=%async_computation | async-start | bytes 589824 | tf_op jit(solution)/shard_map/slice | solution.py:174
  35.2 1.3 %copy-start.1 = (bf16[27,128,128]{2,1,0:T(8,128)(2,1)S(1)}, bf16[27,128,128]{2,1,0:T(8,128)(2,1)}, u32[]{:S(2)}) copy-start(bf16[27,128,128]{2,1,0:T(8,128)(2,1)} %param.8) | copy-start | bytes 2654212
  37.7 0.7 %copy-start.4 = (f32[128]{0:T(128)S(1)}, f32[128]{0:T(128)}, u32[]{:S(2)}) copy-start(f32[128]{0:T(128)} %param.9) | copy-start | bytes 1540
  48.9 8.3 %collective-permute-start.10 = (bf16[2,8,16,128]{3,2,1,0:T(8,128)(2,1)S(1)}, bf16[2,8,16,128]{3,2,1,0:T(8,128)(2,1)S(1)}, u32[]{:S(2)}, u32[]{:S(2)}) collective-permute-start(bf16[2,8,16,128]{3,2,1,0:T(8,128)(2,1)S(1)} %get-tuple-element.22), channel_id=1, source_target_pairs={{0,4},{1,5},{2,6},{3,7},{4,0},{5,1},{6,2},{7,3},{8,12},{9,13},{10,... | collective-permute-start | bytes 196616 | tf_op jit(solution)/shard_map/ppermute | solution.py:296
  53.7 5.2 %collective-permute-start.11 = (bf16[2,8,16,128]{3,2,1,0:T(8,128)(2,1)S(1)}, bf16[2,8,16,128]{3,2,1,0:T(8,128)(2,1)S(1)}, u32[]{:S(2)}, u32[]{:S(2)}) collective-permute-start(bf16[2,8,16,128]{3,2,1,0:T(8,128)(2,1)S(1)} %get-tuple-element.23), channel_id=1, source_target_pairs={{0,2},{1,3},{2,4},{3,5},{4,6},{5,7},{6,0},{7,1},{8,10},{9,11},{10,... | collective-permute-start | bytes 196616 | tf_op jit(solution)/shard_map/ppermute | solution.py:296
  54.8 7.6 %collective-permute-start.13 = (bf16[2,8,16,128]{3,2,1,0:T(8,128)(2,1)S(1)}, bf16[2,8,16,128]{3,2,1,0:T(8,128)(2,1)S(1)}, u32[]{:S(2)}, u32[]{:S(2)}) collective-permute-start(bf16[2,8,16,128]{3,2,1,0:T(8,128)(2,1)S(1)} %get-tuple-element.24), channel_id=1, source_target_pairs={{0,6},{1,7},{2,0},{3,1},{4,2},{5,3},{6,4},{7,5},{8,14},{9,15},{10,... | collective-permute-start | bytes 196616 | tf_op jit(solution)/shard_map/ppermute | solution.py:296
  58.9 4.6 %collective-permute-start.12 = (bf16[3,8,16,128]{3,2,1,0:T(8,128)(2,1)S(1)}, bf16[3,8,16,128]{3,2,1,0:T(8,128)(2,1)S(1)}, u32[]{:S(2)}, u32[]{:S(2)}) collective-permute-start(bf16[3,8,16,128]{3,2,1,0:T(8,128)(2,1)S(1)} %pad_maximum_fusion), channel_id=1, source_target_pairs={{0,1},{1,0},{2,3},{3,2},{4,5},{5,4},{6,7},{7,6},{8,9},{9,8},{10,11... | collective-permute-start | bytes 294920 | tf_op jit(solution)/shard_map/ppermute | solution.py:298
  62.3 1.2 %collective-permute-start.14 = (bf16[1,8,16,128]{3,2,1,0:T(8,128)(2,1)S(1)}, bf16[1,8,16,128]{3,2,1,0:T(8,128)(2,1)S(1)}, u32[]{:S(2)}, u32[]{:S(2)}) collective-permute-start(bf16[1,8,16,128]{3,2,1,0:T(8,128)(2,1)S(1)} %constant_dynamic-slice_fusion), channel_id=1, source_target_pairs={{0,1},{1,0},{2,3},{3,2},{4,5},{5,4},{6,7},{7,6},{8,9},{9,8},{10,11... | collective-permute-start | bytes 98312 | tf_op jit(solution)/shard_map/ppermute | solution.py:299

commit v14 on v12

--- a/solution.py
+++ b/solution.py
@@ -111,7 +111,8 @@
     zero_ref[...] = jnp.zeros_like(zero_ref)
 
 
-def first_near_kernel(kept_ref, other_ref, weight_ref, before_ref, out_ref, joined_ref):
+def first_near_kernel(kept_ref, other_ref, weight_ref, before_ref, out_ref, zero_ref, joined_ref):
+    zero_ref[...] = jnp.zeros_like(zero_ref)
     gather_rows(kept_ref, other_ref, joined_ref)
     near_kernel(joined_ref, weight_ref, before_ref, out_ref)
 
@@ -255,14 +256,15 @@
             name="first_own",
         )
         later_core = core + zero[0, 0]
-        total = call(
+        total, zero = call(
             first_near_kernel,
-            partial,
+            [partial, jax.ShapeDtypeStruct((8, 128), jnp.int32)],
             [near_plane, from_other_core(near_plane, later_core), beside_one, total],
             joined,
             cost_estimate=work,
             name="first_near",
         )
+        later_core = core + zero[0, 0]
         hidden = call(
             first_far_kernel,
             jax.ShapeDtypeStruct((rows + RIM, full, lanes), BF16),

time: 63.9 us -> 66.2 us (1.036)
  waiting for transfers between devices: 21.2 us -> 24.1 us
  local copies, waits for them, and re-layouts: 8.83 us -> 7.62 us
    ppermute x3, waiting for transfers between devices: 0.27 us -> 2.14 us  [from_other_core(): return lax.ppermute(sent, 'chan', swap)]
    ppermute x2, waiting for transfers between devices: 4.79 us -> 6.46 us  [halo(): lax.ppermute(array, 'space', near)]
    squeeze x2, local copies, waits for them, and re-layouts: 1.45 us -> 0.49 us  [arranged(): own = taps[1].transpose(1, 3, 0, 2).reshape(3 * outer, 3 * inner)]
    slice x3, local copies, waits for them, and re-layouts: 1.7 us -> 0.98 us  [arranged(): own = taps[1].transpose(1, 3, 0, 2).reshape(3 * outer, 3 * inner)]
  transfers between devices with their start and end apart: 14 -> 14, of which waited for: 9 -> 10; matrix products, arithmetic and copies ran while one was open for 9% -> 7% of each run, Pallas kernels for 5% -> 4%
where the time goes in v14:
time: 66.2 us; the launch traced here: 66 us
  starting transfers between devices  27.3 us (41%)
  waiting for transfers between devices  24.1 us (36%)
  local copies, waits for them, and re-layouts  7.62 us (12%)
  Pallas kernels  5.46 us (8%)
  between operations  1.54 us (2%)
    ppermute x3, starting transfers between devices, per_device(): got = lax.ppermute(pieces[k], 'chan', ahead(k))  10.6 us
    ppermute x3, starting transfers between devices, per_device(): blocks[k] = lax.ppermute(blocks[k], 'chan', ahead(k))  8.41 us
    ppermute x2, waiting for transfers between devices, halo(): lax.ppermute(array, ('space', 'chan'), far)  8.29 us
    ppermute x2, waiting for transfers between devices, halo(): lax.ppermute(array, 'space', near)  6.46 us
    pallas_call x8, Pallas kernels, call(): pl.pallas_call(kernel, out_shape=shapes, in_specs=[VMEM] * len(inputs), o...  5.46 us
    ppermute x3, waiting for transfers between devices, per_device(): got = lax.ppermute(pieces[k], 'chan', ahead(k))  4.6 us
    ppermute x3, starting transfers between devices, from_other_core(): return lax.ppermute(sent, 'chan', swap)  4.19 us
    unnamed x14, local copies, waits for them, and re-layouts  3.51 us
  transfers between devices with their start and end apart: 14, of which 10 were waited for; matrix products, arithmetic and copies ran while one was open for 7% of the time, Pallas kernels for 4%

profile of v14, /device:TPU:31, one launch (start us, length us, event | category | flops | bytes accessed | tf_op | source)
XLA Modules:
  0.0 66.0 jit_solution(8188385379986560290)
XLA Ops:
  0.0 0.0 copy-start
  0.0 0.9 %copy-done = bf16[16,1,64,128]{3,2,1,0:T(8,128)(2,1)S(1)} copy-done((bf16[16,1,64,128]{3,2,1,0:T(8,128)(2,1)S(1)}, bf16[16,1,64,128]{3,2,1,0:T(8,128)(2,1)}, u32[]{:S(2)}) %copy-start) | copy-done | bytes 262168
  1.0 0.0 copy-start.2
  1.0 0.2 pack_rows.1
  1.1 7.0 %collective-permute-start = (bf16[1,20,16,128]{3,2,1,0:T(8,128)(2,1)S(1)}, bf16[1,20,16,128]{3,2,1,0:T(8,128)(2,1)S(1)}, u32[]{:S(2)}, u32[]{:S(2)}) collective-permute-start(bf16[1,20,16,128]{3,2,1,0:T(8,128)(2,1)S(1)} %get-tuple-element.18), channel_id=1, source_target_pairs={{0,4},{1,5},{2,6},{3,7},{4,0},{5,1},{6,2},{7,3},{8,12},{9,13},{10,... | collective-permute-start | bytes 245768 | tf_op jit(solution)/shard_map/ppermute | solution.py:236
  8.1 1.2 %collective-permute-start.1 = (bf16[1,20,16,128]{3,2,1,0:T(8,128)(2,1)S(1)}, bf16[1,20,16,128]{3,2,1,0:T(8,128)(2,1)S(1)}, u32[]{:S(2)}, u32[]{:S(2)}) collective-permute-start(bf16[1,20,16,128]{3,2,1,0:T(8,128)(2,1)S(1)} %get-tuple-element.19), channel_id=1, source_target_pairs={{0,2},{1,3},{2,4},{3,5},{4,6},{5,7},{6,0},{7,1},{8,10},{9,11},{10,... | collective-permute-start | bytes 245768 | tf_op jit(solution)/shard_map/ppermute | solution.py:236
  9.3 2.4 %collective-permute-start.2 = (bf16[1,20,16,128]{3,2,1,0:T(8,128)(2,1)S(1)}, bf16[1,20,16,128]{3,2,1,0:T(8,128)(2,1)S(1)}, u32[]{:S(2)}, u32[]{:S(2)}) collective-permute-start(bf16[1,20,16,128]{3,2,1,0:T(8,128)(2,1)S(1)} %get-tuple-element.20), channel_id=1, source_target_pairs={{0,6},{1,7},{2,0},{3,1},{4,2},{5,3},{6,4},{7,5},{8,14},{9,15},{10,... | collective-permute-start | bytes 245768 | tf_op jit(solution)/shard_map/ppermute | solution.py:236
  11.8 0.0 collective-permute-done
  11.8 2.3 %collective-permute-done.1 = bf16[1,20,16,128]{3,2,1,0:T(8,128)(2,1)S(1)} collective-permute-done((bf16[1,20,16,128]{3,2,1,0:T(8,128)(2,1)S(1)}, bf16[1,20,16,128]{3,2,1,0:T(8,128)(2,1)S(1)}, u32[]{:S(2)}, u32[]{:S(2)}) %collective-permute-start.1) | collective-permute-done | bytes 81952 | tf_op jit(solution)/shard_map/ppermute | solution.py:236
  14.1 2.3 %collective-permute-done.2 = bf16[1,20,16,128]{3,2,1,0:T(8,128)(2,1)S(1)} collective-permute-done((bf16[1,20,16,128]{3,2,1,0:T(8,128)(2,1)S(1)}, bf16[1,20,16,128]{3,2,1,0:T(8,128)(2,1)S(1)}, u32[]{:S(2)}, u32[]{:S(2)}) %collective-permute-start.2) | collective-permute-done | bytes 81952 | tf_op jit(solution)/shard_map/ppermute | solution.py:236
  16.4 0.6 collective-permute-start.4
  17.0 1.3 %collective-permute-start.5 = (bf16[4,12,16,128]{3,2,1,0:T(8,128)(2,1)S(1)}, bf16[4,12,16,128]{3,2,1,0:T(8,128)(2,1)S(1)}, u32[]{:S(2)}, u32[]{:S(2)}) collective-permute-start(bf16[4,12,16,128]{3,2,1,0:T(8,128)(2,1)S(1)} %constant_dynamic-slice_fusion.3), channel_id=1, source_target_pairs={{0,1},{1,0},{2,3},{3,2},{4,5},{5,4},{6,7},{7,6},{8,9},{9,8},{10,11... | collective-permute-start | bytes 589832 | tf_op jit(solution)/shard_map/ppermute | solution.py:241
  18.3 0.0 copy-done.2
  18.4 0.6 copy.20
  19.0 0.5 reshape.24.later_ref.weight_ref
  19.5 0.0 copy-start.3
  19.6 0.6 copy-done.3
  20.2 0.1 copy.15.bias_ref
  20.3 0.2 copy.13
  20.6 0.3 collective-permute-start.3
  20.9 0.0 collective-permute-done.5.other_ref
  20.9 0.8 %first_own.1 = (f32[10,128,128]{2,1,0:T(8,128)S(1)}, s32[8,128]{1,0:T(8,128)S(1)}) custom-call(bf16[4,20,16,128]{3,2,1,0:T(8,128)(2,1)S(1)} %constant_dynamic-update-slice_fusion.kept_ref, bf16[4,12,16,128]{3,2,1,0:T(8,128)(2,1)S(1)} %collective-permute-done.5.other_ref, bf16[384,384]{1,0:T(8,128)(2,1)S(1)} %bitcast.23, ...), custom_call_target="tpu_custom_call" | custom-call | flops 377487360 | bytes 4000000 | tf_op jit(solution)/shard_map/first_own/pallas_call | solution.py:205
  21.7 0.5 slice.22
  22.9 1.9 %collective-permute-done.4.kept_ref = bf16[4,20,16,128]{3,2,1,0:T(8,128)(2,1)S(1)} collective-permute-done((bf16[4,20,16,128]{3,2,1,0:T(8,128)(2,1)S(1)}, bf16[4,20,16,128]{3,2,1,0:T(8,128)(2,1)S(1)}, u32[]{:S(2)}, u32[]{:S(2)}) %collective-permute-start.4) | collective-permute-done | bytes 327712 | tf_op jit(solution)/shard_map/ppermute | solution.py:244
  24.8 2.0 %collective-permute-start.6 = (bf16[4,12,16,128]{3,2,1,0:T(8,128)(2,1)S(1)}, bf16[4,12,16,128]{3,2,1,0:T(8,128)(2,1)S(1)}, u32[]{:S(2)}, u32[]{:S(2)}) collective-permute-start(bf16[4,12,16,128]{3,2,1,0:T(8,128)(2,1)S(1)} %constant_dynamic-slice_fusion.2), channel_id=1, source_target_pairs={{0,1},{1,0},{2,3},{3,2},{4,5},{5,4},{6,7},{7,6},{8,9},{9,8},{10,11... | collective-permute-start | bytes 589832 | tf_op jit(solution)/shard_map/ppermute | solution.py:241
  26.7 1.1 %collective-permute-done.6.other_ref = bf16[4,12,16,128]{3,2,1,0:T(8,128)(2,1)S(1)} collective-permute-done((bf16[4,12,16,128]{3,2,1,0:T(8,128)(2,1)S(1)}, bf16[4,12,16,128]{3,2,1,0:T(8,128)(2,1)S(1)}, u32[]{:S(2)}, u32[]{:S(2)}) %collective-permute-start.6) | collective-permute-done | bytes 196640 | tf_op jit(solution)/shard_map/ppermute | solution.py:241
  27.8 0.8 %first_near.1 = (f32[10,128,128]{2,1,0:T(8,128)S(1)}, s32[8,128]{1,0:T(8,128)S(1)}) custom-call(bf16[4,20,16,128]{3,2,1,0:T(8,128)(2,1)S(1)} %collective-permute-done.4.kept_ref, bf16[4,12,16,128]{3,2,1,0:T(8,128)(2,1)S(1)} %collective-permute-done.6.other_ref, bf16[2,384,384]{2,1,0:T(8,128)(2,1)S(1)} %reshape.24.later_ref.weight_ref, ...), custom_call_target="tpu_custom_call" | custom-call | flops 377487360 | bytes 4000000 | tf_op jit(solution)/shard_map/first_near/pallas_call | solution.py:205
  28.6 0.5 slice.23
  29.8 4.5 %collective-permute-done.3.kept_ref = bf16[4,20,16,128]{3,2,1,0:T(8,128)(2,1)S(1)} collective-permute-done((bf16[4,20,16,128]{3,2,1,0:T(8,128)(2,1)S(1)}, bf16[4,20,16,128]{3,2,1,0:T(8,128)(2,1)S(1)}, u32[]{:S(2)}, u32[]{:S(2)}) %collective-permute-start.3) | collective-permute-done | bytes 327712 | tf_op jit(solution)/shard_map/ppermute | solution.py:244
  34.3 0.9 %collective-permute-start.7 = (bf16[4,12,16,128]{3,2,1,0:T(8,128)(2,1)S(1)}, bf16[4,12,16,128]{3,2,1,0:T(8,128)(2,1)S(1)}, u32[]{:S(2)}, u32[]{:S(2)}) collective-permute-start(bf16[4,12,16,128]{3,2,1,0:T(8,128)(2,1)S(1)} %constant_dynamic-slice_fusion.1), channel_id=1, source_target_pairs={{0,1},{1,0},{2,3},{3,2},{4,5},{5,4},{6,7},{7,6},{8,9},{9,8},{10,11... | collective-permute-start | bytes 589832 | tf_op jit(solution)/shard_map/ppermute | solution.py:241
  35.2 1.1 %collective-permute-done.7.other_ref = bf16[4,12,16,128]{3,2,1,0:T(8,128)(2,1)S(1)} collective-permute-done((bf16[4,12,16,128]{3,2,1,0:T(8,128)(2,1)S(1)}, bf16[4,12,16,128]{3,2,1,0:T(8,128)(2,1)S(1)}, u32[]{:S(2)}, u32[]{:S(2)}) %collective-permute-start.7) | collective-permute-done | bytes 196640 | tf_op jit(solution)/shard_map/ppermute | solution.py:241
  36.2 0.8 %first_far.1.plane_ref = bf16[10,128,128]{2,1,0:T(8,128)(2,1)S(1)} custom-call(bf16[4,20,16,128]{3,2,1,0:T(8,128)(2,1)S(1)} %collective-permute-done.3.kept_ref, bf16[4,12,16,128]{3,2,1,0:T(8,128)(2,1)S(1)} %collective-permute-done.7.other_ref, bf16[2,384,384]{2,1,0:T(8,128)(2,1)S(1)} %reshape.24.later_ref.weight_ref, ...), custom_call_target="tpu_custom_call" | custom-call | flops 377487360 | bytes 4000000 | tf_op jit(solution)/shard_map/first_far/pallas_call | solution.py:205
  37.1 0.1 collective-permute-start.9
  37.2 0.4 collective-permute-start.8
  37.6 0.0 slice-start
  37.6 0.0 copy-start.1
  37.6 1.0 %slice-done = bf16[9,128,128]{2,1,0:T(8,128)(2,1)S(1)} async-done(((bf16[27,128,128]{2,1,0:T(8,128)(2,1)}), bf16[9,128,128]{2,1,0:T(8,128)(2,1)S(1)}, s32[]{:S(2)}) %slice-start) | async-done | bytes 294936 | tf_op jit(solution)/shard_map/slice | solution.py:173
  38.6 0.2 copy.18
  38.9 0.0 copy-done.1
  38.9 0.6 copy.21
  39.5 0.5 reshape.26.weight_ref
  40.1 0.0 copy-start.4
  40.1 0.6 copy-done.4
  40.7 0.1 copy.19.bias_ref
  40.8 0.7 %second_own.1.before_ref = f32[8,128,128]{2,1,0:T(8,128)S(1)} custom-call(bf16[10,128,128]{2,1,0:T(8,128)(2,1)S(1)} %first_far.1.plane_ref, bf16[384,384]{1,0:T(8,128)(2,1)S(1)} %bitcast.22), custom_call_target="tpu_custom_call" | custom-call | flops 301989888 | bytes 4000000 | tf_op jit(solution)/shard_map/second_own/pallas_call | solution.py:205
  41.5 4.6 %collective-permute-done.9.plane_ref = bf16[10,128,128]{2,1,0:T(8,128)(2,1)S(1)} collective-permute-done((bf16[10,128,128]{2,1,0:T(8,128)(2,1)S(1)}, bf16[10,128,128]{2,1,0:T(8,128)(2,1)S(1)}, u32[]{:S(2)}, u32[]{:S(2)}) %collective-permute-start.9) | collective-permute-done | bytes 327712 | tf_op jit(solution)/shard_map/ppermute | solution.py:244
  46.1 0.7 %second_near.1.before_ref = f32[8,128,128]{2,1,0:T(8,128)S(1)} custom-call(bf16[10,128,128]{2,1,0:T(8,128)(2,1)S(1)} %collective-permute-done.9.plane_ref, bf16[2,384,384]{2,1,0:T(8,128)(2,1)S(1)} %reshape.26.weight_ref, f32[8,128,128]{2,1,0:T(8,128)S(1)} %second_own.1.before_ref), custom_call_target="tpu_custom_call" | custom-call | flops 301989888 | bytes 4000000 | tf_op jit(solution)/shard_map/second_near/pallas_call | solution.py:205
  46.7 3.8 %collective-permute-done.8.plane_ref = bf16[10,128,128]{2,1,0:T(8,128)(2,1)S(1)} collective-permute-done((bf16[10,128,128]{2,1,0:T(8,128)(2,1)S(1)}, bf16[10,128,128]{2,1,0:T(8,128)(2,1)S(1)}, u32[]{:S(2)}, u32[]{:S(2)}) %collective-permute-start.8) | collective-permute-done | bytes 327712 | tf_op jit(solution)/shard_map/ppermute | solution.py:244
  50.6 0.7 %second_far.1 = (bf16[2,8,16,128]{3,2,1,0:T(8,128)(2,1)S(1)}, bf16[2,8,16,128]{3,2,1,0:T(8,128)(2,1)S(1)}, bf16[2,8,16,128]{3,2,1,0:T(8,128)(2,1)S(1)}, bf16[2,8,16,128]{3,2,1,0:T(8,128)(2,1)S(1)}) custom-call(bf16[10,128,128]{2,1,0:T(8,128)(2,1)S(1)} %collective-permute-done.8.plane_ref, bf16[2,384,384]{2,1,0:T(8,128)(2,1)S(1)} %reshape.26.weight_ref, ...), custom_call_target="tpu_custom_call" | custom-call | flops 301989888 | bytes 4000000 | tf_op jit(solution)/shard_map/second_far/pallas_call | solution.py:205
  51.3 4.8 %collective-permute-start.10 = (bf16[2,8,16,128]{3,2,1,0:T(8,128)(2,1)S(1)}, bf16[2,8,16,128]{3,2,1,0:T(8,128)(2,1)S(1)}, u32[]{:S(2)}, u32[]{:S(2)}) collective-permute-start(bf16[2,8,16,128]{3,2,1,0:T(8,128)(2,1)S(1)} %get-tuple-element.26), channel_id=1, source_target_pairs={{0,4},{1,5},{2,6},{3,7},{4,0},{5,1},{6,2},{7,3},{8,12},{9,13},{10,... | collective-permute-start | bytes 196616 | tf_op jit(solution)/shard_map/ppermute | solution.py:295
  56.1 1.2 %collective-permute-start.11 = (bf16[2,8,16,128]{3,2,1,0:T(8,128)(2,1)S(1)}, bf16[2,8,16,128]{3,2,1,0:T(8,128)(2,1)S(1)}, u32[]{:S(2)}, u32[]{:S(2)}) collective-permute-start(bf16[2,8,16,128]{3,2,1,0:T(8,128)(2,1)S(1)} %get-tuple-element.27), channel_id=1, source_target_pairs={{0,2},{1,3},{2,4},{3,5},{4,6},{5,7},{6,0},{7,1},{8,10},{9,11},{10,... | collective-permute-start | bytes 196616 | tf_op jit(solution)/shard_map/ppermute | solution.py:295
  57.2 2.5 %collective-permute-start.12 = (bf16[2,8,16,128]{3,2,1,0:T(8,128)(2,1)S(1)}, bf16[2,8,16,128]{3,2,1,0:T(8,128)(2,1)S(1)}, u32[]{:S(2)}, u32[]{:S(2)}) collective-permute-start(bf16[2,8,16,128]{3,2,1,0:T(8,128)(2,1)S(1)} %get-tuple-element.28), channel_id=1, source_target_pairs={{0,6},{1,7},{2,0},{3,1},{4,2},{5,3},{6,4},{7,5},{8,14},{9,15},{10,... | collective-permute-start | bytes 196616 | tf_op jit(solution)/shard_map/ppermute | solution.py:295
  59.7 0.0 collective-permute-done.10.refs_2_
  59.7 1.6 %collective-permute-done.11.refs_1_ = bf16[2,8,16,128]{3,2,1,0:T(8,128)(2,1)S(1)} collective-permute-done((bf16[2,8,16,128]{3,2,1,0:T(8,128)(2,1)S(1)}, bf16[2,8,16,128]{3,2,1,0:T(8,128)(2,1)S(1)}, u32[]{:S(2)}, u32[]{:S(2)}) %collective-permute-start.11) | collective-permute-done | bytes 65568 | tf_op jit(solution)/shard_map/ppermute | solution.py:295
  61.4 0.0 collective-permute-done.12.refs_3_
  61.4 2.8 %collective-permute-start.13 = (bf16[4,8,16,128]{3,2,1,0:T(8,128)(2,1)S(1)}, bf16[4,8,16,128]{3,2,1,0:T(8,128)(2,1)S(1)}, u32[]{:S(2)}, u32[]{:S(2)}) collective-permute-start(bf16[4,8,16,128]{3,2,1,0:T(8,128)(2,1)S(1)} %dynamic-slice_dynamic-update-slice_fusion), channel_id=1, source_target_pairs={{0,1},{1,0},{2,3},{3,2},{4,5},{5,4},{6,7},{7,6},{8,9},{9,8},{10,11... | collective-permute-start | bytes 393224 | tf_op jit(solution)/shard_map/ppermute | solution.py:298
  64.2 1.0 %collective-permute-done.13.swapped_ref = bf16[4,8,16,128]{3,2,1,0:T(8,128)(2,1)S(1)} collective-permute-done((bf16[4,8,16,128]{3,2,1,0:T(8,128)(2,1)S(1)}, bf16[4,8,16,128]{3,2,1,0:T(8,128)(2,1)S(1)}, u32[]{:S(2)}, u32[]{:S(2)}) %collective-permute-start.13) | collective-permute-done | bytes 131104 | tf_op jit(solution)/shard_map/ppermute | solution.py:298
  65.2 0.8 %unpack_rows.1 = bf16[16,1,64,128]{3,2,1,0:T(8,128)(2,1)} custom-call(bf16[4,8,16,128]{3,2,1,0:T(8,128)(2,1)S(1)} %collective-permute-done.13.swapped_ref, bf16[2,8,16,128]{3,2,1,0:T(8,128)(2,1)S(1)} %get-tuple-element.25.refs_0_, bf16[2,8,16,128]{3,2,1,0:T(8,128)(2,1)S(1)} %collective-permute-done.11.refs_1_, ...), custom_call_target="tpu_custom_call" | custom-call | tf_op jit(solution)/shard_map/unpack_rows/pallas_call | solution.py:205
  (18 shorter events, 0.4 us)
Async XLA Ops:
  0.0 0.9 %copy-start = (bf16[16,1,64,128]{3,2,1,0:T(8,128)(2,1)S(1)}, bf16[16,1,64,128]{3,2,1,0:T(8,128)(2,1)}, u32[]{:S(2)}) copy-start(bf16[16,1,64,128]{3,2,1,0:T(8,128)(2,1)} %volume_ref.1) | copy-start | bytes 786436
  1.0 17.4 %copy-start.2 = (bf16[27,128,128]{2,1,0:T(8,128)(2,1)S(1)}, bf16[27,128,128]{2,1,0:T(8,128)(2,1)}, u32[]{:S(2)}) copy-start(bf16[27,128,128]{2,1,0:T(8,128)(2,1)} %param.6) | copy-start | bytes 2654212
  1.1 10.6 %collective-permute-start = (bf16[1,20,16,128]{3,2,1,0:T(8,128)(2,1)S(1)}, bf16[1,20,16,128]{3,2,1,0:T(8,128)(2,1)S(1)}, u32[]{:S(2)}, u32[]{:S(2)}) collective-permute-start(bf16[1,20,16,128]{3,2,1,0:T(8,128)(2,1)S(1)} %get-tuple-element.18), channel_id=1, source_target_pairs={{0,4},{1,5},{2,6},{3,7},{4,0},{5,1},{6,2},{7,3},{8,12},{9,13},{10,... | collective-permute-start | bytes 245768 | tf_op jit(solution)/shard_map/ppermute | solution.py:236
  8.1 6.0 %collective-permute-start.1 = (bf16[1,20,16,128]{3,2,1,0:T(8,128)(2,1)S(1)}, bf16[1,20,16,128]{3,2,1,0:T(8,128)(2,1)S(1)}, u32[]{:S(2)}, u32[]{:S(2)}) collective-permute-start(bf16[1,20,16,128]{3,2,1,0:T(8,128)(2,1)S(1)} %get-tuple-element.19), channel_id=1, source_target_pairs={{0,2},{1,3},{2,4},{3,5},{4,6},{5,7},{6,0},{7,1},{8,10},{9,11},{10,... | collective-permute-start | bytes 245768 | tf_op jit(solution)/shard_map/ppermute | solution.py:236
  9.3 7.1 %collective-permute-start.2 = (bf16[1,20,16,128]{3,2,1,0:T(8,128)(2,1)S(1)}, bf16[1,20,16,128]{3,2,1,0:T(8,128)(2,1)S(1)}, u32[]{:S(2)}, u32[]{:S(2)}) collective-permute-start(bf16[1,20,16,128]{3,2,1,0:T(8,128)(2,1)S(1)} %get-tuple-element.20), channel_id=1, source_target_pairs={{0,6},{1,7},{2,0},{3,1},{4,2},{5,3},{6,4},{7,5},{8,14},{9,15},{10,... | collective-permute-start | bytes 245768 | tf_op jit(solution)/shard_map/ppermute | solution.py:236
  16.4 8.3 %collective-permute-start.4 = (bf16[4,20,16,128]{3,2,1,0:T(8,128)(2,1)S(1)}, bf16[4,20,16,128]{3,2,1,0:T(8,128)(2,1)S(1)}, u32[]{:S(2)}, u32[]{:S(2)}) collective-permute-start(bf16[4,20,16,128]{3,2,1,0:T(8,128)(2,1)S(1)} %constant_dynamic-update-slice_fusion.kept_ref), channel_id=1, source_target_pairs={{0,8},{8,0},{16,24},{24,16},{32,40},{40,32},{48,56},{56,48},{64,72... | collective-permute-start | bytes 983048 | tf_op jit(solution)/shard_map/ppermute | solution.py:244
  17.0 3.9 %collective-permute-start.5 = (bf16[4,12,16,128]{3,2,1,0:T(8,128)(2,1)S(1)}, bf16[4,12,16,128]{3,2,1,0:T(8,128)(2,1)S(1)}, u32[]{:S(2)}, u32[]{:S(2)}) collective-permute-start(bf16[4,12,16,128]{3,2,1,0:T(8,128)(2,1)S(1)} %constant_dynamic-slice_fusion.3), channel_id=1, source_target_pairs={{0,1},{1,0},{2,3},{3,2},{4,5},{5,4},{6,7},{7,6},{8,9},{9,8},{10,11... | collective-permute-start | bytes 589832 | tf_op jit(solution)/shard_map/ppermute | solution.py:241
  19.5 0.7 copy-start.3
  20.6 13.6 %collective-permute-start.3 = (bf16[4,20,16,128]{3,2,1,0:T(8,128)(2,1)S(1)}, bf16[4,20,16,128]{3,2,1,0:T(8,128)(2,1)S(1)}, u32[]{:S(2)}, u32[]{:S(2)}) collective-permute-start(bf16[4,20,16,128]{3,2,1,0:T(8,128)(2,1)S(1)} %constant_dynamic-update-slice_fusion.kept_ref), channel_id=1, source_target_pairs={{0,1},{1,0},{2,3},{3,2},{4,5},{5,4},{6,7},{7,6},{8,16},{9,17},{10,... | collective-permute-start | bytes 983048 | tf_op jit(solution)/shard_map/ppermute | solution.py:244
  24.8 3.0 %collective-permute-start.6 = (bf16[4,12,16,128]{3,2,1,0:T(8,128)(2,1)S(1)}, bf16[4,12,16,128]{3,2,1,0:T(8,128)(2,1)S(1)}, u32[]{:S(2)}, u32[]{:S(2)}) collective-permute-start(bf16[4,12,16,128]{3,2,1,0:T(8,128)(2,1)S(1)} %constant_dynamic-slice_fusion.2), channel_id=1, source_target_pairs={{0,1},{1,0},{2,3},{3,2},{4,5},{5,4},{6,7},{7,6},{8,9},{9,8},{10,11... | collective-permute-start | bytes 589832 | tf_op jit(solution)/shard_map/ppermute | solution.py:241
  34.3 2.0 %collective-permute-start.7 = (bf16[4,12,16,128]{3,2,1,0:T(8,128)(2,1)S(1)}, bf16[4,12,16,128]{3,2,1,0:T(8,128)(2,1)S(1)}, u32[]{:S(2)}, u32[]{:S(2)}) collective-permute-start(bf16[4,12,16,128]{3,2,1,0:T(8,128)(2,1)S(1)} %constant_dynamic-slice_fusion.1), channel_id=1, source_target_pairs={{0,1},{1,0},{2,3},{3,2},{4,5},{5,4},{6,7},{7,6},{8,9},{9,8},{10,11... | collective-permute-start | bytes 589832 | tf_op jit(solution)/shard_map/ppermute | solution.py:241
  37.1 9.0 %collective-permute-start.9 = (bf16[10,128,128]{2,1,0:T(8,128)(2,1)S(1)}, bf16[10,128,128]{2,1,0:T(8,128)(2,1)S(1)}, u32[]{:S(2)}, u32[]{:S(2)}) collective-permute-start(bf16[10,128,128]{2,1,0:T(8,128)(2,1)S(1)} %first_far.1.plane_ref), channel_id=1, source_target_pairs={{0,8},{8,0},{16,24},{24,16},{32,40},{40,32},{48,56},{56,48},{64,72... | collective-permute-start | bytes 983048 | tf_op jit(solution)/shard_map/ppermute | solution.py:244
  37.2 13.4 %collective-permute-start.8 = (bf16[10,128,128]{2,1,0:T(8,128)(2,1)S(1)}, bf16[10,128,128]{2,1,0:T(8,128)(2,1)S(1)}, u32[]{:S(2)}, u32[]{:S(2)}) collective-permute-start(bf16[10,128,128]{2,1,0:T(8,128)(2,1)S(1)} %first_far.1.plane_ref), channel_id=1, source_target_pairs={{0,1},{1,0},{2,3},{3,2},{4,5},{5,4},{6,7},{7,6},{8,16},{9,17},{10,... | collective-permute-start | bytes 983048 | tf_op jit(solution)/shard_map/ppermute | solution.py:244
  37.6 1.0 %slice-start = ((bf16[27,128,128]{2,1,0:T(8,128)(2,1)}), bf16[9,128,128]{2,1,0:T(8,128)(2,1)S(1)}, s32[]{:S(2)}) async-start(bf16[27,128,128]{2,1,0:T(8,128)(2,1)} %param.8), calls=%async_computation | async-start | bytes 589824 | tf_op jit(solution)/shard_map/slice | solution.py:173
  37.6 1.3 %copy-start.1 = (bf16[27,128,128]{2,1,0:T(8,128)(2,1)S(1)}, bf16[27,128,128]{2,1,0:T(8,128)(2,1)}, u32[]{:S(2)}) copy-start(bf16[27,128,128]{2,1,0:T(8,128)(2,1)} %param.8) | copy-start | bytes 2654212
  40.1 0.7 copy-start.4
  51.3 8.4 %collective-permute-start.10 = (bf16[2,8,16,128]{3,2,1,0:T(8,128)(2,1)S(1)}, bf16[2,8,16,128]{3,2,1,0:T(8,128)(2,1)S(1)}, u32[]{:S(2)}, u32[]{:S(2)}) collective-permute-start(bf16[2,8,16,128]{3,2,1,0:T(8,128)(2,1)S(1)} %get-tuple-element.26), channel_id=1, source_target_pairs={{0,4},{1,5},{2,6},{3,7},{4,0},{5,1},{6,2},{7,3},{8,12},{9,13},{10,... | collective-permute-start | bytes 196616 | tf_op jit(solution)/shard_map/ppermute | solution.py:295
  56.1 5.3 %collective-permute-start.11 = (bf16[2,8,16,128]{3,2,1,0:T(8,128)(2,1)S(1)}, bf16[2,8,16,128]{3,2,1,0:T(8,128)(2,1)S(1)}, u32[]{:S(2)}, u32[]{:S(2)}) collective-permute-start(bf16[2,8,16,128]{3,2,1,0:T(8,128)(2,1)S(1)} %get-tuple-element.27), channel_id=1, source_target_pairs={{0,2},{1,3},{2,4},{3,5},{4,6},{5,7},{6,0},{7,1},{8,10},{9,11},{10,... | collective-permute-start | bytes 196616 | tf_op jit(solution)/shard_map/ppermute | solution.py:295
  57.2 4.1 %collective-permute-start.12 = (bf16[2,8,16,128]{3,2,1,0:T(8,128)(2,1)S(1)}, bf16[2,8,16,128]{3,2,1,0:T(8,128)(2,1)S(1)}, u32[]{:S(2)}, u32[]{:S(2)}) collective-permute-start(bf16[2,8,16,128]{3,2,1,0:T(8,128)(2,1)S(1)} %get-tuple-element.28), channel_id=1, source_target_pairs={{0,6},{1,7},{2,0},{3,1},{4,2},{5,3},{6,4},{7,5},{8,14},{9,15},{10,... | collective-permute-start | bytes 196616 | tf_op jit(solution)/shard_map/ppermute | solution.py:295
  61.4 3.8 %collective-permute-start.13 = (bf16[4,8,16,128]{3,2,1,0:T(8,128)(2,1)S(1)}, bf16[4,8,16,128]{3,2,1,0:T(8,128)(2,1)S(1)}, u32[]{:S(2)}, u32[]{:S(2)}) collective-permute-start(bf16[4,8,16,128]{3,2,1,0:T(8,128)(2,1)S(1)} %dynamic-slice_dynamic-update-slice_fusion), channel_id=1, source_target_pairs={{0,1},{1,0},{2,3},{3,2},{4,5},{5,4},{6,7},{7,6},{8,9},{9,8},{10,11... | collective-permute-start | bytes 393224 | tf_op jit(solution)/shard_map/ppermute | solution.py:298

commit v15 on v12

--- a/solution.py
+++ b/solution.py
@@ -194,7 +194,7 @@
 
     far = [(i * chan + j, far_partner(i, j)) for i in range(space) for j in range(chan)]
 
-    order = sorted(range(1, groups), key=lambda k: abs(k - groups // 2))
+    order = sorted(range(1, groups), key=lambda k: (abs(k - groups // 2), -k))
 
     def ahead(k):
         return [(i, (i + CORES * k) % chan) for i in range(chan)]

time: 63.9 us -> 64.3 us (level)
  starting transfers between devices: 27.3 us -> 25.4 us
  waiting for transfers between devices: 21.2 us -> 23 us
    ppermute x3, waiting for transfers between devices: 4.6 us -> 6.16 us  [per_device(): got = lax.ppermute(pieces[k], 'chan', ahead(k))]
    ppermute x2, starting transfers between devices: 0.61 us -> 2.06 us  [halo(): lax.ppermute(array, ('space', 'chan'), far)]
    ppermute x3, waiting for transfers between devices: 1.64 us -> 2.93 us  [per_device(): blocks[k] = lax.ppermute(blocks[k], 'chan', ahead(k))]
    ppermute x3, starting transfers between devices: 10.6 us -> 9.36 us  [per_device(): got = lax.ppermute(pieces[k], 'chan', ahead(k))]
    ppermute x3, starting transfers between devices: 8.41 us -> 7.24 us  [per_device(): blocks[k] = lax.ppermute(blocks[k], 'chan', ahead(k))]
    ppermute x3, starting transfers between devices: 4.26 us -> 3.46 us  [from_other_core(): return lax.ppermute(sent, 'chan', swap)]
    ppermute x2, waiting for transfers between devices: 4.79 us -> 4.14 us  [halo(): lax.ppermute(array, 'space', near)]
  transfers between devices with their start and end apart: 14 -> 14, of which waited for: 9 -> 10; matrix products, arithmetic and copies ran while one was open for 9% -> 9% of each run, Pallas kernels for 5% -> 5%
where the time goes in v15:
time: 64.3 us; the launch traced here: 63.6 us
  starting transfers between devices  25.4 us (40%)
  waiting for transfers between devices  23 us (36%)
  local copies, waits for them, and re-layouts  8.83 us (14%)
  Pallas kernels  5.48 us (9%)
  between operations  0.89 us (1%)
    ppermute x3, starting transfers between devices, per_device(): got = lax.ppermute(pieces[k], 'chan', ahead(k))  9.36 us
    ppermute x2, waiting for transfers between devices, halo(): lax.ppermute(array, ('space', 'chan'), far)  8.52 us
    ppermute x3, starting transfers between devices, per_device(): blocks[k] = lax.ppermute(blocks[k], 'chan', ahead(k))  7.24 us
    ppermute x3, waiting for transfers between devices, per_device(): got = lax.ppermute(pieces[k], 'chan', ahead(k))  6.16 us
    pallas_call x8, Pallas kernels, call(): pl.pallas_call(kernel, out_shape=shapes, in_specs=[VMEM] * len(inputs), o...  5.48 us
    ppermute x2, waiting for transfers between devices, halo(): lax.ppermute(array, 'space', near)  4.14 us
    unnamed x14, local copies, waits for them, and re-layouts  3.57 us
    ppermute x3, starting transfers between devices, from_other_core(): return lax.ppermute(sent, 'chan', swap)  3.46 us
  transfers between devices with their start and end apart: 14, of which 10 were waited for; matrix products, arithmetic and copies ran while one was open for 9% of the time, Pallas kernels for 5%

profile of v15, /device:TPU:31, one launch (start us, length us, event | category | flops | bytes accessed | tf_op | source)
XLA Modules:
  0.0 63.6 jit_solution(13474383821028614248)
XLA Ops:
  0.0 0.0 copy-start
  0.0 0.9 %copy-done = bf16[16,1,64,128]{3,2,1,0:T(8,128)(2,1)S(1)} copy-done((bf16[16,1,64,128]{3,2,1,0:T(8,128)(2,1)S(1)}, bf16[16,1,64,128]{3,2,1,0:T(8,128)(2,1)}, u32[]{:S(2)}) %copy-start) | copy-done | bytes 262168
  1.0 0.0 copy-start.2
  1.0 0.2 pack_rows.1
  1.1 7.0 %collective-permute-start = (bf16[1,20,16,128]{3,2,1,0:T(8,128)(2,1)S(1)}, bf16[1,20,16,128]{3,2,1,0:T(8,128)(2,1)S(1)}, u32[]{:S(2)}, u32[]{:S(2)}) collective-permute-start(bf16[1,20,16,128]{3,2,1,0:T(8,128)(2,1)S(1)} %get-tuple-element.16), channel_id=1, source_target_pairs={{0,4},{1,5},{2,6},{3,7},{4,0},{5,1},{6,2},{7,3},{8,12},{9,13},{10,... | collective-permute-start | bytes 245768 | tf_op jit(solution)/shard_map/ppermute | solution.py:235
  8.1 0.0 collective-permute-start.1
  8.1 2.4 %collective-permute-start.2 = (bf16[1,20,16,128]{3,2,1,0:T(8,128)(2,1)S(1)}, bf16[1,20,16,128]{3,2,1,0:T(8,128)(2,1)S(1)}, u32[]{:S(2)}, u32[]{:S(2)}) collective-permute-start(bf16[1,20,16,128]{3,2,1,0:T(8,128)(2,1)S(1)} %get-tuple-element.18), channel_id=1, source_target_pairs={{0,2},{1,3},{2,4},{3,5},{4,6},{5,7},{6,0},{7,1},{8,10},{9,11},{10,... | collective-permute-start | bytes 245768 | tf_op jit(solution)/shard_map/ppermute | solution.py:235
  10.6 0.0 collective-permute-done
  10.6 6.2 %collective-permute-done.1 = bf16[1,20,16,128]{3,2,1,0:T(8,128)(2,1)S(1)} collective-permute-done((bf16[1,20,16,128]{3,2,1,0:T(8,128)(2,1)S(1)}, bf16[1,20,16,128]{3,2,1,0:T(8,128)(2,1)S(1)}, u32[]{:S(2)}, u32[]{:S(2)}) %collective-permute-start.1) | collective-permute-done | bytes 81952 | tf_op jit(solution)/shard_map/ppermute | solution.py:235
  16.8 0.0 collective-permute-done.2
  16.8 0.6 collective-permute-start.6
  17.4 1.0 %collective-permute-start.4 = (bf16[4,12,16,128]{3,2,1,0:T(8,128)(2,1)S(1)}, bf16[4,12,16,128]{3,2,1,0:T(8,128)(2,1)S(1)}, u32[]{:S(2)}, u32[]{:S(2)}) collective-permute-start(bf16[4,12,16,128]{3,2,1,0:T(8,128)(2,1)S(1)} %constant_dynamic-slice_fusion.3), channel_id=1, source_target_pairs={{0,1},{1,0},{2,3},{3,2},{4,5},{5,4},{6,7},{7,6},{8,9},{9,8},{10,11... | collective-permute-start | bytes 589832 | tf_op jit(solution)/shard_map/ppermute | solution.py:240
  18.3 0.9 %collective-permute-start.3 = (bf16[4,20,16,128]{3,2,1,0:T(8,128)(2,1)S(1)}, bf16[4,20,16,128]{3,2,1,0:T(8,128)(2,1)S(1)}, u32[]{:S(2)}, u32[]{:S(2)}) collective-permute-start(bf16[4,20,16,128]{3,2,1,0:T(8,128)(2,1)S(1)} %constant_dynamic-update-slice_fusion.kept_ref), channel_id=1, source_target_pairs={{0,1},{1,0},{2,3},{3,2},{4,5},{5,4},{6,7},{7,6},{8,16},{9,17},{10,... | collective-permute-start | bytes 983048 | tf_op jit(solution)/shard_map/ppermute | solution.py:243
  19.2 0.0 copy-done.2
  19.2 0.7 %slice.17 = bf16[9,128,128]{2,1,0:T(8,128)(2,1)} slice(bf16[27,128,128]{2,1,0:T(8,128)(2,1)S(1)} %copy-done.2), slice={[9:18], [0:128], [0:128]} | slice | bytes 589824 | tf_op jit(solution)/shard_map/slice | solution.py:172
  20.0 0.6 copy.20
  20.6 0.5 reshape.24.later_ref.weight_ref
  21.2 0.0 copy-start.3
  21.2 0.6 %copy-done.3 = f32[128]{0:T(128)S(1)} copy-done((f32[128]{0:T(128)S(1)}, f32[128]{0:T(128)}, u32[]{:S(2)}) %copy-start.3) | copy-done | bytes 536
  21.8 0.1 copy.15.bias_ref
  21.9 1.2 %copy.13 = bf16[3,3,128,128]{2,0,3,1:T(4,128)(2,1)S(1)} copy(bf16[3,3,128,128]{3,2,1,0:T(8,128)(2,1)} %bitcast.27) | data formatting | bytes 589824 | tf_op jit(solution)/shard_map/squeeze | solution.py:172
  23.2 0.0 collective-permute-done.4.other_ref
  23.2 0.8 %first_own.1 = (f32[10,128,128]{2,1,0:T(8,128)S(1)}, s32[8,128]{1,0:T(8,128)S(1)}) custom-call(bf16[4,20,16,128]{3,2,1,0:T(8,128)(2,1)S(1)} %constant_dynamic-update-slice_fusion.kept_ref, bf16[4,12,16,128]{3,2,1,0:T(8,128)(2,1)S(1)} %collective-permute-done.4.other_ref, bf16[384,384]{1,0:T(8,128)(2,1)S(1)} %bitcast.22, ...), custom_call_target="tpu_custom_call" | custom-call | flops 377487360 | bytes 4000000 | tf_op jit(solution)/shard_map/first_own/pallas_call | solution.py:204
  24.0 0.5 slice.19
  25.2 0.4 collective-permute-done.6.kept_ref
  25.6 1.5 %collective-permute-start.7 = (bf16[4,12,16,128]{3,2,1,0:T(8,128)(2,1)S(1)}, bf16[4,12,16,128]{3,2,1,0:T(8,128)(2,1)S(1)}, u32[]{:S(2)}, u32[]{:S(2)}) collective-permute-start(bf16[4,12,16,128]{3,2,1,0:T(8,128)(2,1)S(1)} %constant_dynamic-slice_fusion.1), channel_id=1, source_target_pairs={{0,1},{1,0},{2,3},{3,2},{4,5},{5,4},{6,7},{7,6},{8,9},{9,8},{10,11... | collective-permute-start | bytes 589832 | tf_op jit(solution)/shard_map/ppermute | solution.py:240
  27.1 4.7 %collective-permute-done.3.kept_ref = bf16[4,20,16,128]{3,2,1,0:T(8,128)(2,1)S(1)} collective-permute-done((bf16[4,20,16,128]{3,2,1,0:T(8,128)(2,1)S(1)}, bf16[4,20,16,128]{3,2,1,0:T(8,128)(2,1)S(1)}, u32[]{:S(2)}, u32[]{:S(2)}) %collective-permute-start.3) | collective-permute-done | bytes 327712 | tf_op jit(solution)/shard_map/ppermute | solution.py:243
  31.8 1.0 %collective-permute-start.5 = (bf16[4,12,16,128]{3,2,1,0:T(8,128)(2,1)S(1)}, bf16[4,12,16,128]{3,2,1,0:T(8,128)(2,1)S(1)}, u32[]{:S(2)}, u32[]{:S(2)}) collective-permute-start(bf16[4,12,16,128]{3,2,1,0:T(8,128)(2,1)S(1)} %constant_dynamic-slice_fusion.2), channel_id=1, source_target_pairs={{0,1},{1,0},{2,3},{3,2},{4,5},{5,4},{6,7},{7,6},{8,9},{9,8},{10,11... | collective-permute-start | bytes 589832 | tf_op jit(solution)/shard_map/ppermute | solution.py:240
  32.8 0.0 collective-permute-done.7.other_ref
  32.8 0.8 %first_near.1.before_ref = f32[10,128,128]{2,1,0:T(8,128)S(1)} custom-call(bf16[4,20,16,128]{3,2,1,0:T(8,128)(2,1)S(1)} %collective-permute-done.6.kept_ref, bf16[4,12,16,128]{3,2,1,0:T(8,128)(2,1)S(1)} %collective-permute-done.7.other_ref, bf16[2,384,384]{2,1,0:T(8,128)(2,1)S(1)} %reshape.24.later_ref.weight_ref, ...), custom_call_target="tpu_custom_call" | custom-call | flops 377487360 | bytes 4000000 | tf_op jit(solution)/shard_map/first_near/pallas_call | solution.py:204
  33.6 0.3 collective-permute-done.5.other_ref
  33.9 0.8 %first_far.1.plane_ref = bf16[10,128,128]{2,1,0:T(8,128)(2,1)S(1)} custom-call(bf16[4,20,16,128]{3,2,1,0:T(8,128)(2,1)S(1)} %collective-permute-done.3.kept_ref, bf16[4,12,16,128]{3,2,1,0:T(8,128)(2,1)S(1)} %collective-permute-done.5.other_ref, bf16[2,384,384]{2,1,0:T(8,128)(2,1)S(1)} %reshape.24.later_ref.weight_ref, ...), custom_call_target="tpu_custom_call" | custom-call | flops 377487360 | bytes 4000000 | tf_op jit(solution)/shard_map/first_far/pallas_call | solution.py:204
  34.7 0.1 collective-permute-start.9
  34.8 1.2 %collective-permute-start.8 = (bf16[10,128,128]{2,1,0:T(8,128)(2,1)S(1)}, bf16[10,128,128]{2,1,0:T(8,128)(2,1)S(1)}, u32[]{:S(2)}, u32[]{:S(2)}) collective-permute-start(bf16[10,128,128]{2,1,0:T(8,128)(2,1)S(1)} %first_far.1.plane_ref), channel_id=1, source_target_pairs={{0,1},{1,0},{2,3},{3,2},{4,5},{5,4},{6,7},{7,6},{8,16},{9,17},{10,... | collective-permute-start | bytes 983048 | tf_op jit(solution)/shard_map/ppermute | solution.py:243
  35.9 0.0 slice-start
  35.9 0.0 copy-start.1
  35.9 1.0 %slice-done = bf16[9,128,128]{2,1,0:T(8,128)(2,1)S(1)} async-done(((bf16[27,128,128]{2,1,0:T(8,128)(2,1)}), bf16[9,128,128]{2,1,0:T(8,128)(2,1)S(1)}, s32[]{:S(2)}) %slice-start) | async-done | bytes 294936 | tf_op jit(solution)/shard_map/slice | solution.py:172
  36.9 0.2 copy.18
  37.2 0.1 copy-done.1
  37.3 0.6 copy.21
  37.9 0.5 reshape.26.weight_ref
  38.5 0.0 copy-start.4
  38.5 0.6 %copy-done.4 = f32[128]{0:T(128)S(1)} copy-done((f32[128]{0:T(128)S(1)}, f32[128]{0:T(128)}, u32[]{:S(2)}) %copy-start.4) | copy-done | bytes 536
  39.1 0.1 copy.19.bias_ref
  39.2 0.7 %second_own.1.before_ref = f32[8,128,128]{2,1,0:T(8,128)S(1)} custom-call(bf16[10,128,128]{2,1,0:T(8,128)(2,1)S(1)} %first_far.1.plane_ref, bf16[384,384]{1,0:T(8,128)(2,1)S(1)} %bitcast.21), custom_call_target="tpu_custom_call" | custom-call | flops 301989888 | bytes 4000000 | tf_op jit(solution)/shard_map/second_own/pallas_call | solution.py:204
  39.9 3.8 %collective-permute-done.9.plane_ref = bf16[10,128,128]{2,1,0:T(8,128)(2,1)S(1)} collective-permute-done((bf16[10,128,128]{2,1,0:T(8,128)(2,1)S(1)}, bf16[10,128,128]{2,1,0:T(8,128)(2,1)S(1)}, u32[]{:S(2)}, u32[]{:S(2)}) %collective-permute-start.9) | collective-permute-done | bytes 327712 | tf_op jit(solution)/shard_map/ppermute | solution.py:243
  43.7 0.7 %second_near.1.before_ref = f32[8,128,128]{2,1,0:T(8,128)S(1)} custom-call(bf16[10,128,128]{2,1,0:T(8,128)(2,1)S(1)} %collective-permute-done.9.plane_ref, bf16[2,384,384]{2,1,0:T(8,128)(2,1)S(1)} %reshape.26.weight_ref, f32[8,128,128]{2,1,0:T(8,128)S(1)} %second_own.1.before_ref), custom_call_target="tpu_custom_call" | custom-call | flops 301989888 | bytes 4000000 | tf_op jit(solution)/shard_map/second_near/pallas_call | solution.py:204
  44.4 3.8 %collective-permute-done.8.plane_ref = bf16[10,128,128]{2,1,0:T(8,128)(2,1)S(1)} collective-permute-done((bf16[10,128,128]{2,1,0:T(8,128)(2,1)S(1)}, bf16[10,128,128]{2,1,0:T(8,128)(2,1)S(1)}, u32[]{:S(2)}, u32[]{:S(2)}) %collective-permute-start.8) | collective-permute-done | bytes 327712 | tf_op jit(solution)/shard_map/ppermute | solution.py:243
  48.2 0.7 %second_far.1 = (bf16[2,8,16,128]{3,2,1,0:T(8,128)(2,1)S(1)}, bf16[2,8,16,128]{3,2,1,0:T(8,128)(2,1)S(1)}, bf16[2,8,16,128]{3,2,1,0:T(8,128)(2,1)S(1)}, bf16[2,8,16,128]{3,2,1,0:T(8,128)(2,1)S(1)}) custom-call(bf16[10,128,128]{2,1,0:T(8,128)(2,1)S(1)} %collective-permute-done.8.plane_ref, bf16[2,384,384]{2,1,0:T(8,128)(2,1)S(1)} %reshape.26.weight_ref, ...), custom_call_target="tpu_custom_call" | custom-call | flops 301989888 | bytes 4000000 | tf_op jit(solution)/shard_map/second_far/pallas_call | solution.py:204
  48.9 4.8 %collective-permute-start.10 = (bf16[2,8,16,128]{3,2,1,0:T(8,128)(2,1)S(1)}, bf16[2,8,16,128]{3,2,1,0:T(8,128)(2,1)S(1)}, u32[]{:S(2)}, u32[]{:S(2)}) collective-permute-start(bf16[2,8,16,128]{3,2,1,0:T(8,128)(2,1)S(1)} %get-tuple-element.22), channel_id=1, source_target_pairs={{0,4},{1,5},{2,6},{3,7},{4,0},{5,1},{6,2},{7,3},{8,12},{9,13},{10,... | collective-permute-start | bytes 196616 | tf_op jit(solution)/shard_map/ppermute | solution.py:293
  53.7 0.1 collective-permute-start.11
  53.8 2.4 %collective-permute-start.12 = (bf16[2,8,16,128]{3,2,1,0:T(8,128)(2,1)S(1)}, bf16[2,8,16,128]{3,2,1,0:T(8,128)(2,1)S(1)}, u32[]{:S(2)}, u32[]{:S(2)}) collective-permute-start(bf16[2,8,16,128]{3,2,1,0:T(8,128)(2,1)S(1)} %get-tuple-element.24), channel_id=1, source_target_pairs={{0,2},{1,3},{2,4},{3,5},{4,6},{5,7},{6,0},{7,1},{8,10},{9,11},{10,... | collective-permute-start | bytes 196616 | tf_op jit(solution)/shard_map/ppermute | solution.py:293
  56.2 0.3 collective-permute-done.10.refs_2_
  56.5 1.6 %collective-permute-done.11.refs_3_ = bf16[2,8,16,128]{3,2,1,0:T(8,128)(2,1)S(1)} collective-permute-done((bf16[2,8,16,128]{3,2,1,0:T(8,128)(2,1)S(1)}, bf16[2,8,16,128]{3,2,1,0:T(8,128)(2,1)S(1)}, u32[]{:S(2)}, u32[]{:S(2)}) %collective-permute-start.11) | collective-permute-done | bytes 65568 | tf_op jit(solution)/shard_map/ppermute | solution.py:293
  58.1 1.0 %collective-permute-done.12.refs_1_ = bf16[2,8,16,128]{3,2,1,0:T(8,128)(2,1)S(1)} collective-permute-done((bf16[2,8,16,128]{3,2,1,0:T(8,128)(2,1)S(1)}, bf16[2,8,16,128]{3,2,1,0:T(8,128)(2,1)S(1)}, u32[]{:S(2)}, u32[]{:S(2)}) %collective-permute-start.12) | collective-permute-done | bytes 65568 | tf_op jit(solution)/shard_map/ppermute | solution.py:293
  59.1 2.6 %collective-permute-start.13 = (bf16[4,8,16,128]{3,2,1,0:T(8,128)(2,1)S(1)}, bf16[4,8,16,128]{3,2,1,0:T(8,128)(2,1)S(1)}, u32[]{:S(2)}, u32[]{:S(2)}) collective-permute-start(bf16[4,8,16,128]{3,2,1,0:T(8,128)(2,1)S(1)} %dynamic-slice_dynamic-update-slice_fusion), channel_id=1, source_target_pairs={{0,1},{1,0},{2,3},{3,2},{4,5},{5,4},{6,7},{7,6},{8,9},{9,8},{10,11... | collective-permute-start | bytes 393224 | tf_op jit(solution)/shard_map/ppermute | solution.py:296
  61.8 1.0 %collective-permute-done.13.swapped_ref = bf16[4,8,16,128]{3,2,1,0:T(8,128)(2,1)S(1)} collective-permute-done((bf16[4,8,16,128]{3,2,1,0:T(8,128)(2,1)S(1)}, bf16[4,8,16,128]{3,2,1,0:T(8,128)(2,1)S(1)}, u32[]{:S(2)}, u32[]{:S(2)}) %collective-permute-start.13) | collective-permute-done | bytes 131104 | tf_op jit(solution)/shard_map/ppermute | solution.py:296
  62.8 0.8 %unpack_rows.1 = bf16[16,1,64,128]{3,2,1,0:T(8,128)(2,1)} custom-call(bf16[4,8,16,128]{3,2,1,0:T(8,128)(2,1)S(1)} %collective-permute-done.13.swapped_ref, bf16[2,8,16,128]{3,2,1,0:T(8,128)(2,1)S(1)} %get-tuple-element.21.refs_0_, bf16[2,8,16,128]{3,2,1,0:T(8,128)(2,1)S(1)} %collective-permute-done.12.refs_1_, ...), custom_call_target="tpu_custom_call" | custom-call | tf_op jit(solution)/shard_map/unpack_rows/pallas_call | solution.py:204
  (17 shorter events, 0.4 us)
Async XLA Ops:
  0.0 0.9 %copy-start = (bf16[16,1,64,128]{3,2,1,0:T(8,128)(2,1)S(1)}, bf16[16,1,64,128]{3,2,1,0:T(8,128)(2,1)}, u32[]{:S(2)}) copy-start(bf16[16,1,64,128]{3,2,1,0:T(8,128)(2,1)} %volume_ref.1) | copy-start | bytes 786436
  1.0 18.3 %copy-start.2 = (bf16[27,128,128]{2,1,0:T(8,128)(2,1)S(1)}, bf16[27,128,128]{2,1,0:T(8,128)(2,1)}, u32[]{:S(2)}) copy-start(bf16[27,128,128]{2,1,0:T(8,128)(2,1)} %param.6) | copy-start | bytes 2654212
  1.1 9.4 %collective-permute-start = (bf16[1,20,16,128]{3,2,1,0:T(8,128)(2,1)S(1)}, bf16[1,20,16,128]{3,2,1,0:T(8,128)(2,1)S(1)}, u32[]{:S(2)}, u32[]{:S(2)}) collective-permute-start(bf16[1,20,16,128]{3,2,1,0:T(8,128)(2,1)S(1)} %get-tuple-element.16), channel_id=1, source_target_pairs={{0,4},{1,5},{2,6},{3,7},{4,0},{5,1},{6,2},{7,3},{8,12},{9,13},{10,... | collective-permute-start | bytes 245768 | tf_op jit(solution)/shard_map/ppermute | solution.py:235
  8.1 8.6 %collective-permute-start.1 = (bf16[1,20,16,128]{3,2,1,0:T(8,128)(2,1)S(1)}, bf16[1,20,16,128]{3,2,1,0:T(8,128)(2,1)S(1)}, u32[]{:S(2)}, u32[]{:S(2)}) collective-permute-start(bf16[1,20,16,128]{3,2,1,0:T(8,128)(2,1)S(1)} %get-tuple-element.17), channel_id=1, source_target_pairs={{0,6},{1,7},{2,0},{3,1},{4,2},{5,3},{6,4},{7,5},{8,14},{9,15},{10,... | collective-permute-start | bytes 245768 | tf_op jit(solution)/shard_map/ppermute | solution.py:235
  8.1 8.6 %collective-permute-start.2 = (bf16[1,20,16,128]{3,2,1,0:T(8,128)(2,1)S(1)}, bf16[1,20,16,128]{3,2,1,0:T(8,128)(2,1)S(1)}, u32[]{:S(2)}, u32[]{:S(2)}) collective-permute-start(bf16[1,20,16,128]{3,2,1,0:T(8,128)(2,1)S(1)} %get-tuple-element.18), channel_id=1, source_target_pairs={{0,2},{1,3},{2,4},{3,5},{4,6},{5,7},{6,0},{7,1},{8,10},{9,11},{10,... | collective-permute-start | bytes 245768 | tf_op jit(solution)/shard_map/ppermute | solution.py:235
  16.8 8.8 %collective-permute-start.6 = (bf16[4,20,16,128]{3,2,1,0:T(8,128)(2,1)S(1)}, bf16[4,20,16,128]{3,2,1,0:T(8,128)(2,1)S(1)}, u32[]{:S(2)}, u32[]{:S(2)}) collective-permute-start(bf16[4,20,16,128]{3,2,1,0:T(8,128)(2,1)S(1)} %constant_dynamic-update-slice_fusion.kept_ref), channel_id=1, source_target_pairs={{0,8},{8,0},{16,24},{24,16},{32,40},{40,32},{48,56},{56,48},{64,72... | collective-permute-start | bytes 983048 | tf_op jit(solution)/shard_map/ppermute | solution.py:243
  17.4 5.8 %collective-permute-start.4 = (bf16[4,12,16,128]{3,2,1,0:T(8,128)(2,1)S(1)}, bf16[4,12,16,128]{3,2,1,0:T(8,128)(2,1)S(1)}, u32[]{:S(2)}, u32[]{:S(2)}) collective-permute-start(bf16[4,12,16,128]{3,2,1,0:T(8,128)(2,1)S(1)} %constant_dynamic-slice_fusion.3), channel_id=1, source_target_pairs={{0,1},{1,0},{2,3},{3,2},{4,5},{5,4},{6,7},{7,6},{8,9},{9,8},{10,11... | collective-permute-start | bytes 589832 | tf_op jit(solution)/shard_map/ppermute | solution.py:240
  18.3 13.5 %collective-permute-start.3 = (bf16[4,20,16,128]{3,2,1,0:T(8,128)(2,1)S(1)}, bf16[4,20,16,128]{3,2,1,0:T(8,128)(2,1)S(1)}, u32[]{:S(2)}, u32[]{:S(2)}) collective-permute-start(bf16[4,20,16,128]{3,2,1,0:T(8,128)(2,1)S(1)} %constant_dynamic-update-slice_fusion.kept_ref), channel_id=1, source_target_pairs={{0,1},{1,0},{2,3},{3,2},{4,5},{5,4},{6,7},{7,6},{8,16},{9,17},{10,... | collective-permute-start | bytes 983048 | tf_op jit(solution)/shard_map/ppermute | solution.py:243
  21.2 0.7 %copy-start.3 = (f32[128]{0:T(128)S(1)}, f32[128]{0:T(128)}, u32[]{:S(2)}) copy-start(f32[128]{0:T(128)} %param.7) | copy-start | bytes 1540
  25.6 7.2 %collective-permute-start.7 = (bf16[4,12,16,128]{3,2,1,0:T(8,128)(2,1)S(1)}, bf16[4,12,16,128]{3,2,1,0:T(8,128)(2,1)S(1)}, u32[]{:S(2)}, u32[]{:S(2)}) collective-permute-start(bf16[4,12,16,128]{3,2,1,0:T(8,128)(2,1)S(1)} %constant_dynamic-slice_fusion.1), channel_id=1, source_target_pairs={{0,1},{1,0},{2,3},{3,2},{4,5},{5,4},{6,7},{7,6},{8,9},{9,8},{10,11... | collective-permute-start | bytes 589832 | tf_op jit(solution)/shard_map/ppermute | solution.py:240
  31.8 2.0 %collective-permute-start.5 = (bf16[4,12,16,128]{3,2,1,0:T(8,128)(2,1)S(1)}, bf16[4,12,16,128]{3,2,1,0:T(8,128)(2,1)S(1)}, u32[]{:S(2)}, u32[]{:S(2)}) collective-permute-start(bf16[4,12,16,128]{3,2,1,0:T(8,128)(2,1)S(1)} %constant_dynamic-slice_fusion.2), channel_id=1, source_target_pairs={{0,1},{1,0},{2,3},{3,2},{4,5},{5,4},{6,7},{7,6},{8,9},{9,8},{10,11... | collective-permute-start | bytes 589832 | tf_op jit(solution)/shard_map/ppermute | solution.py:240
  34.7 9.0 %collective-permute-start.9 = (bf16[10,128,128]{2,1,0:T(8,128)(2,1)S(1)}, bf16[10,128,128]{2,1,0:T(8,128)(2,1)S(1)}, u32[]{:S(2)}, u32[]{:S(2)}) collective-permute-start(bf16[10,128,128]{2,1,0:T(8,128)(2,1)S(1)} %first_far.1.plane_ref), channel_id=1, source_target_pairs={{0,8},{8,0},{16,24},{24,16},{32,40},{40,32},{48,56},{56,48},{64,72... | collective-permute-start | bytes 983048 | tf_op jit(solution)/shard_map/ppermute | solution.py:243
  34.8 13.4 %collective-permute-start.8 = (bf16[10,128,128]{2,1,0:T(8,128)(2,1)S(1)}, bf16[10,128,128]{2,1,0:T(8,128)(2,1)S(1)}, u32[]{:S(2)}, u32[]{:S(2)}) collective-permute-start(bf16[10,128,128]{2,1,0:T(8,128)(2,1)S(1)} %first_far.1.plane_ref), channel_id=1, source_target_pairs={{0,1},{1,0},{2,3},{3,2},{4,5},{5,4},{6,7},{7,6},{8,16},{9,17},{10,... | collective-permute-start | bytes 983048 | tf_op jit(solution)/shard_map/ppermute | solution.py:243
  35.9 1.0 %slice-start = ((bf16[27,128,128]{2,1,0:T(8,128)(2,1)}), bf16[9,128,128]{2,1,0:T(8,128)(2,1)S(1)}, s32[]{:S(2)}) async-start(bf16[27,128,128]{2,1,0:T(8,128)(2,1)} %param.8), calls=%async_computation | async-start | bytes 589824 | tf_op jit(solution)/shard_map/slice | solution.py:172
  35.9 1.3 %copy-start.1 = (bf16[27,128,128]{2,1,0:T(8,128)(2,1)S(1)}, bf16[27,128,128]{2,1,0:T(8,128)(2,1)}, u32[]{:S(2)}) copy-start(bf16[27,128,128]{2,1,0:T(8,128)(2,1)} %param.8) | copy-start | bytes 2654212
  38.5 0.7 %copy-start.4 = (f32[128]{0:T(128)S(1)}, f32[128]{0:T(128)}, u32[]{:S(2)}) copy-start(f32[128]{0:T(128)} %param.9) | copy-start | bytes 1540
  48.9 7.6 %collective-permute-start.10 = (bf16[2,8,16,128]{3,2,1,0:T(8,128)(2,1)S(1)}, bf16[2,8,16,128]{3,2,1,0:T(8,128)(2,1)S(1)}, u32[]{:S(2)}, u32[]{:S(2)}) collective-permute-start(bf16[2,8,16,128]{3,2,1,0:T(8,128)(2,1)S(1)} %get-tuple-element.22), channel_id=1, source_target_pairs={{0,4},{1,5},{2,6},{3,7},{4,0},{5,1},{6,2},{7,3},{8,12},{9,13},{10,... | collective-permute-start | bytes 196616 | tf_op jit(solution)/shard_map/ppermute | solution.py:293
  53.7 4.4 %collective-permute-start.11 = (bf16[2,8,16,128]{3,2,1,0:T(8,128)(2,1)S(1)}, bf16[2,8,16,128]{3,2,1,0:T(8,128)(2,1)S(1)}, u32[]{:S(2)}, u32[]{:S(2)}) collective-permute-start(bf16[2,8,16,128]{3,2,1,0:T(8,128)(2,1)S(1)} %get-tuple-element.23), channel_id=1, source_target_pairs={{0,6},{1,7},{2,0},{3,1},{4,2},{5,3},{6,4},{7,5},{8,14},{9,15},{10,... | collective-permute-start | bytes 196616 | tf_op jit(solution)/shard_map/ppermute | solution.py:293
  53.8 5.3 %collective-permute-start.12 = (bf16[2,8,16,128]{3,2,1,0:T(8,128)(2,1)S(1)}, bf16[2,8,16,128]{3,2,1,0:T(8,128)(2,1)S(1)}, u32[]{:S(2)}, u32[]{:S(2)}) collective-permute-start(bf16[2,8,16,128]{3,2,1,0:T(8,128)(2,1)S(1)} %get-tuple-element.24), channel_id=1, source_target_pairs={{0,2},{1,3},{2,4},{3,5},{4,6},{5,7},{6,0},{7,1},{8,10},{9,11},{10,... | collective-permute-start | bytes 196616 | tf_op jit(solution)/shard_map/ppermute | solution.py:293
  59.1 3.6 %collective-permute-start.13 = (bf16[4,8,16,128]{3,2,1,0:T(8,128)(2,1)S(1)}, bf16[4,8,16,128]{3,2,1,0:T(8,128)(2,1)S(1)}, u32[]{:S(2)}, u32[]{:S(2)}) collective-permute-start(bf16[4,8,16,128]{3,2,1,0:T(8,128)(2,1)S(1)} %dynamic-slice_dynamic-update-slice_fusion), channel_id=1, source_target_pairs={{0,1},{1,0},{2,3},{3,2},{4,5},{5,4},{6,7},{7,6},{8,9},{9,8},{10,11... | collective-permute-start | bytes 393224 | tf_op jit(solution)/shard_map/ppermute | solution.py:296

commit v16 on v13

--- a/solution.py
+++ b/solution.py
@@ -196,7 +196,7 @@
 
     far = [(i * chan + j, far_partner(i, j)) for i in range(space) for j in range(chan)]
 
-    order = sorted(range(1, groups), key=lambda k: abs(k - groups // 2))
+    order = sorted(range(1, groups), key=lambda k: (abs(k - groups // 2), -k))
 
     def ahead(k):
         return [(i, (i + CORES * k) % chan) for i in range(chan)]

time: 64.6 us -> 64 us (level)
  starting transfers between devices: 28 us -> 26.3 us
    ppermute x3, waiting for transfers between devices: 4.6 us -> 6.16 us  [per_device(): got = lax.ppermute(pieces[k], 'chan', ahead(k))]
    ppermute x2, starting transfers between devices: 0.61 us -> 2.06 us  [halo(): lax.ppermute(array, ('space', 'chan'), far)]
    ppermute x3, starting transfers between devices: 10.6 us -> 9.36 us  [per_device(): got = lax.ppermute(pieces[k], 'chan', ahead(k))]
    ppermute x3, starting transfers between devices: 8.33 us -> 7.17 us  [per_device(): blocks[k] = lax.ppermute(blocks[k], 'chan', ahead(k))]
    ppermute x1, starting transfers between devices: 0.12 us -> 1.15 us  [per_device(): last = lax.ppermute(sent[-1], 'chan', swap)]
    ppermute x1, starting transfers between devices: 3.42 us -> 2.42 us  [per_device(): early = lax.ppermute(jnp.concatenate(sent[:-1]), 'chan', swap)]
    ppermute x3, starting transfers between devices: 4.26 us -> 3.46 us  [from_other_core(): return lax.ppermute(sent, 'chan', swap)]
    ppermute x2, waiting for transfers between devices: 4.8 us -> 4.15 us  [halo(): lax.ppermute(array, 'space', near)]
where the time goes in v16:
time: 64 us; the launch traced here: 63.3 us
  starting transfers between devices  26.3 us (41%)
  waiting for transfers between devices  21.9 us (34%)
  local copies, waits for them, and re-layouts  8.79 us (14%)
  Pallas kernels  5.48 us (9%)
  between operations  0.89 us (1%)
    ppermute x3, starting transfers between devices, per_device(): got = lax.ppermute(pieces[k], 'chan', ahead(k))  9.36 us
    ppermute x2, waiting for transfers between devices, halo(): lax.ppermute(array, ('space', 'chan'), far)  8.52 us
    ppermute x3, starting transfers between devices, per_device(): blocks[k] = lax.ppermute(blocks[k], 'chan', ahead(k))  7.17 us
    ppermute x3, waiting for transfers between devices, per_device(): got = lax.ppermute(pieces[k], 'chan', ahead(k))  6.16 us
    pallas_call x8, Pallas kernels, call(): pl.pallas_call(kernel, out_shape=shapes, in_specs=[VMEM] * len(inputs), o...  5.48 us
    ppermute x2, waiting for transfers between devices, halo(): lax.ppermute(array, 'space', near)  4.15 us
    unnamed x14, local copies, waits for them, and re-layouts  3.57 us
    ppermute x3, starting transfers between devices, from_other_core(): return lax.ppermute(sent, 'chan', swap)  3.46 us
  transfers between devices with their start and end apart: 15, of which 9 were waited for; matrix products, arithmetic and copies ran while one was open for 9% of the time, Pallas kernels for 5%

profile of v16, /device:TPU:31, one launch (start us, length us, event | category | flops | bytes accessed | tf_op | source)
XLA Modules:
  0.0 63.3 jit_solution(6060229663057881549)
XLA Ops:
  0.0 0.0 copy-start
  0.0 0.9 %copy-done = bf16[16,1,64,128]{3,2,1,0:T(8,128)(2,1)S(1)} copy-done((bf16[16,1,64,128]{3,2,1,0:T(8,128)(2,1)S(1)}, bf16[16,1,64,128]{3,2,1,0:T(8,128)(2,1)}, u32[]{:S(2)}) %copy-start) | copy-done | bytes 262168
  1.0 0.0 copy-start.2
  1.0 0.2 pack_rows.1
  1.1 7.0 %collective-permute-start = (bf16[1,20,16,128]{3,2,1,0:T(8,128)(2,1)S(1)}, bf16[1,20,16,128]{3,2,1,0:T(8,128)(2,1)S(1)}, u32[]{:S(2)}, u32[]{:S(2)}) collective-permute-start(bf16[1,20,16,128]{3,2,1,0:T(8,128)(2,1)S(1)} %get-tuple-element.16), channel_id=1, source_target_pairs={{0,4},{1,5},{2,6},{3,7},{4,0},{5,1},{6,2},{7,3},{8,12},{9,13},{10,... | collective-permute-start | bytes 245768 | tf_op jit(solution)/shard_map/ppermute | solution.py:237
  8.1 0.0 collective-permute-start.1
  8.1 2.4 %collective-permute-start.2 = (bf16[1,20,16,128]{3,2,1,0:T(8,128)(2,1)S(1)}, bf16[1,20,16,128]{3,2,1,0:T(8,128)(2,1)S(1)}, u32[]{:S(2)}, u32[]{:S(2)}) collective-permute-start(bf16[1,20,16,128]{3,2,1,0:T(8,128)(2,1)S(1)} %get-tuple-element.18), channel_id=1, source_target_pairs={{0,2},{1,3},{2,4},{3,5},{4,6},{5,7},{6,0},{7,1},{8,10},{9,11},{10,... | collective-permute-start | bytes 245768 | tf_op jit(solution)/shard_map/ppermute | solution.py:237
  10.6 0.0 collective-permute-done
  10.6 6.2 %collective-permute-done.1 = bf16[1,20,16,128]{3,2,1,0:T(8,128)(2,1)S(1)} collective-permute-done((bf16[1,20,16,128]{3,2,1,0:T(8,128)(2,1)S(1)}, bf16[1,20,16,128]{3,2,1,0:T(8,128)(2,1)S(1)}, u32[]{:S(2)}, u32[]{:S(2)}) %collective-permute-start.1) | collective-permute-done | bytes 81952 | tf_op jit(solution)/shard_map/ppermute | solution.py:237
  16.8 0.0 collective-permute-done.2
  16.8 0.6 collective-permute-start.6
  17.4 1.0 %collective-permute-start.4 = (bf16[4,12,16,128]{3,2,1,0:T(8,128)(2,1)S(1)}, bf16[4,12,16,128]{3,2,1,0:T(8,128)(2,1)S(1)}, u32[]{:S(2)}, u32[]{:S(2)}) collective-permute-start(bf16[4,12,16,128]{3,2,1,0:T(8,128)(2,1)S(1)} %constant_dynamic-slice_fusion.6), channel_id=1, source_target_pairs={{0,1},{1,0},{2,3},{3,2},{4,5},{5,4},{6,7},{7,6},{8,9},{9,8},{10,11... | collective-permute-start | bytes 589832 | tf_op jit(solution)/shard_map/ppermute | solution.py:242
  18.3 0.9 %collective-permute-start.3 = (bf16[4,20,16,128]{3,2,1,0:T(8,128)(2,1)S(1)}, bf16[4,20,16,128]{3,2,1,0:T(8,128)(2,1)S(1)}, u32[]{:S(2)}, u32[]{:S(2)}) collective-permute-start(bf16[4,20,16,128]{3,2,1,0:T(8,128)(2,1)S(1)} %constant_dynamic-update-slice_fusion.kept_ref), channel_id=1, source_target_pairs={{0,1},{1,0},{2,3},{3,2},{4,5},{5,4},{6,7},{7,6},{8,16},{9,17},{10,... | collective-permute-start | bytes 983048 | tf_op jit(solution)/shard_map/ppermute | solution.py:245
  19.2 0.0 copy-done.2
  19.2 0.7 %slice.17 = bf16[9,128,128]{2,1,0:T(8,128)(2,1)} slice(bf16[27,128,128]{2,1,0:T(8,128)(2,1)S(1)} %copy-done.2), slice={[9:18], [0:128], [0:128]} | slice | bytes 589824 | tf_op jit(solution)/shard_map/slice | solution.py:174
  20.0 0.6 copy.20
  20.6 0.5 reshape.24.later_ref.weight_ref
  21.2 0.0 copy-start.3
  21.2 0.6 %copy-done.3 = f32[128]{0:T(128)S(1)} copy-done((f32[128]{0:T(128)S(1)}, f32[128]{0:T(128)}, u32[]{:S(2)}) %copy-start.3) | copy-done | bytes 536
  21.8 0.1 copy.15.bias_ref
  21.9 1.2 %copy.13 = bf16[3,3,128,128]{2,0,3,1:T(4,128)(2,1)S(1)} copy(bf16[3,3,128,128]{3,2,1,0:T(8,128)(2,1)} %bitcast.27) | data formatting | bytes 589824 | tf_op jit(solution)/shard_map/squeeze | solution.py:174
  23.2 0.0 collective-permute-done.4.other_ref
  23.2 0.8 %first_own.1 = (f32[10,128,128]{2,1,0:T(8,128)S(1)}, s32[8,128]{1,0:T(8,128)S(1)}) custom-call(bf16[4,20,16,128]{3,2,1,0:T(8,128)(2,1)S(1)} %constant_dynamic-update-slice_fusion.kept_ref, bf16[4,12,16,128]{3,2,1,0:T(8,128)(2,1)S(1)} %collective-permute-done.4.other_ref, bf16[384,384]{1,0:T(8,128)(2,1)S(1)} %bitcast.22, ...), custom_call_target="tpu_custom_call" | custom-call | flops 377487360 | bytes 4000000 | tf_op jit(solution)/shard_map/first_own/pallas_call | solution.py:206
  24.0 0.5 slice.19
  25.2 0.4 collective-permute-done.6.kept_ref
  25.6 1.5 %collective-permute-start.7 = (bf16[4,12,16,128]{3,2,1,0:T(8,128)(2,1)S(1)}, bf16[4,12,16,128]{3,2,1,0:T(8,128)(2,1)S(1)}, u32[]{:S(2)}, u32[]{:S(2)}) collective-permute-start(bf16[4,12,16,128]{3,2,1,0:T(8,128)(2,1)S(1)} %constant_dynamic-slice_fusion.4), channel_id=1, source_target_pairs={{0,1},{1,0},{2,3},{3,2},{4,5},{5,4},{6,7},{7,6},{8,9},{9,8},{10,11... | collective-permute-start | bytes 589832 | tf_op jit(solution)/shard_map/ppermute | solution.py:242
  27.1 4.7 %collective-permute-done.3.kept_ref = bf16[4,20,16,128]{3,2,1,0:T(8,128)(2,1)S(1)} collective-permute-done((bf16[4,20,16,128]{3,2,1,0:T(8,128)(2,1)S(1)}, bf16[4,20,16,128]{3,2,1,0:T(8,128)(2,1)S(1)}, u32[]{:S(2)}, u32[]{:S(2)}) %collective-permute-start.3) | collective-permute-done | bytes 327712 | tf_op jit(solution)/shard_map/ppermute | solution.py:245
  31.8 1.0 %collective-permute-start.5 = (bf16[4,12,16,128]{3,2,1,0:T(8,128)(2,1)S(1)}, bf16[4,12,16,128]{3,2,1,0:T(8,128)(2,1)S(1)}, u32[]{:S(2)}, u32[]{:S(2)}) collective-permute-start(bf16[4,12,16,128]{3,2,1,0:T(8,128)(2,1)S(1)} %constant_dynamic-slice_fusion.5), channel_id=1, source_target_pairs={{0,1},{1,0},{2,3},{3,2},{4,5},{5,4},{6,7},{7,6},{8,9},{9,8},{10,11... | collective-permute-start | bytes 589832 | tf_op jit(solution)/shard_map/ppermute | solution.py:242
  32.8 0.0 collective-permute-done.7.other_ref
  32.8 0.8 %first_near.1.before_ref = f32[10,128,128]{2,1,0:T(8,128)S(1)} custom-call(bf16[4,20,16,128]{3,2,1,0:T(8,128)(2,1)S(1)} %collective-permute-done.6.kept_ref, bf16[4,12,16,128]{3,2,1,0:T(8,128)(2,1)S(1)} %collective-permute-done.7.other_ref, bf16[2,384,384]{2,1,0:T(8,128)(2,1)S(1)} %reshape.24.later_ref.weight_ref, ...), custom_call_target="tpu_custom_call" | custom-call | flops 377487360 | bytes 4000000 | tf_op jit(solution)/shard_map/first_near/pallas_call | solution.py:206
  33.6 0.3 collective-permute-done.5.other_ref
  33.9 0.8 %first_far.1.plane_ref = bf16[10,128,128]{2,1,0:T(8,128)(2,1)S(1)} custom-call(bf16[4,20,16,128]{3,2,1,0:T(8,128)(2,1)S(1)} %collective-permute-done.3.kept_ref, bf16[4,12,16,128]{3,2,1,0:T(8,128)(2,1)S(1)} %collective-permute-done.5.other_ref, bf16[2,384,384]{2,1,0:T(8,128)(2,1)S(1)} %reshape.24.later_ref.weight_ref, ...), custom_call_target="tpu_custom_call" | custom-call | flops 377487360 | bytes 4000000 | tf_op jit(solution)/shard_map/first_far/pallas_call | solution.py:206
  34.7 0.1 collective-permute-start.9
  34.8 1.2 %collective-permute-start.8 = (bf16[10,128,128]{2,1,0:T(8,128)(2,1)S(1)}, bf16[10,128,128]{2,1,0:T(8,128)(2,1)S(1)}, u32[]{:S(2)}, u32[]{:S(2)}) collective-permute-start(bf16[10,128,128]{2,1,0:T(8,128)(2,1)S(1)} %first_far.1.plane_ref), channel_id=1, source_target_pairs={{0,1},{1,0},{2,3},{3,2},{4,5},{5,4},{6,7},{7,6},{8,16},{9,17},{10,... | collective-permute-start | bytes 983048 | tf_op jit(solution)/shard_map/ppermute | solution.py:245
  35.9 0.0 slice-start
  35.9 0.0 copy-start.1
  35.9 1.0 %slice-done = bf16[9,128,128]{2,1,0:T(8,128)(2,1)S(1)} async-done(((bf16[27,128,128]{2,1,0:T(8,128)(2,1)}), bf16[9,128,128]{2,1,0:T(8,128)(2,1)S(1)}, s32[]{:S(2)}) %slice-start) | async-done | bytes 294936 | tf_op jit(solution)/shard_map/slice | solution.py:174
  36.9 0.2 copy.18
  37.2 0.1 copy-done.1
  37.3 0.6 copy.21
  37.9 0.5 reshape.26.weight_ref
  38.5 0.0 copy-start.4
  38.5 0.6 %copy-done.4 = f32[128]{0:T(128)S(1)} copy-done((f32[128]{0:T(128)S(1)}, f32[128]{0:T(128)}, u32[]{:S(2)}) %copy-start.4) | copy-done | bytes 536
  39.1 0.1 copy.19.bias_ref
  39.2 0.7 %second_own.1.before_ref = f32[8,128,128]{2,1,0:T(8,128)S(1)} custom-call(bf16[10,128,128]{2,1,0:T(8,128)(2,1)S(1)} %first_far.1.plane_ref, bf16[384,384]{1,0:T(8,128)(2,1)S(1)} %bitcast.21), custom_call_target="tpu_custom_call" | custom-call | flops 301989888 | bytes 4000000 | tf_op jit(solution)/shard_map/second_own/pallas_call | solution.py:206
  39.9 3.8 %collective-permute-done.9.plane_ref = bf16[10,128,128]{2,1,0:T(8,128)(2,1)S(1)} collective-permute-done((bf16[10,128,128]{2,1,0:T(8,128)(2,1)S(1)}, bf16[10,128,128]{2,1,0:T(8,128)(2,1)S(1)}, u32[]{:S(2)}, u32[]{:S(2)}) %collective-permute-start.9) | collective-permute-done | bytes 327712 | tf_op jit(solution)/shard_map/ppermute | solution.py:245
  43.7 0.7 %second_near.1.before_ref = f32[8,128,128]{2,1,0:T(8,128)S(1)} custom-call(bf16[10,128,128]{2,1,0:T(8,128)(2,1)S(1)} %collective-permute-done.9.plane_ref, bf16[2,384,384]{2,1,0:T(8,128)(2,1)S(1)} %reshape.26.weight_ref, f32[8,128,128]{2,1,0:T(8,128)S(1)} %second_own.1.before_ref), custom_call_target="tpu_custom_call" | custom-call | flops 301989888 | bytes 4000000 | tf_op jit(solution)/shard_map/second_near/pallas_call | solution.py:206
  44.4 3.8 %collective-permute-done.8.plane_ref = bf16[10,128,128]{2,1,0:T(8,128)(2,1)S(1)} collective-permute-done((bf16[10,128,128]{2,1,0:T(8,128)(2,1)S(1)}, bf16[10,128,128]{2,1,0:T(8,128)(2,1)S(1)}, u32[]{:S(2)}, u32[]{:S(2)}) %collective-permute-start.8) | collective-permute-done | bytes 327712 | tf_op jit(solution)/shard_map/ppermute | solution.py:245
  48.2 0.7 %second_far.1 = (bf16[2,8,16,128]{3,2,1,0:T(8,128)(2,1)S(1)}, bf16[2,8,16,128]{3,2,1,0:T(8,128)(2,1)S(1)}, bf16[2,8,16,128]{3,2,1,0:T(8,128)(2,1)S(1)}, bf16[2,8,16,128]{3,2,1,0:T(8,128)(2,1)S(1)}) custom-call(bf16[10,128,128]{2,1,0:T(8,128)(2,1)S(1)} %collective-permute-done.8.plane_ref, bf16[2,384,384]{2,1,0:T(8,128)(2,1)S(1)} %reshape.26.weight_ref, ...), custom_call_target="tpu_custom_call" | custom-call | flops 301989888 | bytes 4000000 | tf_op jit(solution)/shard_map/second_far/pallas_call | solution.py:206
  48.9 4.8 %collective-permute-start.10 = (bf16[2,8,16,128]{3,2,1,0:T(8,128)(2,1)S(1)}, bf16[2,8,16,128]{3,2,1,0:T(8,128)(2,1)S(1)}, u32[]{:S(2)}, u32[]{:S(2)}) collective-permute-start(bf16[2,8,16,128]{3,2,1,0:T(8,128)(2,1)S(1)} %get-tuple-element.22), channel_id=1, source_target_pairs={{0,4},{1,5},{2,6},{3,7},{4,0},{5,1},{6,2},{7,3},{8,12},{9,13},{10,... | collective-permute-start | bytes 196616 | tf_op jit(solution)/shard_map/ppermute | solution.py:296
  53.7 0.0 collective-permute-start.11
  53.7 2.4 %collective-permute-start.13 = (bf16[2,8,16,128]{3,2,1,0:T(8,128)(2,1)S(1)}, bf16[2,8,16,128]{3,2,1,0:T(8,128)(2,1)S(1)}, u32[]{:S(2)}, u32[]{:S(2)}) collective-permute-start(bf16[2,8,16,128]{3,2,1,0:T(8,128)(2,1)S(1)} %get-tuple-element.24), channel_id=1, source_target_pairs={{0,2},{1,3},{2,4},{3,5},{4,6},{5,7},{6,0},{7,1},{8,10},{9,11},{10,... | collective-permute-start | bytes 196616 | tf_op jit(solution)/shard_map/ppermute | solution.py:296
  56.1 0.3 collective-permute-done.10.refs_2_
  56.4 1.6 %collective-permute-done.11.refs_3_ = bf16[2,8,16,128]{3,2,1,0:T(8,128)(2,1)S(1)} collective-permute-done((bf16[2,8,16,128]{3,2,1,0:T(8,128)(2,1)S(1)}, bf16[2,8,16,128]{3,2,1,0:T(8,128)(2,1)S(1)}, u32[]{:S(2)}, u32[]{:S(2)}) %collective-permute-start.11) | collective-permute-done | bytes 65568 | tf_op jit(solution)/shard_map/ppermute | solution.py:296
  58.0 2.4 %collective-permute-start.12 = (bf16[3,8,16,128]{3,2,1,0:T(8,128)(2,1)S(1)}, bf16[3,8,16,128]{3,2,1,0:T(8,128)(2,1)S(1)}, u32[]{:S(2)}, u32[]{:S(2)}) collective-permute-start(bf16[3,8,16,128]{3,2,1,0:T(8,128)(2,1)S(1)} %pad_maximum_fusion), channel_id=1, source_target_pairs={{0,1},{1,0},{2,3},{3,2},{4,5},{5,4},{6,7},{7,6},{8,9},{9,8},{10,11... | collective-permute-start | bytes 294920 | tf_op jit(solution)/shard_map/ppermute | solution.py:298
  60.5 0.0 collective-permute-done.13.refs_1_
  60.5 1.1 %collective-permute-start.14 = (bf16[1,8,16,128]{3,2,1,0:T(8,128)(2,1)S(1)}, bf16[1,8,16,128]{3,2,1,0:T(8,128)(2,1)S(1)}, u32[]{:S(2)}, u32[]{:S(2)}) collective-permute-start(bf16[1,8,16,128]{3,2,1,0:T(8,128)(2,1)S(1)} %constant_dynamic-slice_fusion), channel_id=1, source_target_pairs={{0,1},{1,0},{2,3},{3,2},{4,5},{5,4},{6,7},{7,6},{8,9},{9,8},{10,11... | collective-permute-start | bytes 98312 | tf_op jit(solution)/shard_map/ppermute | solution.py:299
  61.6 0.9 %collective-permute-done.14.last_ref = bf16[1,8,16,128]{3,2,1,0:T(8,128)(2,1)S(1)} collective-permute-done((bf16[1,8,16,128]{3,2,1,0:T(8,128)(2,1)S(1)}, bf16[1,8,16,128]{3,2,1,0:T(8,128)(2,1)S(1)}, u32[]{:S(2)}, u32[]{:S(2)}) %collective-permute-start.14) | collective-permute-done | bytes 32800 | tf_op jit(solution)/shard_map/ppermute | solution.py:299
  62.5 0.0 collective-permute-done.12.early_ref
  62.5 0.9 %unpack_rows.1 = bf16[16,1,64,128]{3,2,1,0:T(8,128)(2,1)} custom-call(bf16[3,8,16,128]{3,2,1,0:T(8,128)(2,1)S(1)} %collective-permute-done.12.early_ref, bf16[1,8,16,128]{3,2,1,0:T(8,128)(2,1)S(1)} %collective-permute-done.14.last_ref, bf16[2,8,16,128]{3,2,1,0:T(8,128)(2,1)S(1)} %get-tuple-element.21.refs_0_, ...), custom_call_target="tpu_custom_call" | custom-call | tf_op jit(solution)/shard_map/unpack_rows/pallas_call | solution.py:206
  (17 shorter events, 0.4 us)
Async XLA Ops:
  0.0 0.9 %copy-start = (bf16[16,1,64,128]{3,2,1,0:T(8,128)(2,1)S(1)}, bf16[16,1,64,128]{3,2,1,0:T(8,128)(2,1)}, u32[]{:S(2)}) copy-start(bf16[16,1,64,128]{3,2,1,0:T(8,128)(2,1)} %volume_ref.1) | copy-start | bytes 786436
  1.0 18.3 %copy-start.2 = (bf16[27,128,128]{2,1,0:T(8,128)(2,1)S(1)}, bf16[27,128,128]{2,1,0:T(8,128)(2,1)}, u32[]{:S(2)}) copy-start(bf16[27,128,128]{2,1,0:T(8,128)(2,1)} %param.6) | copy-start | bytes 2654212
  1.1 9.4 %collective-permute-start = (bf16[1,20,16,128]{3,2,1,0:T(8,128)(2,1)S(1)}, bf16[1,20,16,128]{3,2,1,0:T(8,128)(2,1)S(1)}, u32[]{:S(2)}, u32[]{:S(2)}) collective-permute-start(bf16[1,20,16,128]{3,2,1,0:T(8,128)(2,1)S(1)} %get-tuple-element.16), channel_id=1, source_target_pairs={{0,4},{1,5},{2,6},{3,7},{4,0},{5,1},{6,2},{7,3},{8,12},{9,13},{10,... | collective-permute-start | bytes 245768 | tf_op jit(solution)/shard_map/ppermute | solution.py:237
  8.1 8.6 %collective-permute-start.1 = (bf16[1,20,16,128]{3,2,1,0:T(8,128)(2,1)S(1)}, bf16[1,20,16,128]{3,2,1,0:T(8,128)(2,1)S(1)}, u32[]{:S(2)}, u32[]{:S(2)}) collective-permute-start(bf16[1,20,16,128]{3,2,1,0:T(8,128)(2,1)S(1)} %get-tuple-element.17), channel_id=1, source_target_pairs={{0,6},{1,7},{2,0},{3,1},{4,2},{5,3},{6,4},{7,5},{8,14},{9,15},{10,... | collective-permute-start | bytes 245768 | tf_op jit(solution)/shard_map/ppermute | solution.py:237
  8.1 8.6 %collective-permute-start.2 = (bf16[1,20,16,128]{3,2,1,0:T(8,128)(2,1)S(1)}, bf16[1,20,16,128]{3,2,1,0:T(8,128)(2,1)S(1)}, u32[]{:S(2)}, u32[]{:S(2)}) collective-permute-start(bf16[1,20,16,128]{3,2,1,0:T(8,128)(2,1)S(1)} %get-tuple-element.18), channel_id=1, source_target_pairs={{0,2},{1,3},{2,4},{3,5},{4,6},{5,7},{6,0},{7,1},{8,10},{9,11},{10,... | collective-permute-start | bytes 245768 | tf_op jit(solution)/shard_map/ppermute | solution.py:237
  16.8 8.8 %collective-permute-start.6 = (bf16[4,20,16,128]{3,2,1,0:T(8,128)(2,1)S(1)}, bf16[4,20,16,128]{3,2,1,0:T(8,128)(2,1)S(1)}, u32[]{:S(2)}, u32[]{:S(2)}) collective-permute-start(bf16[4,20,16,128]{3,2,1,0:T(8,128)(2,1)S(1)} %constant_dynamic-update-slice_fusion.kept_ref), channel_id=1, source_target_pairs={{0,8},{8,0},{16,24},{24,16},{32,40},{40,32},{48,56},{56,48},{64,72... | collective-permute-start | bytes 983048 | tf_op jit(solution)/shard_map/ppermute | solution.py:245
  17.4 5.8 %collective-permute-start.4 = (bf16[4,12,16,128]{3,2,1,0:T(8,128)(2,1)S(1)}, bf16[4,12,16,128]{3,2,1,0:T(8,128)(2,1)S(1)}, u32[]{:S(2)}, u32[]{:S(2)}) collective-permute-start(bf16[4,12,16,128]{3,2,1,0:T(8,128)(2,1)S(1)} %constant_dynamic-slice_fusion.6), channel_id=1, source_target_pairs={{0,1},{1,0},{2,3},{3,2},{4,5},{5,4},{6,7},{7,6},{8,9},{9,8},{10,11... | collective-permute-start | bytes 589832 | tf_op jit(solution)/shard_map/ppermute | solution.py:242
  18.3 13.5 %collective-permute-start.3 = (bf16[4,20,16,128]{3,2,1,0:T(8,128)(2,1)S(1)}, bf16[4,20,16,128]{3,2,1,0:T(8,128)(2,1)S(1)}, u32[]{:S(2)}, u32[]{:S(2)}) collective-permute-start(bf16[4,20,16,128]{3,2,1,0:T(8,128)(2,1)S(1)} %constant_dynamic-update-slice_fusion.kept_ref), channel_id=1, source_target_pairs={{0,1},{1,0},{2,3},{3,2},{4,5},{5,4},{6,7},{7,6},{8,16},{9,17},{10,... | collective-permute-start | bytes 983048 | tf_op jit(solution)/shard_map/ppermute | solution.py:245
  21.2 0.7 %copy-start.3 = (f32[128]{0:T(128)S(1)}, f32[128]{0:T(128)}, u32[]{:S(2)}) copy-start(f32[128]{0:T(128)} %param.7) | copy-start | bytes 1540
  25.6 7.2 %collective-permute-start.7 = (bf16[4,12,16,128]{3,2,1,0:T(8,128)(2,1)S(1)}, bf16[4,12,16,128]{3,2,1,0:T(8,128)(2,1)S(1)}, u32[]{:S(2)}, u32[]{:S(2)}) collective-permute-start(bf16[4,12,16,128]{3,2,1,0:T(8,128)(2,1)S(1)} %constant_dynamic-slice_fusion.4), channel_id=1, source_target_pairs={{0,1},{1,0},{2,3},{3,2},{4,5},{5,4},{6,7},{7,6},{8,9},{9,8},{10,11... | collective-permute-start | bytes 589832 | tf_op jit(solution)/shard_map/ppermute | solution.py:242
  31.8 2.0 %collective-permute-start.5 = (bf16[4,12,16,128]{3,2,1,0:T(8,128)(2,1)S(1)}, bf16[4,12,16,128]{3,2,1,0:T(8,128)(2,1)S(1)}, u32[]{:S(2)}, u32[]{:S(2)}) collective-permute-start(bf16[4,12,16,128]{3,2,1,0:T(8,128)(2,1)S(1)} %constant_dynamic-slice_fusion.5), channel_id=1, source_target_pairs={{0,1},{1,0},{2,3},{3,2},{4,5},{5,4},{6,7},{7,6},{8,9},{9,8},{10,11... | collective-permute-start | bytes 589832 | tf_op jit(solution)/shard_map/ppermute | solution.py:242
  34.7 9.0 %collective-permute-start.9 = (bf16[10,128,128]{2,1,0:T(8,128)(2,1)S(1)}, bf16[10,128,128]{2,1,0:T(8,128)(2,1)S(1)}, u32[]{:S(2)}, u32[]{:S(2)}) collective-permute-start(bf16[10,128,128]{2,1,0:T(8,128)(2,1)S(1)} %first_far.1.plane_ref), channel_id=1, source_target_pairs={{0,8},{8,0},{16,24},{24,16},{32,40},{40,32},{48,56},{56,48},{64,72... | collective-permute-start | bytes 983048 | tf_op jit(solution)/shard_map/ppermute | solution.py:245
  34.8 13.4 %collective-permute-start.8 = (bf16[10,128,128]{2,1,0:T(8,128)(2,1)S(1)}, bf16[10,128,128]{2,1,0:T(8,128)(2,1)S(1)}, u32[]{:S(2)}, u32[]{:S(2)}) collective-permute-start(bf16[10,128,128]{2,1,0:T(8,128)(2,1)S(1)} %first_far.1.plane_ref), channel_id=1, source_target_pairs={{0,1},{1,0},{2,3},{3,2},{4,5},{5,4},{6,7},{7,6},{8,16},{9,17},{10,... | collective-permute-start | bytes 983048 | tf_op jit(solution)/shard_map/ppermute | solution.py:245
  35.9 1.0 %slice-start = ((bf16[27,128,128]{2,1,0:T(8,128)(2,1)}), bf16[9,128,128]{2,1,0:T(8,128)(2,1)S(1)}, s32[]{:S(2)}) async-start(bf16[27,128,128]{2,1,0:T(8,128)(2,1)} %param.8), calls=%async_computation | async-start | bytes 589824 | tf_op jit(solution)/shard_map/slice | solution.py:174
  35.9 1.3 %copy-start.1 = (bf16[27,128,128]{2,1,0:T(8,128)(2,1)S(1)}, bf16[27,128,128]{2,1,0:T(8,128)(2,1)}, u32[]{:S(2)}) copy-start(bf16[27,128,128]{2,1,0:T(8,128)(2,1)} %param.8) | copy-start | bytes 2654212
  38.5 0.7 %copy-start.4 = (f32[128]{0:T(128)S(1)}, f32[128]{0:T(128)}, u32[]{:S(2)}) copy-start(f32[128]{0:T(128)} %param.9) | copy-start | bytes 1540
  48.9 7.5 %collective-permute-start.10 = (bf16[2,8,16,128]{3,2,1,0:T(8,128)(2,1)S(1)}, bf16[2,8,16,128]{3,2,1,0:T(8,128)(2,1)S(1)}, u32[]{:S(2)}, u32[]{:S(2)}) collective-permute-start(bf16[2,8,16,128]{3,2,1,0:T(8,128)(2,1)S(1)} %get-tuple-element.22), channel_id=1, source_target_pairs={{0,4},{1,5},{2,6},{3,7},{4,0},{5,1},{6,2},{7,3},{8,12},{9,13},{10,... | collective-permute-start | bytes 196616 | tf_op jit(solution)/shard_map/ppermute | solution.py:296
  53.7 4.3 %collective-permute-start.11 = (bf16[2,8,16,128]{3,2,1,0:T(8,128)(2,1)S(1)}, bf16[2,8,16,128]{3,2,1,0:T(8,128)(2,1)S(1)}, u32[]{:S(2)}, u32[]{:S(2)}) collective-permute-start(bf16[2,8,16,128]{3,2,1,0:T(8,128)(2,1)S(1)} %get-tuple-element.23), channel_id=1, source_target_pairs={{0,6},{1,7},{2,0},{3,1},{4,2},{5,3},{6,4},{7,5},{8,14},{9,15},{10,... | collective-permute-start | bytes 196616 | tf_op jit(solution)/shard_map/ppermute | solution.py:296
  53.7 6.8 %collective-permute-start.13 = (bf16[2,8,16,128]{3,2,1,0:T(8,128)(2,1)S(1)}, bf16[2,8,16,128]{3,2,1,0:T(8,128)(2,1)S(1)}, u32[]{:S(2)}, u32[]{:S(2)}) collective-permute-start(bf16[2,8,16,128]{3,2,1,0:T(8,128)(2,1)S(1)} %get-tuple-element.24), channel_id=1, source_target_pairs={{0,2},{1,3},{2,4},{3,5},{4,6},{5,7},{6,0},{7,1},{8,10},{9,11},{10,... | collective-permute-start | bytes 196616 | tf_op jit(solution)/shard_map/ppermute | solution.py:296
  58.0 4.4 %collective-permute-start.12 = (bf16[3,8,16,128]{3,2,1,0:T(8,128)(2,1)S(1)}, bf16[3,8,16,128]{3,2,1,0:T(8,128)(2,1)S(1)}, u32[]{:S(2)}, u32[]{:S(2)}) collective-permute-start(bf16[3,8,16,128]{3,2,1,0:T(8,128)(2,1)S(1)} %pad_maximum_fusion), channel_id=1, source_target_pairs={{0,1},{1,0},{2,3},{3,2},{4,5},{5,4},{6,7},{7,6},{8,9},{9,8},{10,11... | collective-permute-start | bytes 294920 | tf_op jit(solution)/shard_map/ppermute | solution.py:298
  60.5 2.0 %collective-permute-start.14 = (bf16[1,8,16,128]{3,2,1,0:T(8,128)(2,1)S(1)}, bf16[1,8,16,128]{3,2,1,0:T(8,128)(2,1)S(1)}, u32[]{:S(2)}, u32[]{:S(2)}) collective-permute-start(bf16[1,8,16,128]{3,2,1,0:T(8,128)(2,1)S(1)} %constant_dynamic-slice_fusion), channel_id=1, source_target_pairs={{0,1},{1,0},{2,3},{3,2},{4,5},{5,4},{6,7},{7,6},{8,9},{9,8},{10,11... | collective-permute-start | bytes 98312 | tf_op jit(solution)/shard_map/ppermute | solution.py:299

commit v17 on v12

--- a/solution.py
+++ b/solution.py
@@ -134,6 +134,16 @@
     conv_rows(rows_of(joined_ref, True), 1, weight, store, rows, lanes)
 
 
+def far_kernel(plane_ref, weight_ref, before_ref, out_ref):
+    rows, _, lanes = out_ref.shape
+
+    def store(row, value):
+        out_ref[row] = before_ref[row] + value
+
+    weight = weight_ref[lax.axis_index("space") % 2]
+    conv_rows(rows_of(plane_ref, True), 1, weight, store, rows, lanes)
+
+
 def second_kernel(plane_ref, weight_ref, before_ref, bias_ref, *refs):
     outs, all_ref = refs[:-1], refs[-1]
     groups, cores, rows, width, lanes = all_ref.shape
@@ -146,8 +156,8 @@
                 at = (g * cores + c) * width
                 all_ref[g, c, row] = value[at : at + width]
 
-    weight = weight_ref[lax.axis_index("space") % 2]
-    conv_rows(rows_of(plane_ref, True), 1, weight, store, rows, lanes)
+    weight = weight_ref[1 - lax.axis_index("space") % 2]
+    conv_rows(rows_of(plane_ref, False), 1, weight, store, rows, lanes)
     for k in range(groups):
         outs[k][...] = all_ref[lax.rem(my_group() + k, groups)]
 
@@ -276,14 +286,14 @@
         work = cost(rows, 1, full, lanes)
         far_plane, near_plane = halo(hidden)
         total = call(own_kernel, partial, [hidden, own_two], cost_estimate=work, name="second_own")
-        total = call(near_kernel, partial, [near_plane, beside_two, total], cost_estimate=work, name="second_near")
+        total = call(far_kernel, partial, [far_plane, beside_two, total], cost_estimate=work, name="second_far")
         blocks = call(
             second_kernel,
             [jax.ShapeDtypeStruct((CORES, rows, width, lanes), BF16)] * groups,
-            [far_plane, beside_two, total, bias_two[:, None]],
+            [near_plane, beside_two, total, bias_two[:, None]],
             [pltpu.VMEM((groups, CORES, rows, width, lanes), BF16)],
             cost_estimate=work,
-            name="second_far",
+            name="second_near",
         )
 
         blocks = list(blocks)

time: 63.9 us -> 64.3 us (level)
  waiting for transfers between devices: 21.2 us -> 22.3 us
  starting transfers between devices: 27.3 us -> 26.6 us
    ppermute x2, waiting for transfers between devices: 8.9 us -> 13.9 us  [halo(): lax.ppermute(array, ('space', 'chan'), far)]
    ppermute x2, waiting for transfers between devices: 4.79 us -> 0.29 us  [halo(): lax.ppermute(array, 'space', near)]
    ppermute x3, starting transfers between devices: 8.41 us -> 7.7 us  [per_device(): blocks[k] = lax.ppermute(blocks[k], 'chan', ahead(k))]
where the time goes in v17:
time: 64.3 us; the launch traced here: 64.1 us
  starting transfers between devices  26.6 us (41%)
  waiting for transfers between devices  22.3 us (35%)
  local copies, waits for them, and re-layouts  8.82 us (14%)
  Pallas kernels  5.48 us (9%)
  between operations  0.9 us (1%)
    ppermute x2, waiting for transfers between devices, halo(): lax.ppermute(array, ('space', 'chan'), far)  13.9 us
    ppermute x3, starting transfers between devices, per_device(): got = lax.ppermute(pieces[k], 'chan', ahead(k))  10.6 us
    ppermute x3, starting transfers between devices, per_device(): blocks[k] = lax.ppermute(blocks[k], 'chan', ahead(k))  7.7 us
    pallas_call x8, Pallas kernels, call(): pl.pallas_call(kernel, out_shape=shapes, in_specs=[VMEM] * len(inputs), o...  5.48 us
    ppermute x3, waiting for transfers between devices, per_device(): got = lax.ppermute(pieces[k], 'chan', ahead(k))  4.6 us
    ppermute x3, starting transfers between devices, from_other_core(): return lax.ppermute(sent, 'chan', swap)  4.26 us
    unnamed x14, local copies, waits for them, and re-layouts  3.57 us
    ppermute x1, starting transfers between devices, per_device(): swapped = lax.ppermute(theirs, 'chan', swap)  2.92 us
  transfers between devices with their start and end apart: 14, of which 9 were waited for; matrix products, arithmetic and copies ran while one was open for 9% of the time, Pallas kernels for 5%

profile of v17, /device:TPU:31, one launch (start us, length us, event | category | flops | bytes accessed | tf_op | source)
XLA Modules:
  0.0 64.1 jit_solution(17081396735214663138)
XLA Ops:
  0.0 0.0 copy-start
  0.0 0.9 %copy-done = bf16[16,1,64,128]{3,2,1,0:T(8,128)(2,1)S(1)} copy-done((bf16[16,1,64,128]{3,2,1,0:T(8,128)(2,1)S(1)}, bf16[16,1,64,128]{3,2,1,0:T(8,128)(2,1)}, u32[]{:S(2)}) %copy-start) | copy-done | bytes 262168
  1.0 0.0 copy-start.2
  1.0 0.2 pack_rows.1
  1.1 7.0 %collective-permute-start = (bf16[1,20,16,128]{3,2,1,0:T(8,128)(2,1)S(1)}, bf16[1,20,16,128]{3,2,1,0:T(8,128)(2,1)S(1)}, u32[]{:S(2)}, u32[]{:S(2)}) collective-permute-start(bf16[1,20,16,128]{3,2,1,0:T(8,128)(2,1)S(1)} %get-tuple-element.16), channel_id=1, source_target_pairs={{0,4},{1,5},{2,6},{3,7},{4,0},{5,1},{6,2},{7,3},{8,12},{9,13},{10,... | collective-permute-start | bytes 245768 | tf_op jit(solution)/shard_map/ppermute | solution.py:245
  8.1 1.2 %collective-permute-start.1 = (bf16[1,20,16,128]{3,2,1,0:T(8,128)(2,1)S(1)}, bf16[1,20,16,128]{3,2,1,0:T(8,128)(2,1)S(1)}, u32[]{:S(2)}, u32[]{:S(2)}) collective-permute-start(bf16[1,20,16,128]{3,2,1,0:T(8,128)(2,1)S(1)} %get-tuple-element.17), channel_id=1, source_target_pairs={{0,2},{1,3},{2,4},{3,5},{4,6},{5,7},{6,0},{7,1},{8,10},{9,11},{10,... | collective-permute-start | bytes 245768 | tf_op jit(solution)/shard_map/ppermute | solution.py:245
  9.3 2.4 %collective-permute-start.2 = (bf16[1,20,16,128]{3,2,1,0:T(8,128)(2,1)S(1)}, bf16[1,20,16,128]{3,2,1,0:T(8,128)(2,1)S(1)}, u32[]{:S(2)}, u32[]{:S(2)}) collective-permute-start(bf16[1,20,16,128]{3,2,1,0:T(8,128)(2,1)S(1)} %get-tuple-element.18), channel_id=1, source_target_pairs={{0,6},{1,7},{2,0},{3,1},{4,2},{5,3},{6,4},{7,5},{8,14},{9,15},{10,... | collective-permute-start | bytes 245768 | tf_op jit(solution)/shard_map/ppermute | solution.py:245
  11.8 0.0 collective-permute-done
  11.8 2.3 %collective-permute-done.1 = bf16[1,20,16,128]{3,2,1,0:T(8,128)(2,1)S(1)} collective-permute-done((bf16[1,20,16,128]{3,2,1,0:T(8,128)(2,1)S(1)}, bf16[1,20,16,128]{3,2,1,0:T(8,128)(2,1)S(1)}, u32[]{:S(2)}, u32[]{:S(2)}) %collective-permute-start.1) | collective-permute-done | bytes 81952 | tf_op jit(solution)/shard_map/ppermute | solution.py:245
  14.1 2.3 %collective-permute-done.2 = bf16[1,20,16,128]{3,2,1,0:T(8,128)(2,1)S(1)} collective-permute-done((bf16[1,20,16,128]{3,2,1,0:T(8,128)(2,1)S(1)}, bf16[1,20,16,128]{3,2,1,0:T(8,128)(2,1)S(1)}, u32[]{:S(2)}, u32[]{:S(2)}) %collective-permute-start.2) | collective-permute-done | bytes 81952 | tf_op jit(solution)/shard_map/ppermute | solution.py:245
  16.4 0.6 collective-permute-start.6
  17.0 1.3 %collective-permute-start.4 = (bf16[4,12,16,128]{3,2,1,0:T(8,128)(2,1)S(1)}, bf16[4,12,16,128]{3,2,1,0:T(8,128)(2,1)S(1)}, u32[]{:S(2)}, u32[]{:S(2)}) collective-permute-start(bf16[4,12,16,128]{3,2,1,0:T(8,128)(2,1)S(1)} %constant_dynamic-slice_fusion.3), channel_id=1, source_target_pairs={{0,1},{1,0},{2,3},{3,2},{4,5},{5,4},{6,7},{7,6},{8,9},{9,8},{10,11... | collective-permute-start | bytes 589832 | tf_op jit(solution)/shard_map/ppermute | solution.py:250
  18.3 0.2 collective-permute-start.3
  18.5 0.0 copy-done.2
  18.5 0.7 %slice.17 = bf16[9,128,128]{2,1,0:T(8,128)(2,1)} slice(bf16[27,128,128]{2,1,0:T(8,128)(2,1)S(1)} %copy-done.2), slice={[9:18], [0:128], [0:128]} | slice | bytes 589824 | tf_op jit(solution)/shard_map/slice | solution.py:182
  19.3 0.6 copy.20
  19.9 0.5 reshape.24.later_ref.weight_ref
  20.4 0.0 copy-start.3
  20.5 0.6 %copy-done.3 = f32[128]{0:T(128)S(1)} copy-done((f32[128]{0:T(128)S(1)}, f32[128]{0:T(128)}, u32[]{:S(2)}) %copy-start.3) | copy-done | bytes 536
  21.1 0.1 copy.15.bias_ref
  21.2 1.2 %copy.13 = bf16[3,3,128,128]{2,0,3,1:T(4,128)(2,1)S(1)} copy(bf16[3,3,128,128]{3,2,1,0:T(8,128)(2,1)} %bitcast.27) | data formatting | bytes 589824 | tf_op jit(solution)/shard_map/squeeze | solution.py:182
  22.5 0.0 collective-permute-done.4.other_ref
  22.5 0.8 %first_own.1 = (f32[10,128,128]{2,1,0:T(8,128)S(1)}, s32[8,128]{1,0:T(8,128)S(1)}) custom-call(bf16[4,20,16,128]{3,2,1,0:T(8,128)(2,1)S(1)} %constant_dynamic-update-slice_fusion.kept_ref, bf16[4,12,16,128]{3,2,1,0:T(8,128)(2,1)S(1)} %collective-permute-done.4.other_ref, bf16[384,384]{1,0:T(8,128)(2,1)S(1)} %bitcast.22, ...), custom_call_target="tpu_custom_call" | custom-call | flops 377487360 | bytes 4000000 | tf_op jit(solution)/shard_map/first_own/pallas_call | solution.py:214
  23.3 0.5 slice.19
  24.5 0.3 collective-permute-done.6.kept_ref
  24.8 2.0 %collective-permute-start.7 = (bf16[4,12,16,128]{3,2,1,0:T(8,128)(2,1)S(1)}, bf16[4,12,16,128]{3,2,1,0:T(8,128)(2,1)S(1)}, u32[]{:S(2)}, u32[]{:S(2)}) collective-permute-start(bf16[4,12,16,128]{3,2,1,0:T(8,128)(2,1)S(1)} %constant_dynamic-slice_fusion.1), channel_id=1, source_target_pairs={{0,1},{1,0},{2,3},{3,2},{4,5},{5,4},{6,7},{7,6},{8,9},{9,8},{10,11... | collective-permute-start | bytes 589832 | tf_op jit(solution)/shard_map/ppermute | solution.py:250
  26.7 5.1 %collective-permute-done.3.kept_ref = bf16[4,20,16,128]{3,2,1,0:T(8,128)(2,1)S(1)} collective-permute-done((bf16[4,20,16,128]{3,2,1,0:T(8,128)(2,1)S(1)}, bf16[4,20,16,128]{3,2,1,0:T(8,128)(2,1)S(1)}, u32[]{:S(2)}, u32[]{:S(2)}) %collective-permute-start.3) | collective-permute-done | bytes 327712 | tf_op jit(solution)/shard_map/ppermute | solution.py:253
  31.8 1.0 %collective-permute-start.5 = (bf16[4,12,16,128]{3,2,1,0:T(8,128)(2,1)S(1)}, bf16[4,12,16,128]{3,2,1,0:T(8,128)(2,1)S(1)}, u32[]{:S(2)}, u32[]{:S(2)}) collective-permute-start(bf16[4,12,16,128]{3,2,1,0:T(8,128)(2,1)S(1)} %constant_dynamic-slice_fusion.2), channel_id=1, source_target_pairs={{0,1},{1,0},{2,3},{3,2},{4,5},{5,4},{6,7},{7,6},{8,9},{9,8},{10,11... | collective-permute-start | bytes 589832 | tf_op jit(solution)/shard_map/ppermute | solution.py:250
  32.8 0.0 collective-permute-done.7.other_ref
  32.8 0.8 %first_near.1.before_ref = f32[10,128,128]{2,1,0:T(8,128)S(1)} custom-call(bf16[4,20,16,128]{3,2,1,0:T(8,128)(2,1)S(1)} %collective-permute-done.6.kept_ref, bf16[4,12,16,128]{3,2,1,0:T(8,128)(2,1)S(1)} %collective-permute-done.7.other_ref, bf16[2,384,384]{2,1,0:T(8,128)(2,1)S(1)} %reshape.24.later_ref.weight_ref, ...), custom_call_target="tpu_custom_call" | custom-call | flops 377487360 | bytes 4000000 | tf_op jit(solution)/shard_map/first_near/pallas_call | solution.py:214
  33.6 0.3 collective-permute-done.5.other_ref
  33.9 0.8 %first_far.1.plane_ref = bf16[10,128,128]{2,1,0:T(8,128)(2,1)S(1)} custom-call(bf16[4,20,16,128]{3,2,1,0:T(8,128)(2,1)S(1)} %collective-permute-done.3.kept_ref, bf16[4,12,16,128]{3,2,1,0:T(8,128)(2,1)S(1)} %collective-permute-done.5.other_ref, bf16[2,384,384]{2,1,0:T(8,128)(2,1)S(1)} %reshape.24.later_ref.weight_ref, ...), custom_call_target="tpu_custom_call" | custom-call | flops 377487360 | bytes 4000000 | tf_op jit(solution)/shard_map/first_far/pallas_call | solution.py:214
  34.7 0.3 collective-permute-start.9
  34.9 0.1 collective-permute-start.8
  35.1 0.0 slice-start
  35.1 0.0 copy-start.1
  35.1 0.9 %slice-done = bf16[9,128,128]{2,1,0:T(8,128)(2,1)S(1)} async-done(((bf16[27,128,128]{2,1,0:T(8,128)(2,1)}), bf16[9,128,128]{2,1,0:T(8,128)(2,1)S(1)}, s32[]{:S(2)}) %slice-start) | async-done | bytes 294936 | tf_op jit(solution)/shard_map/slice | solution.py:182
  36.0 0.2 copy.18
  36.4 0.1 copy-done.1
  36.5 0.6 copy.21
  37.1 0.5 reshape.26.weight_ref
  37.6 0.0 copy-start.4
  37.6 0.6 %copy-done.4 = f32[128]{0:T(128)S(1)} copy-done((f32[128]{0:T(128)S(1)}, f32[128]{0:T(128)}, u32[]{:S(2)}) %copy-start.4) | copy-done | bytes 536
  38.3 0.1 copy.19.bias_ref
  38.4 0.7 %second_own.1.before_ref = f32[8,128,128]{2,1,0:T(8,128)S(1)} custom-call(bf16[10,128,128]{2,1,0:T(8,128)(2,1)S(1)} %first_far.1.plane_ref, bf16[384,384]{1,0:T(8,128)(2,1)S(1)} %bitcast.21), custom_call_target="tpu_custom_call" | custom-call | flops 301989888 | bytes 4000000 | tf_op jit(solution)/shard_map/second_own/pallas_call | solution.py:214
  39.1 8.9 %collective-permute-done.9.plane_ref = bf16[10,128,128]{2,1,0:T(8,128)(2,1)S(1)} collective-permute-done((bf16[10,128,128]{2,1,0:T(8,128)(2,1)S(1)}, bf16[10,128,128]{2,1,0:T(8,128)(2,1)S(1)}, u32[]{:S(2)}, u32[]{:S(2)}) %collective-permute-start.9) | collective-permute-done | bytes 327712 | tf_op jit(solution)/shard_map/ppermute | solution.py:253
  47.9 0.7 %second_far.1.before_ref = f32[8,128,128]{2,1,0:T(8,128)S(1)} custom-call(bf16[10,128,128]{2,1,0:T(8,128)(2,1)S(1)} %collective-permute-done.9.plane_ref, bf16[2,384,384]{2,1,0:T(8,128)(2,1)S(1)} %reshape.26.weight_ref, f32[8,128,128]{2,1,0:T(8,128)S(1)} %second_own.1.before_ref), custom_call_target="tpu_custom_call" | custom-call | flops 301989888 | bytes 4000000 | tf_op jit(solution)/shard_map/second_far/pallas_call | solution.py:214
  48.6 0.0 collective-permute-done.8.plane_ref
  48.6 0.7 %second_near.1 = (bf16[2,8,16,128]{3,2,1,0:T(8,128)(2,1)S(1)}, bf16[2,8,16,128]{3,2,1,0:T(8,128)(2,1)S(1)}, bf16[2,8,16,128]{3,2,1,0:T(8,128)(2,1)S(1)}, bf16[2,8,16,128]{3,2,1,0:T(8,128)(2,1)S(1)}) custom-call(bf16[10,128,128]{2,1,0:T(8,128)(2,1)S(1)} %collective-permute-done.8.plane_ref, bf16[2,384,384]{2,1,0:T(8,128)(2,1)S(1)} %reshape.26.weight_ref, ...), custom_call_target="tpu_custom_call" | custom-call | flops 301989888 | bytes 4000000 | tf_op jit(solution)/shard_map/second_near/pallas_call | solution.py:214
  49.3 4.1 %collective-permute-start.10 = (bf16[2,8,16,128]{3,2,1,0:T(8,128)(2,1)S(1)}, bf16[2,8,16,128]{3,2,1,0:T(8,128)(2,1)S(1)}, u32[]{:S(2)}, u32[]{:S(2)}) collective-permute-start(bf16[2,8,16,128]{3,2,1,0:T(8,128)(2,1)S(1)} %get-tuple-element.22), channel_id=1, source_target_pairs={{0,4},{1,5},{2,6},{3,7},{4,0},{5,1},{6,2},{7,3},{8,12},{9,13},{10,... | collective-permute-start | bytes 196616 | tf_op jit(solution)/shard_map/ppermute | solution.py:303
  53.4 1.9 %collective-permute-start.11 = (bf16[2,8,16,128]{3,2,1,0:T(8,128)(2,1)S(1)}, bf16[2,8,16,128]{3,2,1,0:T(8,128)(2,1)S(1)}, u32[]{:S(2)}, u32[]{:S(2)}) collective-permute-start(bf16[2,8,16,128]{3,2,1,0:T(8,128)(2,1)S(1)} %get-tuple-element.23), channel_id=1, source_target_pairs={{0,2},{1,3},{2,4},{3,5},{4,6},{5,7},{6,0},{7,1},{8,10},{9,11},{10,... | collective-permute-start | bytes 196616 | tf_op jit(solution)/shard_map/ppermute | solution.py:303
  55.3 1.8 %collective-permute-start.12 = (bf16[2,8,16,128]{3,2,1,0:T(8,128)(2,1)S(1)}, bf16[2,8,16,128]{3,2,1,0:T(8,128)(2,1)S(1)}, u32[]{:S(2)}, u32[]{:S(2)}) collective-permute-start(bf16[2,8,16,128]{3,2,1,0:T(8,128)(2,1)S(1)} %get-tuple-element.24), channel_id=1, source_target_pairs={{0,6},{1,7},{2,0},{3,1},{4,2},{5,3},{6,4},{7,5},{8,14},{9,15},{10,... | collective-permute-start | bytes 196616 | tf_op jit(solution)/shard_map/ppermute | solution.py:303
  57.1 0.0 collective-permute-done.10.refs_2_
  57.1 2.0 %collective-permute-done.11.refs_1_ = bf16[2,8,16,128]{3,2,1,0:T(8,128)(2,1)S(1)} collective-permute-done((bf16[2,8,16,128]{3,2,1,0:T(8,128)(2,1)S(1)}, bf16[2,8,16,128]{3,2,1,0:T(8,128)(2,1)S(1)}, u32[]{:S(2)}, u32[]{:S(2)}) %collective-permute-start.11) | collective-permute-done | bytes 65568 | tf_op jit(solution)/shard_map/ppermute | solution.py:303
  59.1 0.2 collective-permute-done.12.refs_3_
  59.3 2.9 %collective-permute-start.13 = (bf16[4,8,16,128]{3,2,1,0:T(8,128)(2,1)S(1)}, bf16[4,8,16,128]{3,2,1,0:T(8,128)(2,1)S(1)}, u32[]{:S(2)}, u32[]{:S(2)}) collective-permute-start(bf16[4,8,16,128]{3,2,1,0:T(8,128)(2,1)S(1)} %dynamic-slice_dynamic-update-slice_fusion), channel_id=1, source_target_pairs={{0,1},{1,0},{2,3},{3,2},{4,5},{5,4},{6,7},{7,6},{8,9},{9,8},{10,11... | collective-permute-start | bytes 393224 | tf_op jit(solution)/shard_map/ppermute | solution.py:306
  62.2 1.0 %collective-permute-done.13.swapped_ref = bf16[4,8,16,128]{3,2,1,0:T(8,128)(2,1)S(1)} collective-permute-done((bf16[4,8,16,128]{3,2,1,0:T(8,128)(2,1)S(1)}, bf16[4,8,16,128]{3,2,1,0:T(8,128)(2,1)S(1)}, u32[]{:S(2)}, u32[]{:S(2)}) %collective-permute-start.13) | collective-permute-done | bytes 131104 | tf_op jit(solution)/shard_map/ppermute | solution.py:306
  63.2 0.8 %unpack_rows.1 = bf16[16,1,64,128]{3,2,1,0:T(8,128)(2,1)} custom-call(bf16[4,8,16,128]{3,2,1,0:T(8,128)(2,1)S(1)} %collective-permute-done.13.swapped_ref, bf16[2,8,16,128]{3,2,1,0:T(8,128)(2,1)S(1)} %get-tuple-element.21.refs_0_, bf16[2,8,16,128]{3,2,1,0:T(8,128)(2,1)S(1)} %collective-permute-done.11.refs_1_, ...), custom_call_target="tpu_custom_call" | custom-call | tf_op jit(solution)/shard_map/unpack_rows/pallas_call | solution.py:214
  (17 shorter events, 0.4 us)
Async XLA Ops:
  0.0 0.9 %copy-start = (bf16[16,1,64,128]{3,2,1,0:T(8,128)(2,1)S(1)}, bf16[16,1,64,128]{3,2,1,0:T(8,128)(2,1)}, u32[]{:S(2)}) copy-start(bf16[16,1,64,128]{3,2,1,0:T(8,128)(2,1)} %volume_ref.1) | copy-start | bytes 786436
  1.0 17.6 %copy-start.2 = (bf16[27,128,128]{2,1,0:T(8,128)(2,1)S(1)}, bf16[27,128,128]{2,1,0:T(8,128)(2,1)}, u32[]{:S(2)}) copy-start(bf16[27,128,128]{2,1,0:T(8,128)(2,1)} %param.6) | copy-start | bytes 2654212
  1.1 10.6 %collective-permute-start = (bf16[1,20,16,128]{3,2,1,0:T(8,128)(2,1)S(1)}, bf16[1,20,16,128]{3,2,1,0:T(8,128)(2,1)S(1)}, u32[]{:S(2)}, u32[]{:S(2)}) collective-permute-start(bf16[1,20,16,128]{3,2,1,0:T(8,128)(2,1)S(1)} %get-tuple-element.16), channel_id=1, source_target_pairs={{0,4},{1,5},{2,6},{3,7},{4,0},{5,1},{6,2},{7,3},{8,12},{9,13},{10,... | collective-permute-start | bytes 245768 | tf_op jit(solution)/shard_map/ppermute | solution.py:245
  8.1 6.0 %collective-permute-start.1 = (bf16[1,20,16,128]{3,2,1,0:T(8,128)(2,1)S(1)}, bf16[1,20,16,128]{3,2,1,0:T(8,128)(2,1)S(1)}, u32[]{:S(2)}, u32[]{:S(2)}) collective-permute-start(bf16[1,20,16,128]{3,2,1,0:T(8,128)(2,1)S(1)} %get-tuple-element.17), channel_id=1, source_target_pairs={{0,2},{1,3},{2,4},{3,5},{4,6},{5,7},{6,0},{7,1},{8,10},{9,11},{10,... | collective-permute-start | bytes 245768 | tf_op jit(solution)/shard_map/ppermute | solution.py:245
  9.3 7.1 %collective-permute-start.2 = (bf16[1,20,16,128]{3,2,1,0:T(8,128)(2,1)S(1)}, bf16[1,20,16,128]{3,2,1,0:T(8,128)(2,1)S(1)}, u32[]{:S(2)}, u32[]{:S(2)}) collective-permute-start(bf16[1,20,16,128]{3,2,1,0:T(8,128)(2,1)S(1)} %get-tuple-element.18), channel_id=1, source_target_pairs={{0,6},{1,7},{2,0},{3,1},{4,2},{5,3},{6,4},{7,5},{8,14},{9,15},{10,... | collective-permute-start | bytes 245768 | tf_op jit(solution)/shard_map/ppermute | solution.py:245
  16.4 8.3 %collective-permute-start.6 = (bf16[4,20,16,128]{3,2,1,0:T(8,128)(2,1)S(1)}, bf16[4,20,16,128]{3,2,1,0:T(8,128)(2,1)S(1)}, u32[]{:S(2)}, u32[]{:S(2)}) collective-permute-start(bf16[4,20,16,128]{3,2,1,0:T(8,128)(2,1)S(1)} %constant_dynamic-update-slice_fusion.kept_ref), channel_id=1, source_target_pairs={{0,8},{8,0},{16,24},{24,16},{32,40},{40,32},{48,56},{56,48},{64,72... | collective-permute-start | bytes 983048 | tf_op jit(solution)/shard_map/ppermute | solution.py:253
  17.0 5.5 %collective-permute-start.4 = (bf16[4,12,16,128]{3,2,1,0:T(8,128)(2,1)S(1)}, bf16[4,12,16,128]{3,2,1,0:T(8,128)(2,1)S(1)}, u32[]{:S(2)}, u32[]{:S(2)}) collective-permute-start(bf16[4,12,16,128]{3,2,1,0:T(8,128)(2,1)S(1)} %constant_dynamic-slice_fusion.3), channel_id=1, source_target_pairs={{0,1},{1,0},{2,3},{3,2},{4,5},{5,4},{6,7},{7,6},{8,9},{9,8},{10,11... | collective-permute-start | bytes 589832 | tf_op jit(solution)/shard_map/ppermute | solution.py:250
  18.3 13.5 %collective-permute-start.3 = (bf16[4,20,16,128]{3,2,1,0:T(8,128)(2,1)S(1)}, bf16[4,20,16,128]{3,2,1,0:T(8,128)(2,1)S(1)}, u32[]{:S(2)}, u32[]{:S(2)}) collective-permute-start(bf16[4,20,16,128]{3,2,1,0:T(8,128)(2,1)S(1)} %constant_dynamic-update-slice_fusion.kept_ref), channel_id=1, source_target_pairs={{0,1},{1,0},{2,3},{3,2},{4,5},{5,4},{6,7},{7,6},{8,16},{9,17},{10,... | collective-permute-start | bytes 983048 | tf_op jit(solution)/shard_map/ppermute | solution.py:253
  20.4 0.7 %copy-start.3 = (f32[128]{0:T(128)S(1)}, f32[128]{0:T(128)}, u32[]{:S(2)}) copy-start(f32[128]{0:T(128)} %param.7) | copy-start | bytes 1540
  24.8 8.0 %collective-permute-start.7 = (bf16[4,12,16,128]{3,2,1,0:T(8,128)(2,1)S(1)}, bf16[4,12,16,128]{3,2,1,0:T(8,128)(2,1)S(1)}, u32[]{:S(2)}, u32[]{:S(2)}) collective-permute-start(bf16[4,12,16,128]{3,2,1,0:T(8,128)(2,1)S(1)} %constant_dynamic-slice_fusion.1), channel_id=1, source_target_pairs={{0,1},{1,0},{2,3},{3,2},{4,5},{5,4},{6,7},{7,6},{8,9},{9,8},{10,11... | collective-permute-start | bytes 589832 | tf_op jit(solution)/shard_map/ppermute | solution.py:250
  31.8 2.0 %collective-permute-start.5 = (bf16[4,12,16,128]{3,2,1,0:T(8,128)(2,1)S(1)}, bf16[4,12,16,128]{3,2,1,0:T(8,128)(2,1)S(1)}, u32[]{:S(2)}, u32[]{:S(2)}) collective-permute-start(bf16[4,12,16,128]{3,2,1,0:T(8,128)(2,1)S(1)} %constant_dynamic-slice_fusion.2), channel_id=1, source_target_pairs={{0,1},{1,0},{2,3},{3,2},{4,5},{5,4},{6,7},{7,6},{8,9},{9,8},{10,11... | collective-permute-start | bytes 589832 | tf_op jit(solution)/shard_map/ppermute | solution.py:250
  34.7 13.2 %collective-permute-start.9 = (bf16[10,128,128]{2,1,0:T(8,128)(2,1)S(1)}, bf16[10,128,128]{2,1,0:T(8,128)(2,1)S(1)}, u32[]{:S(2)}, u32[]{:S(2)}) collective-permute-start(bf16[10,128,128]{2,1,0:T(8,128)(2,1)S(1)} %first_far.1.plane_ref), channel_id=1, source_target_pairs={{0,1},{1,0},{2,3},{3,2},{4,5},{5,4},{6,7},{7,6},{8,16},{9,17},{10,... | collective-permute-start | bytes 983048 | tf_op jit(solution)/shard_map/ppermute | solution.py:253
  34.9 13.7 %collective-permute-start.8 = (bf16[10,128,128]{2,1,0:T(8,128)(2,1)S(1)}, bf16[10,128,128]{2,1,0:T(8,128)(2,1)S(1)}, u32[]{:S(2)}, u32[]{:S(2)}) collective-permute-start(bf16[10,128,128]{2,1,0:T(8,128)(2,1)S(1)} %first_far.1.plane_ref), channel_id=1, source_target_pairs={{0,8},{8,0},{16,24},{24,16},{32,40},{40,32},{48,56},{56,48},{64,72... | collective-permute-start | bytes 983048 | tf_op jit(solution)/shard_map/ppermute | solution.py:253
  35.1 1.0 %slice-start = ((bf16[27,128,128]{2,1,0:T(8,128)(2,1)}), bf16[9,128,128]{2,1,0:T(8,128)(2,1)S(1)}, s32[]{:S(2)}) async-start(bf16[27,128,128]{2,1,0:T(8,128)(2,1)} %param.8), calls=%async_computation | async-start | bytes 589824 | tf_op jit(solution)/shard_map/slice | solution.py:182
  35.1 1.3 %copy-start.1 = (bf16[27,128,128]{2,1,0:T(8,128)(2,1)S(1)}, bf16[27,128,128]{2,1,0:T(8,128)(2,1)}, u32[]{:S(2)}) copy-start(bf16[27,128,128]{2,1,0:T(8,128)(2,1)} %param.8) | copy-start | bytes 2654212
  37.6 0.7 %copy-start.4 = (f32[128]{0:T(128)S(1)}, f32[128]{0:T(128)}, u32[]{:S(2)}) copy-start(f32[128]{0:T(128)} %param.9) | copy-start | bytes 1540
  49.3 7.7 %collective-permute-start.10 = (bf16[2,8,16,128]{3,2,1,0:T(8,128)(2,1)S(1)}, bf16[2,8,16,128]{3,2,1,0:T(8,128)(2,1)S(1)}, u32[]{:S(2)}, u32[]{:S(2)}) collective-permute-start(bf16[2,8,16,128]{3,2,1,0:T(8,128)(2,1)S(1)} %get-tuple-element.22), channel_id=1, source_target_pairs={{0,4},{1,5},{2,6},{3,7},{4,0},{5,1},{6,2},{7,3},{8,12},{9,13},{10,... | collective-permute-start | bytes 196616 | tf_op jit(solution)/shard_map/ppermute | solution.py:303
  53.4 5.7 %collective-permute-start.11 = (bf16[2,8,16,128]{3,2,1,0:T(8,128)(2,1)S(1)}, bf16[2,8,16,128]{3,2,1,0:T(8,128)(2,1)S(1)}, u32[]{:S(2)}, u32[]{:S(2)}) collective-permute-start(bf16[2,8,16,128]{3,2,1,0:T(8,128)(2,1)S(1)} %get-tuple-element.23), channel_id=1, source_target_pairs={{0,2},{1,3},{2,4},{3,5},{4,6},{5,7},{6,0},{7,1},{8,10},{9,11},{10,... | collective-permute-start | bytes 196616 | tf_op jit(solution)/shard_map/ppermute | solution.py:303
  55.3 4.0 %collective-permute-start.12 = (bf16[2,8,16,128]{3,2,1,0:T(8,128)(2,1)S(1)}, bf16[2,8,16,128]{3,2,1,0:T(8,128)(2,1)S(1)}, u32[]{:S(2)}, u32[]{:S(2)}) collective-permute-start(bf16[2,8,16,128]{3,2,1,0:T(8,128)(2,1)S(1)} %get-tuple-element.24), channel_id=1, source_target_pairs={{0,6},{1,7},{2,0},{3,1},{4,2},{5,3},{6,4},{7,5},{8,14},{9,15},{10,... | collective-permute-start | bytes 196616 | tf_op jit(solution)/shard_map/ppermute | solution.py:303
  59.3 3.9 %collective-permute-start.13 = (bf16[4,8,16,128]{3,2,1,0:T(8,128)(2,1)S(1)}, bf16[4,8,16,128]{3,2,1,0:T(8,128)(2,1)S(1)}, u32[]{:S(2)}, u32[]{:S(2)}) collective-permute-start(bf16[4,8,16,128]{3,2,1,0:T(8,128)(2,1)S(1)} %dynamic-slice_dynamic-update-slice_fusion), channel_id=1, source_target_pairs={{0,1},{1,0},{2,3},{3,2},{4,5},{5,4},{6,7},{7,6},{8,9},{9,8},{10,11... | collective-permute-start | bytes 393224 | tf_op jit(solution)/shard_map/ppermute | solution.py:306
